TPU v7x, 512 devices: a whole 4x4x16 slice. The times are simulated.
512 devices in a mesh: gx: 32 (over z, core), gy: 4 (over x), col: 4 (over y).
Axes of the slice: x: 4, y: 4, z: 16, core: 2. Of those that a mesh axis runs over, the one named last changes fastest.
Arguments:
- divergence: float32 [24, 24, 6144], P('gy', 'col', 'gx'), may hold values from -15 to 15
- elem_size: float32 [3, 16384], P(None, ('gx', 'gy', 'col')), may hold values from 1.5 to 4
- helm_diag: float32 [32, 32, 8192], P('gy', 'col', 'gx'), may hold values from 0.02 to 0.1
- fdm_vectors: float32 [3, 8, 8, 16384], P(None, None, None, ('gx', 'gy', 'col')), may hold values from -2 to 2
- fdm_values: float32 [3, 8, 16384], P(None, None, ('gx', 'gy', 'col')), may hold values from 0.3 to 3
- coarse_rows: float32 [16384, 512], P(('gx', 'gy', 'col')), may hold values from -3 to 56, as said below
- axial_link: float32 [32, 4, 4], P('gx', 'gy', 'col'), may hold values from 3 to 9
Outputs:
- pressure: float32 [24, 24, 6144], P('gy', 'col', 'gx')
- residual: float32 [24, 24, 6144], P('gy', 'col', 'gx')
Inputs may be any that keep to these rules, and one draw needn't show every extreme that they name: `coarse_rows`: for every slab s, rows s * 512 to s * 512 + 511 form a symmetric 512 x 512 matrix.
All inputs are finite; a program needn't handle non-finite values.
Results may differ from a plain program's by a relative error of at most 0.0023.
Values sent between devices are 32-bit elements; how exact they have to be, the bound alone decides.
No kernel may reach another device: no remote copies, remote signals or barrier semaphores. Data moves between devices by JAX's collectives and lax.ppermute only.
A program may use at most 64 MiB of HBM per device.

v0:
```python
import jax
import jax.numpy as jnp
import numpy as np
from jax import lax
from jax.sharding import PartitionSpec as P

EB = 1
EC = 1
EA = 32
ITERS = 2
CHEB = 6


LOBATTO_NODES = [
    -1.0,
    -0.8717401485096066,
    -0.5917001814331423,
    -0.2092992179024789,
    0.2092992179024789,
    0.5917001814331423,
    0.8717401485096066,
    1.0,
]
GAUSS_NODES = [
    -0.932469514203152,
    -0.6612093864662645,
    -0.2386191860831909,
    0.2386191860831909,
    0.6612093864662645,
    0.932469514203152,
]
GAUSS_WEIGHTS = [
    0.1713244923791704,
    0.3607615730481386,
    0.467913934572691,
    0.467913934572691,
    0.3607615730481386,
    0.1713244923791704,
]
SPECTRUM_LOW = 8.0
SPECTRUM_HIGH = 90.0
HIGHEST = lax.Precision.HIGHEST


def padded_2(cells, sides, width, closed):
    for axis, dim in sides:
        count = lax.axis_size(axis)
        ends = count if closed else count - 1
        head = lax.slice_in_dim(cells, 0, width, axis=dim)
        tail = lax.slice_in_dim(cells, cells.shape[dim] - width, cells.shape[dim], axis=dim)
        cells = jnp.concatenate(
            [
                lax.ppermute(tail, axis, [(i, (i + 1) % count) for i in range(ends)]),
                cells,
                lax.ppermute(head, axis, [((i + 1) % count, i) for i in range(ends)]),
            ],
            axis=dim,
        )
    return cells


def basis_tables():
    lobatto = np.array(LOBATTO_NODES)
    points = np.array(GAUSS_NODES)
    interp = np.ones((6, 8))
    slopes = np.zeros((6, 8))
    for p in range(6):
        for m in range(8):
            product = 1.0
            for q in range(8):
                if q != m:
                    product = product * (points[p] - lobatto[q]) / (lobatto[m] - lobatto[q])
            interp[p, m] = product
            running = 0.0
            for q in range(8):
                if q != m:
                    factor = 1.0 / (lobatto[m] - lobatto[q])
                    for k in range(8):
                        if k != m and k != q:
                            factor = factor * (points[p] - lobatto[k]) / (lobatto[m] - lobatto[k])
                    running = running + factor
            slopes[p, m] = running
    return (jnp.asarray(interp, jnp.float32), jnp.asarray(slopes, jnp.float32))


def block_table(table, copies):
    return jnp.kron(jnp.eye(copies, dtype=jnp.float32), table)


def window_table(copies, inner, stride):
    row_ids = jnp.arange(copies * inner)
    target = row_ids // inner * stride + row_ids % inner
    col_ids = jnp.arange(copies * stride + inner - stride)
    return (target[:, None] == col_ids[None, :]).astype(jnp.float32)


def owner_table(copies):
    row_ids = jnp.arange(6 * copies)
    col_ids = jnp.arange(copies)
    return ((row_ids // 6)[:, None] == col_ids[None, :]).astype(jnp.float32)


def apply_side(field, matrix, which):
    if which == 0:
        return jnp.einsum("pb,...bcz->...pcz", matrix, field, precision=HIGHEST)
    if which == 1:
        return jnp.einsum("pc,...bcz->...bpz", matrix, field, precision=HIGHEST)
    return jnp.einsum("pz,...bcz->...bcp", matrix, field, precision=HIGHEST)


def expand_nodes(values_in):
    return jnp.repeat(jnp.repeat(jnp.repeat(values_in, 6, -3), 6, -2), 6, -1)


def wall_mask(padded, axis_at):
    position = lax.axis_index("gy")
    devices_gy = lax.axis_size("gy")
    length = padded.shape[axis_at]
    places = lax.broadcasted_iota(jnp.int32, padded.shape, axis_at)
    lower_cut = (places == 0) & (position == 0)
    upper_cut = (places == length - 1) & (position == devices_gy - 1)
    return jnp.where(lower_cut | upper_cut, jnp.zeros_like(padded), padded)


def fold_rims(padded, axis_at, skip):
    length = padded.shape[axis_at]
    lower_rim = lax.slice_in_dim(padded, 0, 1, axis=axis_at)
    upper_rim = lax.slice_in_dim(padded, length - 1, length, axis=axis_at)
    kept_part = lax.slice_in_dim(padded, skip, length - skip, axis=axis_at)
    inner_len = length - 2 * skip
    head_row = lax.slice_in_dim(kept_part, 0, 1, axis=axis_at) + lower_rim
    tail_row = lax.slice_in_dim(kept_part, inner_len - 1, inner_len, axis=axis_at) + upper_rim
    middle = lax.slice_in_dim(kept_part, 1, inner_len - 1, axis=axis_at)
    return jnp.concatenate([head_row, middle, tail_row], axis=axis_at)


def share_nodes(unique):
    padded = padded_2(unique, (("gx", 3),), 1, True)
    unique = fold_rims(padded, 3, 1)
    padded = padded_2(unique, (("gy", 1),), 1, False)
    unique = fold_rims(padded, 1, 1)
    padded = padded_2(unique, (("col", 2),), 1, True)
    return fold_rims(padded, 2, 1)


def chebyshev_solve(source, operator):
    center = (SPECTRUM_HIGH + SPECTRUM_LOW) / 2.0
    spread = (SPECTRUM_HIGH - SPECTRUM_LOW) / 2.0
    ratio_cs = center / spread
    rho_now = 1.0 / ratio_cs
    solution = jnp.zeros_like(source)
    remainder = source
    update = source / center
    for sweep_at in range(CHEB):
        solution = solution + update
        remainder = remainder - operator(update)
        rho_next = 1.0 / (2.0 * ratio_cs - rho_now)
        update = rho_next * rho_now * update + 2.0 * rho_next / spread * remainder
        rho_now = rho_next
    return solution + update


def local(divergence, elem_size, helm_diag, fdm_vectors, fdm_values, coarse_rows, axial_link):
    interp, slopes = basis_tables()
    counts = (EB, EC, EA)
    interp_side = [block_table(interp, counts[w]) for w in range(3)]
    slopes_side = [block_table(slopes, counts[w]) for w in range(3)]
    merge_side = [window_table(counts[w], 8, 7) for w in range(3)]
    pick_side = [window_table(counts[w], 8, 6) for w in range(3)]
    owner_side = [owner_table(counts[w]) for w in range(3)]
    sizes_local = elem_size.reshape(3, EB, EC, EA)
    volume = sizes_local[0] * sizes_local[1] * sizes_local[2] / 8.0
    weights_1d = jnp.asarray(GAUSS_WEIGHTS, jnp.float32)
    weights = (
        jnp.tile(weights_1d, EB)[:, None, None]
        * jnp.tile(weights_1d, EC)[None, :, None]
        * jnp.tile(weights_1d, EA)[None, None, :]
        * expand_nodes(volume)
    )
    factors = 2.0 / expand_nodes(sizes_local)
    link_local = axial_link.reshape(EB, EC)

    def local_assemble(field):
        for which in range(3):
            field = apply_side(field, merge_side[which].T, which)
        return field

    helm_total = share_nodes(local_assemble(helm_diag[None]))

    def coarse_apply(vector):
        dense_part = jnp.dot(
            coarse_rows,
            lax.all_gather(vector, ("gy", "col"), axis=0, tiled=True),
            precision=HIGHEST,
        )
        vector_grid = vector.reshape(EB, EC, EA)
        face_pair = jnp.stack([vector_grid[:, :, 0], link_local * vector_grid[:, :, EA - 1]])
        padded = padded_2(face_pair, (("gx", 0),), 1, True)
        result = dense_part.reshape(EB, EC, EA)
        result = result.at[:, :, 0].add(-padded[0])
        result = result.at[:, :, EA - 1].add(-(link_local * padded[3]))
        return result.reshape(-1)

    pressure = jnp.zeros_like(divergence)
    residual = divergence
    direction = divergence
    previous = jnp.float32(1.0)
    for turn in range(ITERS):
        extended = padded_2(residual, (("gx", 2), ("gy", 0), ("col", 1)), 1, True)
        extended = wall_mask(extended, 0)
        boxes = extended
        for schwarz_which in range(3):
            boxes = apply_side(boxes, pick_side[schwarz_which], schwarz_which)
        boxes = (
            boxes.reshape(EB, 8, EC, 8, EA, 8)
            .transpose(1, 3, 5, 0, 2, 4)
            .reshape(8, 8, 8, EB * EC * EA)
        )
        modes = jnp.einsum("ime,ijke->mjke", fdm_vectors[0], boxes, precision=HIGHEST)
        modes = jnp.einsum("jne,mjke->mnke", fdm_vectors[1], modes, precision=HIGHEST)
        modes = jnp.einsum("kle,mnke->mnle", fdm_vectors[2], modes, precision=HIGHEST)
        denominator = (
            fdm_values[0][:, None, None, :]
            + fdm_values[1][None, :, None, :]
            + fdm_values[2][None, None, :, :]
        )
        modes = modes / denominator
        local_part = jnp.einsum("ime,mnle->inle", fdm_vectors[0], modes, precision=HIGHEST)
        local_part = jnp.einsum("jne,inle->ijle", fdm_vectors[1], local_part, precision=HIGHEST)
        local_part = jnp.einsum("kle,ijle->ijke", fdm_vectors[2], local_part, precision=HIGHEST)
        returned_box = (
            local_part.reshape(8, 8, 8, EB, EC, EA)
            .transpose(3, 0, 4, 1, 5, 2)
            .reshape(8 * EB, 8 * EC, 8 * EA)
        )
        for schwarz_which in range(3):
            returned_box = apply_side(returned_box, pick_side[schwarz_which].T, schwarz_which)
        returned = padded_2(returned_box, (("gx", 2), ("gy", 0), ("col", 1)), 1, True)
        returned = wall_mask(returned, 0)
        for axis_at in (0, 1, 2):
            returned = fold_rims(returned, axis_at, 2)
        sums = residual
        for precondition_which in range(3):
            sums = apply_side(sums, owner_side[precondition_which].T, precondition_which)
        coarse = chebyshev_solve(sums.reshape(-1), coarse_apply).reshape(EB, EC, EA)
        for precondition_which in range(3):
            coarse = apply_side(coarse, owner_side[precondition_which], precondition_which)
        precond = returned + coarse
        r_dot_z = lax.psum(jnp.sum(residual * precond), ("gx", "gy", "col"))
        if turn == 0:
            direction = precond
        else:
            direction = precond + r_dot_z / previous * direction
        scaled = weights * direction
        gradients = []
        for comp in range(3):
            schur_field = scaled * factors[comp]
            for schur_which in range(3):
                table = (
                    slopes_side[schur_which] if schur_which == comp else interp_side[schur_which]
                )
                schur_field = apply_side(schur_field, table.T, schur_which)
            gradients.append(schur_field)
        schur_unique = share_nodes(local_assemble(jnp.stack(gradients))) / helm_total
        unique = schur_unique
        for local_which in range(3):
            unique = apply_side(unique, merge_side[local_which], local_which)
        combined = None
        for comp in range(3):
            schur_field = unique[comp]
            for schur_which in range(3):
                table = (
                    slopes_side[schur_which] if schur_which == comp else interp_side[schur_which]
                )
                schur_field = apply_side(schur_field, table, schur_which)
            if combined is None:
                combined = factors[comp] * schur_field
            else:
                combined = combined + factors[comp] * schur_field
        image = weights * combined
        curvature = lax.psum(jnp.sum(direction * image), ("gx", "gy", "col"))
        step_len = r_dot_z / curvature
        pressure = pressure + step_len * direction
        residual = residual - step_len * image
        previous = r_dot_z
    return (pressure, residual)


def solution(mesh):
    in_specs = (
        P("gy", "col", "gx"),
        P(None, ("gx", "gy", "col")),
        P("gy", "col", "gx"),
        P(None, None, None, ("gx", "gy", "col")),
        P(None, None, ("gx", "gy", "col")),
        P(("gx", "gy", "col"), None),
        P("gx", "gy", "col"),
    )
    out_specs = (P("gy", "col", "gx"), P("gy", "col", "gx"))
    return jax.shard_map(local, mesh=mesh, in_specs=in_specs, out_specs=out_specs, check_vma=False)
```

profile of v0, /device:TPU:1, one launch (start us, length us, event | category | flops | bytes accessed | tf_op | source)
XLA Modules:
  0.0 1078.8 jit_solution(8407912104866225846)
XLA Ops:
  5.8 3.8 collective-permute-start.12
  9.6 4.0 collective-permute-start.13
  15.0 3.5 collective-permute-start.1
  30.1 34.0 %all-reduce = f32[512]{0:T(512)} all-reduce(f32[512]{0:T(512)S(1)} %get-tuple-element.435), channel_id=1, replica_groups=mesh['gx'=32,'gy'=4,'col'=4] {'gy','col'}, use_global_device_ids=true, to_apply=%add | all-reduce | flops 512 | bytes 4096
  69.9 2.8 broadcast_multiply_fusion.1
  72.8 4.0 reshape.1357
  80.6 8.0 collective-permute-start.31
  92.6 28.5 %all-reduce.1 = f32[512]{0:T(512)S(1)} all-reduce(f32[512]{0:T(512)S(1)} %fusion.231), channel_id=1, replica_groups=mesh['gx'=32,'gy'=4,'col'=4] {'gy','col'}, use_global_device_ids=true, to_apply=%add.1 | all-reduce | flops 512 | bytes 4096
  122.4 3.3 collective-permute-start.14
  125.7 4.3 collective-permute-done.14
  130.0 3.5 collective-permute-start.15
  136.9 30.2 %all-reduce.2 = f32[512]{0:T(512)S(1)} all-reduce(f32[512]{0:T(512)S(1)} %get-tuple-element.321), channel_id=1, replica_groups=mesh['gx'=32,'gy'=4,'col'=4] {'gy','col'}, use_global_device_ids=true, to_apply=%add.2 | all-reduce | flops 512 | bytes 4096
  168.5 6.3 collective-permute-start.16
  176.4 3.5 collective-permute-start.17
  182.8 28.5 %all-reduce.3 = f32[512]{0:T(512)S(1)} all-reduce(f32[512]{0:T(512)S(1)} %fusion.233), channel_id=1, replica_groups=mesh['gx'=32,'gy'=4,'col'=4] {'gy','col'}, use_global_device_ids=true, to_apply=%add.3 | all-reduce | flops 512 | bytes 4096
  212.6 6.0 collective-permute-start.18
  220.3 3.5 collective-permute-start.19
  226.6 30.2 %all-reduce.4 = f32[512]{0:T(512)S(1)} all-reduce(f32[512]{0:T(512)S(1)} %get-tuple-element.316), channel_id=1, replica_groups=mesh['gx'=32,'gy'=4,'col'=4] {'gy','col'}, use_global_device_ids=true, to_apply=%add.4 | all-reduce | flops 512 | bytes 4096
  258.1 6.3 collective-permute-start.20
  266.1 3.5 collective-permute-start.21
  272.4 28.5 %all-reduce.5 = f32[512]{0:T(512)S(1)} all-reduce(f32[512]{0:T(512)S(1)} %fusion.226), channel_id=1, replica_groups=mesh['gx'=32,'gy'=4,'col'=4] {'gy','col'}, use_global_device_ids=true, to_apply=%add.5 | all-reduce | flops 512 | bytes 4096
  302.2 6.0 collective-permute-start.22
  309.9 3.5 collective-permute-start.23
  318.8 3.4 collective-permute-start.2
  325.4 4.0 collective-permute-start.5
  332.4 2.6 collective-permute-done.4
  339.1 3.4 convolution_bitcast_fusion.11
  353.4 3.0 collective-permute-start.7
  359.8 3.4 collective-permute-start.8
  367.4 3.4 collective-permute-start.10
  376.8 4.3 collective-permute-start.24
  385.2 2.8 collective-permute-start.26
  388.1 2.4 collective-permute-start.34
  390.6 4.1 collective-permute-start.35
  396.1 3.2 collective-permute-done.27
  401.4 4.6 collective-permute-start.29
  411.0 105.5 %all-reduce.12 = (f32[]{:T(128)}, f32[]{:T(128)}) all-reduce(f32[]{:T(128)} %get-tuple-element.291, f32[]{:T(128)} %get-tuple-element.290), channel_id=1, replica_groups=mesh['gx'=32,'gy'=4,'col'=4] {'gx','gy','col'}, use_global_device_ids=true, to_apply=%region_1.2 | all-reduce | flops 2 | bytes 16 | tf_op jit(solution)/shard_map/psum | solution.py:249
  518.4 30.3 %all-reduce.6 = f32[512]{0:T(512)S(1)} all-reduce(f32[512]{0:T(512)S(1)} %get-tuple-element.421), channel_id=1, replica_groups=mesh['gx'=32,'gy'=4,'col'=4] {'gy','col'}, use_global_device_ids=true, to_apply=%add.6 | all-reduce | flops 512 | bytes 4096
  550.0 9.7 collective-permute-start.48
  564.2 29.1 %all-reduce.7 = f32[512]{0:T(512)S(1)} all-reduce(f32[512]{0:T(512)S(1)} %fusion.235), channel_id=1, replica_groups=mesh['gx'=32,'gy'=4,'col'=4] {'gy','col'}, use_global_device_ids=true, to_apply=%add.7 | all-reduce | flops 512 | bytes 4096
  594.7 8.2 collective-permute-start.50
  607.3 29.5 %all-reduce.8 = f32[512]{0:T(512)S(1)} all-reduce(f32[512]{0:T(512)S(1)} %get-tuple-element.305), channel_id=1, replica_groups=mesh['gx'=32,'gy'=4,'col'=4] {'gy','col'}, use_global_device_ids=true, to_apply=%add.8 | all-reduce | flops 512 | bytes 4096
  638.1 8.5 collective-permute-start.52
  651.0 28.9 %all-reduce.9 = f32[512]{0:T(512)S(1)} all-reduce(f32[512]{0:T(512)S(1)} %fusion.237), channel_id=1, replica_groups=mesh['gx'=32,'gy'=4,'col'=4] {'gy','col'}, use_global_device_ids=true, to_apply=%add.9 | all-reduce | flops 512 | bytes 4096
  681.2 8.5 collective-permute-start.54
  694.4 29.7 %all-reduce.10 = f32[512]{0:T(512)S(1)} all-reduce(f32[512]{0:T(512)S(1)} %get-tuple-element.300), channel_id=1, replica_groups=mesh['gx'=32,'gy'=4,'col'=4] {'gy','col'}, use_global_device_ids=true, to_apply=%add.10 | all-reduce | flops 512 | bytes 4096
  725.4 8.1 collective-permute-start.56
  733.5 3.3 collective-permute-start.57
  739.5 28.7 %all-reduce.11 = f32[512]{0:T(512)S(1)} all-reduce(f32[512]{0:T(512)S(1)} %fusion.228), channel_id=1, replica_groups=mesh['gx'=32,'gy'=4,'col'=4] {'gy','col'}, use_global_device_ids=true, to_apply=%add.11 | all-reduce | flops 512 | bytes 4096
  770.2 3.4 collective-permute-start.38
  776.2 3.4 collective-permute-start.41
  782.8 8.4 collective-permute-start.58
  791.2 4.5 collective-permute-start.59
  799.5 2.4 convolution_bitcast_fusion.5
  812.6 3.3 collective-permute-start.43
  820.6 3.4 collective-permute-start.44
  826.4 4.9 collective-permute-start.47
  833.2 3.6 collective-permute-done.46
  838.1 103.5 %psum.30 = f32[]{:T(128)} all-reduce(f32[]{:T(128)} %get-tuple-element.438), channel_id=1, replica_groups=mesh['gx'=32,'gy'=4,'col'=4] {'gx','gy','col'}, use_global_device_ids=true, to_apply=%region_5.6 | all-reduce | flops 1 | bytes 8 | tf_op jit(solution)/shard_map/psum | solution.py:249
  950.1 2.4 collective-permute-done.61
  952.7 2.6 collective-permute-start.62
  957.7 4.0 collective-permute-done.63
  963.8 4.6 collective-permute-start.65
  973.4 103.3 %psum.31 = f32[]{:T(128)} all-reduce(f32[]{:T(128)} %get-tuple-element.440), channel_id=1, replica_groups=mesh['gx'=32,'gy'=4,'col'=4] {'gx','gy','col'}, use_global_device_ids=true, to_apply=%region_7.8 | all-reduce | flops 1 | bytes 8 | tf_op jit(solution)/shard_map/psum | solution.py:281
  (461 shorter events, 154.3 us)
Async XLA Ops:
  5.8 74.7 %collective-permute-start.12 = (f32[1,1,1]{2,1,0:T(1,128)}, f32[1,1,1]{2,1,0:T(1,128)}, u32[]{:S(2)}, u32[]{:S(2)}) collective-permute-start(f32[1,1,1]{2,1,0:T(1,128)} %mul.454), channel_id=1, source_target_pairs={{0,16},{16,32},{32,48},{48,64},{64,80},{80,96},{96,112},{112,128},... | collective-permute-start | bytes 20 | tf_op jit(solution)/shard_map/ppermute | solution.py:53
  9.6 80.4 %collective-permute-start.13 = (f32[1,1,1]{2,1,0:T(1,128)}, f32[1,1,1]{2,1,0:T(1,128)}, u32[]{:S(2)}, u32[]{:S(2)}) collective-permute-start(f32[1,1,1]{2,1,0:T(1,128)} %get-tuple-element.432), channel_id=1, source_target_pairs={{16,0},{32,16},{48,32},{64,48},{80,64},{96,80},{112,96},{128,112},... | collective-permute-start | bytes 20 | tf_op jit(solution)/shard_map/ppermute | solution.py:55
  15.0 301.2 %collective-permute-start.1 = (f32[6,6,1]{2,1,0:T(8,128)}, f32[6,6,1]{2,1,0:T(8,128)S(1)}, u32[]{:S(2)}, u32[]{:S(2)}) collective-permute-start(f32[6,6,1]{2,1,0:T(8,128)} %get-tuple-element.399), channel_id=1, source_target_pairs={{16,0},{32,16},{48,32},{64,48},{80,64},{96,80},{112,96},{128,112},... | collective-permute-start | bytes 440 | tf_op jit(solution)/shard_map/ppermute | solution.py:55
  18.4 297.7 %collective-permute-start = (f32[6,6,1]{2,1,0:T(8,128)}, f32[6,6,1]{2,1,0:T(8,128)}, u32[]{:S(2)}, u32[]{:S(2)}) collective-permute-start(f32[6,6,1]{2,1,0:T(8,128)} %get-tuple-element.398), channel_id=1, source_target_pairs={{0,16},{16,32},{32,48},{48,64},{64,80},{80,96},{96,112},{112,128},... | collective-permute-start | bytes 440 | tf_op jit(solution)/shard_map/ppermute | solution.py:53
  20.1 311.5 %collective-permute-start.30 = (f32[1,8,8,1]{3,2,1,0:T(8,128)}, f32[1,8,8,1]{3,2,1,0:T(8,128)}, u32[]{:S(2)}, u32[]{:S(2)}) collective-permute-start(f32[1,8,8,1]{3,2,1,0:T(8,128)} %get-tuple-element.383), channel_id=1, source_target_pairs={{0,16},{16,32},{32,48},{48,64},{64,80},{80,96},{96,112},{112,128},... | collective-permute-start | bytes 776 | tf_op jit(solution)/shard_map/ppermute | solution.py:53
  80.6 251.0 %collective-permute-start.31 = (f32[1,8,8,1]{3,2,1,0:T(8,128)}, f32[1,8,8,1]{3,2,1,0:T(8,128)S(1)}, u32[]{:S(2)}, u32[]{:S(2)}) collective-permute-start(f32[1,8,8,1]{3,2,1,0:T(8,128)} %get-tuple-element.384), channel_id=1, source_target_pairs={{16,0},{32,16},{48,32},{64,48},{80,64},{96,80},{112,96},{128,112},... | collective-permute-start | bytes 776 | tf_op jit(solution)/shard_map/ppermute | solution.py:55
  122.4 7.6 collective-permute-start.14
  130.0 4.9 collective-permute-start.15
  168.5 8.0 collective-permute-start.16
  176.4 4.9 collective-permute-start.17
  212.6 7.7 collective-permute-start.18
  220.3 4.9 collective-permute-start.19
  258.1 8.0 collective-permute-start.20
  266.1 4.9 collective-permute-start.21
  302.2 7.7 collective-permute-start.22
  309.9 4.9 collective-permute-start.23
  316.9 5.9 collective-permute-start.3
  318.8 5.6 collective-permute-start.2
  325.4 7.0 collective-permute-start.5
  329.4 5.6 collective-permute-start.4
  353.4 4.4 collective-permute-start.7
  356.5 6.7 collective-permute-start.32
  357.8 6.7 collective-permute-start.9
  359.8 5.6 collective-permute-start.8
  363.2 7.7 collective-permute-start.33
  365.5 5.4 collective-permute-start.11
  367.4 5.6 collective-permute-start.10
  376.8 6.6 collective-permute-start.24
  381.0 4.0 collective-permute-start.25
  385.2 9.4 collective-permute-start.26
  388.1 7.9 collective-permute-start.34
  390.6 5.5 collective-permute-start.35
  394.7 4.6 collective-permute-start.27
  399.5 6.6 collective-permute-start.28
  401.4 5.5 collective-permute-start.29
  550.0 11.5 %collective-permute-start.48 = (f32[1,1,1]{2,1,0:T(1,128)}, f32[1,1,1]{2,1,0:T(1,128)}, u32[]{:S(2)}, u32[]{:S(2)}) collective-permute-start(f32[1,1,1]{2,1,0:T(1,128)} %mul.510), channel_id=1, source_target_pairs={{0,16},{16,32},{32,48},{48,64},{64,80},{80,96},{96,112},{112,128},... | collective-permute-start | bytes 20 | tf_op jit(solution)/shard_map/ppermute | solution.py:53
  559.7 3.2 collective-permute-start.49
  559.7 208.5 %collective-permute-start.37 = (f32[6,6,1]{2,1,0:T(8,128)S(1)}, f32[6,6,1]{2,1,0:T(8,128)S(1)}, u32[]{:S(2)}, u32[]{:S(2)}) collective-permute-start(f32[6,6,1]{2,1,0:T(8,128)S(1)} %get-tuple-element.395), channel_id=1, source_target_pairs={{16,0},{32,16},{48,32},{64,48},{80,64},{96,80},{112,96},{128,112},... | collective-permute-start | bytes 440 | tf_op jit(solution)/shard_map/ppermute | solution.py:55
  561.0 207.2 %collective-permute-start.36 = (f32[6,6,1]{2,1,0:T(8,128)S(1)}, f32[6,6,1]{2,1,0:T(8,128)S(1)}, u32[]{:S(2)}, u32[]{:S(2)}) collective-permute-start(f32[6,6,1]{2,1,0:T(8,128)S(1)} %get-tuple-element.394), channel_id=1, source_target_pairs={{0,16},{16,32},{32,48},{48,64},{64,80},{80,96},{96,112},{112,128},... | collective-permute-start | bytes 440 | tf_op jit(solution)/shard_map/ppermute | solution.py:53
  594.7 8.2 collective-permute-start.50
  602.9 3.1 collective-permute-start.51
  638.1 9.4 collective-permute-start.52
  646.6 3.1 collective-permute-start.53
  681.2 10.4 collective-permute-start.54
  689.7 3.3 collective-permute-start.55
  725.4 11.4 %collective-permute-start.56 = (f32[1,1,1]{2,1,0:T(1,128)}, f32[1,1,1]{2,1,0:T(1,128)}, u32[]{:S(2)}, u32[]{:S(2)}) collective-permute-start(f32[1,1,1]{2,1,0:T(1,128)} %mul.526), channel_id=1, source_target_pairs={{0,16},{16,32},{32,48},{48,64},{64,80},{80,96},{96,112},{112,128},... | collective-permute-start | bytes 20 | tf_op jit(solution)/shard_map/ppermute | solution.py:53
  733.5 4.7 collective-permute-start.57
  768.3 5.4 collective-permute-start.39
  770.2 5.9 collective-permute-start.38
  776.2 21.8 %collective-permute-start.41 = (f32[8,1,194]{2,1,0:T(1,128)S(1)}, f32[8,1,194]{2,1,0:T(1,128)S(1)}, u32[]{:S(2)}, u32[]{:S(2)}) collective-permute-start(f32[8,1,194]{2,1,0:T(1,128)S(1)} %get-tuple-element.361), channel_id=1, source_target_pairs={{1,0},{2,1},{3,2},{0,3},{5,4},{6,5},{7,6},{4,7},{9,8},{10,9},{11,1... | collective-permute-start | bytes 18632 | tf_op jit(solution)/shard_map/ppermute | solution.py:55
  779.6 18.4 %collective-permute-start.40 = (f32[8,1,194]{2,1,0:T(1,128)S(1)}, f32[8,1,194]{2,1,0:T(1,128)S(1)}, u32[]{:S(2)}, u32[]{:S(2)}) collective-permute-start(f32[8,1,194]{2,1,0:T(1,128)S(1)} %get-tuple-element.360), channel_id=1, source_target_pairs={{0,1},{1,2},{2,3},{3,0},{4,5},{5,6},{6,7},{7,4},{8,9},{9,10},{10,1... | collective-permute-start | bytes 18632 | tf_op jit(solution)/shard_map/ppermute | solution.py:53
  782.8 12.9 %collective-permute-start.58 = (f32[1,1,1]{2,1,0:T(1,128)}, f32[1,1,1]{2,1,0:T(1,128)}, u32[]{:S(2)}, u32[]{:S(2)}) collective-permute-start(f32[1,1,1]{2,1,0:T(1,128)} %mul.530), channel_id=1, source_target_pairs={{0,16},{16,32},{32,48},{48,64},{64,80},{80,96},{96,112},{112,128},... | collective-permute-start | bytes 20 | tf_op jit(solution)/shard_map/ppermute | solution.py:53
  791.2 6.2 collective-permute-start.59
  812.6 4.2 collective-permute-start.43
  818.7 5.3 collective-permute-start.45
  820.6 5.6 collective-permute-start.44
  826.4 6.9 collective-permute-start.47
  831.2 5.6 collective-permute-start.46
  946.2 4.0 collective-permute-start.60
  948.5 4.0 collective-permute-start.61
  952.7 3.6 collective-permute-start.62
  956.4 5.3 collective-permute-start.63
  961.9 6.5 collective-permute-start.64
  963.8 5.5 collective-permute-start.65
  (45 other events, 2657.3 us)
where the time goes:
time: 1090 us; the launch traced here: 1080 us
  blocking collectives  668 us (61%)
  starting transfers between devices  218 us (20%)
  waiting for transfers between devices  47.2 us (4%)
  matrix products  44.5 us (4%)
  local copies, waits for them, and re-layouts  43 us (4%)
  between operations  38.5 us (4%)
  other arithmetic  19.5 us (2%)
    unnamed x12, blocking collectives  356 us
    psum x2, blocking collectives, local(): r_dot_z = lax.psum(jnp.sum(residual * precond), ('gx', 'gy', 'col'))  209 us
    ppermute x33, starting transfers between devices, padded_2(): lax.ppermute(tail, axis, [(i, (i + 1) % count) for i in range(ends)])  126 us
    psum x1, blocking collectives, local(): curvature = lax.psum(jnp.sum(direction * image), ('gx', 'gy', 'col'))  103 us
    ppermute x33, starting transfers between devices, padded_2(): lax.ppermute(head, axis, [((i + 1) % count, i) for i in range(ends)])  91.7 us
    ppermute x33, waiting for transfers between devices, padded_2(): lax.ppermute(tail, axis, [(i, (i + 1) % count) for i in range(ends)])  31.4 us
  transfers between devices with their start and end apart: 66, of which 25 were waited for; matrix products, arithmetic and copies ran while one was open for 5% of the time, Pallas kernels for 0%

commit v1 on v0

v1 whole, which is shorter than its diff:
```python
import jax
import jax.numpy as jnp
import ml_dtypes
import numpy as np
from jax import lax
from jax.experimental import pallas as pl
from jax.experimental.pallas import tpu as pltpu
from jax.sharding import PartitionSpec as P

EA = 32
CHEB = 6
NB = 4

LOBATTO_NODES = [
    -1.0,
    -0.8717401485096066,
    -0.5917001814331423,
    -0.2092992179024789,
    0.2092992179024789,
    0.5917001814331423,
    0.8717401485096066,
    1.0,
]
GAUSS_NODES = [
    -0.932469514203152,
    -0.6612093864662645,
    -0.2386191860831909,
    0.2386191860831909,
    0.6612093864662645,
    0.932469514203152,
]
GAUSS_WEIGHTS = [
    0.1713244923791704,
    0.3607615730481386,
    0.467913934572691,
    0.467913934572691,
    0.3607615730481386,
    0.1713244923791704,
]
SPECTRUM_LOW = 8.0
SPECTRUM_HIGH = 90.0
HIGHEST = lax.Precision.HIGHEST
F32 = jnp.float32
BF16 = jnp.bfloat16

ROWS_P = 288
ROWS_V = 512
ROWS_A = 176
ROWS_B = 224


def basis_tables():
    lobatto = np.array(LOBATTO_NODES)
    points = np.array(GAUSS_NODES)
    interp = np.ones((6, 8))
    slopes = np.zeros((6, 8))
    for p in range(6):
        for m in range(8):
            product = 1.0
            for q in range(8):
                if q != m:
                    product = product * (points[p] - lobatto[q]) / (lobatto[m] - lobatto[q])
            interp[p, m] = product
            running = 0.0
            for q in range(8):
                if q != m:
                    factor = 1.0 / (lobatto[m] - lobatto[q])
                    for k in range(8):
                        if k != m and k != q:
                            factor = factor * (points[p] - lobatto[k]) / (lobatto[m] - lobatto[k])
                    running = running + factor
            slopes[p, m] = running
    return interp, slopes


def gradient_tables():
    interp, slopes = basis_tables()
    weight = np.array(GAUSS_WEIGHTS)
    tables = []
    for comp in range(3):
        sides = [(slopes if side == comp else interp) * weight[:, None] for side in range(3)]
        full = np.zeros((8, 8, 8, 6, 6, 8))
        full[..., 1:7] = np.einsum("iu,jv,kw->wuvkij", sides[0], sides[1], sides[2])
        tables.append(full.reshape(ROWS_V, ROWS_P))
    table = np.concatenate(tables, axis=0).astype(np.float32)
    high = table.astype(ml_dtypes.bfloat16)
    low = (table - high.astype(np.float32)).astype(ml_dtypes.bfloat16)
    forward = np.concatenate([high, high, low], axis=1)
    backward = np.concatenate([high.T, high.T, low.T], axis=1)
    return forward, backward


def order_table(nodes):
    table = np.zeros((nodes * EA, nodes * EA), np.float32)
    for k in range(nodes):
        for a in range(EA):
            table[a * nodes + k, k * EA + a] = 1.0
    return table


def sweep_factors():
    center = (SPECTRUM_HIGH + SPECTRUM_LOW) / 2.0
    spread = (SPECTRUM_HIGH - SPECTRUM_LOW) / 2.0
    ratio_cs = center / spread
    rho_now = 1.0 / ratio_cs
    keep, add = [], []
    for _ in range(CHEB):
        rho_next = 1.0 / (2.0 * ratio_cs - rho_now)
        keep.append(rho_next * rho_now)
        add.append(2.0 * rho_next / spread)
        rho_now = rho_next
    return center, keep, add


CENTER, KEEP, ADD = sweep_factors()


def lanes(shape):
    return lax.broadcasted_iota(jnp.int32, shape, len(shape) - 1)


def turn(value, shift):
    shift = shift % 128
    return value if shift == 0 else pltpu.roll(value, shift, value.ndim - 1)


def at_first(value, slot=0):
    moved = turn(value, 97 + slot)
    return jnp.where(lanes(moved.shape) % EA == 0, moved, 0.0)


def at_last(value, slot=0):
    moved = turn(value, 31 - slot)
    return jnp.where(lanes(moved.shape) % EA == EA - 1, moved, 0.0)


def pack_last(blocks):
    packed = None
    for slot, block in enumerate(blocks):
        part = turn(jnp.where(lanes(block.shape) % EA == EA - 1, block, 0.0), -slot)
        packed = part if packed is None else packed + part
    return packed


def pack_first(blocks):
    packed = None
    for slot, block in enumerate(blocks):
        part = turn(jnp.where(lanes(block.shape) % EA == 0, block, 0.0), slot)
        packed = part if packed is None else packed + part
    return packed


def times(dense_ref, vector):
    columns = jnp.concatenate([vector, jnp.zeros_like(vector)], axis=0).T
    total = None
    for b in range(NB):
        part = dense_ref[b * 128 : (b + 1) * 128, :] * columns[:, b : b + 1]
        total = part if total is None else total + part
    row = jnp.sum(total, axis=0, keepdims=True)
    return jnp.concatenate([row[:, b * 128 : (b + 1) * 128] for b in range(NB)], axis=0)


def sweep_begin(dense_ref, source, link):
    update = source * (1.0 / CENTER)
    remainder = source - times(dense_ref, update)
    free = KEEP[0] * update + ADD[0] * remainder
    state = jnp.concatenate([update, remainder, update, link], axis=0)
    return state, jnp.concatenate([update, free, link, link], axis=0)


def sweep_pair(dense_ref, state, from_left, from_right, sweep_at):
    update, remainder, solution, link = [state[4 * n : 4 * n + 4] for n in range(4)]
    left = at_first(from_left)
    right = at_last(from_right)
    place = lanes(update.shape) % EA
    link_left = left[8:12]
    link_right = jnp.where(place == EA - 1, link, 0.0)
    remainder = remainder + link_left * left[0:4] + link_right * right[0:4]
    left_next = left[4:8] + ADD[sweep_at] * link_left * update
    right_next = right[4:8] + ADD[sweep_at] * link_right * update
    update = KEEP[sweep_at] * update + ADD[sweep_at] * remainder
    solution = solution + update
    remainder = remainder - times(dense_ref, update)
    remainder = remainder + link_left * left_next + link_right * right_next
    update = KEEP[sweep_at + 1] * update + ADD[sweep_at + 1] * remainder
    solution = solution + update
    if sweep_at + 2 == CHEB:
        return solution
    remainder = remainder - times(dense_ref, update)
    free = KEEP[sweep_at + 2] * update + ADD[sweep_at + 2] * remainder
    state = jnp.concatenate([update, remainder, solution, link], axis=0)
    return state, jnp.concatenate([update, free, link, link], axis=0)


def fill_boxes(field_ref, box_ref):
    box_ref[...] = jnp.zeros(box_ref.shape, F32)
    for b in range(NB):
        for k in range(6):
            box_ref[b, (k + 1) * 64 + 8 : (k + 1) * 64 + 56, :] = field_ref[b, k * 48 : (k + 1) * 48, :]
        before = box_ref[b, pl.ds(6, 64, stride=8), :]
        after = box_ref[b, pl.ds(1, 64, stride=8), :]
        box_ref[b, pl.ds(0, 64, stride=8), :] = turn(before, 32)
        box_ref[b, pl.ds(7, 64, stride=8), :] = turn(after, -32)
    for b in range(NB):
        for k in range(1, 7):
            if b > 0:
                box_ref[b, k * 64 : k * 64 + 8, :] = box_ref[b - 1, k * 64 + 48 : k * 64 + 56, :]
            if b < NB - 1:
                box_ref[b, k * 64 + 56 : k * 64 + 64, :] = box_ref[b + 1, k * 64 + 8 : k * 64 + 16, :]


def begin_kernel_part(field_ref, small_ref, dense_ref, box_ref, state_ref, ahead_ref, behind_ref, extra):
    fill_boxes(field_ref, box_ref)
    source = jnp.concatenate(
        [jnp.sum(field_ref[b], axis=0, keepdims=True) for b in range(NB)], axis=0
    )
    link = jnp.concatenate([small_ref[b, 32:33, :] for b in range(NB)], axis=0)
    state, message = sweep_begin(dense_ref, source, link)
    state_ref[...] = state
    ahead_ref[0:16, :] = message
    behind_ref[0:16, :] = message
    ahead_ref[16:80, :] = pack_last([box_ref[b, 384:448, :] for b in range(NB)] + extra[0])
    behind_ref[16:80, :] = pack_first([box_ref[b, 64:128, :] for b in range(NB)] + extra[1])


def pack_body(rhs_ref, helm_ref, vec_ref, val_ref, size_ref, rows_ref, link_ref, six_ref, eight_ref, a_ref, b_ref, tmp):
    for t in range(4):
        a_ref[t * 32 : (t + 1) * 32, :] = rows_ref[:, t * 128 : (t + 1) * 128]
        a_ref[128:176, t * 32 : (t + 1) * 32] = vec_ref[t * 48 : (t + 1) * 48, :]
    tmp[...] = jnp.zeros(tmp.shape, F32)
    for i in range(6):
        tmp[i * 8 + 1 : i * 8 + 7, :] = rhs_ref[i]
    nodes = jnp.dot(tmp[...], six_ref[...], precision=HIGHEST, preferred_element_type=F32)
    b_ref[0:48, :] = nodes[:, 0:128]
    b_ref[48:96, :] = jnp.zeros((48, 128), F32)
    b_ref[48:96, 0:64] = nodes[:, 128:192]
    b_ref[48:72, 64:96] = val_ref[...]
    b_ref[72:75, 64:96] = size_ref[...]
    b_ref[80:81, 64:96] = jnp.broadcast_to(link_ref[...], (1, 32))
    helm = jnp.dot(
        helm_ref[...].reshape(64, 256), eight_ref[...], precision=HIGHEST, preferred_element_type=F32
    )
    b_ref[96:160, :] = helm[:, 0:128]
    b_ref[160:224, :] = helm[:, 128:256]


def unpack_body(
    me_ref, a_own, a_new, b_own, b_new,
    dense_ref, rhs_ref, helm_ref, vec_ref, small_ref, box_ref, state_ref, ahead_ref, behind_ref,
):
    mine_b = me_ref[0]
    mine_c = me_ref[1]
    place = lanes((1, 128)) // EA

    for tb in range(NB):
        b = mine_b ^ tb
        halves_a, halves_b, where_c = [], [], []
        for tc in range(NB):
            c = mine_c ^ tc
            at_a = tc | (tb << 2)
            at_b = tb | (tc << 2)
            half_a = a_own.at[at_a] if at_a < 8 else a_new.at[at_a - 8]
            half_b = b_own.at[at_b] if at_b < 8 else b_new.at[at_b - 8]
            for t in range(4):
                start = pl.multiple_of((b * 4 + c) * 32, 32)
                dense_ref[pl.ds(start, 32), t * 128 : (t + 1) * 128] = half_a[t * 32 : (t + 1) * 32, :]
            halves_a.append(half_a)
            halves_b.append(half_b)
            where_c.append(c)

        def joined(halves, start, rows, quarter):
            total = None
            for half, c in zip(halves, where_c):
                moved = pltpu.roll(half[start : start + rows, :], ((c - quarter) & 3) * 32, 1)
                part = jnp.where(place == c, moved, 0.0)
                total = part if total is None else total + part
            return total

        for k in range(6):
            rhs_ref[b, k * 48 : (k + 1) * 48, :] = joined(halves_b, 48 * (k // 4), 48, k % 4)
        small_ref[b, :, :] = joined(halves_b, 48, 48, 2)
        for k in range(8):
            helm_ref[b, k * 64 : (k + 1) * 64, :] = joined(halves_b, 96 + 64 * (k // 4), 64, k % 4)
        for t in range(4):
            vec_ref[b, t * 48 : (t + 1) * 48, :] = joined(halves_a, 128, 48, t)

    begin_kernel_part(
        rhs_ref, small_ref, dense_ref, box_ref, state_ref, ahead_ref, behind_ref,
        ([helm_ref[b, 448:512, :] for b in range(NB)], [helm_ref[b, 0:64, :] for b in range(NB)]),
    )


def middle_body(dense_ref, state_ref, left_ref, right_ref, state_out, message_out):
    state, message = sweep_pair(dense_ref, state_ref[...], left_ref[0:16, :], right_ref[0:16, :], 0)
    state_out[...] = state
    message_out[...] = message


def late_body(dense_ref, state_ref, left_ref, right_ref, up_ref, down_ref, state_out, ahead_ref, behind_ref):
    state, message = sweep_pair(dense_ref, state_ref[...], left_ref[...], right_ref[...], 2)
    state_out[...] = state
    ahead_ref[0:16, :] = message
    behind_ref[0:16, :] = message
    ahead_ref[16:80, :] = up_ref[...]
    behind_ref[16:80, :] = down_ref[...]


def join_rows(ref, groups, cross):
    for b in range(NB):
        low = ref[b, pl.ds(0, groups * 8, stride=8), :]
        high = ref[b, pl.ds(7, groups * 8, stride=8), :]
        ref[b, pl.ds(0, groups * 8, stride=8), :] = low + turn(high, 32)
        ref[b, pl.ds(7, groups * 8, stride=8), :] = high + turn(low, -32)
    for b in range(NB - 1):
        for g in range(groups):
            both = ref[b, g * 64 + 56 : g * 64 + 64, :] + ref[b + 1, g * 64 : g * 64 + 8, :]
            ref[b, g * 64 + 56 : g * 64 + 64, :] = both
            ref[b + 1, g * 64 : g * 64 + 8, :] = both


def join_layers(low, high):
    place = lanes(low.shape) % EA
    new_low = low + jnp.where(place > 0, turn(high, 1), 0.0)
    new_high = high + jnp.where(place < EA - 1, turn(low, -1), 0.0)
    return new_low, new_high


def helm_body(helm_ref, left_ref, right_ref, out_ref):
    out_ref[...] = helm_ref[...]
    for b in range(NB):
        low, high = join_layers(helm_ref[b, 0:64, :], helm_ref[b, 448:512, :])
        out_ref[b, 0:64, :] = low + at_first(left_ref[16:80, :], 4 + b)
        out_ref[b, 448:512, :] = high + at_last(right_ref[16:80, :], 4 + b)
    join_rows(out_ref, 8, None)
    for b in range(NB):
        out_ref[b] = 1.0 / out_ref[b]


def schwarz_body(box_ref, vec_ref, small_ref, left_ref, right_ref, out_ref, up_ref, down_ref, one, two, full):
    def element_row(b, carry):
        def row(side, first, second):
            return vec_ref[b, pl.ds(side * 64 + first * 8 + second, 1), :]

        last = pltpu.roll(box_ref[b, 384:448, :], 1, 1)
        first = pltpu.roll(box_ref[b, 64:128, :], 127, 1)
        place = lanes((64, 128)) % EA
        from_left = pltpu.roll(left_ref[16:80, :], 97 + b, 1)
        from_right = pltpu.roll(right_ref[16:80, :], 31 - b, 1)
        one[0] = jnp.where(place == 0, from_left, last).reshape(8, 8, 128)
        one[7] = jnp.where(place == EA - 1, from_right, first).reshape(8, 8, 128)
        one[1:7] = box_ref[b, 64:448, :].reshape(6, 8, 8, 128)
        for m in range(8):
            total = None
            for i in range(8):
                part = one[:, i] * row(0, i, m)[None]
                total = part if total is None else total + part
            two[:, m] = total
        for m in range(8):
            total = None
            for i in range(8):
                part = two[i] * row(2, i, m)[None]
                total = part if total is None else total + part
            one[m] = total
        for k in range(8):
            total = None
            for j in range(8):
                part = one[k, :, j : j + 1, :] * vec_ref[b, 64 + j * 8 : 72 + j * 8, :][None]
                total = part if total is None else total + part
            bottom = small_ref[b, 0:8, :][:, None, :] + small_ref[b, 8:16, :][None, :, :]
            two[k] = total / (bottom + small_ref[b, 16 + k : 17 + k, :][None])
        for k in range(8):
            total = None
            for n in range(8):
                part = two[k, :, n : n + 1, :] * vec_ref[b, pl.ds(64 + n, 8, stride=8), :][None]
                total = part if total is None else total + part
            one[k] = total
        for i in range(8):
            total = None
            for m in range(8):
                part = one[m] * row(2, i, m)[None]
                total = part if total is None else total + part
            two[i] = total
        for i in range(8):
            total = None
            for m in range(8):
                part = two[:, m] * row(0, i, m)[None]
                total = part if total is None else total + part
            one[:, i] = total
        full[b] = one[...].reshape(512, 128)
        return carry

    lax.fori_loop(0, NB, element_row, 0)
    for b in range(NB):
        low = full[b, pl.ds(0, 64, stride=8), :]
        high = full[b, pl.ds(7, 64, stride=8), :]
        full[b, pl.ds(6, 64, stride=8), :] = full[b, pl.ds(6, 64, stride=8), :] + turn(low, -32)
        full[b, pl.ds(1, 64, stride=8), :] = full[b, pl.ds(1, 64, stride=8), :] + turn(high, 32)
        full[b, pl.ds(0, 64, stride=8), :] = jnp.zeros((64, 128), F32)
        full[b, pl.ds(7, 64, stride=8), :] = jnp.zeros((64, 128), F32)
    for b in range(NB - 1):
        for k in range(8):
            full[b, k * 64 + 48 : k * 64 + 56, :] = (
                full[b, k * 64 + 48 : k * 64 + 56, :] + full[b + 1, k * 64 : k * 64 + 8, :]
            )
            full[b + 1, k * 64 + 8 : k * 64 + 16, :] = (
                full[b + 1, k * 64 + 8 : k * 64 + 16, :] + full[b, k * 64 + 56 : k * 64 + 64, :]
            )
    up_ref[...] = pack_last([full[b, 448:512, :] for b in range(NB)])
    down_ref[...] = pack_first([full[b, 0:64, :] for b in range(NB)])
    place = lanes((48, 128)) % EA
    for b in range(NB):
        for k in range(6):
            value = full[b, (k + 1) * 64 + 8 : (k + 1) * 64 + 56, :]
            if k == 0:
                value = value + jnp.where(place > 0, turn(full[b, 456:504, :], 1), 0.0)
            if k == 5:
                value = value + jnp.where(place < EA - 1, turn(full[b, 8:56, :], -1), 0.0)
            out_ref[b, k * 48 : (k + 1) * 48, :] = value


def volume_factors(small_ref, b):
    size = [small_ref[b, 24 + d : 25 + d, :] for d in range(3)]
    volume = size[0] * size[1] * size[2] * 0.125
    return [volume * (2.0 / size[d]) for d in range(3)]


def split_parts(value):
    high = value.astype(BF16)
    return high, (value - high.astype(F32)).astype(BF16)


def gradient_body(
    dense_ref, state_ref, left_ref, right_ref, part_ref, small_ref, table_ref, z_ref, t_ref, ahead_ref, behind_ref
):
    solution = sweep_pair(dense_ref, state_ref[...], left_ref[0:16, :], right_ref[0:16, :], 4)
    inside = lax.broadcasted_iota(jnp.int32, (ROWS_P, 128), 0) % 8
    inside = (inside > 0) & (inside < 7)
    for b in range(NB):
        coarse = jnp.where(inside, solution[b : b + 1, :], 0.0)
        z_ref[b] = part_ref[b] + coarse
        z_ref[b, 0:48, :] = z_ref[b, 0:48, :] + at_first(left_ref[24:72, :], b)
        z_ref[b, 240:288, :] = z_ref[b, 240:288, :] + at_last(right_ref[24:72, :], b)
    parts = [split_parts(z_ref[b]) for b in range(NB)]
    high = jnp.concatenate([part[0] for part in parts], axis=1)
    low = jnp.concatenate([part[1] for part in parts], axis=1)
    both = jnp.concatenate([high, low, high], axis=0)
    factors = [volume_factors(small_ref, b) for b in range(NB)]
    for d in range(3):
        result = jnp.dot(table_ref[d * 512 : (d + 1) * 512, :], both, preferred_element_type=F32)
        for b in range(NB):
            t_ref[b, d * 512 : (d + 1) * 512, :] = result[:, b * 128 : (b + 1) * 128] * factors[b][d]
    join_rows(t_ref, 24, None)
    lows = [t_ref[b, d * 512 : d * 512 + 64, :] for b in range(NB) for d in range(3)]
    highs = [t_ref[b, d * 512 + 448 : d * 512 + 512, :] for b in range(NB) for d in range(3)]
    ahead_ref[...] = pack_last(highs)
    behind_ref[...] = pack_first(lows)
    for b in range(NB):
        for d in range(3):
            low, high = join_layers(lows[b * 3 + d], highs[b * 3 + d])
            t_ref[b, d * 512 : d * 512 + 64, :] = low
            t_ref[b, d * 512 + 448 : d * 512 + 512, :] = high


def divergence_part(t_ref, left_ref, right_ref, inverse_ref, small_ref, table_ref, image_ref, spread):
    for b in range(NB):
        factors = volume_factors(small_ref, b)
        for d in range(3):
            base = d * 512
            for start, rows, extra in (
                (0, 64, at_first(left_ref[...], b * 3 + d)),
                (64, 384, None),
                (448, 64, at_last(right_ref[...], b * 3 + d)),
            ):
                value = t_ref[b, base + start : base + start + rows, :]
                if extra is not None:
                    value = value + extra
                value = value * inverse_ref[b, start : start + rows, :] * factors[d]
                high, low = split_parts(value)
                spread[base + start : base + start + rows, b * 128 : (b + 1) * 128] = high
                spread[1536 + base + start : 1536 + base + start + rows, b * 128 : (b + 1) * 128] = low
    image = jnp.dot(table_ref[:, 0:3072], spread[...], preferred_element_type=F32)
    image = image + jnp.dot(table_ref[:, 3072:4608], spread[0:1536, :], preferred_element_type=F32)
    for b in range(NB):
        image_ref[b] = image[:, b * 128 : (b + 1) * 128]


def first_image_body(
    t_ref, left_ref, right_ref, inverse_ref, small_ref, table_ref, dense_ref,
    image_ref, box_ref, state_ref, ahead_ref, behind_ref, spread,
):
    divergence_part(t_ref, left_ref, right_ref, inverse_ref, small_ref, table_ref, image_ref, spread)
    begin_kernel_part(
        image_ref, small_ref, dense_ref, box_ref, state_ref, ahead_ref, behind_ref, ([], [])
    )


def last_image_body(
    t_ref, left_ref, right_ref, inverse_ref, small_ref, table_ref, r_ref, z_ref, w_ref, q_ref,
    image_ref, sums_ref, spread,
):
    divergence_part(t_ref, left_ref, right_ref, inverse_ref, small_ref, table_ref, image_ref, spread)
    products = ((r_ref, z_ref), (z_ref, w_ref), (w_ref, q_ref), (r_ref, q_ref), (q_ref, image_ref), (z_ref, image_ref))
    sums_ref[...] = jnp.zeros(sums_ref.shape, F32)
    for n, (one, two) in enumerate(products):
        total = None
        for b in range(NB):
            part = jnp.sum(one[b] * two[b], axis=0, keepdims=True)
            total = part if total is None else total + part
        sums_ref[n : n + 1, :] = total


def own_body(me_ref, z_ref, w_ref, q_ref, v_ref, table_ref, z_out, w_out, q_out, v_out):
    mine_b = me_ref[0]
    mine_c = me_ref[1]
    for field_ref, out_ref in ((z_ref, z_out), (w_ref, w_out), (q_ref, q_out), (v_ref, v_out)):
        moved = pltpu.roll(field_ref[mine_b], ((4 - mine_c) & 3) * 32, 1)
        nodes = jnp.concatenate([moved[k * 48 : (k + 1) * 48, 0:32] for k in range(6)], axis=1)
        nodes = jnp.dot(nodes, table_ref[...], precision=HIGHEST, preferred_element_type=F32)
        for i in range(6):
            out_ref[i] = nodes[i * 8 + 1 : i * 8 + 7, :]


def call(body, outs, scratch=(), scalars=0):
    vmem = pl.BlockSpec(memory_space=pltpu.VMEM)
    smem = pl.BlockSpec(memory_space=pltpu.SMEM)

    def run(*operands):
        return pl.pallas_call(
            body,
            out_shape=[jax.ShapeDtypeStruct(shape, F32) for shape in outs],
            in_specs=[smem] * scalars + [vmem] * (len(operands) - scalars),
            out_specs=[vmem] * len(outs),
            scratch_shapes=list(scratch),
            compiler_params=pltpu.CompilerParams(vmem_limit_bytes=40 * 1024 * 1024),
        )(*operands)

    return run


def swap(block, axis, bit):
    count = lax.axis_size(axis)
    return lax.ppermute(block, axis, [(i, i ^ (1 << bit)) for i in range(count)])


def local(divergence, elem_size, helm_diag, fdm_vectors, fdm_values, coarse_rows, axial_link):
    count = lax.axis_size("gx")
    ahead = [(i, (i + 1) % count) for i in range(count)]
    behind = [((i + 1) % count, i) for i in range(count)]

    def exchange(up, down):
        return lax.ppermute(up, "gx", ahead), lax.ppermute(down, "gx", behind)

    forward, backward = gradient_tables()
    six = order_table(6)
    me = jnp.stack([lax.axis_index("gy"), lax.axis_index("col")]).astype(jnp.int32)
    field = (NB, ROWS_P, 128)
    velocity = (NB, ROWS_V, 128)
    state_shape = (16, 128)
    wide = (80, 128)
    plane = (64, 128)

    half_a, half_b = call(
        pack_body, [(ROWS_A, 128), (ROWS_B, 128)], [pltpu.VMEM((48, 192), F32)]
    )(
        divergence,
        helm_diag,
        fdm_vectors.reshape(192, EA),
        fdm_values.reshape(24, EA),
        elem_size,
        coarse_rows,
        axial_link.reshape(1, 1),
        six,
        order_table(8),
    )
    a_own, b_own = half_a[None], half_b[None]
    steps_a = (("col", 0), ("col", 1), ("gy", 0), ("gy", 1))
    steps_b = (("gy", 0), ("gy", 1), ("col", 0), ("col", 1))
    for n in range(4):
        a_new = swap(a_own, *steps_a[n])
        b_new = swap(b_own, *steps_b[n])
        if n < 3:
            a_own = jnp.concatenate([a_own, a_new], axis=0)
            b_own = jnp.concatenate([b_own, b_new], axis=0)

    dense, rhs, helm, vectors, small, boxes, state, up, down = call(
        unpack_body,
        [(512, 512), field, velocity, (NB, 192, 128), (NB, 48, 128), velocity, state_shape, wide, wide],
        scalars=1,
    )(me, a_own, a_new, b_own, b_new)

    def precondition(boxes, state, left, right):
        state, message = call(middle_body, [state_shape, state_shape])(dense, state, left, right)
        left_mid, right_mid = exchange(message, message)
        part, up, down = call(
            schwarz_body,
            [field, plane, plane],
            [pltpu.VMEM((8, 8, 8, 128), F32), pltpu.VMEM((8, 8, 8, 128), F32), pltpu.VMEM(velocity, F32)],
        )(boxes, vectors, small, left, right)
        state, up, down = call(late_body, [state_shape, wide, wide])(
            dense, state, left_mid, right_mid, up, down
        )
        left, right = exchange(up, down)
        z, t, up, down = call(gradient_body, [field, (NB, 1536, 128), plane, plane])(
            dense, state, left, right, part, small, forward
        )
        left, right = exchange(up, down)
        return z, t, left, right

    spread = [pltpu.VMEM((3072, 512), BF16)]
    left, right = exchange(up, down)
    (inverse,) = call(helm_body, [velocity])(helm, left, right)
    z, t, left, right = precondition(boxes, state, left, right)
    w, boxes, state, up, down = call(
        first_image_body, [field, velocity, state_shape, wide, wide], spread
    )(t, left, right, inverse, small, backward, dense)
    left, right = exchange(up, down)
    q, t, left, right = precondition(boxes, state, left, right)
    v, sums = call(last_image_body, [field, (8, 128)], spread)(
        t, left, right, inverse, small, backward, rhs, z, w, q
    )
    own = call(own_body, [(6, 6, 192)] * 4, scalars=1)(me, z, w, q, v, six.T.copy())
    z, w, q, v = own
    for bit in range(count.bit_length() - 1):
        sums = sums + swap(sums, "gx", bit)
    rz, zw, wq, rq, qv, zv = [jnp.sum(sums[n]) for n in range(6)]
    step_first = rz / zw
    rz_next = step_first * (step_first * wq - rq)
    share = 1.0 + rz_next / rz
    curvature = share * share * zw - share * step_first * (zv + wq) + step_first * step_first * qv
    step_next = rz_next / curvature
    z_factor = step_first + step_next * share
    q_factor = step_next * step_first
    pressure = z_factor * z - q_factor * q
    residual = divergence - z_factor * w + q_factor * v
    return (pressure, residual)


def solution(mesh):
    in_specs = (
        P("gy", "col", "gx"),
        P(None, ("gx", "gy", "col")),
        P("gy", "col", "gx"),
        P(None, None, None, ("gx", "gy", "col")),
        P(None, None, ("gx", "gy", "col")),
        P(("gx", "gy", "col"), None),
        P("gx", "gy", "col"),
    )
    out_specs = (P("gy", "col", "gx"), P("gy", "col", "gx"))
    return jax.shard_map(local, mesh=mesh, in_specs=in_specs, out_specs=out_specs, check_vma=False)
```

time: 1090 us -> 178 us (0.16)
  blocking collectives: 668 us -> 0 us
  starting transfers between devices: 218 us -> 86.2 us
  matrix products: 44.5 us -> 0 us
  local copies, waits for them, and re-layouts: 43 us -> 6.64 us
  between operations: 38.5 us -> 7.37 us
  Pallas kernels: 0 us -> 25.6 us
  other arithmetic: 19.5 us -> 1.63 us
    unnamed x12 -> x0, blocking collectives: 356 us -> none
    psum x3 -> x0, blocking collectives: 312 us -> none  [the longest x2 209 us: local(): r_dot_z = lax.psum(jnp.sum(residual * precond), ('gx', 'gy', 'col'))]
    ppermute x66 -> x29, starting transfers between devices: 218 us -> 86.2 us  [the longest x13 57 us: swap(): return lax.ppermute(block, axis, [(i, i ^ 1 << bit) for i in range(count)])]
    dot_general x95 -> x0, matrix products: 44.5 us -> none  [the longest x25 8.64 us: apply_side(): return jnp.einsum('pz,...bcz->...bcp', matrix, field, precision=HIGHEST)]
    pallas_call x0 -> x14, Pallas kernels: none -> 25.6 us  [run(): pl.pallas_call(body, out_shape=[jax.ShapeDtypeStruct(shape, F32) for shap...]
    slice x37 -> x0, local copies, waits for them, and re-layouts: 13.8 us -> none  [the longest x12 7.26 us: coarse_apply(): vector_grid[:, :, 0]]
    ppermute x66 -> x29, waiting for transfers between devices: 47.2 us -> 47.3 us  [the longest x13 39.7 us: swap(): return lax.ppermute(block, axis, [(i, i ^ 1 << bit) for i in range(count)])]
  transfers between devices with their start and end apart: 66 -> 29, of which waited for: 25 -> 23; matrix products, arithmetic and copies ran while one was open for 5% -> 0% of each run, Pallas kernels for 0% -> 6%
where the time goes in v1:
time: 178 us; the launch traced here: 175 us
  starting transfers between devices  86.2 us (48%)
  waiting for transfers between devices  47.3 us (27%)
  Pallas kernels  25.6 us (14%)
  between operations  7.37 us (4%)
  local copies, waits for them, and re-layouts  6.64 us (4%)
    ppermute x13, starting transfers between devices, swap(): return lax.ppermute(block, axis, [(i, i ^ 1 << bit) for i in range(count)])  57 us
    ppermute x13, waiting for transfers between devices, swap(): return lax.ppermute(block, axis, [(i, i ^ 1 << bit) for i in range(count)])  39.7 us
    ppermute x16, starting transfers between devices, exchange(): return (lax.ppermute(up, 'gx', ahead), lax.ppermute(down, 'gx', behind))  29.2 us
    pallas_call x14, Pallas kernels, run(): pl.pallas_call(body, out_shape=[jax.ShapeDtypeStruct(shape, F32) for shap...  25.6 us
    ppermute x16, waiting for transfers between devices, exchange(): return (lax.ppermute(up, 'gx', ahead), lax.ppermute(down, 'gx', behind))  7.56 us
    unnamed x24, local copies, waits for them, and re-layouts  6.64 us
  transfers between devices with their start and end apart: 29, of which 23 were waited for; matrix products, arithmetic and copies ran while one was open for 0% of the time, Pallas kernels for 6%

profile of v1, /device:TPU:1, one launch (start us, length us, event | category | flops | bytes accessed | tf_op | source)
XLA Modules:
  0.0 174.7 jit_solution(11825691509860667455)
XLA Ops:
  1.3 0.9 copy-done.2
  2.2 0.9 copy-done.3
  3.2 0.8 copy-done.4
  4.0 0.9 copy-done.7
  4.9 0.8 copy-done.8
  5.7 0.8 copy-done.9
  6.5 0.7 copy-done.10
  7.2 0.7 copy-done.11
  7.9 0.4 shard_map.131
  8.3 3.9 %collective-permute-start.4 = (f32[1,224,128]{2,1,0:T(8,128)S(1)}, f32[1,224,128]{2,1,0:T(8,128)S(1)}, u32[]{:S(2)}, u32[]{:S(2)}) collective-permute-start(f32[1,224,128]{2,1,0:T(8,128)S(1)} %bitcast.8), channel_id=1, source_target_pairs={{0,4},{4,0},{8,12},{12,8},{1,5},{5,1},{9,13},{13,9},{2,6},{6,2},{1... | collective-permute-start | bytes 344072 | tf_op jit(solution)/shard_map/ppermute | solution.py:542
  12.3 2.2 %collective-permute-done.4 = f32[1,224,128]{2,1,0:T(8,128)S(1)} collective-permute-done((f32[1,224,128]{2,1,0:T(8,128)S(1)}, f32[1,224,128]{2,1,0:T(8,128)S(1)}, u32[]{:S(2)}, u32[]{:S(2)}) %collective-permute-start.4) | collective-permute-done | bytes 114720 | tf_op jit(solution)/shard_map/ppermute | solution.py:542
  14.5 5.3 %collective-permute-start.5 = (f32[2,224,128]{2,1,0:T(8,128)S(1)}, f32[2,224,128]{2,1,0:T(8,128)S(1)}, u32[]{:S(2)}, u32[]{:S(2)}) collective-permute-start(f32[2,224,128]{2,1,0:T(8,128)S(1)} %pad_maximum_fusion.4), channel_id=1, source_target_pairs={{0,8},{4,12},{8,0},{12,4},{1,9},{5,13},{9,1},{13,5},{2,10},{6,14},... | collective-permute-start | bytes 688136 | tf_op jit(solution)/shard_map/ppermute | solution.py:542
  19.7 3.2 %collective-permute-start = (f32[1,176,128]{2,1,0:T(8,128)S(1)}, f32[1,176,128]{2,1,0:T(8,128)S(1)}, u32[]{:S(2)}, u32[]{:S(2)}) collective-permute-start(f32[1,176,128]{2,1,0:T(8,128)S(1)} %bitcast.12), channel_id=1, source_target_pairs={{0,1},{1,0},{2,3},{3,2},{4,5},{5,4},{6,7},{7,6},{8,9},{9,8},{10,11... | collective-permute-start | bytes 270344 | tf_op jit(solution)/shard_map/ppermute | solution.py:542
  23.0 2.1 %collective-permute-done = f32[1,176,128]{2,1,0:T(8,128)S(1)} collective-permute-done((f32[1,176,128]{2,1,0:T(8,128)S(1)}, f32[1,176,128]{2,1,0:T(8,128)S(1)}, u32[]{:S(2)}, u32[]{:S(2)}) %collective-permute-start) | collective-permute-done | bytes 90144 | tf_op jit(solution)/shard_map/ppermute | solution.py:542
  25.0 5.1 %collective-permute-start.1 = (f32[2,176,128]{2,1,0:T(8,128)S(1)}, f32[2,176,128]{2,1,0:T(8,128)S(1)}, u32[]{:S(2)}, u32[]{:S(2)}) collective-permute-start(f32[2,176,128]{2,1,0:T(8,128)S(1)} %pad_maximum_fusion.5), channel_id=1, source_target_pairs={{0,2},{1,3},{2,0},{3,1},{4,6},{5,7},{6,4},{7,5},{8,10},{9,11},{10,... | collective-permute-start | bytes 540680 | tf_op jit(solution)/shard_map/ppermute | solution.py:542
  30.2 2.3 %collective-permute-start.6 = (f32[4,224,128]{2,1,0:T(8,128)S(1)}, f32[4,224,128]{2,1,0:T(8,128)S(1)}, u32[]{:S(2)}, u32[]{:S(2)}) collective-permute-start(f32[4,224,128]{2,1,0:T(8,128)S(1)} %pad_maximum_fusion.2), channel_id=1, source_target_pairs={{0,1},{1,0},{2,3},{3,2},{4,5},{5,4},{6,7},{7,6},{8,9},{9,8},{10,11... | collective-permute-start | bytes 1376264 | tf_op jit(solution)/shard_map/ppermute | solution.py:542
  32.5 0.5 collective-permute-done.1
  33.1 2.2 %collective-permute-start.2 = (f32[4,176,128]{2,1,0:T(8,128)S(1)}, f32[4,176,128]{2,1,0:T(8,128)S(1)}, u32[]{:S(2)}, u32[]{:S(2)}) collective-permute-start(f32[4,176,128]{2,1,0:T(8,128)S(1)} %pad_maximum_fusion.3), channel_id=1, source_target_pairs={{0,4},{4,0},{8,12},{12,8},{1,5},{5,1},{9,13},{13,9},{2,6},{6,2},{1... | collective-permute-start | bytes 1081352 | tf_op jit(solution)/shard_map/ppermute | solution.py:542
  35.3 9.2 %collective-permute-done.6 = f32[4,224,128]{2,1,0:T(8,128)S(1)} collective-permute-done((f32[4,224,128]{2,1,0:T(8,128)S(1)}, f32[4,224,128]{2,1,0:T(8,128)S(1)}, u32[]{:S(2)}, u32[]{:S(2)}) %collective-permute-start.6) | collective-permute-done | bytes 458784 | tf_op jit(solution)/shard_map/ppermute | solution.py:542
  44.6 1.9 %collective-permute-start.7 = (f32[8,224,128]{2,1,0:T(8,128)S(1)}, f32[8,224,128]{2,1,0:T(8,128)S(1)}, u32[]{:S(2)}, u32[]{:S(2)}) collective-permute-start(f32[8,224,128]{2,1,0:T(8,128)S(1)} %pad_maximum_fusion.b_own), channel_id=1, source_target_pairs={{0,2},{1,3},{2,0},{3,1},{4,6},{5,7},{6,4},{7,5},{8,10},{9,11},{10,... | collective-permute-start | bytes 2752520 | tf_op jit(solution)/shard_map/ppermute | solution.py:542
  46.6 1.9 %collective-permute-start.3 = (f32[8,176,128]{2,1,0:T(8,128)S(1)}, f32[8,176,128]{2,1,0:T(8,128)S(1)}, u32[]{:S(2)}, u32[]{:S(2)}) collective-permute-start(f32[8,176,128]{2,1,0:T(8,128)S(1)} %pad_maximum_fusion.1.a_own), channel_id=1, source_target_pairs={{0,8},{4,12},{8,0},{12,4},{1,9},{5,13},{9,1},{13,5},{2,10},{6,14},... | collective-permute-start | bytes 2162696 | tf_op jit(solution)/shard_map/ppermute | solution.py:542
  48.6 14.1 %collective-permute-done.3.a_new = f32[8,176,128]{2,1,0:T(8,128)S(1)} collective-permute-done((f32[8,176,128]{2,1,0:T(8,128)S(1)}, f32[8,176,128]{2,1,0:T(8,128)S(1)}, u32[]{:S(2)}, u32[]{:S(2)}) %collective-permute-start.3) | collective-permute-done | bytes 720928 | tf_op jit(solution)/shard_map/ppermute | solution.py:542
  62.7 4.6 %collective-permute-done.7.b_new = f32[8,224,128]{2,1,0:T(8,128)S(1)} collective-permute-done((f32[8,224,128]{2,1,0:T(8,128)S(1)}, f32[8,224,128]{2,1,0:T(8,128)S(1)}, u32[]{:S(2)}, u32[]{:S(2)}) %collective-permute-start.7) | collective-permute-done | bytes 917536 | tf_op jit(solution)/shard_map/ppermute | solution.py:542
  67.4 3.3 %shard_map.132 = (f32[512,512]{1,0:T(8,128)S(1)}, f32[4,288,128]{2,1,0:T(8,128)S(1)}, f32[4,512,128]{2,1,0:T(8,128)S(1)}, f32[4,192,128]{2,1,0:T(8,128)S(1)}, f3...) custom-call(s32[2]{0:T(128)S(1)} %pad_add_fusion.me_ref, ...), custom_call_target="tpu_custom_call" | custom-call | tf_op jit(solution)/shard_map/pallas_call | solution.py:528
  70.7 4.9 %collective-permute-start.8 = (f32[80,128]{1,0:T(8,128)S(1)}, f32[80,128]{1,0:T(8,128)S(1)}, u32[]{:S(2)}, u32[]{:S(2)}) collective-permute-start(f32[80,128]{1,0:T(8,128)S(1)} %get-tuple-element.52), channel_id=1, source_target_pairs={{0,16},{16,32},{32,48},{48,64},{64,80},{80,96},{96,112},{112,128},... | collective-permute-start | bytes 122888 | tf_op jit(solution)/shard_map/ppermute | solution.py:551
  75.6 1.1 collective-permute-done.8.left_ref
  76.7 2.3 %collective-permute-done.9.right_ref = f32[80,128]{1,0:T(8,128)S(1)} collective-permute-done((f32[80,128]{1,0:T(8,128)S(1)}, f32[80,128]{1,0:T(8,128)S(1)}, u32[]{:S(2)}, u32[]{:S(2)}) %collective-permute-start.9) | collective-permute-done | bytes 40992 | tf_op jit(solution)/shard_map/ppermute | solution.py:551
  79.1 0.6 shard_map.133
  79.7 3.0 %collective-permute-start.11 = (f32[16,128]{1,0:T(8,128)S(1)}, f32[16,128]{1,0:T(8,128)S(1)}, u32[]{:S(2)}, u32[]{:S(2)}) collective-permute-start(f32[16,128]{1,0:T(8,128)S(1)} %get-tuple-element.55), channel_id=1, source_target_pairs={{16,0},{32,16},{48,32},{64,48},{80,64},{96,80},{112,96},{128,112},... | collective-permute-start | bytes 24584 | tf_op jit(solution)/shard_map/ppermute | solution.py:551
  82.7 4.1 %shard_map.134 = (f32[4,288,128]{2,1,0:T(8,128)S(1)}, f32[64,128]{1,0:T(8,128)S(1)}, f32[64,128]{1,0:T(8,128)S(1)}) custom-call(f32[4,512,128]{2,1,0:T(8,128)S(1)} %get-tuple-element.56.box_ref, f32[4,192,128]{2,1,0:T(8,128)S(1)} %get-tuple-element.57.vec_ref, f32[4,48,128]{2,1,0:T(8,128)S(1)} %get-tuple-element.58.small_ref, ...), custom_call_target="tpu_custom_call" | custom-call | tf_op jit(solution)/shard_map/pallas_call | solution.py:528
  86.8 0.6 shard_map.135
  87.5 3.2 %collective-permute-start.13 = (f32[80,128]{1,0:T(8,128)S(1)}, f32[80,128]{1,0:T(8,128)S(1)}, u32[]{:S(2)}, u32[]{:S(2)}) collective-permute-start(f32[80,128]{1,0:T(8,128)S(1)} %get-tuple-element.63), channel_id=1, source_target_pairs={{16,0},{32,16},{48,32},{64,48},{80,64},{96,80},{112,96},{128,112},... | collective-permute-start | bytes 122888 | tf_op jit(solution)/shard_map/ppermute | solution.py:551
  90.6 0.7 collective-permute-done.12.left_ref
  91.5 2.6 %shard_map.136 = (f32[4,288,128]{2,1,0:T(8,128)S(1)}, f32[4,1536,128]{2,1,0:T(8,128)S(1)}, f32[64,128]{1,0:T(8,128)S(1)}, f32[64,128]{1,0:T(8,128)S(1)}) custom-call(f32[512,512]{1,0:T(8,128)S(1)} %get-tuple-element.50.dense_ref, f32[16,128]{1,0:T(8,128)S(1)} %get-tuple-element.61.state_ref, f32[80,128]{1,0:T(8,128)S(1)} %collective-permute-done.12.left_ref, ...), custom_call_target="tpu_custom_call" | custom-call | tf_op jit(solution)/shard_map/pallas_call | solution.py:528
  94.1 3.8 %collective-permute-start.15 = (f32[64,128]{1,0:T(8,128)S(1)}, f32[64,128]{1,0:T(8,128)S(1)}, u32[]{:S(2)}, u32[]{:S(2)}) collective-permute-start(f32[64,128]{1,0:T(8,128)S(1)} %get-tuple-element.67), channel_id=1, source_target_pairs={{16,0},{32,16},{48,32},{64,48},{80,64},{96,80},{112,96},{128,112},... | collective-permute-start | bytes 98312 | tf_op jit(solution)/shard_map/ppermute | solution.py:551
  97.9 0.4 shard_map.137.inverse_ref
  98.3 0.3 collective-permute-done.14.left_ref
  98.8 2.3 %shard_map.138 = (f32[4,288,128]{2,1,0:T(8,128)S(1)}, f32[4,512,128]{2,1,0:T(8,128)S(1)}, f32[16,128]{1,0:T(8,128)S(1)}, f32[80,128]{1,0:T(8,128)S(1)}, f32[80,128]{1,0:T(8,128)S(1)}) custom-call(f32[4,1536,128]{2,1,0:T(8,128)S(1)} %get-tuple-element.65.t_ref, f32[64,128]{1,0:T(8,128)S(1)} %collective-permute-done.14.left_ref, ...), custom_call_target="tpu_custom_call" | custom-call | tf_op jit(solution)/shard_map/pallas_call | solution.py:528
  101.1 3.7 %collective-permute-start.17 = (f32[80,128]{1,0:T(8,128)S(1)}, f32[80,128]{1,0:T(8,128)S(1)}, u32[]{:S(2)}, u32[]{:S(2)}) collective-permute-start(f32[80,128]{1,0:T(8,128)S(1)} %get-tuple-element.71), channel_id=1, source_target_pairs={{16,0},{32,16},{48,32},{64,48},{80,64},{96,80},{112,96},{128,112},... | collective-permute-start | bytes 122888 | tf_op jit(solution)/shard_map/ppermute | solution.py:551
  104.8 0.7 collective-permute-done.16.left_ref
  105.5 0.4 collective-permute-done.17.right_ref
  105.8 0.6 shard_map.139
  106.4 3.6 %collective-permute-start.19 = (f32[16,128]{1,0:T(8,128)S(1)}, f32[16,128]{1,0:T(8,128)S(1)}, u32[]{:S(2)}, u32[]{:S(2)}) collective-permute-start(f32[16,128]{1,0:T(8,128)S(1)} %get-tuple-element.73), channel_id=1, source_target_pairs={{16,0},{32,16},{48,32},{64,48},{80,64},{96,80},{112,96},{128,112},... | collective-permute-start | bytes 24584 | tf_op jit(solution)/shard_map/ppermute | solution.py:551
  110.0 4.1 %shard_map.140 = (f32[4,288,128]{2,1,0:T(8,128)S(1)}, f32[64,128]{1,0:T(8,128)S(1)}, f32[64,128]{1,0:T(8,128)S(1)}) custom-call(f32[4,512,128]{2,1,0:T(8,128)S(1)} %get-tuple-element.74.box_ref, f32[4,192,128]{2,1,0:T(8,128)S(1)} %get-tuple-element.57.vec_ref, f32[4,48,128]{2,1,0:T(8,128)S(1)} %get-tuple-element.58.small_ref, ...), custom_call_target="tpu_custom_call" | custom-call | tf_op jit(solution)/shard_map/pallas_call | solution.py:528
  114.1 0.6 shard_map.141
  114.8 3.2 %collective-permute-start.21 = (f32[80,128]{1,0:T(8,128)S(1)}, f32[80,128]{1,0:T(8,128)S(1)}, u32[]{:S(2)}, u32[]{:S(2)}) collective-permute-start(f32[80,128]{1,0:T(8,128)S(1)} %get-tuple-element.79), channel_id=1, source_target_pairs={{16,0},{32,16},{48,32},{64,48},{80,64},{96,80},{112,96},{128,112},... | collective-permute-start | bytes 122888 | tf_op jit(solution)/shard_map/ppermute | solution.py:551
  118.0 0.7 collective-permute-done.20.left_ref
  118.8 2.6 %shard_map.142 = (f32[4,288,128]{2,1,0:T(8,128)S(1)}, f32[4,1536,128]{2,1,0:T(8,128)S(1)}, f32[64,128]{1,0:T(8,128)S(1)}, f32[64,128]{1,0:T(8,128)S(1)}) custom-call(f32[512,512]{1,0:T(8,128)S(1)} %get-tuple-element.50.dense_ref, f32[16,128]{1,0:T(8,128)S(1)} %get-tuple-element.77.state_ref, f32[80,128]{1,0:T(8,128)S(1)} %collective-permute-done.20.left_ref, ...), custom_call_target="tpu_custom_call" | custom-call | tf_op jit(solution)/shard_map/pallas_call | solution.py:528
  121.5 3.8 %collective-permute-start.23 = (f32[64,128]{1,0:T(8,128)S(1)}, f32[64,128]{1,0:T(8,128)S(1)}, u32[]{:S(2)}, u32[]{:S(2)}) collective-permute-start(f32[64,128]{1,0:T(8,128)S(1)} %get-tuple-element.83), channel_id=1, source_target_pairs={{16,0},{32,16},{48,32},{64,48},{80,64},{96,80},{112,96},{128,112},... | collective-permute-start | bytes 98312 | tf_op jit(solution)/shard_map/ppermute | solution.py:551
  125.2 0.7 collective-permute-done.22.left_ref
  126.1 2.1 %shard_map.143 = (f32[4,288,128]{2,1,0:T(8,128)S(1)}, f32[8,128]{1,0:T(8,128)S(1)}) custom-call(f32[4,1536,128]{2,1,0:T(8,128)S(1)} %get-tuple-element.81.t_ref, f32[64,128]{1,0:T(8,128)S(1)} %collective-permute-done.22.left_ref, f32[64,128]{1,0:T(8,128)S(1)} %collective-permute-done.23.right_ref, f32[4,512,128]{2,1,0:T(8,128)S(1)} %shard_map.137.inverse_ref, ...), custom_call_target="tpu_custom_call" | custom-call | tf_op jit(solution)/shard_map/pallas_call | solution.py:528
  128.2 5.6 %collective-permute-start.24 = (f32[8,128]{1,0:T(8,128)S(1)}, f32[8,128]{1,0:T(8,128)S(1)}, u32[]{:S(2)}, u32[]{:S(2)}) collective-permute-start(f32[8,128]{1,0:T(8,128)S(1)} %get-tuple-element.88), channel_id=1, source_target_pairs={{0,16},{16,0},{32,48},{48,32},{64,80},{80,64},{96,112},{112,96},{1... | collective-permute-start | bytes 12296 | tf_op jit(solution)/shard_map/ppermute | solution.py:542
  133.8 0.8 collective-permute-done.24
  134.6 1.9 %collective-permute-start.25 = (f32[8,128]{1,0:T(8,128)S(1)}, f32[8,128]{1,0:T(8,128)S(1)}, u32[]{:S(2)}, u32[]{:S(2)}) collective-permute-start(f32[8,128]{1,0:T(8,128)S(1)} %add.27), channel_id=1, source_target_pairs={{0,32},{16,48},{32,0},{48,16},{64,96},{80,112},{96,64},{112,80},{1... | collective-permute-start | bytes 12296 | tf_op jit(solution)/shard_map/ppermute | solution.py:542
  136.5 2.4 %collective-permute-done.25 = f32[8,128]{1,0:T(8,128)S(1)} collective-permute-done((f32[8,128]{1,0:T(8,128)S(1)}, f32[8,128]{1,0:T(8,128)S(1)}, u32[]{:S(2)}, u32[]{:S(2)}) %collective-permute-start.25) | collective-permute-done | bytes 4128 | tf_op jit(solution)/shard_map/ppermute | solution.py:542
  139.0 4.8 %collective-permute-start.26 = (f32[8,128]{1,0:T(8,128)S(1)}, f32[8,128]{1,0:T(8,128)S(1)}, u32[]{:S(2)}, u32[]{:S(2)}) collective-permute-start(f32[8,128]{1,0:T(8,128)S(1)} %add.28), channel_id=1, source_target_pairs={{0,64},{16,80},{32,96},{48,112},{64,0},{80,16},{96,32},{112,48},{1... | collective-permute-start | bytes 12296 | tf_op jit(solution)/shard_map/ppermute | solution.py:542
  143.8 1.0 collective-permute-done.26
  144.8 8.8 %collective-permute-start.27 = (f32[8,128]{1,0:T(8,128)S(1)}, f32[8,128]{1,0:T(8,128)S(1)}, u32[]{:S(2)}, u32[]{:S(2)}) collective-permute-start(f32[8,128]{1,0:T(8,128)S(1)} %add.29), channel_id=1, source_target_pairs={{0,128},{16,144},{32,160},{48,176},{64,192},{80,208},{96,224},{112... | collective-permute-start | bytes 12296 | tf_op jit(solution)/shard_map/ppermute | solution.py:542
  153.6 1.0 collective-permute-done.27
  154.6 10.0 %collective-permute-start.28 = (f32[8,128]{1,0:T(8,128)S(1)}, f32[8,128]{1,0:T(8,128)S(1)}, u32[]{:S(2)}, u32[]{:S(2)}) collective-permute-start(f32[8,128]{1,0:T(8,128)S(1)} %add.30), channel_id=1, source_target_pairs={{0,256},{16,272},{32,288},{48,304},{64,320},{80,336},{96,352},{112... | collective-permute-start | bytes 12296 | tf_op jit(solution)/shard_map/ppermute | solution.py:542
  164.6 1.2 shard_map.144
  165.8 1.8 %collective-permute-done.28 = f32[8,128]{1,0:T(8,128)S(1)} collective-permute-done((f32[8,128]{1,0:T(8,128)S(1)}, f32[8,128]{1,0:T(8,128)S(1)}, u32[]{:S(2)}, u32[]{:S(2)}) %collective-permute-start.28) | collective-permute-done | bytes 4128 | tf_op jit(solution)/shard_map/ppermute | solution.py:542
  167.6 0.7 slice_reduce_fusion
  174.1 0.7 multiply_add_fusion
  (46 shorter events, 1.2 us)
Async XLA Ops:
  1.3 1.0 copy-start.2
  2.2 0.9 copy-start.3
  3.2 0.8 copy-start.4
  4.0 0.9 copy-start.7
  4.9 0.8 copy-start.8
  5.7 0.8 copy-start.9
  6.5 0.7 copy-start.10
  7.2 0.7 copy-start.11
  8.3 6.1 %collective-permute-start.4 = (f32[1,224,128]{2,1,0:T(8,128)S(1)}, f32[1,224,128]{2,1,0:T(8,128)S(1)}, u32[]{:S(2)}, u32[]{:S(2)}) collective-permute-start(f32[1,224,128]{2,1,0:T(8,128)S(1)} %bitcast.8), channel_id=1, source_target_pairs={{0,4},{4,0},{8,12},{12,8},{1,5},{5,1},{9,13},{13,9},{2,6},{6,2},{1... | collective-permute-start | bytes 344072 | tf_op jit(solution)/shard_map/ppermute | solution.py:542
  14.5 15.7 %collective-permute-start.5 = (f32[2,224,128]{2,1,0:T(8,128)S(1)}, f32[2,224,128]{2,1,0:T(8,128)S(1)}, u32[]{:S(2)}, u32[]{:S(2)}) collective-permute-start(f32[2,224,128]{2,1,0:T(8,128)S(1)} %pad_maximum_fusion.4), channel_id=1, source_target_pairs={{0,8},{4,12},{8,0},{12,4},{1,9},{5,13},{9,1},{13,5},{2,10},{6,14},... | collective-permute-start | bytes 688136 | tf_op jit(solution)/shard_map/ppermute | solution.py:542
  19.7 5.3 %collective-permute-start = (f32[1,176,128]{2,1,0:T(8,128)S(1)}, f32[1,176,128]{2,1,0:T(8,128)S(1)}, u32[]{:S(2)}, u32[]{:S(2)}) collective-permute-start(f32[1,176,128]{2,1,0:T(8,128)S(1)} %bitcast.12), channel_id=1, source_target_pairs={{0,1},{1,0},{2,3},{3,2},{4,5},{5,4},{6,7},{7,6},{8,9},{9,8},{10,11... | collective-permute-start | bytes 270344 | tf_op jit(solution)/shard_map/ppermute | solution.py:542
  25.0 8.0 %collective-permute-start.1 = (f32[2,176,128]{2,1,0:T(8,128)S(1)}, f32[2,176,128]{2,1,0:T(8,128)S(1)}, u32[]{:S(2)}, u32[]{:S(2)}) collective-permute-start(f32[2,176,128]{2,1,0:T(8,128)S(1)} %pad_maximum_fusion.5), channel_id=1, source_target_pairs={{0,2},{1,3},{2,0},{3,1},{4,6},{5,7},{6,4},{7,5},{8,10},{9,11},{10,... | collective-permute-start | bytes 540680 | tf_op jit(solution)/shard_map/ppermute | solution.py:542
  30.2 14.3 %collective-permute-start.6 = (f32[4,224,128]{2,1,0:T(8,128)S(1)}, f32[4,224,128]{2,1,0:T(8,128)S(1)}, u32[]{:S(2)}, u32[]{:S(2)}) collective-permute-start(f32[4,224,128]{2,1,0:T(8,128)S(1)} %pad_maximum_fusion.2), channel_id=1, source_target_pairs={{0,1},{1,0},{2,3},{3,2},{4,5},{5,4},{6,7},{7,6},{8,9},{9,8},{10,11... | collective-permute-start | bytes 1376264 | tf_op jit(solution)/shard_map/ppermute | solution.py:542
  33.1 13.5 %collective-permute-start.2 = (f32[4,176,128]{2,1,0:T(8,128)S(1)}, f32[4,176,128]{2,1,0:T(8,128)S(1)}, u32[]{:S(2)}, u32[]{:S(2)}) collective-permute-start(f32[4,176,128]{2,1,0:T(8,128)S(1)} %pad_maximum_fusion.3), channel_id=1, source_target_pairs={{0,4},{4,0},{8,12},{12,8},{1,5},{5,1},{9,13},{13,9},{2,6},{6,2},{1... | collective-permute-start | bytes 1081352 | tf_op jit(solution)/shard_map/ppermute | solution.py:542
  44.6 22.8 %collective-permute-start.7 = (f32[8,224,128]{2,1,0:T(8,128)S(1)}, f32[8,224,128]{2,1,0:T(8,128)S(1)}, u32[]{:S(2)}, u32[]{:S(2)}) collective-permute-start(f32[8,224,128]{2,1,0:T(8,128)S(1)} %pad_maximum_fusion.b_own), channel_id=1, source_target_pairs={{0,2},{1,3},{2,0},{3,1},{4,6},{5,7},{6,4},{7,5},{8,10},{9,11},{10,... | collective-permute-start | bytes 2752520 | tf_op jit(solution)/shard_map/ppermute | solution.py:542
  46.6 16.2 %collective-permute-start.3 = (f32[8,176,128]{2,1,0:T(8,128)S(1)}, f32[8,176,128]{2,1,0:T(8,128)S(1)}, u32[]{:S(2)}, u32[]{:S(2)}) collective-permute-start(f32[8,176,128]{2,1,0:T(8,128)S(1)} %pad_maximum_fusion.1.a_own), channel_id=1, source_target_pairs={{0,8},{4,12},{8,0},{12,4},{1,9},{5,13},{9,1},{13,5},{2,10},{6,14},... | collective-permute-start | bytes 2162696 | tf_op jit(solution)/shard_map/ppermute | solution.py:542
  48.6 42.9 %copy-start = (bf16[1536,864]{1,0:T(8,128)(2,1)S(1)}, bf16[1536,864]{1,0:T(8,128)(2,1)}, u32[]{:S(2)}) copy-start(bf16[1536,864]{1,0:T(8,128)(2,1)} %constant.23.clone.table_ref) | copy-start | bytes 7962628
  70.7 6.0 %collective-permute-start.8 = (f32[80,128]{1,0:T(8,128)S(1)}, f32[80,128]{1,0:T(8,128)S(1)}, u32[]{:S(2)}, u32[]{:S(2)}) collective-permute-start(f32[80,128]{1,0:T(8,128)S(1)} %get-tuple-element.52), channel_id=1, source_target_pairs={{0,16},{16,32},{32,48},{48,64},{64,80},{80,96},{96,112},{112,128},... | collective-permute-start | bytes 122888 | tf_op jit(solution)/shard_map/ppermute | solution.py:551
  75.6 3.4 %collective-permute-start.9 = (f32[80,128]{1,0:T(8,128)S(1)}, f32[80,128]{1,0:T(8,128)S(1)}, u32[]{:S(2)}, u32[]{:S(2)}) collective-permute-start(f32[80,128]{1,0:T(8,128)S(1)} %get-tuple-element.53), channel_id=1, source_target_pairs={{16,0},{32,16},{48,32},{64,48},{80,64},{96,80},{112,96},{128,112},... | collective-permute-start | bytes 122888 | tf_op jit(solution)/shard_map/ppermute | solution.py:551
  79.7 7.1 %collective-permute-start.11 = (f32[16,128]{1,0:T(8,128)S(1)}, f32[16,128]{1,0:T(8,128)S(1)}, u32[]{:S(2)}, u32[]{:S(2)}) collective-permute-start(f32[16,128]{1,0:T(8,128)S(1)} %get-tuple-element.55), channel_id=1, source_target_pairs={{16,0},{32,16},{48,32},{64,48},{80,64},{96,80},{112,96},{128,112},... | collective-permute-start | bytes 24584 | tf_op jit(solution)/shard_map/ppermute | solution.py:551
  82.7 4.1 %collective-permute-start.10 = (f32[16,128]{1,0:T(8,128)S(1)}, f32[16,128]{1,0:T(8,128)S(1)}, u32[]{:S(2)}, u32[]{:S(2)}) collective-permute-start(f32[16,128]{1,0:T(8,128)S(1)} %get-tuple-element.55), channel_id=1, source_target_pairs={{0,16},{16,32},{32,48},{48,64},{64,80},{80,96},{96,112},{112,128},... | collective-permute-start | bytes 24584 | tf_op jit(solution)/shard_map/ppermute | solution.py:551
  87.4 3.9 %collective-permute-start.12 = (f32[80,128]{1,0:T(8,128)S(1)}, f32[80,128]{1,0:T(8,128)S(1)}, u32[]{:S(2)}, u32[]{:S(2)}) collective-permute-start(f32[80,128]{1,0:T(8,128)S(1)} %get-tuple-element.62), channel_id=1, source_target_pairs={{0,16},{16,32},{32,48},{48,64},{64,80},{80,96},{96,112},{112,128},... | collective-permute-start | bytes 122888 | tf_op jit(solution)/shard_map/ppermute | solution.py:551
  87.5 4.0 %collective-permute-start.13 = (f32[80,128]{1,0:T(8,128)S(1)}, f32[80,128]{1,0:T(8,128)S(1)}, u32[]{:S(2)}, u32[]{:S(2)}) collective-permute-start(f32[80,128]{1,0:T(8,128)S(1)} %get-tuple-element.63), channel_id=1, source_target_pairs={{16,0},{32,16},{48,32},{64,48},{80,64},{96,80},{112,96},{128,112},... | collective-permute-start | bytes 122888 | tf_op jit(solution)/shard_map/ppermute | solution.py:551
  91.5 7.2 %copy-start.1 = (bf16[288,4608]{1,0:T(8,128)(2,1)S(1)}, bf16[288,4608]{1,0:T(8,128)(2,1)}, u32[]{:S(2)}) copy-start(bf16[288,4608]{1,0:T(8,128)(2,1)} %constant.24.clone.table_ref) | copy-start | bytes 7962628
  94.1 4.5 %collective-permute-start.14 = (f32[64,128]{1,0:T(8,128)S(1)}, f32[64,128]{1,0:T(8,128)S(1)}, u32[]{:S(2)}, u32[]{:S(2)}) collective-permute-start(f32[64,128]{1,0:T(8,128)S(1)} %get-tuple-element.66), channel_id=1, source_target_pairs={{0,16},{16,32},{32,48},{48,64},{64,80},{80,96},{96,112},{112,128},... | collective-permute-start | bytes 98312 | tf_op jit(solution)/shard_map/ppermute | solution.py:551
  94.1 4.6 %collective-permute-start.15 = (f32[64,128]{1,0:T(8,128)S(1)}, f32[64,128]{1,0:T(8,128)S(1)}, u32[]{:S(2)}, u32[]{:S(2)}) collective-permute-start(f32[64,128]{1,0:T(8,128)S(1)} %get-tuple-element.67), channel_id=1, source_target_pairs={{16,0},{32,16},{48,32},{64,48},{80,64},{96,80},{112,96},{128,112},... | collective-permute-start | bytes 98312 | tf_op jit(solution)/shard_map/ppermute | solution.py:551
  101.0 4.4 %collective-permute-start.16 = (f32[80,128]{1,0:T(8,128)S(1)}, f32[80,128]{1,0:T(8,128)S(1)}, u32[]{:S(2)}, u32[]{:S(2)}) collective-permute-start(f32[80,128]{1,0:T(8,128)S(1)} %get-tuple-element.70), channel_id=1, source_target_pairs={{0,16},{16,32},{32,48},{48,64},{64,80},{80,96},{96,112},{112,128},... | collective-permute-start | bytes 122888 | tf_op jit(solution)/shard_map/ppermute | solution.py:551
  101.1 4.7 %collective-permute-start.17 = (f32[80,128]{1,0:T(8,128)S(1)}, f32[80,128]{1,0:T(8,128)S(1)}, u32[]{:S(2)}, u32[]{:S(2)}) collective-permute-start(f32[80,128]{1,0:T(8,128)S(1)} %get-tuple-element.71), channel_id=1, source_target_pairs={{16,0},{32,16},{48,32},{64,48},{80,64},{96,80},{112,96},{128,112},... | collective-permute-start | bytes 122888 | tf_op jit(solution)/shard_map/ppermute | solution.py:551
  106.4 7.7 %collective-permute-start.19 = (f32[16,128]{1,0:T(8,128)S(1)}, f32[16,128]{1,0:T(8,128)S(1)}, u32[]{:S(2)}, u32[]{:S(2)}) collective-permute-start(f32[16,128]{1,0:T(8,128)S(1)} %get-tuple-element.73), channel_id=1, source_target_pairs={{16,0},{32,16},{48,32},{64,48},{80,64},{96,80},{112,96},{128,112},... | collective-permute-start | bytes 24584 | tf_op jit(solution)/shard_map/ppermute | solution.py:551
  110.0 4.1 %collective-permute-start.18 = (f32[16,128]{1,0:T(8,128)S(1)}, f32[16,128]{1,0:T(8,128)S(1)}, u32[]{:S(2)}, u32[]{:S(2)}) collective-permute-start(f32[16,128]{1,0:T(8,128)S(1)} %get-tuple-element.73), channel_id=1, source_target_pairs={{0,16},{16,32},{32,48},{48,64},{64,80},{80,96},{96,112},{112,128},... | collective-permute-start | bytes 24584 | tf_op jit(solution)/shard_map/ppermute | solution.py:551
  114.8 3.9 %collective-permute-start.20 = (f32[80,128]{1,0:T(8,128)S(1)}, f32[80,128]{1,0:T(8,128)S(1)}, u32[]{:S(2)}, u32[]{:S(2)}) collective-permute-start(f32[80,128]{1,0:T(8,128)S(1)} %get-tuple-element.78), channel_id=1, source_target_pairs={{0,16},{16,32},{32,48},{48,64},{64,80},{80,96},{96,112},{112,128},... | collective-permute-start | bytes 122888 | tf_op jit(solution)/shard_map/ppermute | solution.py:551
  114.8 4.0 %collective-permute-start.21 = (f32[80,128]{1,0:T(8,128)S(1)}, f32[80,128]{1,0:T(8,128)S(1)}, u32[]{:S(2)}, u32[]{:S(2)}) collective-permute-start(f32[80,128]{1,0:T(8,128)S(1)} %get-tuple-element.79), channel_id=1, source_target_pairs={{16,0},{32,16},{48,32},{64,48},{80,64},{96,80},{112,96},{128,112},... | collective-permute-start | bytes 122888 | tf_op jit(solution)/shard_map/ppermute | solution.py:551
  121.4 4.5 %collective-permute-start.22 = (f32[64,128]{1,0:T(8,128)S(1)}, f32[64,128]{1,0:T(8,128)S(1)}, u32[]{:S(2)}, u32[]{:S(2)}) collective-permute-start(f32[64,128]{1,0:T(8,128)S(1)} %get-tuple-element.82), channel_id=1, source_target_pairs={{0,16},{16,32},{32,48},{48,64},{64,80},{80,96},{96,112},{112,128},... | collective-permute-start | bytes 98312 | tf_op jit(solution)/shard_map/ppermute | solution.py:551
  121.5 4.6 %collective-permute-start.23 = (f32[64,128]{1,0:T(8,128)S(1)}, f32[64,128]{1,0:T(8,128)S(1)}, u32[]{:S(2)}, u32[]{:S(2)}) collective-permute-start(f32[64,128]{1,0:T(8,128)S(1)} %get-tuple-element.83), channel_id=1, source_target_pairs={{16,0},{32,16},{48,32},{64,48},{80,64},{96,80},{112,96},{128,112},... | collective-permute-start | bytes 98312 | tf_op jit(solution)/shard_map/ppermute | solution.py:551
  126.1 38.5 %copy-start.6 = (f32[192,192]{1,0:T(8,128)S(1)}, f32[192,192]{1,0:T(8,128)}, u32[]{:S(2)}) copy-start(f32[192,192]{1,0:T(8,128)} %constant.25.clone.table_ref) | copy-start | bytes 442372
  126.1 48.0 %copy-start.5 = (f32[6,6,192]{2,1,0:T(8,128)S(1)}, f32[6,6,192]{2,1,0:T(8,128)}, u32[]{:S(2)}) copy-start(f32[6,6,192]{2,1,0:T(8,128)} %rhs_ref.1) | copy-start | bytes 82948
  128.2 6.4 %collective-permute-start.24 = (f32[8,128]{1,0:T(8,128)S(1)}, f32[8,128]{1,0:T(8,128)S(1)}, u32[]{:S(2)}, u32[]{:S(2)}) collective-permute-start(f32[8,128]{1,0:T(8,128)S(1)} %get-tuple-element.88), channel_id=1, source_target_pairs={{0,16},{16,0},{32,48},{48,32},{64,80},{80,64},{96,112},{112,96},{1... | collective-permute-start | bytes 12296 | tf_op jit(solution)/shard_map/ppermute | solution.py:542
  134.6 4.3 %collective-permute-start.25 = (f32[8,128]{1,0:T(8,128)S(1)}, f32[8,128]{1,0:T(8,128)S(1)}, u32[]{:S(2)}, u32[]{:S(2)}) collective-permute-start(f32[8,128]{1,0:T(8,128)S(1)} %add.27), channel_id=1, source_target_pairs={{0,32},{16,48},{32,0},{48,16},{64,96},{80,112},{96,64},{112,80},{1... | collective-permute-start | bytes 12296 | tf_op jit(solution)/shard_map/ppermute | solution.py:542
  139.0 5.8 %collective-permute-start.26 = (f32[8,128]{1,0:T(8,128)S(1)}, f32[8,128]{1,0:T(8,128)S(1)}, u32[]{:S(2)}, u32[]{:S(2)}) collective-permute-start(f32[8,128]{1,0:T(8,128)S(1)} %add.28), channel_id=1, source_target_pairs={{0,64},{16,80},{32,96},{48,112},{64,0},{80,16},{96,32},{112,48},{1... | collective-permute-start | bytes 12296 | tf_op jit(solution)/shard_map/ppermute | solution.py:542
  144.8 9.8 %collective-permute-start.27 = (f32[8,128]{1,0:T(8,128)S(1)}, f32[8,128]{1,0:T(8,128)S(1)}, u32[]{:S(2)}, u32[]{:S(2)}) collective-permute-start(f32[8,128]{1,0:T(8,128)S(1)} %add.29), channel_id=1, source_target_pairs={{0,128},{16,144},{32,160},{48,176},{64,192},{80,208},{96,224},{112... | collective-permute-start | bytes 12296 | tf_op jit(solution)/shard_map/ppermute | solution.py:542
  154.6 13.1 %collective-permute-start.28 = (f32[8,128]{1,0:T(8,128)S(1)}, f32[8,128]{1,0:T(8,128)S(1)}, u32[]{:S(2)}, u32[]{:S(2)}) collective-permute-start(f32[8,128]{1,0:T(8,128)S(1)} %add.30), channel_id=1, source_target_pairs={{0,256},{16,272},{32,288},{48,304},{64,320},{80,336},{96,352},{112... | collective-permute-start | bytes 12296 | tf_op jit(solution)/shard_map/ppermute | solution.py:542

commit v2 on v1

--- a/solution.py
+++ b/solution.py
@@ -223,7 +223,14 @@
     behind_ref[16:80, :] = pack_first([box_ref[b, 64:128, :] for b in range(NB)] + extra[1])
 
 
-def pack_body(rhs_ref, helm_ref, vec_ref, val_ref, size_ref, rows_ref, link_ref, six_ref, eight_ref, a_ref, b_ref, tmp):
+def pack_body(*refs):
+    sources, (a_ref, b_ref), held, (tmp, ready) = refs[:9], refs[9:11], refs[11:20], refs[20:]
+    copies = [pltpu.make_async_copy(sources[n], held[n], ready.at[n]) for n in range(9)]
+    for copy in copies:
+        copy.start()
+    for copy in copies:
+        copy.wait()
+    rhs_ref, helm_ref, vec_ref, val_ref, size_ref, rows_ref, link_ref, six_ref, eight_ref = held
     for t in range(4):
         a_ref[t * 32 : (t + 1) * 32, :] = rows_ref[:, t * 128 : (t + 1) * 128]
         a_ref[128:176, t * 32 : (t + 1) * 32] = vec_ref[t * 48 : (t + 1) * 48, :]
@@ -236,7 +243,7 @@
     b_ref[48:96, 0:64] = nodes[:, 128:192]
     b_ref[48:72, 64:96] = val_ref[...]
     b_ref[72:75, 64:96] = size_ref[...]
-    b_ref[80:81, 64:96] = jnp.broadcast_to(link_ref[...], (1, 32))
+    b_ref[80:81, 64:96] = jnp.broadcast_to(link_ref[0], (1, 32))
     helm = jnp.dot(
         helm_ref[...].reshape(64, 256), eight_ref[...], precision=HIGHEST, preferred_element_type=F32
     )
@@ -245,7 +252,7 @@
 
 
 def unpack_body(
-    me_ref, a_own, a_new, b_own, b_new,
+    me_ref, a_0, a_1, a_2, a_3, b_0, b_1, b_2, b_3,
     dense_ref, rhs_ref, helm_ref, vec_ref, small_ref, box_ref, state_ref, ahead_ref, behind_ref,
 ):
     mine_b = me_ref[0]
@@ -257,10 +264,8 @@
         halves_a, halves_b, where_c = [], [], []
         for tc in range(NB):
             c = mine_c ^ tc
-            at_a = tc | (tb << 2)
-            at_b = tb | (tc << 2)
-            half_a = a_own.at[at_a] if at_a < 8 else a_new.at[at_a - 8]
-            half_b = b_own.at[at_b] if at_b < 8 else b_new.at[at_b - 8]
+            half_a = (a_0, a_1, a_2, a_3)[tb].at[tc]
+            half_b = (b_0, b_1, b_2, b_3)[tc].at[tb]
             for t in range(4):
                 start = pl.multiple_of((b * 4 + c) * 32, 32)
                 dense_ref[pl.ds(start, 32), t * 128 : (t + 1) * 128] = half_a[t * 32 : (t + 1) * 32, :]
@@ -520,6 +525,28 @@
             out_ref[i] = nodes[i * 8 + 1 : i * 8 + 7, :]
 
 
+def last_body(
+    sums_ref, z_ref, w_ref, q_ref, v_ref, rhs_ref, pressure_ref, residual_ref, pressure, residual, done
+):
+    totals = jnp.sum(sums_ref[...], axis=1, keepdims=True)
+    rz, zw, wq, rq, qv, zv = [totals[n : n + 1] for n in range(6)]
+    step_first = rz / zw
+    rz_next = step_first * (step_first * wq - rq)
+    share = 1.0 + rz_next / rz
+    curvature = share * share * zw - share * step_first * (zv + wq) + step_first * step_first * qv
+    step_next = rz_next / curvature
+    z_factor = (step_first + step_next * share)[None]
+    q_factor = (step_next * step_first)[None]
+    pressure[...] = z_factor * z_ref[...] - q_factor * q_ref[...]
+    first = pltpu.make_async_copy(pressure, pressure_ref, done.at[0])
+    first.start()
+    residual[...] = rhs_ref[...] - z_factor * w_ref[...] + q_factor * v_ref[...]
+    second = pltpu.make_async_copy(residual, residual_ref, done.at[1])
+    second.start()
+    first.wait()
+    second.wait()
+
+
 def call(body, outs, scratch=(), scalars=0):
     vmem = pl.BlockSpec(memory_space=pltpu.VMEM)
     smem = pl.BlockSpec(memory_space=pltpu.SMEM)
@@ -537,9 +564,32 @@
     return run
 
 
-def swap(block, axis, bit):
+def swap(block, axis, mask):
     count = lax.axis_size(axis)
-    return lax.ppermute(block, axis, [(i, i ^ (1 << bit)) for i in range(count)])
+    return lax.ppermute(block, axis, [(i, i ^ mask) for i in range(count)])
+
+
+def sum_slabs(sums):
+    slabs, across, around = (lax.axis_size(axis) for axis in ("gx", "gy", "col"))
+    sums = sums + swap(sums, "gx", 1)
+    group = across * around
+    chips = slabs // 2
+    span = -(-chips // group)
+    total = None
+    for round_at in range(span):
+        pairs = []
+        for slab in range(slabs):
+            for n in range(group):
+                away = n + group * round_at
+                if away < chips:
+                    source = (slab // 2 + away) % chips * 2 + slab % 2
+                    pairs.append((source * group + n, slab * group + n))
+        part = lax.ppermute(sums, ("gx", "gy", "col"), pairs)
+        total = part if total is None else total + part
+    for axis in ("col", "gy"):
+        first, second, third = [swap(total, axis, n) for n in (1, 2, 3)]
+        total = (total + first) + (second + third)
+    return total
 
 
 def local(divergence, elem_size, helm_diag, fdm_vectors, fdm_values, coarse_rows, axial_link):
@@ -559,34 +609,38 @@
     wide = (80, 128)
     plane = (64, 128)
 
-    half_a, half_b = call(
-        pack_body, [(ROWS_A, 128), (ROWS_B, 128)], [pltpu.VMEM((48, 192), F32)]
-    )(
+    arguments = (
         divergence,
         helm_diag,
         fdm_vectors.reshape(192, EA),
         fdm_values.reshape(24, EA),
         elem_size,
         coarse_rows,
-        axial_link.reshape(1, 1),
+        axial_link,
         six,
         order_table(8),
     )
-    a_own, b_own = half_a[None], half_b[None]
-    steps_a = (("col", 0), ("col", 1), ("gy", 0), ("gy", 1))
-    steps_b = (("gy", 0), ("gy", 1), ("col", 0), ("col", 1))
-    for n in range(4):
-        a_new = swap(a_own, *steps_a[n])
-        b_new = swap(b_own, *steps_b[n])
-        if n < 3:
-            a_own = jnp.concatenate([a_own, a_new], axis=0)
-            b_own = jnp.concatenate([b_own, b_new], axis=0)
+    half_a, half_b = pl.pallas_call(
+        pack_body,
+        out_shape=[jax.ShapeDtypeStruct((rows, 128), F32) for rows in (ROWS_A, ROWS_B)],
+        in_specs=[pl.BlockSpec(memory_space=pl.ANY)] * 9,
+        out_specs=[pl.BlockSpec(memory_space=pltpu.VMEM)] * 2,
+        scratch_shapes=[pltpu.VMEM(value.shape, F32) for value in arguments]
+        + [pltpu.VMEM((48, 192), F32), pltpu.SemaphoreType.DMA((9,))],
+        compiler_params=pltpu.CompilerParams(vmem_limit_bytes=60 * 1024 * 1024),
+    )(*arguments)
+    stack_a = [half_a] + [swap(half_a, "col", n) for n in (1, 2, 3)]
+    stack_b = [half_b] + [swap(half_b, "gy", n) for n in (1, 2, 3)]
+    stack_a, stack_b = lax.optimization_barrier((stack_a, stack_b))
+    four_a, four_b = jnp.stack(stack_a), jnp.stack(stack_b)
+    parts_a = [four_a] + [swap(four_a, "gy", n) for n in (1, 2, 3)]
+    parts_b = [four_b] + [swap(four_b, "col", n) for n in (1, 2, 3)]
 
     dense, rhs, helm, vectors, small, boxes, state, up, down = call(
         unpack_body,
         [(512, 512), field, velocity, (NB, 192, 128), (NB, 48, 128), velocity, state_shape, wide, wide],
         scalars=1,
-    )(me, a_own, a_new, b_own, b_new)
+    )(me, *parts_a, *parts_b)
 
     def precondition(boxes, state, left, right):
         state, message = call(middle_body, [state_shape, state_shape])(dense, state, left, right)
@@ -619,20 +673,17 @@
         t, left, right, inverse, small, backward, rhs, z, w, q
     )
     own = call(own_body, [(6, 6, 192)] * 4, scalars=1)(me, z, w, q, v, six.T.copy())
-    z, w, q, v = own
-    for bit in range(count.bit_length() - 1):
-        sums = sums + swap(sums, "gx", bit)
-    rz, zw, wq, rq, qv, zv = [jnp.sum(sums[n]) for n in range(6)]
-    step_first = rz / zw
-    rz_next = step_first * (step_first * wq - rq)
-    share = 1.0 + rz_next / rz
-    curvature = share * share * zw - share * step_first * (zv + wq) + step_first * step_first * qv
-    step_next = rz_next / curvature
-    z_factor = step_first + step_next * share
-    q_factor = step_next * step_first
-    pressure = z_factor * z - q_factor * q
-    residual = divergence - z_factor * w + q_factor * v
-    return (pressure, residual)
+    sums = sum_slabs(sums)
+    return tuple(
+        pl.pallas_call(
+            last_body,
+            out_shape=[jax.ShapeDtypeStruct((6, 6, 192), F32)] * 2,
+            in_specs=[pl.BlockSpec(memory_space=pltpu.VMEM)] * 6,
+            out_specs=[pl.BlockSpec(memory_space=pl.ANY)] * 2,
+            scratch_shapes=[pltpu.VMEM((6, 6, 192), F32)] * 2 + [pltpu.SemaphoreType.DMA((2,))],
+            compiler_params=pltpu.CompilerParams(vmem_limit_bytes=40 * 1024 * 1024),
+        )(sums, *own, divergence)
+    )
 
 
 def solution(mesh):

time: 178 us -> 165 us (0.927)
  the two profiles are of different devices: /device:TPU:1 before, /device:TPU:16 now
where the time goes in v2:
time: 165 us; the launch traced here: 164 us
  starting transfers between devices  102 us (62%)
  waiting for transfers between devices  30.8 us (19%)
  Pallas kernels  28.3 us (17%)
  other arithmetic  1.95 us (1%)
  between operations  1.84 us (1%)
    ppermute x19, starting transfers between devices, swap(): return lax.ppermute(block, axis, [(i, i ^ mask) for i in range(count)])  71.2 us
    ppermute x16, starting transfers between devices, exchange(): return (lax.ppermute(up, 'gx', ahead), lax.ppermute(down, 'gx', behind))  26.9 us
    pallas_call x13, Pallas kernels, run(): pl.pallas_call(body, out_shape=[jax.ShapeDtypeStruct(shape, F32) for shap...  25.2 us
    ppermute x19, waiting for transfers between devices, swap(): return lax.ppermute(block, axis, [(i, i ^ mask) for i in range(count)])  17.9 us
    ppermute x16, waiting for transfers between devices, exchange(): return (lax.ppermute(up, 'gx', ahead), lax.ppermute(down, 'gx', behind))  9.95 us
    ppermute x1, starting transfers between devices, sum_slabs(): part = lax.ppermute(sums, ('gx', 'gy', 'col'), pairs)  3.5 us
  transfers between devices with their start and end apart: 36, of which 15 were waited for; matrix products, arithmetic and copies ran while one was open for 1% of the time, Pallas kernels for 6%

profile of v2, /device:TPU:16, one launch (start us, length us, event | category | flops | bytes accessed | tf_op | source)
XLA Modules:
  0.0 164.5 jit_solution(5523967152245304404)
XLA Ops:
  1.3 2.3 %shard_map.131 = (f32[176,128]{1,0:T(8,128)}, f32[224,128]{1,0:T(8,128)}) custom-call(f32[6,6,192]{2,1,0:T(8,128)} %rhs_ref.1, f32[8,8,256]{2,1,0:T(8,128)} %refs_1_.1, f32[192,32]{1,0:T(8,128)} %bitcast.16, f32[24,32]{1,0:T(8,128)} %bitcast.21, f32[3,32]{1,0:T(4,128)} %refs_4_.1, f32[32,512]{1,0:T(8,128)} %refs_5_.1, f32[1,1,1]{2,1,0:T(1,128)S(6)} %copy.14.refs_6_, ...), custom_call_target="tpu_custom_call" | custom-call | tf_op jit(solution)/shard_map/pallas_call | solution.py:623
  3.6 2.4 %collective-permute-start.2 = (f32[176,128]{1,0:T(8,128)}, f32[176,128]{1,0:T(8,128)S(1)}, u32[]{:S(2)}, u32[]{:S(2)}) collective-permute-start(f32[176,128]{1,0:T(8,128)} %get-tuple-element.58), channel_id=1, source_target_pairs={{0,3},{1,2},{2,1},{3,0},{4,7},{5,6},{6,5},{7,4},{8,11},{9,10},{10,... | collective-permute-start | bytes 270344 | tf_op jit(solution)/shard_map/ppermute | solution.py:569
  6.0 4.7 %collective-permute-start.5 = (f32[224,128]{1,0:T(8,128)}, f32[224,128]{1,0:T(8,128)S(1)}, u32[]{:S(2)}, u32[]{:S(2)}) collective-permute-start(f32[224,128]{1,0:T(8,128)} %get-tuple-element.62), channel_id=1, source_target_pairs={{0,12},{4,8},{8,4},{12,0},{1,13},{5,9},{9,5},{13,1},{2,14},{6,10},... | collective-permute-start | bytes 344072 | tf_op jit(solution)/shard_map/ppermute | solution.py:569
  10.7 2.7 %collective-permute-start.4 = (f32[224,128]{1,0:T(8,128)}, f32[224,128]{1,0:T(8,128)S(1)}, u32[]{:S(2)}, u32[]{:S(2)}) collective-permute-start(f32[224,128]{1,0:T(8,128)} %get-tuple-element.62), channel_id=1, source_target_pairs={{0,8},{4,12},{8,0},{12,4},{1,9},{5,13},{9,1},{13,5},{2,10},{6,14},... | collective-permute-start | bytes 344072 | tf_op jit(solution)/shard_map/ppermute | solution.py:569
  13.4 2.4 %collective-permute-start.3 = (f32[224,128]{1,0:T(8,128)}, f32[224,128]{1,0:T(8,128)S(1)}, u32[]{:S(2)}, u32[]{:S(2)}) collective-permute-start(f32[224,128]{1,0:T(8,128)} %get-tuple-element.62), channel_id=1, source_target_pairs={{0,4},{4,0},{8,12},{12,8},{1,5},{5,1},{9,13},{13,9},{2,6},{6,2},{1... | collective-permute-start | bytes 344072 | tf_op jit(solution)/shard_map/ppermute | solution.py:569
  15.8 7.2 %collective-permute-start.1 = (f32[176,128]{1,0:T(8,128)}, f32[176,128]{1,0:T(8,128)S(1)}, u32[]{:S(2)}, u32[]{:S(2)}) collective-permute-start(f32[176,128]{1,0:T(8,128)} %get-tuple-element.58), channel_id=1, source_target_pairs={{0,2},{1,3},{2,0},{3,1},{4,6},{5,7},{6,4},{7,5},{8,10},{9,11},{10,... | collective-permute-start | bytes 270344 | tf_op jit(solution)/shard_map/ppermute | solution.py:569
  23.0 3.1 %collective-permute-start = (f32[176,128]{1,0:T(8,128)}, f32[176,128]{1,0:T(8,128)S(1)}, u32[]{:S(2)}, u32[]{:S(2)}) collective-permute-start(f32[176,128]{1,0:T(8,128)} %get-tuple-element.58), channel_id=1, source_target_pairs={{0,1},{1,0},{2,3},{3,2},{4,5},{5,4},{6,7},{7,6},{8,9},{9,8},{10,11... | collective-permute-start | bytes 270344 | tf_op jit(solution)/shard_map/ppermute | solution.py:569
  26.1 3.5 %collective-permute-done = f32[176,128]{1,0:T(8,128)S(1)} collective-permute-done((f32[176,128]{1,0:T(8,128)}, f32[176,128]{1,0:T(8,128)S(1)}, u32[]{:S(2)}, u32[]{:S(2)}) %collective-permute-start) | collective-permute-done | bytes 90144 | tf_op jit(solution)/shard_map/ppermute | solution.py:569
  29.7 0.9 pad_maximum_fusion.1.a_0
  30.6 2.3 %collective-permute-start.8 = (f32[4,176,128]{2,1,0:T(8,128)S(1)}, f32[4,176,128]{2,1,0:T(8,128)S(1)}, u32[]{:S(2)}, u32[]{:S(2)}) collective-permute-start(f32[4,176,128]{2,1,0:T(8,128)S(1)} %pad_maximum_fusion.1.a_0), channel_id=1, source_target_pairs={{0,12},{4,8},{8,4},{12,0},{1,13},{5,9},{9,5},{13,1},{2,14},{6,10},... | collective-permute-start | bytes 1081352 | tf_op jit(solution)/shard_map/ppermute | solution.py:569
  32.9 0.9 pad_maximum_fusion.b_0
  33.8 4.2 %collective-permute-start.11 = (f32[4,224,128]{2,1,0:T(8,128)S(1)}, f32[4,224,128]{2,1,0:T(8,128)S(1)}, u32[]{:S(2)}, u32[]{:S(2)}) collective-permute-start(f32[4,224,128]{2,1,0:T(8,128)S(1)} %pad_maximum_fusion.b_0), channel_id=1, source_target_pairs={{0,3},{1,2},{2,1},{3,0},{4,7},{5,6},{6,5},{7,4},{8,11},{9,10},{10,... | collective-permute-start | bytes 1376264 | tf_op jit(solution)/shard_map/ppermute | solution.py:569
  38.0 2.5 %collective-permute-start.10 = (f32[4,224,128]{2,1,0:T(8,128)S(1)}, f32[4,224,128]{2,1,0:T(8,128)S(1)}, u32[]{:S(2)}, u32[]{:S(2)}) collective-permute-start(f32[4,224,128]{2,1,0:T(8,128)S(1)} %pad_maximum_fusion.b_0), channel_id=1, source_target_pairs={{0,2},{1,3},{2,0},{3,1},{4,6},{5,7},{6,4},{7,5},{8,10},{9,11},{10,... | collective-permute-start | bytes 1376264 | tf_op jit(solution)/shard_map/ppermute | solution.py:569
  40.5 3.4 %collective-permute-start.9 = (f32[4,224,128]{2,1,0:T(8,128)S(1)}, f32[4,224,128]{2,1,0:T(8,128)S(1)}, u32[]{:S(2)}, u32[]{:S(2)}) collective-permute-start(f32[4,224,128]{2,1,0:T(8,128)S(1)} %pad_maximum_fusion.b_0), channel_id=1, source_target_pairs={{0,1},{1,0},{2,3},{3,2},{4,5},{5,4},{6,7},{7,6},{8,9},{9,8},{10,11... | collective-permute-start | bytes 1376264 | tf_op jit(solution)/shard_map/ppermute | solution.py:569
  43.9 4.0 %collective-permute-start.7 = (f32[4,176,128]{2,1,0:T(8,128)S(1)}, f32[4,176,128]{2,1,0:T(8,128)S(1)}, u32[]{:S(2)}, u32[]{:S(2)}) collective-permute-start(f32[4,176,128]{2,1,0:T(8,128)S(1)} %pad_maximum_fusion.1.a_0), channel_id=1, source_target_pairs={{0,8},{4,12},{8,0},{12,4},{1,9},{5,13},{9,1},{13,5},{2,10},{6,14},... | collective-permute-start | bytes 1081352 | tf_op jit(solution)/shard_map/ppermute | solution.py:569
  47.9 3.9 %collective-permute-start.6 = (f32[4,176,128]{2,1,0:T(8,128)S(1)}, f32[4,176,128]{2,1,0:T(8,128)S(1)}, u32[]{:S(2)}, u32[]{:S(2)}) collective-permute-start(f32[4,176,128]{2,1,0:T(8,128)S(1)} %pad_maximum_fusion.1.a_0), channel_id=1, source_target_pairs={{0,4},{4,0},{8,12},{12,8},{1,5},{5,1},{9,13},{13,9},{2,6},{6,2},{1... | collective-permute-start | bytes 1081352 | tf_op jit(solution)/shard_map/ppermute | solution.py:569
  51.8 0.1 pad_add_fusion.me_ref
  51.9 5.9 %collective-permute-done.7.a_2 = f32[4,176,128]{2,1,0:T(8,128)S(1)} collective-permute-done((f32[4,176,128]{2,1,0:T(8,128)S(1)}, f32[4,176,128]{2,1,0:T(8,128)S(1)}, u32[]{:S(2)}, u32[]{:S(2)}) %collective-permute-start.7) | collective-permute-done | bytes 360480 | tf_op jit(solution)/shard_map/ppermute | solution.py:569
  57.8 1.5 collective-permute-done.6.a_1
  59.3 3.4 %shard_map.132 = (f32[512,512]{1,0:T(8,128)S(1)}, f32[4,288,128]{2,1,0:T(8,128)S(1)}, f32[4,512,128]{2,1,0:T(8,128)S(1)}, f32[4,192,128]{2,1,0:T(8,128)S(1)}, f3...) custom-call(s32[2]{0:T(128)S(1)} %pad_add_fusion.me_ref, ...), custom_call_target="tpu_custom_call" | custom-call | tf_op jit(solution)/shard_map/pallas_call | solution.py:555
  62.7 0.0 collective-permute-start.12
  62.7 5.2 %collective-permute-start.13 = (f32[80,128]{1,0:T(8,128)S(1)}, f32[80,128]{1,0:T(8,128)S(1)}, u32[]{:S(2)}, u32[]{:S(2)}) collective-permute-start(f32[80,128]{1,0:T(8,128)S(1)} %get-tuple-element.69), channel_id=1, source_target_pairs={{16,0},{32,16},{48,32},{64,48},{80,64},{96,80},{112,96},{128,112},... | collective-permute-start | bytes 122888 | tf_op jit(solution)/shard_map/ppermute | solution.py:601
  67.8 1.7 %collective-permute-done.12.left_ref = f32[80,128]{1,0:T(8,128)S(1)} collective-permute-done((f32[80,128]{1,0:T(8,128)S(1)}, f32[80,128]{1,0:T(8,128)S(1)}, u32[]{:S(2)}, u32[]{:S(2)}) %collective-permute-start.12) | collective-permute-done | bytes 40992 | tf_op jit(solution)/shard_map/ppermute | solution.py:601
  69.5 0.6 shard_map.133
  70.2 3.9 %collective-permute-start.15 = (f32[16,128]{1,0:T(8,128)S(1)}, f32[16,128]{1,0:T(8,128)S(1)}, u32[]{:S(2)}, u32[]{:S(2)}) collective-permute-start(f32[16,128]{1,0:T(8,128)S(1)} %get-tuple-element.71), channel_id=1, source_target_pairs={{16,0},{32,16},{48,32},{64,48},{80,64},{96,80},{112,96},{128,112},... | collective-permute-start | bytes 24584 | tf_op jit(solution)/shard_map/ppermute | solution.py:601
  74.0 4.1 %shard_map.134 = (f32[4,288,128]{2,1,0:T(8,128)S(1)}, f32[64,128]{1,0:T(8,128)S(1)}, f32[64,128]{1,0:T(8,128)S(1)}) custom-call(f32[4,512,128]{2,1,0:T(8,128)S(1)} %get-tuple-element.72.box_ref, f32[4,192,128]{2,1,0:T(8,128)S(1)} %get-tuple-element.73.vec_ref, f32[4,48,128]{2,1,0:T(8,128)S(1)} %get-tuple-element.74.small_ref, ...), custom_call_target="tpu_custom_call" | custom-call | tf_op jit(solution)/shard_map/pallas_call | solution.py:555
  78.1 0.2 collective-permute-done.14.left_ref
  78.3 0.6 shard_map.135
  79.0 2.9 %collective-permute-start.17 = (f32[80,128]{1,0:T(8,128)S(1)}, f32[80,128]{1,0:T(8,128)S(1)}, u32[]{:S(2)}, u32[]{:S(2)}) collective-permute-start(f32[80,128]{1,0:T(8,128)S(1)} %get-tuple-element.79), channel_id=1, source_target_pairs={{16,0},{32,16},{48,32},{64,48},{80,64},{96,80},{112,96},{128,112},... | collective-permute-start | bytes 122888 | tf_op jit(solution)/shard_map/ppermute | solution.py:601
  81.9 1.7 %collective-permute-done.16.left_ref = f32[80,128]{1,0:T(8,128)S(1)} collective-permute-done((f32[80,128]{1,0:T(8,128)S(1)}, f32[80,128]{1,0:T(8,128)S(1)}, u32[]{:S(2)}, u32[]{:S(2)}) %collective-permute-start.16) | collective-permute-done | bytes 40992 | tf_op jit(solution)/shard_map/ppermute | solution.py:601
  83.6 2.6 %shard_map.136 = (f32[4,288,128]{2,1,0:T(8,128)S(1)}, f32[4,1536,128]{2,1,0:T(8,128)S(1)}, f32[64,128]{1,0:T(8,128)S(1)}, f32[64,128]{1,0:T(8,128)S(1)}) custom-call(f32[512,512]{1,0:T(8,128)S(1)} %get-tuple-element.66.dense_ref, f32[16,128]{1,0:T(8,128)S(1)} %get-tuple-element.77.state_ref, f32[80,128]{1,0:T(8,128)S(1)} %collective-permute-done.16.left_ref, ...), custom_call_target="tpu_custom_call" | custom-call | tf_op jit(solution)/shard_map/pallas_call | solution.py:555
  86.2 3.0 %collective-permute-start.19 = (f32[64,128]{1,0:T(8,128)S(1)}, f32[64,128]{1,0:T(8,128)S(1)}, u32[]{:S(2)}, u32[]{:S(2)}) collective-permute-start(f32[64,128]{1,0:T(8,128)S(1)} %get-tuple-element.83), channel_id=1, source_target_pairs={{16,0},{32,16},{48,32},{64,48},{80,64},{96,80},{112,96},{128,112},... | collective-permute-start | bytes 98312 | tf_op jit(solution)/shard_map/ppermute | solution.py:601
  89.2 0.4 shard_map.137.inverse_ref
  89.6 1.2 collective-permute-done.18.left_ref
  90.8 0.0 collective-permute-done.19.right_ref
  90.8 2.3 %shard_map.138 = (f32[4,288,128]{2,1,0:T(8,128)S(1)}, f32[4,512,128]{2,1,0:T(8,128)S(1)}, f32[16,128]{1,0:T(8,128)S(1)}, f32[80,128]{1,0:T(8,128)S(1)}, f32[80,128]{1,0:T(8,128)S(1)}) custom-call(f32[4,1536,128]{2,1,0:T(8,128)S(1)} %get-tuple-element.81.t_ref, f32[64,128]{1,0:T(8,128)S(1)} %collective-permute-done.18.left_ref, ...), custom_call_target="tpu_custom_call" | custom-call | tf_op jit(solution)/shard_map/pallas_call | solution.py:555
  93.1 3.0 %collective-permute-start.21 = (f32[80,128]{1,0:T(8,128)S(1)}, f32[80,128]{1,0:T(8,128)S(1)}, u32[]{:S(2)}, u32[]{:S(2)}) collective-permute-start(f32[80,128]{1,0:T(8,128)S(1)} %get-tuple-element.87), channel_id=1, source_target_pairs={{16,0},{32,16},{48,32},{64,48},{80,64},{96,80},{112,96},{128,112},... | collective-permute-start | bytes 122888 | tf_op jit(solution)/shard_map/ppermute | solution.py:601
  96.1 1.7 %collective-permute-done.20.left_ref = f32[80,128]{1,0:T(8,128)S(1)} collective-permute-done((f32[80,128]{1,0:T(8,128)S(1)}, f32[80,128]{1,0:T(8,128)S(1)}, u32[]{:S(2)}, u32[]{:S(2)}) %collective-permute-start.20) | collective-permute-done | bytes 40992 | tf_op jit(solution)/shard_map/ppermute | solution.py:601
  97.7 0.6 shard_map.139
  98.4 3.0 %collective-permute-start.23 = (f32[16,128]{1,0:T(8,128)S(1)}, f32[16,128]{1,0:T(8,128)S(1)}, u32[]{:S(2)}, u32[]{:S(2)}) collective-permute-start(f32[16,128]{1,0:T(8,128)S(1)} %get-tuple-element.89), channel_id=1, source_target_pairs={{16,0},{32,16},{48,32},{64,48},{80,64},{96,80},{112,96},{128,112},... | collective-permute-start | bytes 24584 | tf_op jit(solution)/shard_map/ppermute | solution.py:601
  101.4 4.1 %shard_map.140 = (f32[4,288,128]{2,1,0:T(8,128)S(1)}, f32[64,128]{1,0:T(8,128)S(1)}, f32[64,128]{1,0:T(8,128)S(1)}) custom-call(f32[4,512,128]{2,1,0:T(8,128)S(1)} %get-tuple-element.90.box_ref, f32[4,192,128]{2,1,0:T(8,128)S(1)} %get-tuple-element.73.vec_ref, f32[4,48,128]{2,1,0:T(8,128)S(1)} %get-tuple-element.74.small_ref, ...), custom_call_target="tpu_custom_call" | custom-call | tf_op jit(solution)/shard_map/pallas_call | solution.py:555
  105.4 0.2 collective-permute-done.22.left_ref
  105.6 0.6 shard_map.141
  106.3 2.9 %collective-permute-start.25 = (f32[80,128]{1,0:T(8,128)S(1)}, f32[80,128]{1,0:T(8,128)S(1)}, u32[]{:S(2)}, u32[]{:S(2)}) collective-permute-start(f32[80,128]{1,0:T(8,128)S(1)} %get-tuple-element.95), channel_id=1, source_target_pairs={{16,0},{32,16},{48,32},{64,48},{80,64},{96,80},{112,96},{128,112},... | collective-permute-start | bytes 122888 | tf_op jit(solution)/shard_map/ppermute | solution.py:601
  109.3 1.7 %collective-permute-done.24.left_ref = f32[80,128]{1,0:T(8,128)S(1)} collective-permute-done((f32[80,128]{1,0:T(8,128)S(1)}, f32[80,128]{1,0:T(8,128)S(1)}, u32[]{:S(2)}, u32[]{:S(2)}) %collective-permute-start.24) | collective-permute-done | bytes 40992 | tf_op jit(solution)/shard_map/ppermute | solution.py:601
  110.9 2.6 %shard_map.142 = (f32[4,288,128]{2,1,0:T(8,128)S(1)}, f32[4,1536,128]{2,1,0:T(8,128)S(1)}, f32[64,128]{1,0:T(8,128)S(1)}, f32[64,128]{1,0:T(8,128)S(1)}) custom-call(f32[512,512]{1,0:T(8,128)S(1)} %get-tuple-element.66.dense_ref, f32[16,128]{1,0:T(8,128)S(1)} %get-tuple-element.93.state_ref, f32[80,128]{1,0:T(8,128)S(1)} %collective-permute-done.24.left_ref, ...), custom_call_target="tpu_custom_call" | custom-call | tf_op jit(solution)/shard_map/pallas_call | solution.py:555
  113.6 3.0 %collective-permute-start.27 = (f32[64,128]{1,0:T(8,128)S(1)}, f32[64,128]{1,0:T(8,128)S(1)}, u32[]{:S(2)}, u32[]{:S(2)}) collective-permute-start(f32[64,128]{1,0:T(8,128)S(1)} %get-tuple-element.99), channel_id=1, source_target_pairs={{16,0},{32,16},{48,32},{64,48},{80,64},{96,80},{112,96},{128,112},... | collective-permute-start | bytes 98312 | tf_op jit(solution)/shard_map/ppermute | solution.py:601
  116.5 1.6 collective-permute-done.26.left_ref
  118.1 0.0 collective-permute-done.27.right_ref
  118.1 2.1 %shard_map.143 = (f32[4,288,128]{2,1,0:T(8,128)S(1)}, f32[8,128]{1,0:T(8,128)S(1)}) custom-call(f32[4,1536,128]{2,1,0:T(8,128)S(1)} %get-tuple-element.97.t_ref, f32[64,128]{1,0:T(8,128)S(1)} %collective-permute-done.26.left_ref, f32[64,128]{1,0:T(8,128)S(1)} %collective-permute-done.27.right_ref, f32[4,512,128]{2,1,0:T(8,128)S(1)} %shard_map.137.inverse_ref, ...), custom_call_target="tpu_custom_call" | custom-call | tf_op jit(solution)/shard_map/pallas_call | solution.py:555
  120.2 1.9 %collective-permute-start.28 = (f32[8,128]{1,0:T(8,128)S(1)}, f32[8,128]{1,0:T(8,128)S(1)}, u32[]{:S(2)}, u32[]{:S(2)}) collective-permute-start(f32[8,128]{1,0:T(8,128)S(1)} %get-tuple-element.104), channel_id=1, source_target_pairs={{0,16},{16,0},{32,48},{48,32},{64,80},{80,64},{96,112},{112,96},{1... | collective-permute-start | bytes 12296 | tf_op jit(solution)/shard_map/ppermute | solution.py:569
  122.2 1.1 collective-permute-done.28
  123.3 3.5 %collective-permute-start.29 = (f32[8,128]{1,0:T(8,128)S(1)}, f32[8,128]{1,0:T(8,128)S(1)}, u32[]{:S(2)}, u32[]{:S(2)}) collective-permute-start(f32[8,128]{1,0:T(8,128)S(1)} %add.21), channel_id=1, source_target_pairs={{0,0},{33,1},{66,2},{99,3},{132,4},{165,5},{198,6},{231,7},{264,8}... | collective-permute-start | bytes 12296 | tf_op jit(solution)/shard_map/ppermute | solution.py:587
  126.8 2.9 %collective-permute-done.29 = f32[8,128]{1,0:T(8,128)S(1)} collective-permute-done((f32[8,128]{1,0:T(8,128)S(1)}, f32[8,128]{1,0:T(8,128)S(1)}, u32[]{:S(2)}, u32[]{:S(2)}) %collective-permute-start.29) | collective-permute-done | bytes 4128 | tf_op jit(solution)/shard_map/ppermute | solution.py:587
  129.7 2.2 %collective-permute-start.32 = (f32[8,128]{1,0:T(8,128)S(1)}, f32[8,128]{1,0:T(8,128)S(1)}, u32[]{:S(2)}, u32[]{:S(2)}) collective-permute-start(f32[8,128]{1,0:T(8,128)S(1)} %collective-permute-done.29), channel_id=1, source_target_pairs={{0,3},{1,2},{2,1},{3,0},{4,7},{5,6},{6,5},{7,4},{8,11},{9,10},{10,... | collective-permute-start | bytes 12296 | tf_op jit(solution)/shard_map/ppermute | solution.py:569
  131.9 6.6 %collective-permute-start.31 = (f32[8,128]{1,0:T(8,128)S(1)}, f32[8,128]{1,0:T(8,128)S(1)}, u32[]{:S(2)}, u32[]{:S(2)}) collective-permute-start(f32[8,128]{1,0:T(8,128)S(1)} %collective-permute-done.29), channel_id=1, source_target_pairs={{0,2},{1,3},{2,0},{3,1},{4,6},{5,7},{6,4},{7,5},{8,10},{9,11},{10,... | collective-permute-start | bytes 12296 | tf_op jit(solution)/shard_map/ppermute | solution.py:569
  138.5 1.9 %collective-permute-start.30 = (f32[8,128]{1,0:T(8,128)S(1)}, f32[8,128]{1,0:T(8,128)S(1)}, u32[]{:S(2)}, u32[]{:S(2)}) collective-permute-start(f32[8,128]{1,0:T(8,128)S(1)} %collective-permute-done.29), channel_id=1, source_target_pairs={{0,1},{1,0},{2,3},{3,2},{4,5},{5,4},{6,7},{7,6},{8,9},{9,8},{10,11... | collective-permute-start | bytes 12296 | tf_op jit(solution)/shard_map/ppermute | solution.py:569
  140.4 3.6 %collective-permute-done.30 = f32[8,128]{1,0:T(8,128)S(1)} collective-permute-done((f32[8,128]{1,0:T(8,128)S(1)}, f32[8,128]{1,0:T(8,128)S(1)}, u32[]{:S(2)}, u32[]{:S(2)}) %collective-permute-start.30) | collective-permute-done | bytes 4128 | tf_op jit(solution)/shard_map/ppermute | solution.py:569
  144.0 5.0 %collective-permute-start.35 = (f32[8,128]{1,0:T(8,128)S(1)}, f32[8,128]{1,0:T(8,128)S(1)}, u32[]{:S(2)}, u32[]{:S(2)}) collective-permute-start(f32[8,128]{1,0:T(8,128)S(1)} %add_add_fusion.1), channel_id=1, source_target_pairs={{0,12},{4,8},{8,4},{12,0},{1,13},{5,9},{9,5},{13,1},{2,14},{6,10},... | collective-permute-start | bytes 12296 | tf_op jit(solution)/shard_map/ppermute | solution.py:569
  149.0 9.0 %collective-permute-start.34 = (f32[8,128]{1,0:T(8,128)S(1)}, f32[8,128]{1,0:T(8,128)S(1)}, u32[]{:S(2)}, u32[]{:S(2)}) collective-permute-start(f32[8,128]{1,0:T(8,128)S(1)} %add_add_fusion.1), channel_id=1, source_target_pairs={{0,8},{4,12},{8,0},{12,4},{1,9},{5,13},{9,1},{13,5},{2,10},{6,14},... | collective-permute-start | bytes 12296 | tf_op jit(solution)/shard_map/ppermute | solution.py:569
  158.0 1.9 %collective-permute-start.33 = (f32[8,128]{1,0:T(8,128)S(1)}, f32[8,128]{1,0:T(8,128)S(1)}, u32[]{:S(2)}, u32[]{:S(2)}) collective-permute-start(f32[8,128]{1,0:T(8,128)S(1)} %add_add_fusion.1), channel_id=1, source_target_pairs={{0,4},{4,0},{8,12},{12,8},{1,5},{5,1},{9,13},{13,9},{2,6},{6,2},{1... | collective-permute-start | bytes 12296 | tf_op jit(solution)/shard_map/ppermute | solution.py:569
  159.9 1.2 shard_map.144
  161.2 2.3 %collective-permute-done.33 = f32[8,128]{1,0:T(8,128)S(1)} collective-permute-done((f32[8,128]{1,0:T(8,128)S(1)}, f32[8,128]{1,0:T(8,128)S(1)}, u32[]{:S(2)}, u32[]{:S(2)}) %collective-permute-start.33) | collective-permute-done | bytes 4128 | tf_op jit(solution)/shard_map/ppermute | solution.py:569
  163.5 0.8 shard_map.145
  (37 shorter events, 0.2 us)
Async XLA Ops:
  3.6 19.4 %collective-permute-start.2 = (f32[176,128]{1,0:T(8,128)}, f32[176,128]{1,0:T(8,128)S(1)}, u32[]{:S(2)}, u32[]{:S(2)}) collective-permute-start(f32[176,128]{1,0:T(8,128)} %get-tuple-element.58), channel_id=1, source_target_pairs={{0,3},{1,2},{2,1},{3,0},{4,7},{5,6},{6,5},{7,4},{8,11},{9,10},{10,... | collective-permute-start | bytes 270344 | tf_op jit(solution)/shard_map/ppermute | solution.py:569
  6.0 23.7 %collective-permute-start.5 = (f32[224,128]{1,0:T(8,128)}, f32[224,128]{1,0:T(8,128)S(1)}, u32[]{:S(2)}, u32[]{:S(2)}) collective-permute-start(f32[224,128]{1,0:T(8,128)} %get-tuple-element.62), channel_id=1, source_target_pairs={{0,12},{4,8},{8,4},{12,0},{1,13},{5,9},{9,5},{13,1},{2,14},{6,10},... | collective-permute-start | bytes 344072 | tf_op jit(solution)/shard_map/ppermute | solution.py:569
  10.7 19.0 %collective-permute-start.4 = (f32[224,128]{1,0:T(8,128)}, f32[224,128]{1,0:T(8,128)S(1)}, u32[]{:S(2)}, u32[]{:S(2)}) collective-permute-start(f32[224,128]{1,0:T(8,128)} %get-tuple-element.62), channel_id=1, source_target_pairs={{0,8},{4,12},{8,0},{12,4},{1,9},{5,13},{9,1},{13,5},{2,10},{6,14},... | collective-permute-start | bytes 344072 | tf_op jit(solution)/shard_map/ppermute | solution.py:569
  13.4 16.3 %collective-permute-start.3 = (f32[224,128]{1,0:T(8,128)}, f32[224,128]{1,0:T(8,128)S(1)}, u32[]{:S(2)}, u32[]{:S(2)}) collective-permute-start(f32[224,128]{1,0:T(8,128)} %get-tuple-element.62), channel_id=1, source_target_pairs={{0,4},{4,0},{8,12},{12,8},{1,5},{5,1},{9,13},{13,9},{2,6},{6,2},{1... | collective-permute-start | bytes 344072 | tf_op jit(solution)/shard_map/ppermute | solution.py:569
  15.8 10.3 %collective-permute-start.1 = (f32[176,128]{1,0:T(8,128)}, f32[176,128]{1,0:T(8,128)S(1)}, u32[]{:S(2)}, u32[]{:S(2)}) collective-permute-start(f32[176,128]{1,0:T(8,128)} %get-tuple-element.58), channel_id=1, source_target_pairs={{0,2},{1,3},{2,0},{3,1},{4,6},{5,7},{6,4},{7,5},{8,10},{9,11},{10,... | collective-permute-start | bytes 270344 | tf_op jit(solution)/shard_map/ppermute | solution.py:569
  23.0 6.6 %collective-permute-start = (f32[176,128]{1,0:T(8,128)}, f32[176,128]{1,0:T(8,128)S(1)}, u32[]{:S(2)}, u32[]{:S(2)}) collective-permute-start(f32[176,128]{1,0:T(8,128)} %get-tuple-element.58), channel_id=1, source_target_pairs={{0,1},{1,0},{2,3},{3,2},{4,5},{5,4},{6,7},{7,6},{8,9},{9,8},{10,11... | collective-permute-start | bytes 270344 | tf_op jit(solution)/shard_map/ppermute | solution.py:569
  30.6 17.3 %collective-permute-start.8 = (f32[4,176,128]{2,1,0:T(8,128)S(1)}, f32[4,176,128]{2,1,0:T(8,128)S(1)}, u32[]{:S(2)}, u32[]{:S(2)}) collective-permute-start(f32[4,176,128]{2,1,0:T(8,128)S(1)} %pad_maximum_fusion.1.a_0), channel_id=1, source_target_pairs={{0,12},{4,8},{8,4},{12,0},{1,13},{5,9},{9,5},{13,1},{2,14},{6,10},... | collective-permute-start | bytes 1081352 | tf_op jit(solution)/shard_map/ppermute | solution.py:569
  33.8 25.5 %collective-permute-start.11 = (f32[4,224,128]{2,1,0:T(8,128)S(1)}, f32[4,224,128]{2,1,0:T(8,128)S(1)}, u32[]{:S(2)}, u32[]{:S(2)}) collective-permute-start(f32[4,224,128]{2,1,0:T(8,128)S(1)} %pad_maximum_fusion.b_0), channel_id=1, source_target_pairs={{0,3},{1,2},{2,1},{3,0},{4,7},{5,6},{6,5},{7,4},{8,11},{9,10},{10,... | collective-permute-start | bytes 1376264 | tf_op jit(solution)/shard_map/ppermute | solution.py:569
  38.0 21.3 %collective-permute-start.10 = (f32[4,224,128]{2,1,0:T(8,128)S(1)}, f32[4,224,128]{2,1,0:T(8,128)S(1)}, u32[]{:S(2)}, u32[]{:S(2)}) collective-permute-start(f32[4,224,128]{2,1,0:T(8,128)S(1)} %pad_maximum_fusion.b_0), channel_id=1, source_target_pairs={{0,2},{1,3},{2,0},{3,1},{4,6},{5,7},{6,4},{7,5},{8,10},{9,11},{10,... | collective-permute-start | bytes 1376264 | tf_op jit(solution)/shard_map/ppermute | solution.py:569
  40.5 18.8 %collective-permute-start.9 = (f32[4,224,128]{2,1,0:T(8,128)S(1)}, f32[4,224,128]{2,1,0:T(8,128)S(1)}, u32[]{:S(2)}, u32[]{:S(2)}) collective-permute-start(f32[4,224,128]{2,1,0:T(8,128)S(1)} %pad_maximum_fusion.b_0), channel_id=1, source_target_pairs={{0,1},{1,0},{2,3},{3,2},{4,5},{5,4},{6,7},{7,6},{8,9},{9,8},{10,11... | collective-permute-start | bytes 1376264 | tf_op jit(solution)/shard_map/ppermute | solution.py:569
  43.9 13.9 %collective-permute-start.7 = (f32[4,176,128]{2,1,0:T(8,128)S(1)}, f32[4,176,128]{2,1,0:T(8,128)S(1)}, u32[]{:S(2)}, u32[]{:S(2)}) collective-permute-start(f32[4,176,128]{2,1,0:T(8,128)S(1)} %pad_maximum_fusion.1.a_0), channel_id=1, source_target_pairs={{0,8},{4,12},{8,0},{12,4},{1,9},{5,13},{9,1},{13,5},{2,10},{6,14},... | collective-permute-start | bytes 1081352 | tf_op jit(solution)/shard_map/ppermute | solution.py:569
  47.9 11.4 %collective-permute-start.6 = (f32[4,176,128]{2,1,0:T(8,128)S(1)}, f32[4,176,128]{2,1,0:T(8,128)S(1)}, u32[]{:S(2)}, u32[]{:S(2)}) collective-permute-start(f32[4,176,128]{2,1,0:T(8,128)S(1)} %pad_maximum_fusion.1.a_0), channel_id=1, source_target_pairs={{0,4},{4,0},{8,12},{12,8},{1,5},{5,1},{9,13},{13,9},{2,6},{6,2},{1... | collective-permute-start | bytes 1081352 | tf_op jit(solution)/shard_map/ppermute | solution.py:569
  51.9 31.7 %copy-start = (bf16[1536,864]{1,0:T(8,128)(2,1)S(1)}, bf16[1536,864]{1,0:T(8,128)(2,1)}, u32[]{:S(2)}) copy-start(bf16[1536,864]{1,0:T(8,128)(2,1)} %constant.19.clone.table_ref) | copy-start | bytes 7962628
  62.7 6.8 %collective-permute-start.12 = (f32[80,128]{1,0:T(8,128)S(1)}, f32[80,128]{1,0:T(8,128)S(1)}, u32[]{:S(2)}, u32[]{:S(2)}) collective-permute-start(f32[80,128]{1,0:T(8,128)S(1)} %get-tuple-element.68), channel_id=1, source_target_pairs={{0,16},{16,32},{32,48},{48,64},{64,80},{80,96},{96,112},{112,128},... | collective-permute-start | bytes 122888 | tf_op jit(solution)/shard_map/ppermute | solution.py:601
  62.7 6.8 %collective-permute-start.13 = (f32[80,128]{1,0:T(8,128)S(1)}, f32[80,128]{1,0:T(8,128)S(1)}, u32[]{:S(2)}, u32[]{:S(2)}) collective-permute-start(f32[80,128]{1,0:T(8,128)S(1)} %get-tuple-element.69), channel_id=1, source_target_pairs={{16,0},{32,16},{48,32},{64,48},{80,64},{96,80},{112,96},{128,112},... | collective-permute-start | bytes 122888 | tf_op jit(solution)/shard_map/ppermute | solution.py:601
  70.2 7.9 %collective-permute-start.15 = (f32[16,128]{1,0:T(8,128)S(1)}, f32[16,128]{1,0:T(8,128)S(1)}, u32[]{:S(2)}, u32[]{:S(2)}) collective-permute-start(f32[16,128]{1,0:T(8,128)S(1)} %get-tuple-element.71), channel_id=1, source_target_pairs={{16,0},{32,16},{48,32},{64,48},{80,64},{96,80},{112,96},{128,112},... | collective-permute-start | bytes 24584 | tf_op jit(solution)/shard_map/ppermute | solution.py:601
  74.0 4.3 %collective-permute-start.14 = (f32[16,128]{1,0:T(8,128)S(1)}, f32[16,128]{1,0:T(8,128)S(1)}, u32[]{:S(2)}, u32[]{:S(2)}) collective-permute-start(f32[16,128]{1,0:T(8,128)S(1)} %get-tuple-element.71), channel_id=1, source_target_pairs={{0,16},{16,32},{32,48},{48,64},{64,80},{80,96},{96,112},{112,128},... | collective-permute-start | bytes 24584 | tf_op jit(solution)/shard_map/ppermute | solution.py:601
  78.9 4.7 %collective-permute-start.16 = (f32[80,128]{1,0:T(8,128)S(1)}, f32[80,128]{1,0:T(8,128)S(1)}, u32[]{:S(2)}, u32[]{:S(2)}) collective-permute-start(f32[80,128]{1,0:T(8,128)S(1)} %get-tuple-element.78), channel_id=1, source_target_pairs={{0,16},{16,32},{32,48},{48,64},{64,80},{80,96},{96,112},{112,128},... | collective-permute-start | bytes 122888 | tf_op jit(solution)/shard_map/ppermute | solution.py:601
  79.0 4.6 %collective-permute-start.17 = (f32[80,128]{1,0:T(8,128)S(1)}, f32[80,128]{1,0:T(8,128)S(1)}, u32[]{:S(2)}, u32[]{:S(2)}) collective-permute-start(f32[80,128]{1,0:T(8,128)S(1)} %get-tuple-element.79), channel_id=1, source_target_pairs={{16,0},{32,16},{48,32},{64,48},{80,64},{96,80},{112,96},{128,112},... | collective-permute-start | bytes 122888 | tf_op jit(solution)/shard_map/ppermute | solution.py:601
  83.6 7.2 %copy-start.1 = (bf16[288,4608]{1,0:T(8,128)(2,1)S(1)}, bf16[288,4608]{1,0:T(8,128)(2,1)}, u32[]{:S(2)}) copy-start(bf16[288,4608]{1,0:T(8,128)(2,1)} %constant.20.clone.table_ref) | copy-start | bytes 7962628
  86.2 4.6 %collective-permute-start.18 = (f32[64,128]{1,0:T(8,128)S(1)}, f32[64,128]{1,0:T(8,128)S(1)}, u32[]{:S(2)}, u32[]{:S(2)}) collective-permute-start(f32[64,128]{1,0:T(8,128)S(1)} %get-tuple-element.82), channel_id=1, source_target_pairs={{0,16},{16,32},{32,48},{48,64},{64,80},{80,96},{96,112},{112,128},... | collective-permute-start | bytes 98312 | tf_op jit(solution)/shard_map/ppermute | solution.py:601
  86.2 4.6 %collective-permute-start.19 = (f32[64,128]{1,0:T(8,128)S(1)}, f32[64,128]{1,0:T(8,128)S(1)}, u32[]{:S(2)}, u32[]{:S(2)}) collective-permute-start(f32[64,128]{1,0:T(8,128)S(1)} %get-tuple-element.83), channel_id=1, source_target_pairs={{16,0},{32,16},{48,32},{64,48},{80,64},{96,80},{112,96},{128,112},... | collective-permute-start | bytes 98312 | tf_op jit(solution)/shard_map/ppermute | solution.py:601
  93.1 4.7 %collective-permute-start.20 = (f32[80,128]{1,0:T(8,128)S(1)}, f32[80,128]{1,0:T(8,128)S(1)}, u32[]{:S(2)}, u32[]{:S(2)}) collective-permute-start(f32[80,128]{1,0:T(8,128)S(1)} %get-tuple-element.86), channel_id=1, source_target_pairs={{0,16},{16,32},{32,48},{48,64},{64,80},{80,96},{96,112},{112,128},... | collective-permute-start | bytes 122888 | tf_op jit(solution)/shard_map/ppermute | solution.py:601
  93.1 4.6 %collective-permute-start.21 = (f32[80,128]{1,0:T(8,128)S(1)}, f32[80,128]{1,0:T(8,128)S(1)}, u32[]{:S(2)}, u32[]{:S(2)}) collective-permute-start(f32[80,128]{1,0:T(8,128)S(1)} %get-tuple-element.87), channel_id=1, source_target_pairs={{16,0},{32,16},{48,32},{64,48},{80,64},{96,80},{112,96},{128,112},... | collective-permute-start | bytes 122888 | tf_op jit(solution)/shard_map/ppermute | solution.py:601
  98.4 7.0 %collective-permute-start.23 = (f32[16,128]{1,0:T(8,128)S(1)}, f32[16,128]{1,0:T(8,128)S(1)}, u32[]{:S(2)}, u32[]{:S(2)}) collective-permute-start(f32[16,128]{1,0:T(8,128)S(1)} %get-tuple-element.89), channel_id=1, source_target_pairs={{16,0},{32,16},{48,32},{64,48},{80,64},{96,80},{112,96},{128,112},... | collective-permute-start | bytes 24584 | tf_op jit(solution)/shard_map/ppermute | solution.py:601
  101.4 4.3 %collective-permute-start.22 = (f32[16,128]{1,0:T(8,128)S(1)}, f32[16,128]{1,0:T(8,128)S(1)}, u32[]{:S(2)}, u32[]{:S(2)}) collective-permute-start(f32[16,128]{1,0:T(8,128)S(1)} %get-tuple-element.89), channel_id=1, source_target_pairs={{0,16},{16,32},{32,48},{48,64},{64,80},{80,96},{96,112},{112,128},... | collective-permute-start | bytes 24584 | tf_op jit(solution)/shard_map/ppermute | solution.py:601
  106.3 4.7 %collective-permute-start.24 = (f32[80,128]{1,0:T(8,128)S(1)}, f32[80,128]{1,0:T(8,128)S(1)}, u32[]{:S(2)}, u32[]{:S(2)}) collective-permute-start(f32[80,128]{1,0:T(8,128)S(1)} %get-tuple-element.94), channel_id=1, source_target_pairs={{0,16},{16,32},{32,48},{48,64},{64,80},{80,96},{96,112},{112,128},... | collective-permute-start | bytes 122888 | tf_op jit(solution)/shard_map/ppermute | solution.py:601
  106.3 4.6 %collective-permute-start.25 = (f32[80,128]{1,0:T(8,128)S(1)}, f32[80,128]{1,0:T(8,128)S(1)}, u32[]{:S(2)}, u32[]{:S(2)}) collective-permute-start(f32[80,128]{1,0:T(8,128)S(1)} %get-tuple-element.95), channel_id=1, source_target_pairs={{16,0},{32,16},{48,32},{64,48},{80,64},{96,80},{112,96},{128,112},... | collective-permute-start | bytes 122888 | tf_op jit(solution)/shard_map/ppermute | solution.py:601
  113.5 4.6 %collective-permute-start.26 = (f32[64,128]{1,0:T(8,128)S(1)}, f32[64,128]{1,0:T(8,128)S(1)}, u32[]{:S(2)}, u32[]{:S(2)}) collective-permute-start(f32[64,128]{1,0:T(8,128)S(1)} %get-tuple-element.98), channel_id=1, source_target_pairs={{0,16},{16,32},{32,48},{48,64},{64,80},{80,96},{96,112},{112,128},... | collective-permute-start | bytes 98312 | tf_op jit(solution)/shard_map/ppermute | solution.py:601
  113.6 4.6 %collective-permute-start.27 = (f32[64,128]{1,0:T(8,128)S(1)}, f32[64,128]{1,0:T(8,128)S(1)}, u32[]{:S(2)}, u32[]{:S(2)}) collective-permute-start(f32[64,128]{1,0:T(8,128)S(1)} %get-tuple-element.99), channel_id=1, source_target_pairs={{16,0},{32,16},{48,32},{64,48},{80,64},{96,80},{112,96},{128,112},... | collective-permute-start | bytes 98312 | tf_op jit(solution)/shard_map/ppermute | solution.py:601
  118.1 41.8 %copy-start.3 = (f32[192,192]{1,0:T(8,128)S(1)}, f32[192,192]{1,0:T(8,128)}, u32[]{:S(2)}) copy-start(f32[192,192]{1,0:T(8,128)} %constant.21.clone.table_ref) | copy-start | bytes 442372
  118.1 45.4 %copy-start.2 = (f32[6,6,192]{2,1,0:T(8,128)S(1)}, f32[6,6,192]{2,1,0:T(8,128)}, u32[]{:S(2)}) copy-start(f32[6,6,192]{2,1,0:T(8,128)} %rhs_ref.1) | copy-start | bytes 82948
  120.2 3.1 %collective-permute-start.28 = (f32[8,128]{1,0:T(8,128)S(1)}, f32[8,128]{1,0:T(8,128)S(1)}, u32[]{:S(2)}, u32[]{:S(2)}) collective-permute-start(f32[8,128]{1,0:T(8,128)S(1)} %get-tuple-element.104), channel_id=1, source_target_pairs={{0,16},{16,0},{32,48},{48,32},{64,80},{80,64},{96,112},{112,96},{1... | collective-permute-start | bytes 12296 | tf_op jit(solution)/shard_map/ppermute | solution.py:569
  123.3 6.4 %collective-permute-start.29 = (f32[8,128]{1,0:T(8,128)S(1)}, f32[8,128]{1,0:T(8,128)S(1)}, u32[]{:S(2)}, u32[]{:S(2)}) collective-permute-start(f32[8,128]{1,0:T(8,128)S(1)} %add.21), channel_id=1, source_target_pairs={{0,0},{33,1},{66,2},{99,3},{132,4},{165,5},{198,6},{231,7},{264,8}... | collective-permute-start | bytes 12296 | tf_op jit(solution)/shard_map/ppermute | solution.py:587
  129.7 10.7 %collective-permute-start.32 = (f32[8,128]{1,0:T(8,128)S(1)}, f32[8,128]{1,0:T(8,128)S(1)}, u32[]{:S(2)}, u32[]{:S(2)}) collective-permute-start(f32[8,128]{1,0:T(8,128)S(1)} %collective-permute-done.29), channel_id=1, source_target_pairs={{0,3},{1,2},{2,1},{3,0},{4,7},{5,6},{6,5},{7,4},{8,11},{9,10},{10,... | collective-permute-start | bytes 12296 | tf_op jit(solution)/shard_map/ppermute | solution.py:569
  131.9 8.5 %collective-permute-start.31 = (f32[8,128]{1,0:T(8,128)S(1)}, f32[8,128]{1,0:T(8,128)S(1)}, u32[]{:S(2)}, u32[]{:S(2)}) collective-permute-start(f32[8,128]{1,0:T(8,128)S(1)} %collective-permute-done.29), channel_id=1, source_target_pairs={{0,2},{1,3},{2,0},{3,1},{4,6},{5,7},{6,4},{7,5},{8,10},{9,11},{10,... | collective-permute-start | bytes 12296 | tf_op jit(solution)/shard_map/ppermute | solution.py:569
  138.5 5.5 %collective-permute-start.30 = (f32[8,128]{1,0:T(8,128)S(1)}, f32[8,128]{1,0:T(8,128)S(1)}, u32[]{:S(2)}, u32[]{:S(2)}) collective-permute-start(f32[8,128]{1,0:T(8,128)S(1)} %collective-permute-done.29), channel_id=1, source_target_pairs={{0,1},{1,0},{2,3},{3,2},{4,5},{5,4},{6,7},{7,6},{8,9},{9,8},{10,11... | collective-permute-start | bytes 12296 | tf_op jit(solution)/shard_map/ppermute | solution.py:569
  144.0 17.2 %collective-permute-start.35 = (f32[8,128]{1,0:T(8,128)S(1)}, f32[8,128]{1,0:T(8,128)S(1)}, u32[]{:S(2)}, u32[]{:S(2)}) collective-permute-start(f32[8,128]{1,0:T(8,128)S(1)} %add_add_fusion.1), channel_id=1, source_target_pairs={{0,12},{4,8},{8,4},{12,0},{1,13},{5,9},{9,5},{13,1},{2,14},{6,10},... | collective-permute-start | bytes 12296 | tf_op jit(solution)/shard_map/ppermute | solution.py:569
  149.0 12.2 %collective-permute-start.34 = (f32[8,128]{1,0:T(8,128)S(1)}, f32[8,128]{1,0:T(8,128)S(1)}, u32[]{:S(2)}, u32[]{:S(2)}) collective-permute-start(f32[8,128]{1,0:T(8,128)S(1)} %add_add_fusion.1), channel_id=1, source_target_pairs={{0,8},{4,12},{8,0},{12,4},{1,9},{5,13},{9,1},{13,5},{2,10},{6,14},... | collective-permute-start | bytes 12296 | tf_op jit(solution)/shard_map/ppermute | solution.py:569
  158.0 5.5 %collective-permute-start.33 = (f32[8,128]{1,0:T(8,128)S(1)}, f32[8,128]{1,0:T(8,128)S(1)}, u32[]{:S(2)}, u32[]{:S(2)}) collective-permute-start(f32[8,128]{1,0:T(8,128)S(1)} %add_add_fusion.1), channel_id=1, source_target_pairs={{0,4},{4,0},{8,12},{12,8},{1,5},{5,1},{9,13},{13,9},{2,6},{6,2},{1... | collective-permute-start | bytes 12296 | tf_op jit(solution)/shard_map/ppermute | solution.py:569

commit v3 on v2

--- a/solution.py
+++ b/solution.py
@@ -46,7 +46,7 @@
 ROWS_P = 288
 ROWS_V = 512
 ROWS_A = 176
-ROWS_B = 224
+ROWS = 400
 
 
 def basis_tables():
@@ -224,7 +224,8 @@
 
 
 def pack_body(*refs):
-    sources, (a_ref, b_ref), held, (tmp, ready) = refs[:9], refs[9:11], refs[11:20], refs[20:]
+    sources, out_ref, held, (tmp, ready) = refs[:9], refs[9], refs[10:19], refs[19:]
+    a_ref, b_ref = out_ref.at[0:ROWS_A], out_ref.at[ROWS_A:ROWS]
     copies = [pltpu.make_async_copy(sources[n], held[n], ready.at[n]) for n in range(9)]
     for copy in copies:
         copy.start()
@@ -251,44 +252,33 @@
     b_ref[160:224, :] = helm[:, 128:256]
 
 
+def joined(all_ref, b, start, rows, quarter):
+    place = lanes((rows, 128)) // EA
+    total = None
+    for c in range(4):
+        moved = turn(all_ref[b * 4 + c, start : start + rows, :], (c - quarter) * 32)
+        part = jnp.where(place == c, moved, 0.0)
+        total = part if total is None else total + part
+    return total
+
+
 def unpack_body(
-    me_ref, a_0, a_1, a_2, a_3, b_0, b_1, b_2, b_3,
-    dense_ref, rhs_ref, helm_ref, vec_ref, small_ref, box_ref, state_ref, ahead_ref, behind_ref,
+    all_ref, dense_ref, rhs_ref, helm_ref, vec_ref, small_ref, box_ref, state_ref, ahead_ref, behind_ref
 ):
-    mine_b = me_ref[0]
-    mine_c = me_ref[1]
-    place = lanes((1, 128)) // EA
-
-    for tb in range(NB):
-        b = mine_b ^ tb
-        halves_a, halves_b, where_c = [], [], []
-        for tc in range(NB):
-            c = mine_c ^ tc
-            half_a = (a_0, a_1, a_2, a_3)[tb].at[tc]
-            half_b = (b_0, b_1, b_2, b_3)[tc].at[tb]
+    for b in range(NB):
+        for c in range(4):
+            at = (b * 4 + c) * 32
             for t in range(4):
-                start = pl.multiple_of((b * 4 + c) * 32, 32)
-                dense_ref[pl.ds(start, 32), t * 128 : (t + 1) * 128] = half_a[t * 32 : (t + 1) * 32, :]
-            halves_a.append(half_a)
-            halves_b.append(half_b)
-            where_c.append(c)
-
-        def joined(halves, start, rows, quarter):
-            total = None
-            for half, c in zip(halves, where_c):
-                moved = pltpu.roll(half[start : start + rows, :], ((c - quarter) & 3) * 32, 1)
-                part = jnp.where(place == c, moved, 0.0)
-                total = part if total is None else total + part
-            return total
-
+                dense_ref[at : at + 32, t * 128 : (t + 1) * 128] = all_ref[b * 4 + c, t * 32 : (t + 1) * 32, :]
+        for t in range(4):
+            vec_ref[b, t * 48 : (t + 1) * 48, :] = joined(all_ref, b, 128, 48, t)
         for k in range(6):
-            rhs_ref[b, k * 48 : (k + 1) * 48, :] = joined(halves_b, 48 * (k // 4), 48, k % 4)
-        small_ref[b, :, :] = joined(halves_b, 48, 48, 2)
+            rhs_ref[b, k * 48 : (k + 1) * 48, :] = joined(all_ref, b, ROWS_A + 48 * (k // 4), 48, k % 4)
+        small_ref[b, :, :] = joined(all_ref, b, ROWS_A + 48, 48, 2)
         for k in range(8):
-            helm_ref[b, k * 64 : (k + 1) * 64, :] = joined(halves_b, 96 + 64 * (k // 4), 64, k % 4)
-        for t in range(4):
-            vec_ref[b, t * 48 : (t + 1) * 48, :] = joined(halves_a, 128, 48, t)
-
+            helm_ref[b, k * 64 : (k + 1) * 64, :] = joined(
+                all_ref, b, ROWS_A + 96 + 64 * (k // 4), 64, k % 4
+            )
     begin_kernel_part(
         rhs_ref, small_ref, dense_ref, box_ref, state_ref, ahead_ref, behind_ref,
         ([helm_ref[b, 448:512, :] for b in range(NB)], [helm_ref[b, 0:64, :] for b in range(NB)]),
@@ -528,7 +518,7 @@
 def last_body(
     sums_ref, z_ref, w_ref, q_ref, v_ref, rhs_ref, pressure_ref, residual_ref, pressure, residual, done
 ):
-    totals = jnp.sum(sums_ref[...], axis=1, keepdims=True)
+    totals = jnp.sum(jnp.sum(sums_ref[...], axis=0), axis=1, keepdims=True)
     rz, zw, wq, rq, qv, zv = [totals[n : n + 1] for n in range(6)]
     step_first = rz / zw
     rz_next = step_first * (step_first * wq - rq)
@@ -564,32 +554,8 @@
     return run
 
 
-def swap(block, axis, mask):
-    count = lax.axis_size(axis)
-    return lax.ppermute(block, axis, [(i, i ^ mask) for i in range(count)])
-
-
-def sum_slabs(sums):
-    slabs, across, around = (lax.axis_size(axis) for axis in ("gx", "gy", "col"))
-    sums = sums + swap(sums, "gx", 1)
-    group = across * around
-    chips = slabs // 2
-    span = -(-chips // group)
-    total = None
-    for round_at in range(span):
-        pairs = []
-        for slab in range(slabs):
-            for n in range(group):
-                away = n + group * round_at
-                if away < chips:
-                    source = (slab // 2 + away) % chips * 2 + slab % 2
-                    pairs.append((source * group + n, slab * group + n))
-        part = lax.ppermute(sums, ("gx", "gy", "col"), pairs)
-        total = part if total is None else total + part
-    for axis in ("col", "gy"):
-        first, second, third = [swap(total, axis, n) for n in (1, 2, 3)]
-        total = (total + first) + (second + third)
-    return total
+def tell_all(block, axes, count):
+    return lax.all_to_all(jnp.broadcast_to(block[None], (count,) + block.shape), axes, 0, 0)
 
 
 def local(divergence, elem_size, helm_diag, fdm_vectors, fdm_values, coarse_rows, axial_link):
@@ -620,27 +586,21 @@
         six,
         order_table(8),
     )
-    half_a, half_b = pl.pallas_call(
+    own_part = pl.pallas_call(
         pack_body,
-        out_shape=[jax.ShapeDtypeStruct((rows, 128), F32) for rows in (ROWS_A, ROWS_B)],
+        out_shape=jax.ShapeDtypeStruct((ROWS, 128), F32),
         in_specs=[pl.BlockSpec(memory_space=pl.ANY)] * 9,
-        out_specs=[pl.BlockSpec(memory_space=pltpu.VMEM)] * 2,
+        out_specs=pl.BlockSpec(memory_space=pltpu.VMEM),
         scratch_shapes=[pltpu.VMEM(value.shape, F32) for value in arguments]
         + [pltpu.VMEM((48, 192), F32), pltpu.SemaphoreType.DMA((9,))],
         compiler_params=pltpu.CompilerParams(vmem_limit_bytes=60 * 1024 * 1024),
     )(*arguments)
-    stack_a = [half_a] + [swap(half_a, "col", n) for n in (1, 2, 3)]
-    stack_b = [half_b] + [swap(half_b, "gy", n) for n in (1, 2, 3)]
-    stack_a, stack_b = lax.optimization_barrier((stack_a, stack_b))
-    four_a, four_b = jnp.stack(stack_a), jnp.stack(stack_b)
-    parts_a = [four_a] + [swap(four_a, "gy", n) for n in (1, 2, 3)]
-    parts_b = [four_b] + [swap(four_b, "col", n) for n in (1, 2, 3)]
+    everything = tell_all(own_part, ("gy", "col"), 16)
 
     dense, rhs, helm, vectors, small, boxes, state, up, down = call(
         unpack_body,
         [(512, 512), field, velocity, (NB, 192, 128), (NB, 48, 128), velocity, state_shape, wide, wide],
-        scalars=1,
-    )(me, *parts_a, *parts_b)
+    )(everything)
 
     def precondition(boxes, state, left, right):
         state, message = call(middle_body, [state_shape, state_shape])(dense, state, left, right)
@@ -673,7 +633,7 @@
         t, left, right, inverse, small, backward, rhs, z, w, q
     )
     own = call(own_body, [(6, 6, 192)] * 4, scalars=1)(me, z, w, q, v, six.T.copy())
-    sums = sum_slabs(sums)
+    sums = tell_all(sums, "gx", count)
     return tuple(
         pl.pallas_call(
             last_body,

time: 165 us -> 144 us (0.87)
  the two profiles are of different devices: /device:TPU:16 before, /device:TPU:1 now
where the time goes in v3:
time: 144 us; the launch traced here: 143 us
  blocking collectives  46 us (32%)
  starting transfers between devices  45.2 us (31%)
  Pallas kernels  26.8 us (19%)
  waiting for transfers between devices  21.9 us (15%)
  local copies, waits for them, and re-layouts  1.82 us (1%)
  between operations  1.63 us (1%)
    all_to_all x1, blocking collectives, tell_all(): lax.all_to_all(jnp.broadcast_to(block[None], (count,) + block.shape), axe...  46 us
    ppermute x16, starting transfers between devices, exchange(): return (lax.ppermute(up, 'gx', ahead), lax.ppermute(down, 'gx', behind))  30.6 us
    pallas_call x13, Pallas kernels, run(): pl.pallas_call(body, out_shape=[jax.ShapeDtypeStruct(shape, F32) for shap...  23.6 us
    all_to_all x1, starting transfers between devices, tell_all(): lax.all_to_all(jnp.broadcast_to(block[None], (count,) + block.shape), axe...  14.6 us
    all_to_all x1, waiting for transfers between devices, tell_all(): lax.all_to_all(jnp.broadcast_to(block[None], (count,) + block.shape), axe...  14.5 us
    ppermute x16, waiting for transfers between devices, exchange(): return (lax.ppermute(up, 'gx', ahead), lax.ppermute(down, 'gx', behind))  7.39 us
  transfers between devices with their start and end apart: 17, of which 13 were waited for; matrix products, arithmetic and copies ran while one was open for 0% of the time, Pallas kernels for 7%

profile of v3, /device:TPU:1, one launch (start us, length us, event | category | flops | bytes accessed | tf_op | source)
XLA Modules:
  0.0 143.4 jit_solution(8805013680626029211)
XLA Ops:
  1.3 2.4 %shard_map.131 = f32[400,128]{1,0:T(8,128)} custom-call(f32[6,6,192]{2,1,0:T(8,128)} %rhs_ref.1, f32[8,8,256]{2,1,0:T(8,128)} %refs_1_.1, f32[192,32]{1,0:T(8,128)} %bitcast.4, f32[24,32]{1,0:T(8,128)} %bitcast.5, f32[3,32]{1,0:T(4,128)} %refs_4_.1, f32[32,512]{1,0:T(8,128)} %refs_5_.1, f32[1,1,1]{2,1,0:T(1,128)S(6)} %copy.14.refs_6_, ...), custom_call_target="tpu_custom_call" | custom-call | tf_op jit(solution)/shard_map/pallas_call | solution.py:589
  3.7 1.1 broadcast_in_dim.4
  4.8 46.0 %all_to_all.10.all_ref = f32[16,400,128]{2,1,0:T(8,128)S(1)} all-to-all(f32[16,400,128]{2,1,0:T(8,128)S(1)} %broadcast_in_dim.4), channel_id=1, replica_groups=mesh['gx'=32,'gy'=4,'col'=4] {'gy','col'}, dimensions={0} | all-to-all | bytes 6553600 | tf_op jit(solution)/shard_map/all_to_all | solution.py:558
  50.8 0.0 copy-start
  50.8 2.1 %shard_map.132 = (f32[512,512]{1,0:T(8,128)S(1)}, f32[4,288,128]{2,1,0:T(8,128)S(1)}, f32[4,512,128]{2,1,0:T(8,128)S(1)}, f32[4,192,128]{2,1,0:T(8,128)S(1)}, f3...) custom-call(f32[16,400,128]{2,1,0:T(8,128)S(1)} %all_to_all.10.all_ref), custom_call_target="tpu_custom_call" | custom-call | tf_op jit(solution)/shard_map/pallas_call | solution.py:545
  52.9 5.2 %collective-permute-start = (f32[80,128]{1,0:T(8,128)S(1)}, f32[80,128]{1,0:T(8,128)S(1)}, u32[]{:S(2)}, u32[]{:S(2)}) collective-permute-start(f32[80,128]{1,0:T(8,128)S(1)} %get-tuple-element.48), channel_id=1, source_target_pairs={{0,16},{16,32},{32,48},{48,64},{64,80},{80,96},{96,112},{112,128},... | collective-permute-start | bytes 122888 | tf_op jit(solution)/shard_map/ppermute | solution.py:567
  58.1 0.0 collective-permute-start.1
  58.1 1.1 collective-permute-done.left_ref
  59.2 2.3 %collective-permute-done.1.right_ref = f32[80,128]{1,0:T(8,128)S(1)} collective-permute-done((f32[80,128]{1,0:T(8,128)S(1)}, f32[80,128]{1,0:T(8,128)S(1)}, u32[]{:S(2)}, u32[]{:S(2)}) %collective-permute-start.1) | collective-permute-done | bytes 40992 | tf_op jit(solution)/shard_map/ppermute | solution.py:567
  61.5 0.6 shard_map.133
  62.2 0.0 collective-permute-start.2
  62.2 4.3 %collective-permute-start.3 = (f32[16,128]{1,0:T(8,128)S(1)}, f32[16,128]{1,0:T(8,128)S(1)}, u32[]{:S(2)}, u32[]{:S(2)}) collective-permute-start(f32[16,128]{1,0:T(8,128)S(1)} %get-tuple-element.51), channel_id=1, source_target_pairs={{16,0},{32,16},{48,32},{64,48},{80,64},{96,80},{112,96},{128,112},... | collective-permute-start | bytes 24584 | tf_op jit(solution)/shard_map/ppermute | solution.py:567
  66.5 3.9 %shard_map.134 = (f32[4,288,128]{2,1,0:T(8,128)S(1)}, f32[64,128]{1,0:T(8,128)S(1)}, f32[64,128]{1,0:T(8,128)S(1)}) custom-call(f32[4,512,128]{2,1,0:T(8,128)S(1)} %get-tuple-element.52.box_ref, f32[4,192,128]{2,1,0:T(8,128)S(1)} %get-tuple-element.53.vec_ref, f32[4,48,128]{2,1,0:T(8,128)S(1)} %get-tuple-element.54.small_ref, ...), custom_call_target="tpu_custom_call" | custom-call | tf_op jit(solution)/shard_map/pallas_call | solution.py:545
  70.4 0.0 collective-permute-done.2.left_ref
  70.4 0.0 collective-permute-done.3.right_ref
  70.4 0.6 shard_map.135
  71.0 0.0 collective-permute-start.4
  71.1 3.0 %collective-permute-start.5 = (f32[80,128]{1,0:T(8,128)S(1)}, f32[80,128]{1,0:T(8,128)S(1)}, u32[]{:S(2)}, u32[]{:S(2)}) collective-permute-start(f32[80,128]{1,0:T(8,128)S(1)} %get-tuple-element.59), channel_id=1, source_target_pairs={{16,0},{32,16},{48,32},{64,48},{80,64},{96,80},{112,96},{128,112},... | collective-permute-start | bytes 122888 | tf_op jit(solution)/shard_map/ppermute | solution.py:567
  74.0 0.7 collective-permute-done.4.left_ref
  74.7 0.2 collective-permute-done.5.right_ref
  74.9 0.0 copy-done
  74.9 0.0 copy-start.1
  74.9 2.5 %shard_map.136 = (f32[4,288,128]{2,1,0:T(8,128)S(1)}, f32[4,1536,128]{2,1,0:T(8,128)S(1)}, f32[64,128]{1,0:T(8,128)S(1)}, f32[64,128]{1,0:T(8,128)S(1)}) custom-call(f32[512,512]{1,0:T(8,128)S(1)} %get-tuple-element.46.dense_ref, f32[16,128]{1,0:T(8,128)S(1)} %get-tuple-element.57.state_ref, f32[80,128]{1,0:T(8,128)S(1)} %collective-permute-done.4.left_ref, ...), custom_call_target="tpu_custom_call" | custom-call | tf_op jit(solution)/shard_map/pallas_call | solution.py:545
  77.5 0.0 collective-permute-start.6
  77.5 3.8 %collective-permute-start.7 = (f32[64,128]{1,0:T(8,128)S(1)}, f32[64,128]{1,0:T(8,128)S(1)}, u32[]{:S(2)}, u32[]{:S(2)}) collective-permute-start(f32[64,128]{1,0:T(8,128)S(1)} %get-tuple-element.63), channel_id=1, source_target_pairs={{16,0},{32,16},{48,32},{64,48},{80,64},{96,80},{112,96},{128,112},... | collective-permute-start | bytes 98312 | tf_op jit(solution)/shard_map/ppermute | solution.py:567
  81.3 0.4 shard_map.137.inverse_ref
  81.6 0.3 collective-permute-done.6.left_ref
  81.9 0.2 collective-permute-done.7.right_ref
  82.1 0.0 copy-done.1
  82.1 2.3 %shard_map.138 = (f32[4,288,128]{2,1,0:T(8,128)S(1)}, f32[4,512,128]{2,1,0:T(8,128)S(1)}, f32[16,128]{1,0:T(8,128)S(1)}, f32[80,128]{1,0:T(8,128)S(1)}, f32[80,128]{1,0:T(8,128)S(1)}) custom-call(f32[4,1536,128]{2,1,0:T(8,128)S(1)} %get-tuple-element.61.t_ref, f32[64,128]{1,0:T(8,128)S(1)} %collective-permute-done.6.left_ref, ...), custom_call_target="tpu_custom_call" | custom-call | tf_op jit(solution)/shard_map/pallas_call | solution.py:545
  84.4 0.0 collective-permute-start.8
  84.4 3.7 %collective-permute-start.9 = (f32[80,128]{1,0:T(8,128)S(1)}, f32[80,128]{1,0:T(8,128)S(1)}, u32[]{:S(2)}, u32[]{:S(2)}) collective-permute-start(f32[80,128]{1,0:T(8,128)S(1)} %get-tuple-element.67), channel_id=1, source_target_pairs={{16,0},{32,16},{48,32},{64,48},{80,64},{96,80},{112,96},{128,112},... | collective-permute-start | bytes 122888 | tf_op jit(solution)/shard_map/ppermute | solution.py:567
  88.1 0.7 collective-permute-done.8.left_ref
  88.8 0.2 collective-permute-done.9.right_ref
  89.0 0.6 shard_map.139
  89.6 0.0 collective-permute-start.10
  89.7 3.8 %collective-permute-start.11 = (f32[16,128]{1,0:T(8,128)S(1)}, f32[16,128]{1,0:T(8,128)S(1)}, u32[]{:S(2)}, u32[]{:S(2)}) collective-permute-start(f32[16,128]{1,0:T(8,128)S(1)} %get-tuple-element.69), channel_id=1, source_target_pairs={{16,0},{32,16},{48,32},{64,48},{80,64},{96,80},{112,96},{128,112},... | collective-permute-start | bytes 24584 | tf_op jit(solution)/shard_map/ppermute | solution.py:567
  93.4 4.0 %shard_map.140 = (f32[4,288,128]{2,1,0:T(8,128)S(1)}, f32[64,128]{1,0:T(8,128)S(1)}, f32[64,128]{1,0:T(8,128)S(1)}) custom-call(f32[4,512,128]{2,1,0:T(8,128)S(1)} %get-tuple-element.70.box_ref, f32[4,192,128]{2,1,0:T(8,128)S(1)} %get-tuple-element.53.vec_ref, f32[4,48,128]{2,1,0:T(8,128)S(1)} %get-tuple-element.54.small_ref, ...), custom_call_target="tpu_custom_call" | custom-call | tf_op jit(solution)/shard_map/pallas_call | solution.py:545
  97.5 0.0 collective-permute-done.10.left_ref
  97.5 0.0 collective-permute-done.11.right_ref
  97.5 0.6 shard_map.141
  98.2 0.0 collective-permute-start.12
  98.2 3.0 %collective-permute-start.13 = (f32[80,128]{1,0:T(8,128)S(1)}, f32[80,128]{1,0:T(8,128)S(1)}, u32[]{:S(2)}, u32[]{:S(2)}) collective-permute-start(f32[80,128]{1,0:T(8,128)S(1)} %get-tuple-element.75), channel_id=1, source_target_pairs={{16,0},{32,16},{48,32},{64,48},{80,64},{96,80},{112,96},{128,112},... | collective-permute-start | bytes 122888 | tf_op jit(solution)/shard_map/ppermute | solution.py:567
  101.2 0.7 collective-permute-done.12.left_ref
  101.8 0.2 collective-permute-done.13.right_ref
  102.0 2.5 %shard_map.142 = (f32[4,288,128]{2,1,0:T(8,128)S(1)}, f32[4,1536,128]{2,1,0:T(8,128)S(1)}, f32[64,128]{1,0:T(8,128)S(1)}, f32[64,128]{1,0:T(8,128)S(1)}) custom-call(f32[512,512]{1,0:T(8,128)S(1)} %get-tuple-element.46.dense_ref, f32[16,128]{1,0:T(8,128)S(1)} %get-tuple-element.73.state_ref, f32[80,128]{1,0:T(8,128)S(1)} %collective-permute-done.12.left_ref, ...), custom_call_target="tpu_custom_call" | custom-call | tf_op jit(solution)/shard_map/pallas_call | solution.py:545
  104.6 0.0 collective-permute-start.14
  104.6 3.8 %collective-permute-start.15 = (f32[64,128]{1,0:T(8,128)S(1)}, f32[64,128]{1,0:T(8,128)S(1)}, u32[]{:S(2)}, u32[]{:S(2)}) collective-permute-start(f32[64,128]{1,0:T(8,128)S(1)} %get-tuple-element.79), channel_id=1, source_target_pairs={{16,0},{32,16},{48,32},{64,48},{80,64},{96,80},{112,96},{128,112},... | collective-permute-start | bytes 98312 | tf_op jit(solution)/shard_map/ppermute | solution.py:567
  108.4 0.7 collective-permute-done.14.left_ref
  109.0 0.2 collective-permute-done.15.right_ref
  109.2 0.0 copy-start.3
  109.2 0.0 copy-start.2
  109.2 2.0 %shard_map.143 = (f32[4,288,128]{2,1,0:T(8,128)S(1)}, f32[8,128]{1,0:T(8,128)S(1)}) custom-call(f32[4,1536,128]{2,1,0:T(8,128)S(1)} %get-tuple-element.77.t_ref, f32[64,128]{1,0:T(8,128)S(1)} %collective-permute-done.14.left_ref, f32[64,128]{1,0:T(8,128)S(1)} %collective-permute-done.15.right_ref, f32[4,512,128]{2,1,0:T(8,128)S(1)} %shard_map.137.inverse_ref, ...), custom_call_target="tpu_custom_call" | custom-call | tf_op jit(solution)/shard_map/pallas_call | solution.py:545
  111.3 0.7 broadcast_in_dim.5
  112.0 14.6 %all-to-all-start.1 = ((f32[32,8,128]{2,1,0:T(8,128)}), f32[32,8,128]{2,1,0:T(8,128)S(1)}, u32[]{:S(2)}, u32[]{:S(2)}) async-start(f32[32,8,128]{2,1,0:T(8,128)} %broadcast_in_dim.5), calls=%async_computation.1 | async-start | bytes 262144 | tf_op jit(solution)/shard_map/all_to_all | solution.py:558
  126.6 0.1 pad_add_fusion.me_ref
  126.6 0.0 copy-done.3
  126.6 1.2 shard_map.144
  127.9 14.5 %all-to-all-done.1.sums_ref = f32[32,8,128]{2,1,0:T(8,128)S(1)} async-done(((f32[32,8,128]{2,1,0:T(8,128)}), f32[32,8,128]{2,1,0:T(8,128)S(1)}, u32[]{:S(2)}, u32[]{:S(2)}) %all-to-all-start.1) | async-done | bytes 131104 | tf_op jit(solution)/shard_map/all_to_all | solution.py:558
  142.4 0.0 copy-done.2
  142.4 0.8 shard_map.145
Async XLA Ops:
  50.8 24.2 %copy-start = (bf16[1536,864]{1,0:T(8,128)(2,1)S(1)}, bf16[1536,864]{1,0:T(8,128)(2,1)}, u32[]{:S(2)}) copy-start(bf16[1536,864]{1,0:T(8,128)(2,1)} %constant.19.clone.table_ref) | copy-start | bytes 7962628
  52.9 6.3 %collective-permute-start = (f32[80,128]{1,0:T(8,128)S(1)}, f32[80,128]{1,0:T(8,128)S(1)}, u32[]{:S(2)}, u32[]{:S(2)}) collective-permute-start(f32[80,128]{1,0:T(8,128)S(1)} %get-tuple-element.48), channel_id=1, source_target_pairs={{0,16},{16,32},{32,48},{48,64},{64,80},{80,96},{96,112},{112,128},... | collective-permute-start | bytes 122888 | tf_op jit(solution)/shard_map/ppermute | solution.py:567
  58.1 3.4 %collective-permute-start.1 = (f32[80,128]{1,0:T(8,128)S(1)}, f32[80,128]{1,0:T(8,128)S(1)}, u32[]{:S(2)}, u32[]{:S(2)}) collective-permute-start(f32[80,128]{1,0:T(8,128)S(1)} %get-tuple-element.49), channel_id=1, source_target_pairs={{16,0},{32,16},{48,32},{64,48},{80,64},{96,80},{112,96},{128,112},... | collective-permute-start | bytes 122888 | tf_op jit(solution)/shard_map/ppermute | solution.py:567
  62.2 8.2 %collective-permute-start.2 = (f32[16,128]{1,0:T(8,128)S(1)}, f32[16,128]{1,0:T(8,128)S(1)}, u32[]{:S(2)}, u32[]{:S(2)}) collective-permute-start(f32[16,128]{1,0:T(8,128)S(1)} %get-tuple-element.51), channel_id=1, source_target_pairs={{0,16},{16,32},{32,48},{48,64},{64,80},{80,96},{96,112},{112,128},... | collective-permute-start | bytes 24584 | tf_op jit(solution)/shard_map/ppermute | solution.py:567
  62.2 8.2 %collective-permute-start.3 = (f32[16,128]{1,0:T(8,128)S(1)}, f32[16,128]{1,0:T(8,128)S(1)}, u32[]{:S(2)}, u32[]{:S(2)}) collective-permute-start(f32[16,128]{1,0:T(8,128)S(1)} %get-tuple-element.51), channel_id=1, source_target_pairs={{16,0},{32,16},{48,32},{64,48},{80,64},{96,80},{112,96},{128,112},... | collective-permute-start | bytes 24584 | tf_op jit(solution)/shard_map/ppermute | solution.py:567
  71.0 3.7 %collective-permute-start.4 = (f32[80,128]{1,0:T(8,128)S(1)}, f32[80,128]{1,0:T(8,128)S(1)}, u32[]{:S(2)}, u32[]{:S(2)}) collective-permute-start(f32[80,128]{1,0:T(8,128)S(1)} %get-tuple-element.58), channel_id=1, source_target_pairs={{0,16},{16,32},{32,48},{48,64},{64,80},{80,96},{96,112},{112,128},... | collective-permute-start | bytes 122888 | tf_op jit(solution)/shard_map/ppermute | solution.py:567
  71.1 3.8 %collective-permute-start.5 = (f32[80,128]{1,0:T(8,128)S(1)}, f32[80,128]{1,0:T(8,128)S(1)}, u32[]{:S(2)}, u32[]{:S(2)}) collective-permute-start(f32[80,128]{1,0:T(8,128)S(1)} %get-tuple-element.59), channel_id=1, source_target_pairs={{16,0},{32,16},{48,32},{64,48},{80,64},{96,80},{112,96},{128,112},... | collective-permute-start | bytes 122888 | tf_op jit(solution)/shard_map/ppermute | solution.py:567
  74.9 7.2 %copy-start.1 = (bf16[288,4608]{1,0:T(8,128)(2,1)S(1)}, bf16[288,4608]{1,0:T(8,128)(2,1)}, u32[]{:S(2)}) copy-start(bf16[288,4608]{1,0:T(8,128)(2,1)} %constant.20.clone.table_ref) | copy-start | bytes 7962628
  77.5 4.5 %collective-permute-start.6 = (f32[64,128]{1,0:T(8,128)S(1)}, f32[64,128]{1,0:T(8,128)S(1)}, u32[]{:S(2)}, u32[]{:S(2)}) collective-permute-start(f32[64,128]{1,0:T(8,128)S(1)} %get-tuple-element.62), channel_id=1, source_target_pairs={{0,16},{16,32},{32,48},{48,64},{64,80},{80,96},{96,112},{112,128},... | collective-permute-start | bytes 98312 | tf_op jit(solution)/shard_map/ppermute | solution.py:567
  77.5 4.6 %collective-permute-start.7 = (f32[64,128]{1,0:T(8,128)S(1)}, f32[64,128]{1,0:T(8,128)S(1)}, u32[]{:S(2)}, u32[]{:S(2)}) collective-permute-start(f32[64,128]{1,0:T(8,128)S(1)} %get-tuple-element.63), channel_id=1, source_target_pairs={{16,0},{32,16},{48,32},{64,48},{80,64},{96,80},{112,96},{128,112},... | collective-permute-start | bytes 98312 | tf_op jit(solution)/shard_map/ppermute | solution.py:567
  84.4 4.4 %collective-permute-start.8 = (f32[80,128]{1,0:T(8,128)S(1)}, f32[80,128]{1,0:T(8,128)S(1)}, u32[]{:S(2)}, u32[]{:S(2)}) collective-permute-start(f32[80,128]{1,0:T(8,128)S(1)} %get-tuple-element.66), channel_id=1, source_target_pairs={{0,16},{16,32},{32,48},{48,64},{64,80},{80,96},{96,112},{112,128},... | collective-permute-start | bytes 122888 | tf_op jit(solution)/shard_map/ppermute | solution.py:567
  84.4 4.6 %collective-permute-start.9 = (f32[80,128]{1,0:T(8,128)S(1)}, f32[80,128]{1,0:T(8,128)S(1)}, u32[]{:S(2)}, u32[]{:S(2)}) collective-permute-start(f32[80,128]{1,0:T(8,128)S(1)} %get-tuple-element.67), channel_id=1, source_target_pairs={{16,0},{32,16},{48,32},{64,48},{80,64},{96,80},{112,96},{128,112},... | collective-permute-start | bytes 122888 | tf_op jit(solution)/shard_map/ppermute | solution.py:567
  89.6 7.9 %collective-permute-start.10 = (f32[16,128]{1,0:T(8,128)S(1)}, f32[16,128]{1,0:T(8,128)S(1)}, u32[]{:S(2)}, u32[]{:S(2)}) collective-permute-start(f32[16,128]{1,0:T(8,128)S(1)} %get-tuple-element.69), channel_id=1, source_target_pairs={{0,16},{16,32},{32,48},{48,64},{64,80},{80,96},{96,112},{112,128},... | collective-permute-start | bytes 24584 | tf_op jit(solution)/shard_map/ppermute | solution.py:567
  89.7 7.8 %collective-permute-start.11 = (f32[16,128]{1,0:T(8,128)S(1)}, f32[16,128]{1,0:T(8,128)S(1)}, u32[]{:S(2)}, u32[]{:S(2)}) collective-permute-start(f32[16,128]{1,0:T(8,128)S(1)} %get-tuple-element.69), channel_id=1, source_target_pairs={{16,0},{32,16},{48,32},{64,48},{80,64},{96,80},{112,96},{128,112},... | collective-permute-start | bytes 24584 | tf_op jit(solution)/shard_map/ppermute | solution.py:567
  98.2 3.7 %collective-permute-start.12 = (f32[80,128]{1,0:T(8,128)S(1)}, f32[80,128]{1,0:T(8,128)S(1)}, u32[]{:S(2)}, u32[]{:S(2)}) collective-permute-start(f32[80,128]{1,0:T(8,128)S(1)} %get-tuple-element.74), channel_id=1, source_target_pairs={{0,16},{16,32},{32,48},{48,64},{64,80},{80,96},{96,112},{112,128},... | collective-permute-start | bytes 122888 | tf_op jit(solution)/shard_map/ppermute | solution.py:567
  98.2 3.8 %collective-permute-start.13 = (f32[80,128]{1,0:T(8,128)S(1)}, f32[80,128]{1,0:T(8,128)S(1)}, u32[]{:S(2)}, u32[]{:S(2)}) collective-permute-start(f32[80,128]{1,0:T(8,128)S(1)} %get-tuple-element.75), channel_id=1, source_target_pairs={{16,0},{32,16},{48,32},{64,48},{80,64},{96,80},{112,96},{128,112},... | collective-permute-start | bytes 122888 | tf_op jit(solution)/shard_map/ppermute | solution.py:567
  104.6 4.5 %collective-permute-start.14 = (f32[64,128]{1,0:T(8,128)S(1)}, f32[64,128]{1,0:T(8,128)S(1)}, u32[]{:S(2)}, u32[]{:S(2)}) collective-permute-start(f32[64,128]{1,0:T(8,128)S(1)} %get-tuple-element.78), channel_id=1, source_target_pairs={{0,16},{16,32},{32,48},{48,64},{64,80},{80,96},{96,112},{112,128},... | collective-permute-start | bytes 98312 | tf_op jit(solution)/shard_map/ppermute | solution.py:567
  104.6 4.6 %collective-permute-start.15 = (f32[64,128]{1,0:T(8,128)S(1)}, f32[64,128]{1,0:T(8,128)S(1)}, u32[]{:S(2)}, u32[]{:S(2)}) collective-permute-start(f32[64,128]{1,0:T(8,128)S(1)} %get-tuple-element.79), channel_id=1, source_target_pairs={{16,0},{32,16},{48,32},{64,48},{80,64},{96,80},{112,96},{128,112},... | collective-permute-start | bytes 98312 | tf_op jit(solution)/shard_map/ppermute | solution.py:567
  109.2 17.4 %copy-start.3 = (f32[192,192]{1,0:T(8,128)S(1)}, f32[192,192]{1,0:T(8,128)}, u32[]{:S(2)}) copy-start(f32[192,192]{1,0:T(8,128)} %constant.21.clone.table_ref) | copy-start | bytes 442372
  109.2 33.2 %copy-start.2 = (f32[6,6,192]{2,1,0:T(8,128)S(1)}, f32[6,6,192]{2,1,0:T(8,128)}, u32[]{:S(2)}) copy-start(f32[6,6,192]{2,1,0:T(8,128)} %rhs_ref.1) | copy-start | bytes 82948
  112.0 30.5 %all-to-all-start.1 = ((f32[32,8,128]{2,1,0:T(8,128)}), f32[32,8,128]{2,1,0:T(8,128)S(1)}, u32[]{:S(2)}, u32[]{:S(2)}) async-start(f32[32,8,128]{2,1,0:T(8,128)} %broadcast_in_dim.5), calls=%async_computation.1 | async-start | bytes 262144 | tf_op jit(solution)/shard_map/all_to_all | solution.py:558

commit v4 on v3

--- a/solution.py
+++ b/solution.py
@@ -46,7 +46,7 @@
 ROWS_P = 288
 ROWS_V = 512
 ROWS_A = 176
-ROWS = 400
+ROWS_B = 224
 
 
 def basis_tables():
@@ -224,8 +224,8 @@
 
 
 def pack_body(*refs):
-    sources, out_ref, held, (tmp, ready) = refs[:9], refs[9], refs[10:19], refs[19:]
-    a_ref, b_ref = out_ref.at[0:ROWS_A], out_ref.at[ROWS_A:ROWS]
+    sources, (a_out, b_out), held, (tmp, ready) = refs[:9], refs[9:11], refs[11:20], refs[20:]
+    a_ref, b_ref = a_out.at[0], b_out.at[0]
     copies = [pltpu.make_async_copy(sources[n], held[n], ready.at[n]) for n in range(9)]
     for copy in copies:
         copy.start()
@@ -250,35 +250,38 @@
     )
     b_ref[96:160, :] = helm[:, 0:128]
     b_ref[160:224, :] = helm[:, 128:256]
-
-
-def joined(all_ref, b, start, rows, quarter):
+    for n in range(1, 4):
+        a_out[n] = a_out[0]
+        b_out[n] = b_out[0]
+
+
+def joined(column, start, rows, quarter):
     place = lanes((rows, 128)) // EA
     total = None
     for c in range(4):
-        moved = turn(all_ref[b * 4 + c, start : start + rows, :], (c - quarter) * 32)
+        moved = turn(column[c][start : start + rows, :], (c - quarter) * 32)
         part = jnp.where(place == c, moved, 0.0)
         total = part if total is None else total + part
     return total
 
 
 def unpack_body(
-    all_ref, dense_ref, rhs_ref, helm_ref, vec_ref, small_ref, box_ref, state_ref, ahead_ref, behind_ref
+    a_ref, b_ref, dense_ref, rhs_ref, helm_ref, vec_ref, small_ref, box_ref, state_ref, ahead_ref, behind_ref
 ):
     for b in range(NB):
+        column_a = [a_ref.at[b, c] for c in range(4)]
+        column_b = [b_ref.at[c, b] for c in range(4)]
         for c in range(4):
             at = (b * 4 + c) * 32
             for t in range(4):
-                dense_ref[at : at + 32, t * 128 : (t + 1) * 128] = all_ref[b * 4 + c, t * 32 : (t + 1) * 32, :]
+                dense_ref[at : at + 32, t * 128 : (t + 1) * 128] = column_a[c][t * 32 : (t + 1) * 32, :]
         for t in range(4):
-            vec_ref[b, t * 48 : (t + 1) * 48, :] = joined(all_ref, b, 128, 48, t)
+            vec_ref[b, t * 48 : (t + 1) * 48, :] = joined(column_a, 128, 48, t)
         for k in range(6):
-            rhs_ref[b, k * 48 : (k + 1) * 48, :] = joined(all_ref, b, ROWS_A + 48 * (k // 4), 48, k % 4)
-        small_ref[b, :, :] = joined(all_ref, b, ROWS_A + 48, 48, 2)
+            rhs_ref[b, k * 48 : (k + 1) * 48, :] = joined(column_b, 48 * (k // 4), 48, k % 4)
+        small_ref[b, :, :] = joined(column_b, 48, 48, 2)
         for k in range(8):
-            helm_ref[b, k * 64 : (k + 1) * 64, :] = joined(
-                all_ref, b, ROWS_A + 96 + 64 * (k // 4), 64, k % 4
-            )
+            helm_ref[b, k * 64 : (k + 1) * 64, :] = joined(column_b, 96 + 64 * (k // 4), 64, k % 4)
     begin_kernel_part(
         rhs_ref, small_ref, dense_ref, box_ref, state_ref, ahead_ref, behind_ref,
         ([helm_ref[b, 448:512, :] for b in range(NB)], [helm_ref[b, 0:64, :] for b in range(NB)]),
@@ -554,8 +557,17 @@
     return run
 
 
-def tell_all(block, axes, count):
-    return lax.all_to_all(jnp.broadcast_to(block[None], (count,) + block.shape), axes, 0, 0)
+def tell_all(block, axis, count, groups=None):
+    copies = jnp.broadcast_to(block[None], (count,) + block.shape)
+    return lax.all_to_all(copies, axis, 0, 0, axis_index_groups=groups)
+
+
+def sum_slabs(sums):
+    slabs = lax.axis_size("gx")
+    near = [list(range(start, start + 8)) for start in range(0, slabs, 8)]
+    far = [list(range(start, slabs, 8)) for start in range(8)]
+    sums = jnp.sum(tell_all(sums, "gx", 8, near), axis=0)
+    return tell_all(sums, "gx", slabs // 8, far)
 
 
 def local(divergence, elem_size, helm_diag, fdm_vectors, fdm_values, coarse_rows, axial_link):
@@ -586,21 +598,25 @@
         six,
         order_table(8),
     )
-    own_part = pl.pallas_call(
+    half_a, half_b = pl.pallas_call(
         pack_body,
-        out_shape=jax.ShapeDtypeStruct((ROWS, 128), F32),
+        out_shape=[jax.ShapeDtypeStruct((4, rows, 128), F32) for rows in (ROWS_A, ROWS_B)],
         in_specs=[pl.BlockSpec(memory_space=pl.ANY)] * 9,
-        out_specs=pl.BlockSpec(memory_space=pltpu.VMEM),
+        out_specs=[pl.BlockSpec(memory_space=pltpu.VMEM)] * 2,
         scratch_shapes=[pltpu.VMEM(value.shape, F32) for value in arguments]
         + [pltpu.VMEM((48, 192), F32), pltpu.SemaphoreType.DMA((9,))],
         compiler_params=pltpu.CompilerParams(vmem_limit_bytes=60 * 1024 * 1024),
     )(*arguments)
-    everything = tell_all(own_part, ("gy", "col"), 16)
+    four_a = lax.all_to_all(half_a, "col", 0, 0)
+    four_b = lax.all_to_all(half_b, "gy", 0, 0)
+    four_a, four_b = lax.optimization_barrier((four_a, four_b))
+    all_a = tell_all(four_a, "gy", 4)
+    all_b = tell_all(four_b, "col", 4)
 
     dense, rhs, helm, vectors, small, boxes, state, up, down = call(
         unpack_body,
         [(512, 512), field, velocity, (NB, 192, 128), (NB, 48, 128), velocity, state_shape, wide, wide],
-    )(everything)
+    )(all_a, all_b)
 
     def precondition(boxes, state, left, right):
         state, message = call(middle_body, [state_shape, state_shape])(dense, state, left, right)
@@ -633,7 +649,7 @@
         t, left, right, inverse, small, backward, rhs, z, w, q
     )
     own = call(own_body, [(6, 6, 192)] * 4, scalars=1)(me, z, w, q, v, six.T.copy())
-    sums = tell_all(sums, "gx", count)
+    sums = sum_slabs(sums)
     return tuple(
         pl.pallas_call(
             last_body,

time: 144 us -> 166 us (1.15)
  starting transfers between devices: 45.2 us -> 56.1 us
  blocking collectives: 46 us -> 56.2 us
    all_to_all x1 -> x4, blocking collectives: 46 us -> 56.2 us  [the longest x2 33.8 us: tell_all(): return lax.all_to_all(copies, axis, 0, 0, axis_index_groups=groups)]
    ppermute x16, starting transfers between devices: 30.6 us -> 36.6 us  [exchange(): return (lax.ppermute(up, 'gx', ahead), lax.ppermute(down, 'gx', behind))]
    all_to_all x1 -> x2, starting transfers between devices: 14.6 us -> 19.5 us  [tell_all(): return lax.all_to_all(copies, axis, 0, 0, axis_index_groups=groups)]
    all_to_all x1 -> x2, waiting for transfers between devices: 14.5 us -> 15.1 us  [tell_all(): return lax.all_to_all(copies, axis, 0, 0, axis_index_groups=groups)]
  transfers between devices with their start and end apart: 17 -> 18, of which waited for: 13 -> 14; matrix products, arithmetic and copies ran while one was open for 0% -> 0% of each run, Pallas kernels for 7% -> 6%
where the time goes in v4:
time: 166 us; the launch traced here: 165 us
  blocking collectives  56.2 us (34%)
  starting transfers between devices  56.1 us (34%)
  Pallas kernels  27.1 us (16%)
  waiting for transfers between devices  22.8 us (14%)
    ppermute x16, starting transfers between devices, exchange(): return (lax.ppermute(up, 'gx', ahead), lax.ppermute(down, 'gx', behind))  36.6 us
    all_to_all x2, blocking collectives, tell_all(): return lax.all_to_all(copies, axis, 0, 0, axis_index_groups=groups)  33.8 us
    pallas_call x13, Pallas kernels, run(): pl.pallas_call(body, out_shape=[jax.ShapeDtypeStruct(shape, F32) for shap...  23.8 us
    all_to_all x2, starting transfers between devices, tell_all(): return lax.all_to_all(copies, axis, 0, 0, axis_index_groups=groups)  19.5 us
    all_to_all x2, waiting for transfers between devices, tell_all(): return lax.all_to_all(copies, axis, 0, 0, axis_index_groups=groups)  15.1 us
    all_to_all x1, blocking collectives, local(): four_b = lax.all_to_all(half_b, 'gy', 0, 0)  11.3 us
    all_to_all x1, blocking collectives, local(): four_a = lax.all_to_all(half_a, 'col', 0, 0)  11.1 us
    ppermute x16, waiting for transfers between devices, exchange(): return (lax.ppermute(up, 'gx', ahead), lax.ppermute(down, 'gx', behind))  7.68 us
  transfers between devices with their start and end apart: 18, of which 14 were waited for; matrix products, arithmetic and copies ran while one was open for 0% of the time, Pallas kernels for 6%

profile of v4, /device:TPU:1, one launch (start us, length us, event | category | flops | bytes accessed | tf_op | source)
XLA Modules:
  0.0 165.4 jit_solution(11888515224497407312)
XLA Ops:
  1.3 2.5 %shard_map.131 = (f32[4,176,128]{2,1,0:T(8,128)}, f32[4,224,128]{2,1,0:T(8,128)}) custom-call(f32[6,6,192]{2,1,0:T(8,128)} %rhs_ref.1, f32[8,8,256]{2,1,0:T(8,128)} %refs_1_.1, f32[192,32]{1,0:T(8,128)} %bitcast.4, f32[24,32]{1,0:T(8,128)} %bitcast.5, f32[3,32]{1,0:T(4,128)} %refs_4_.1, f32[32,512]{1,0:T(8,128)} %refs_5_.1, f32[1,1,1]{2,1,0:T(1,128)S(6)} %copy.14.refs_6_, ...), custom_call_target="tpu_custom_call" | custom-call | tf_op jit(solution)/shard_map/pallas_call | solution.py:601
  3.8 11.1 %all_to_all.30 = f32[4,176,128]{2,1,0:T(8,128)S(1)} all-to-all(f32[4,176,128]{2,1,0:T(8,128)} %get-tuple-element.50), channel_id=1, replica_groups=mesh['gx'=32,'gy'=4,'col'=4] {'col'}, dimensions={0} | all-to-all | bytes 720896 | tf_op jit(solution)/shard_map/all_to_all | solution.py:610
  14.9 11.3 %all_to_all.31 = f32[4,224,128]{2,1,0:T(8,128)S(1)} all-to-all(f32[4,224,128]{2,1,0:T(8,128)} %get-tuple-element.51), channel_id=1, replica_groups=mesh['gx'=32,'gy'=4,'col'=4] {'gy'}, dimensions={0} | all-to-all | bytes 917504 | tf_op jit(solution)/shard_map/all_to_all | solution.py:611
  26.2 0.1 broadcast_in_dim.8
  26.3 15.2 %all_to_all.32.a_ref = f32[4,4,176,128]{3,2,1,0:T(8,128)S(1)} all-to-all(f32[4,4,176,128]{3,2,1,0:T(8,128)S(1)} %broadcast_in_dim.8), channel_id=1, replica_groups=mesh['gx'=32,'gy'=4,'col'=4] {'gy'}, dimensions={0} | all-to-all | bytes 2883584 | tf_op jit(solution)/shard_map/all_to_all | solution.py:562
  41.6 0.2 broadcast_in_dim.9
  41.8 18.5 %all_to_all.33.b_ref = f32[4,4,224,128]{3,2,1,0:T(8,128)S(1)} all-to-all(f32[4,4,224,128]{3,2,1,0:T(8,128)S(1)} %broadcast_in_dim.9), channel_id=1, replica_groups=mesh['gx'=32,'gy'=4,'col'=4] {'col'}, dimensions={0} | all-to-all | bytes 3670016 | tf_op jit(solution)/shard_map/all_to_all | solution.py:562
  60.3 2.2 %shard_map.132 = (f32[512,512]{1,0:T(8,128)S(1)}, f32[4,288,128]{2,1,0:T(8,128)S(1)}, f32[4,512,128]{2,1,0:T(8,128)S(1)}, f32[4,192,128]{2,1,0:T(8,128)S(1)}, f3...) custom-call(f32[4,4,176,128]{3,2,1,0:T(8,128)S(1)} %all_to_all.32.a_, ...), custom_call_target="tpu_custom_call" | custom-call | tf_op jit(solution)/shard_map/pallas_call | solution.py:548
  62.5 0.0 copy-start
  62.5 13.2 %collective-permute-start = (f32[80,128]{1,0:T(8,128)S(1)}, f32[80,128]{1,0:T(8,128)S(1)}, u32[]{:S(2)}, u32[]{:S(2)}) collective-permute-start(f32[80,128]{1,0:T(8,128)S(1)} %get-tuple-element.56), channel_id=1, source_target_pairs={{0,16},{16,32},{32,48},{48,64},{64,80},{80,96},{96,112},{112,128},... | collective-permute-start | bytes 122888 | tf_op jit(solution)/shard_map/ppermute | solution.py:579
  75.7 0.0 collective-permute-start.1
  75.7 1.1 collective-permute-done.left_ref
  76.8 2.6 %collective-permute-done.1.right_ref = f32[80,128]{1,0:T(8,128)S(1)} collective-permute-done((f32[80,128]{1,0:T(8,128)S(1)}, f32[80,128]{1,0:T(8,128)S(1)}, u32[]{:S(2)}, u32[]{:S(2)}) %collective-permute-start.1) | collective-permute-done | bytes 40992 | tf_op jit(solution)/shard_map/ppermute | solution.py:579
  79.4 0.6 shard_map.133
  80.0 0.0 collective-permute-start.2
  80.1 0.7 collective-permute-start.3
  80.7 3.9 %shard_map.134 = (f32[4,288,128]{2,1,0:T(8,128)S(1)}, f32[64,128]{1,0:T(8,128)S(1)}, f32[64,128]{1,0:T(8,128)S(1)}) custom-call(f32[4,512,128]{2,1,0:T(8,128)S(1)} %get-tuple-element.60.box_ref, f32[4,192,128]{2,1,0:T(8,128)S(1)} %get-tuple-element.61.vec_ref, f32[4,48,128]{2,1,0:T(8,128)S(1)} %get-tuple-element.62.small_ref, ...), custom_call_target="tpu_custom_call" | custom-call | tf_op jit(solution)/shard_map/pallas_call | solution.py:548
  84.6 0.0 collective-permute-done.2.left_ref
  84.6 0.0 collective-permute-done.3.right_ref
  84.6 0.6 shard_map.135
  85.3 1.1 collective-permute-start.4
  86.4 3.5 %collective-permute-start.5 = (f32[80,128]{1,0:T(8,128)S(1)}, f32[80,128]{1,0:T(8,128)S(1)}, u32[]{:S(2)}, u32[]{:S(2)}) collective-permute-start(f32[80,128]{1,0:T(8,128)S(1)} %get-tuple-element.67), channel_id=1, source_target_pairs={{16,0},{32,16},{48,32},{64,48},{80,64},{96,80},{112,96},{128,112},... | collective-permute-start | bytes 122888 | tf_op jit(solution)/shard_map/ppermute | solution.py:579
  89.9 0.7 collective-permute-done.4.left_ref
  90.6 0.2 collective-permute-done.5.right_ref
  90.8 2.6 %shard_map.136 = (f32[4,288,128]{2,1,0:T(8,128)S(1)}, f32[4,1536,128]{2,1,0:T(8,128)S(1)}, f32[64,128]{1,0:T(8,128)S(1)}, f32[64,128]{1,0:T(8,128)S(1)}) custom-call(f32[512,512]{1,0:T(8,128)S(1)} %get-tuple-element.54.dense_ref, f32[16,128]{1,0:T(8,128)S(1)} %get-tuple-element.65.state_ref, f32[80,128]{1,0:T(8,128)S(1)} %collective-permute-done.4.left_ref, ...), custom_call_target="tpu_custom_call" | custom-call | tf_op jit(solution)/shard_map/pallas_call | solution.py:548
  93.4 0.0 collective-permute-start.6
  93.4 3.8 %collective-permute-start.7 = (f32[64,128]{1,0:T(8,128)S(1)}, f32[64,128]{1,0:T(8,128)S(1)}, u32[]{:S(2)}, u32[]{:S(2)}) collective-permute-start(f32[64,128]{1,0:T(8,128)S(1)} %get-tuple-element.71), channel_id=1, source_target_pairs={{16,0},{32,16},{48,32},{64,48},{80,64},{96,80},{112,96},{128,112},... | collective-permute-start | bytes 98312 | tf_op jit(solution)/shard_map/ppermute | solution.py:579
  97.2 0.4 shard_map.137.inverse_ref
  97.6 0.3 collective-permute-done.6.left_ref
  97.9 0.2 collective-permute-done.7.right_ref
  98.0 2.3 %shard_map.138 = (f32[4,288,128]{2,1,0:T(8,128)S(1)}, f32[4,512,128]{2,1,0:T(8,128)S(1)}, f32[16,128]{1,0:T(8,128)S(1)}, f32[80,128]{1,0:T(8,128)S(1)}, f32[80,128]{1,0:T(8,128)S(1)}) custom-call(f32[4,1536,128]{2,1,0:T(8,128)S(1)} %get-tuple-element.69.t_ref, f32[64,128]{1,0:T(8,128)S(1)} %collective-permute-done.6.left_ref, ...), custom_call_target="tpu_custom_call" | custom-call | tf_op jit(solution)/shard_map/pallas_call | solution.py:548
  100.3 0.0 collective-permute-start.8
  100.4 3.7 %collective-permute-start.9 = (f32[80,128]{1,0:T(8,128)S(1)}, f32[80,128]{1,0:T(8,128)S(1)}, u32[]{:S(2)}, u32[]{:S(2)}) collective-permute-start(f32[80,128]{1,0:T(8,128)S(1)} %get-tuple-element.75), channel_id=1, source_target_pairs={{16,0},{32,16},{48,32},{64,48},{80,64},{96,80},{112,96},{128,112},... | collective-permute-start | bytes 122888 | tf_op jit(solution)/shard_map/ppermute | solution.py:579
  104.1 0.7 collective-permute-done.8.left_ref
  104.8 0.2 collective-permute-done.9.right_ref
  104.9 0.6 shard_map.139
  105.6 0.0 collective-permute-start.10
  105.6 3.8 %collective-permute-start.11 = (f32[16,128]{1,0:T(8,128)S(1)}, f32[16,128]{1,0:T(8,128)S(1)}, u32[]{:S(2)}, u32[]{:S(2)}) collective-permute-start(f32[16,128]{1,0:T(8,128)S(1)} %get-tuple-element.77), channel_id=1, source_target_pairs={{16,0},{32,16},{48,32},{64,48},{80,64},{96,80},{112,96},{128,112},... | collective-permute-start | bytes 24584 | tf_op jit(solution)/shard_map/ppermute | solution.py:579
  109.4 4.1 %shard_map.140 = (f32[4,288,128]{2,1,0:T(8,128)S(1)}, f32[64,128]{1,0:T(8,128)S(1)}, f32[64,128]{1,0:T(8,128)S(1)}) custom-call(f32[4,512,128]{2,1,0:T(8,128)S(1)} %get-tuple-element.78.box_ref, f32[4,192,128]{2,1,0:T(8,128)S(1)} %get-tuple-element.61.vec_ref, f32[4,48,128]{2,1,0:T(8,128)S(1)} %get-tuple-element.62.small_ref, ...), custom_call_target="tpu_custom_call" | custom-call | tf_op jit(solution)/shard_map/pallas_call | solution.py:548
  113.4 0.0 collective-permute-done.10.left_ref
  113.4 0.0 collective-permute-done.11.right_ref
  113.5 0.6 shard_map.141
  114.1 0.1 collective-permute-start.12
  114.2 2.9 %collective-permute-start.13 = (f32[80,128]{1,0:T(8,128)S(1)}, f32[80,128]{1,0:T(8,128)S(1)}, u32[]{:S(2)}, u32[]{:S(2)}) collective-permute-start(f32[80,128]{1,0:T(8,128)S(1)} %get-tuple-element.83), channel_id=1, source_target_pairs={{16,0},{32,16},{48,32},{64,48},{80,64},{96,80},{112,96},{128,112},... | collective-permute-start | bytes 122888 | tf_op jit(solution)/shard_map/ppermute | solution.py:579
  117.1 0.7 collective-permute-done.12.left_ref
  117.8 0.2 collective-permute-done.13.right_ref
  118.0 2.6 %shard_map.142 = (f32[4,288,128]{2,1,0:T(8,128)S(1)}, f32[4,1536,128]{2,1,0:T(8,128)S(1)}, f32[64,128]{1,0:T(8,128)S(1)}, f32[64,128]{1,0:T(8,128)S(1)}) custom-call(f32[512,512]{1,0:T(8,128)S(1)} %get-tuple-element.54.dense_ref, f32[16,128]{1,0:T(8,128)S(1)} %get-tuple-element.81.state_ref, f32[80,128]{1,0:T(8,128)S(1)} %collective-permute-done.12.left_ref, ...), custom_call_target="tpu_custom_call" | custom-call | tf_op jit(solution)/shard_map/pallas_call | solution.py:548
  120.6 0.0 collective-permute-start.14
  120.6 3.8 %collective-permute-start.15 = (f32[64,128]{1,0:T(8,128)S(1)}, f32[64,128]{1,0:T(8,128)S(1)}, u32[]{:S(2)}, u32[]{:S(2)}) collective-permute-start(f32[64,128]{1,0:T(8,128)S(1)} %get-tuple-element.87), channel_id=1, source_target_pairs={{16,0},{32,16},{48,32},{64,48},{80,64},{96,80},{112,96},{128,112},... | collective-permute-start | bytes 98312 | tf_op jit(solution)/shard_map/ppermute | solution.py:579
  124.3 0.7 collective-permute-done.14.left_ref
  125.0 0.2 collective-permute-done.15.right_ref
  125.2 2.1 %shard_map.143 = (f32[4,288,128]{2,1,0:T(8,128)S(1)}, f32[8,128]{1,0:T(8,128)S(1)}) custom-call(f32[4,1536,128]{2,1,0:T(8,128)S(1)} %get-tuple-element.85.t_ref, f32[64,128]{1,0:T(8,128)S(1)} %collective-permute-done.14.left_ref, f32[64,128]{1,0:T(8,128)S(1)} %collective-permute-done.15.right_ref, f32[4,512,128]{2,1,0:T(8,128)S(1)} %shard_map.137.inverse_ref, ...), custom_call_target="tpu_custom_call" | custom-call | tf_op jit(solution)/shard_map/pallas_call | solution.py:548
  127.3 0.0 copy-start.2
  127.3 0.6 broadcast_in_dim.10
  127.9 9.5 %all-to-all-start.4 = ((f32[8,8,128]{2,1,0:T(8,128)}), f32[8,8,128]{2,1,0:T(8,128)S(1)}, u32[]{:S(2)}, u32[]{:S(2)}) async-start(f32[8,8,128]{2,1,0:T(8,128)} %broadcast_in_dim.10), calls=%async_computation.4 | async-start | bytes 65536 | tf_op jit(solution)/shard_map/all_to_all | solution.py:562
  137.5 5.0 %all-to-all-done.4 = f32[8,8,128]{2,1,0:T(8,128)S(1)} async-done(((f32[8,8,128]{2,1,0:T(8,128)}), f32[8,8,128]{2,1,0:T(8,128)S(1)}, u32[]{:S(2)}, u32[]{:S(2)}) %all-to-all-start.4) | async-done | bytes 32800 | tf_op jit(solution)/shard_map/all_to_all | solution.py:562
  142.4 0.6 broadcast_in_dim.11
  143.1 10.0 %all-to-all-start.5 = ((f32[4,8,128]{2,1,0:T(8,128)}), f32[4,8,128]{2,1,0:T(8,128)S(1)}, u32[]{:S(2)}, u32[]{:S(2)}) async-start(f32[4,8,128]{2,1,0:T(8,128)} %broadcast_in_dim.11), calls=%async_computation.5 | async-start | bytes 32768 | tf_op jit(solution)/shard_map/all_to_all | solution.py:562
  153.1 0.1 pad_add_fusion.me_ref
  153.1 0.0 copy-done.3
  153.1 1.2 shard_map.144
  154.4 10.1 %all-to-all-done.5.sums_ref = f32[4,8,128]{2,1,0:T(8,128)S(1)} async-done(((f32[4,8,128]{2,1,0:T(8,128)}), f32[4,8,128]{2,1,0:T(8,128)S(1)}, u32[]{:S(2)}, u32[]{:S(2)}) %all-to-all-start.5) | async-done | bytes 16416 | tf_op jit(solution)/shard_map/all_to_all | solution.py:562
  164.5 0.0 copy-done.2
  164.5 0.8 shard_map.145
  (5 shorter events, 0.0 us)
Async XLA Ops:
  62.5 28.3 %copy-start = (bf16[1536,864]{1,0:T(8,128)(2,1)S(1)}, bf16[1536,864]{1,0:T(8,128)(2,1)}, u32[]{:S(2)}) copy-start(bf16[1536,864]{1,0:T(8,128)(2,1)} %constant.21.clone.table_ref) | copy-start | bytes 7962628
  62.5 14.3 %collective-permute-start = (f32[80,128]{1,0:T(8,128)S(1)}, f32[80,128]{1,0:T(8,128)S(1)}, u32[]{:S(2)}, u32[]{:S(2)}) collective-permute-start(f32[80,128]{1,0:T(8,128)S(1)} %get-tuple-element.56), channel_id=1, source_target_pairs={{0,16},{16,32},{32,48},{48,64},{64,80},{80,96},{96,112},{112,128},... | collective-permute-start | bytes 122888 | tf_op jit(solution)/shard_map/ppermute | solution.py:579
  75.7 3.7 %collective-permute-start.1 = (f32[80,128]{1,0:T(8,128)S(1)}, f32[80,128]{1,0:T(8,128)S(1)}, u32[]{:S(2)}, u32[]{:S(2)}) collective-permute-start(f32[80,128]{1,0:T(8,128)S(1)} %get-tuple-element.57), channel_id=1, source_target_pairs={{16,0},{32,16},{48,32},{64,48},{80,64},{96,80},{112,96},{128,112},... | collective-permute-start | bytes 122888 | tf_op jit(solution)/shard_map/ppermute | solution.py:579
  80.0 4.6 %collective-permute-start.2 = (f32[16,128]{1,0:T(8,128)S(1)}, f32[16,128]{1,0:T(8,128)S(1)}, u32[]{:S(2)}, u32[]{:S(2)}) collective-permute-start(f32[16,128]{1,0:T(8,128)S(1)} %get-tuple-element.59), channel_id=1, source_target_pairs={{0,16},{16,32},{32,48},{48,64},{64,80},{80,96},{96,112},{112,128},... | collective-permute-start | bytes 24584 | tf_op jit(solution)/shard_map/ppermute | solution.py:579
  80.1 4.6 %collective-permute-start.3 = (f32[16,128]{1,0:T(8,128)S(1)}, f32[16,128]{1,0:T(8,128)S(1)}, u32[]{:S(2)}, u32[]{:S(2)}) collective-permute-start(f32[16,128]{1,0:T(8,128)S(1)} %get-tuple-element.59), channel_id=1, source_target_pairs={{16,0},{32,16},{48,32},{64,48},{80,64},{96,80},{112,96},{128,112},... | collective-permute-start | bytes 24584 | tf_op jit(solution)/shard_map/ppermute | solution.py:579
  85.3 5.3 %collective-permute-start.4 = (f32[80,128]{1,0:T(8,128)S(1)}, f32[80,128]{1,0:T(8,128)S(1)}, u32[]{:S(2)}, u32[]{:S(2)}) collective-permute-start(f32[80,128]{1,0:T(8,128)S(1)} %get-tuple-element.66), channel_id=1, source_target_pairs={{0,16},{16,32},{32,48},{48,64},{64,80},{80,96},{96,112},{112,128},... | collective-permute-start | bytes 122888 | tf_op jit(solution)/shard_map/ppermute | solution.py:579
  86.4 4.4 %collective-permute-start.5 = (f32[80,128]{1,0:T(8,128)S(1)}, f32[80,128]{1,0:T(8,128)S(1)}, u32[]{:S(2)}, u32[]{:S(2)}) collective-permute-start(f32[80,128]{1,0:T(8,128)S(1)} %get-tuple-element.67), channel_id=1, source_target_pairs={{16,0},{32,16},{48,32},{64,48},{80,64},{96,80},{112,96},{128,112},... | collective-permute-start | bytes 122888 | tf_op jit(solution)/shard_map/ppermute | solution.py:579
  90.8 7.2 %copy-start.1 = (bf16[288,4608]{1,0:T(8,128)(2,1)S(1)}, bf16[288,4608]{1,0:T(8,128)(2,1)}, u32[]{:S(2)}) copy-start(bf16[288,4608]{1,0:T(8,128)(2,1)} %constant.22.clone.table_ref) | copy-start | bytes 7962628
  93.4 4.5 %collective-permute-start.6 = (f32[64,128]{1,0:T(8,128)S(1)}, f32[64,128]{1,0:T(8,128)S(1)}, u32[]{:S(2)}, u32[]{:S(2)}) collective-permute-start(f32[64,128]{1,0:T(8,128)S(1)} %get-tuple-element.70), channel_id=1, source_target_pairs={{0,16},{16,32},{32,48},{48,64},{64,80},{80,96},{96,112},{112,128},... | collective-permute-start | bytes 98312 | tf_op jit(solution)/shard_map/ppermute | solution.py:579
  93.4 4.6 %collective-permute-start.7 = (f32[64,128]{1,0:T(8,128)S(1)}, f32[64,128]{1,0:T(8,128)S(1)}, u32[]{:S(2)}, u32[]{:S(2)}) collective-permute-start(f32[64,128]{1,0:T(8,128)S(1)} %get-tuple-element.71), channel_id=1, source_target_pairs={{16,0},{32,16},{48,32},{64,48},{80,64},{96,80},{112,96},{128,112},... | collective-permute-start | bytes 98312 | tf_op jit(solution)/shard_map/ppermute | solution.py:579
  100.3 4.4 %collective-permute-start.8 = (f32[80,128]{1,0:T(8,128)S(1)}, f32[80,128]{1,0:T(8,128)S(1)}, u32[]{:S(2)}, u32[]{:S(2)}) collective-permute-start(f32[80,128]{1,0:T(8,128)S(1)} %get-tuple-element.74), channel_id=1, source_target_pairs={{0,16},{16,32},{32,48},{48,64},{64,80},{80,96},{96,112},{112,128},... | collective-permute-start | bytes 122888 | tf_op jit(solution)/shard_map/ppermute | solution.py:579
  100.4 4.6 %collective-permute-start.9 = (f32[80,128]{1,0:T(8,128)S(1)}, f32[80,128]{1,0:T(8,128)S(1)}, u32[]{:S(2)}, u32[]{:S(2)}) collective-permute-start(f32[80,128]{1,0:T(8,128)S(1)} %get-tuple-element.75), channel_id=1, source_target_pairs={{16,0},{32,16},{48,32},{64,48},{80,64},{96,80},{112,96},{128,112},... | collective-permute-start | bytes 122888 | tf_op jit(solution)/shard_map/ppermute | solution.py:579
  105.6 7.9 %collective-permute-start.10 = (f32[16,128]{1,0:T(8,128)S(1)}, f32[16,128]{1,0:T(8,128)S(1)}, u32[]{:S(2)}, u32[]{:S(2)}) collective-permute-start(f32[16,128]{1,0:T(8,128)S(1)} %get-tuple-element.77), channel_id=1, source_target_pairs={{0,16},{16,32},{32,48},{48,64},{64,80},{80,96},{96,112},{112,128},... | collective-permute-start | bytes 24584 | tf_op jit(solution)/shard_map/ppermute | solution.py:579
  105.6 7.8 %collective-permute-start.11 = (f32[16,128]{1,0:T(8,128)S(1)}, f32[16,128]{1,0:T(8,128)S(1)}, u32[]{:S(2)}, u32[]{:S(2)}) collective-permute-start(f32[16,128]{1,0:T(8,128)S(1)} %get-tuple-element.77), channel_id=1, source_target_pairs={{16,0},{32,16},{48,32},{64,48},{80,64},{96,80},{112,96},{128,112},... | collective-permute-start | bytes 24584 | tf_op jit(solution)/shard_map/ppermute | solution.py:579
  114.1 3.7 %collective-permute-start.12 = (f32[80,128]{1,0:T(8,128)S(1)}, f32[80,128]{1,0:T(8,128)S(1)}, u32[]{:S(2)}, u32[]{:S(2)}) collective-permute-start(f32[80,128]{1,0:T(8,128)S(1)} %get-tuple-element.82), channel_id=1, source_target_pairs={{0,16},{16,32},{32,48},{48,64},{64,80},{80,96},{96,112},{112,128},... | collective-permute-start | bytes 122888 | tf_op jit(solution)/shard_map/ppermute | solution.py:579
  114.2 3.8 %collective-permute-start.13 = (f32[80,128]{1,0:T(8,128)S(1)}, f32[80,128]{1,0:T(8,128)S(1)}, u32[]{:S(2)}, u32[]{:S(2)}) collective-permute-start(f32[80,128]{1,0:T(8,128)S(1)} %get-tuple-element.83), channel_id=1, source_target_pairs={{16,0},{32,16},{48,32},{64,48},{80,64},{96,80},{112,96},{128,112},... | collective-permute-start | bytes 122888 | tf_op jit(solution)/shard_map/ppermute | solution.py:579
  120.6 4.5 %collective-permute-start.14 = (f32[64,128]{1,0:T(8,128)S(1)}, f32[64,128]{1,0:T(8,128)S(1)}, u32[]{:S(2)}, u32[]{:S(2)}) collective-permute-start(f32[64,128]{1,0:T(8,128)S(1)} %get-tuple-element.86), channel_id=1, source_target_pairs={{0,16},{16,32},{32,48},{48,64},{64,80},{80,96},{96,112},{112,128},... | collective-permute-start | bytes 98312 | tf_op jit(solution)/shard_map/ppermute | solution.py:579
  120.6 4.6 %collective-permute-start.15 = (f32[64,128]{1,0:T(8,128)S(1)}, f32[64,128]{1,0:T(8,128)S(1)}, u32[]{:S(2)}, u32[]{:S(2)}) collective-permute-start(f32[64,128]{1,0:T(8,128)S(1)} %get-tuple-element.87), channel_id=1, source_target_pairs={{16,0},{32,16},{48,32},{64,48},{80,64},{96,80},{112,96},{128,112},... | collective-permute-start | bytes 98312 | tf_op jit(solution)/shard_map/ppermute | solution.py:579
  125.2 27.9 %copy-start.3 = (f32[192,192]{1,0:T(8,128)S(1)}, f32[192,192]{1,0:T(8,128)}, u32[]{:S(2)}) copy-start(f32[192,192]{1,0:T(8,128)} %constant.23.clone.table_ref) | copy-start | bytes 442372
  127.3 37.2 %copy-start.2 = (f32[6,6,192]{2,1,0:T(8,128)S(1)}, f32[6,6,192]{2,1,0:T(8,128)}, u32[]{:S(2)}) copy-start(f32[6,6,192]{2,1,0:T(8,128)} %rhs_ref.1) | copy-start | bytes 82948
  127.9 14.5 %all-to-all-start.4 = ((f32[8,8,128]{2,1,0:T(8,128)}), f32[8,8,128]{2,1,0:T(8,128)S(1)}, u32[]{:S(2)}, u32[]{:S(2)}) async-start(f32[8,8,128]{2,1,0:T(8,128)} %broadcast_in_dim.10), calls=%async_computation.4 | async-start | bytes 65536 | tf_op jit(solution)/shard_map/all_to_all | solution.py:562
  143.1 21.4 %all-to-all-start.5 = ((f32[4,8,128]{2,1,0:T(8,128)}), f32[4,8,128]{2,1,0:T(8,128)S(1)}, u32[]{:S(2)}, u32[]{:S(2)}) async-start(f32[4,8,128]{2,1,0:T(8,128)} %broadcast_in_dim.11), calls=%async_computation.5 | async-start | bytes 32768 | tf_op jit(solution)/shard_map/all_to_all | solution.py:562

commit v5 on v3

--- a/solution.py
+++ b/solution.py
@@ -45,8 +45,7 @@
 
 ROWS_P = 288
 ROWS_V = 512
-ROWS_A = 176
-ROWS = 400
+ROWS = 312
 
 
 def basis_tables():
@@ -115,6 +114,29 @@
 CENTER, KEEP, ADD = sweep_factors()
 
 
+def parity(value):
+    return bin(value).count("1") % 2
+
+
+def block_choice():
+    def extend(taken):
+        t = len(taken) + 1
+        if t == 16:
+            return taken
+        for mask in range(1, 16):
+            if mask not in taken and parity(mask & t):
+                done = extend(taken + [mask])
+                if done:
+                    return done
+        return None
+
+    masks = extend([])
+    return [[0] + [t for t in range(1, 16) if not parity(masks[t - 1] & r)] for r in range(16)]
+
+
+BLOCKS = block_choice()
+
+
 def lanes(shape):
     return lax.broadcasted_iota(jnp.int32, shape, len(shape) - 1)
 
@@ -154,10 +176,9 @@
     columns = jnp.concatenate([vector, jnp.zeros_like(vector)], axis=0).T
     total = None
     for b in range(NB):
-        part = dense_ref[b * 128 : (b + 1) * 128, :] * columns[:, b : b + 1]
+        part = dense_ref[:, b * 128 : (b + 1) * 128, :] * columns[:, b : b + 1][None]
         total = part if total is None else total + part
-    row = jnp.sum(total, axis=0, keepdims=True)
-    return jnp.concatenate([row[:, b * 128 : (b + 1) * 128] for b in range(NB)], axis=0)
+    return jnp.sum(total, axis=1)
 
 
 def sweep_begin(dense_ref, source, link):
@@ -223,62 +244,115 @@
     behind_ref[16:80, :] = pack_first([box_ref[b, 64:128, :] for b in range(NB)] + extra[1])
 
 
+def flip_blocks(value, mine_c):
+    block = lanes(value.shape) // EA
+    swapped = jnp.where(block % 2 == 0, turn(value, -32), turn(value, 32))
+    value = jnp.where((mine_c & 1) == 1, swapped, value)
+    return jnp.where((mine_c & 2) == 2, turn(value, 64), value)
+
+
+def place_blocks(pieces):
+    total = None
+    for value, source, target in pieces:
+        part = jnp.where(lanes(value.shape) // EA == target, turn(value, (target - source) * 32), 0.0)
+        total = part if total is None else total + part
+    return total
+
+
 def pack_body(*refs):
-    sources, out_ref, held, (tmp, ready) = refs[:9], refs[9], refs[10:19], refs[19:]
-    a_ref, b_ref = out_ref.at[0:ROWS_A], out_ref.at[ROWS_A:ROWS]
+    me_ref, sources, (out_ref, own_ref), held, (tmp, common, tiles, ready) = (
+        refs[0], refs[1:10], refs[10:12], refs[12:21], refs[21:]
+    )
     copies = [pltpu.make_async_copy(sources[n], held[n], ready.at[n]) for n in range(9)]
     for copy in copies:
         copy.start()
     for copy in copies:
         copy.wait()
     rhs_ref, helm_ref, vec_ref, val_ref, size_ref, rows_ref, link_ref, six_ref, eight_ref = held
+    mine_b = me_ref[0]
+    mine_c = me_ref[1]
     for t in range(4):
-        a_ref[t * 32 : (t + 1) * 32, :] = rows_ref[:, t * 128 : (t + 1) * 128]
-        a_ref[128:176, t * 32 : (t + 1) * 32] = vec_ref[t * 48 : (t + 1) * 48, :]
+        tiles[t] = rows_ref[:, t * 128 : (t + 1) * 128]
+    for t in range(4):
+        own_ref[t] = flip_blocks(tiles[mine_b ^ t], mine_c)
     tmp[...] = jnp.zeros(tmp.shape, F32)
     for i in range(6):
-        tmp[i * 8 + 1 : i * 8 + 7, :] = rhs_ref[i]
+        tmp[i * 6 : i * 6 + 6, :] = rhs_ref[i]
     nodes = jnp.dot(tmp[...], six_ref[...], precision=HIGHEST, preferred_element_type=F32)
-    b_ref[0:48, :] = nodes[:, 0:128]
-    b_ref[48:96, :] = jnp.zeros((48, 128), F32)
-    b_ref[48:96, 0:64] = nodes[:, 128:192]
-    b_ref[48:72, 64:96] = val_ref[...]
-    b_ref[72:75, 64:96] = size_ref[...]
-    b_ref[80:81, 64:96] = jnp.broadcast_to(link_ref[0], (1, 32))
+    common[0:40, :] = nodes[:, 0:128]
+    common[40:80, :] = jnp.zeros((40, 128), F32)
+    common[40:80, 0:64] = nodes[:, 128:192]
+    common[40:64, 64:96] = val_ref[...]
+    common[64:67, 64:96] = size_ref[...]
+    common[72:73, 64:96] = jnp.broadcast_to(link_ref[0], (1, 32))
+    common[40:80, 96:128] = vec_ref[0:40, :]
+    common[80:120, :] = jnp.zeros((40, 128), F32)
+    for t in range(4):
+        rows = 40 if t < 3 else 32
+        common[80 : 80 + rows, t * 32 : (t + 1) * 32] = vec_ref[40 + t * 40 : 40 + t * 40 + rows, :]
     helm = jnp.dot(
         helm_ref[...].reshape(64, 256), eight_ref[...], precision=HIGHEST, preferred_element_type=F32
     )
-    b_ref[96:160, :] = helm[:, 0:128]
-    b_ref[160:224, :] = helm[:, 128:256]
-
-
-def joined(all_ref, b, start, rows, quarter):
-    place = lanes((rows, 128)) // EA
-    total = None
-    for c in range(4):
-        moved = turn(all_ref[b * 4 + c, start : start + rows, :], (c - quarter) * 32)
-        part = jnp.where(place == c, moved, 0.0)
-        total = part if total is None else total + part
-    return total
+    common[120:184, :] = helm[:, 0:128]
+    common[184:248, :] = helm[:, 128:256]
+    for r in range(16):
+        other = ((mine_b ^ (r >> 2)) << 2) | (mine_c ^ (r & 3))
+        out_ref[other, 64:312, :] = common[...]
+        for half in range(2):
+            chosen = BLOCKS[r][half * 4 : half * 4 + 4]
+            out_ref[other, half * 32 : half * 32 + 32, :] = place_blocks(
+                [(own_ref[t >> 2], t & 3, n) for n, t in enumerate(chosen)]
+            )
+
+
+def joined(column, start, rows, quarter):
+    return place_blocks([(column[c][start : start + rows, :], quarter, c) for c in range(4)])
 
 
 def unpack_body(
-    all_ref, dense_ref, rhs_ref, helm_ref, vec_ref, small_ref, box_ref, state_ref, ahead_ref, behind_ref
+    me_ref, all_ref, own_ref,
+    dense_ref, rhs_ref, helm_ref, vec_ref, small_ref, box_ref, state_ref, ahead_ref, behind_ref, near,
 ):
-    for b in range(NB):
-        for c in range(4):
-            at = (b * 4 + c) * 32
-            for t in range(4):
-                dense_ref[at : at + 32, t * 128 : (t + 1) * 128] = all_ref[b * 4 + c, t * 32 : (t + 1) * 32, :]
+    mine_b = me_ref[0]
+    mine_c = me_ref[1]
+    for t in range(4):
+        near[t, 0:32, :] = own_ref[t]
+    for r in range(1, 16):
+        other = ((mine_b ^ (r >> 2)) << 2) | (mine_c ^ (r & 3))
+        halves = [all_ref[other, half * 32 : half * 32 + 32, :] for half in range(2)]
+        for tile in range(4):
+            pieces = []
+            for q in range(4):
+                t = r ^ (tile * 4 + q)
+                if t in BLOCKS[r]:
+                    slot = BLOCKS[r].index(t)
+                    pieces.append((halves[slot // 4], slot % 4, q))
+            near[tile, r * 32 : r * 32 + 32, :] = place_blocks(pieces) if pieces else jnp.zeros((32, 128), F32)
+    row_block = lax.broadcasted_iota(jnp.int32, (128, 128), 0) // 32
+    for tile in range(4):
+        for row_tile in range(4):
+            mirrored = near[row_tile, tile * 128 : (tile + 1) * 128, :].T
+            if tile == row_tile:
+                mirrored = jnp.where(row_block == lanes((128, 128)) // EA, 0.0, mirrored)
+            value = near[tile, row_tile * 128 : (row_tile + 1) * 128, :] + mirrored
+            value = flip_blocks(value, mine_c)
+            for q in range(4):
+                start = pl.multiple_of((mine_b ^ row_tile) * 128 + (mine_c ^ q) * 32, 32)
+                dense_ref[mine_b ^ tile, pl.ds(start, 32), :] = value[q * 32 : (q + 1) * 32, :]
+    rhs_ref[...] = jnp.zeros(rhs_ref.shape, F32)
+    for b in range(NB):
+        column = [all_ref.at[b * 4 + c] for c in range(4)]
+        for k in range(6):
+            value = joined(column, 64 + 40 * (k // 4), 40, k % 4)
+            for i in range(6):
+                rhs_ref[b, k * 48 + i * 8 + 1 : k * 48 + i * 8 + 7, :] = value[i * 6 : i * 6 + 6, :]
+        small_ref[b, :, :] = joined(column, 104, 40, 2)
+        vec_ref[b, 0:40, :] = joined(column, 104, 40, 3)
         for t in range(4):
-            vec_ref[b, t * 48 : (t + 1) * 48, :] = joined(all_ref, b, 128, 48, t)
-        for k in range(6):
-            rhs_ref[b, k * 48 : (k + 1) * 48, :] = joined(all_ref, b, ROWS_A + 48 * (k // 4), 48, k % 4)
-        small_ref[b, :, :] = joined(all_ref, b, ROWS_A + 48, 48, 2)
+            rows = 40 if t < 3 else 32
+            vec_ref[b, 40 + t * 40 : 40 + t * 40 + rows, :] = joined(column, 144, rows, t)
         for k in range(8):
-            helm_ref[b, k * 64 : (k + 1) * 64, :] = joined(
-                all_ref, b, ROWS_A + 96 + 64 * (k // 4), 64, k % 4
-            )
+            helm_ref[b, k * 64 : (k + 1) * 64, :] = joined(column, 184 + 64 * (k // 4), 64, k % 4)
     begin_kernel_part(
         rhs_ref, small_ref, dense_ref, box_ref, state_ref, ahead_ref, behind_ref,
         ([helm_ref[b, 448:512, :] for b in range(NB)], [helm_ref[b, 0:64, :] for b in range(NB)]),
@@ -489,19 +563,43 @@
     )
 
 
-def last_image_body(
-    t_ref, left_ref, right_ref, inverse_ref, small_ref, table_ref, r_ref, z_ref, w_ref, q_ref,
-    image_ref, sums_ref, spread,
-):
+def last_image_body(t_ref, left_ref, right_ref, inverse_ref, small_ref, table_ref, image_ref, spread):
     divergence_part(t_ref, left_ref, right_ref, inverse_ref, small_ref, table_ref, image_ref, spread)
-    products = ((r_ref, z_ref), (z_ref, w_ref), (w_ref, q_ref), (r_ref, q_ref), (q_ref, image_ref), (z_ref, image_ref))
+
+
+def products_body(r_ref, z_ref, w_ref, q_ref, sums_ref):
     sums_ref[...] = jnp.zeros(sums_ref.shape, F32)
-    for n, (one, two) in enumerate(products):
+    for n, (one, two) in enumerate(((r_ref, z_ref), (z_ref, w_ref), (w_ref, q_ref), (r_ref, q_ref))):
         total = None
         for b in range(NB):
             part = jnp.sum(one[b] * two[b], axis=0, keepdims=True)
             total = part if total is None else total + part
         sums_ref[n : n + 1, :] = total
+
+
+def energy_body(t_ref, left_ref, right_ref, inverse_ref, products_ref, sums_ref):
+    row = lax.broadcasted_iota(jnp.int32, (64, 128), 0)
+    i, j = row // 8, row % 8
+    total = None
+    for b in range(NB):
+        share = jnp.where((j == 0) | (j == 7), 0.5, 1.0)
+        shared_b = ((i == 0) & (b > 0)) | ((i == 7) & (b < NB - 1))
+        share = jnp.where(shared_b, 0.5 * share, share)
+        for k in range(8):
+            squares = None
+            for d in range(3):
+                value = t_ref[b, d * 512 + k * 64 : d * 512 + k * 64 + 64, :]
+                if k == 0:
+                    value = value + at_first(left_ref[...], b * 3 + d)
+                if k == 7:
+                    value = value + at_last(right_ref[...], b * 3 + d)
+                squares = value * value if squares is None else squares + value * value
+            part = squares * inverse_ref[b, k * 64 : k * 64 + 64, :] * share
+            if k in (0, 7):
+                part = part * 0.5
+            total = part if total is None else total + part
+    sums_ref[...] = products_ref[...]
+    sums_ref[4:5, :] = jnp.sum(total, axis=0, keepdims=True)
 
 
 def own_body(me_ref, z_ref, w_ref, q_ref, v_ref, table_ref, z_out, w_out, q_out, v_out):
@@ -519,11 +617,11 @@
     sums_ref, z_ref, w_ref, q_ref, v_ref, rhs_ref, pressure_ref, residual_ref, pressure, residual, done
 ):
     totals = jnp.sum(jnp.sum(sums_ref[...], axis=0), axis=1, keepdims=True)
-    rz, zw, wq, rq, qv, zv = [totals[n : n + 1] for n in range(6)]
+    rz, zw, wq, rq, qv = [totals[n : n + 1] for n in range(5)]
     step_first = rz / zw
     rz_next = step_first * (step_first * wq - rq)
     share = 1.0 + rz_next / rz
-    curvature = share * share * zw - share * step_first * (zv + wq) + step_first * step_first * qv
+    curvature = share * share * zw - 2.0 * share * step_first * wq + step_first * step_first * qv
     step_next = rz_next / curvature
     z_factor = (step_first + step_next * share)[None]
     q_factor = (step_next * step_first)[None]
@@ -558,6 +656,23 @@
     return lax.all_to_all(jnp.broadcast_to(block[None], (count,) + block.shape), axes, 0, 0)
 
 
+def sum_slabs(sums):
+    slabs, across, around = (lax.axis_size(axis) for axis in ("gx", "gy", "col"))
+    group = across * around
+    chips = slabs // 2
+    assert chips == group
+    total = None
+    for core in range(2):
+        pairs = []
+        for slab in range(slabs):
+            for n in range(group):
+                source = (slab // 2 + n) % chips * 2 + (slab + core) % 2
+                pairs.append((source * group + n, slab * group + n))
+        part = lax.ppermute(sums, ("gx", "gy", "col"), pairs)
+        total = part if total is None else total + part
+    return tell_all(total, ("gy", "col"), group)
+
+
 def local(divergence, elem_size, helm_diag, fdm_vectors, fdm_values, coarse_rows, axial_link):
     count = lax.axis_size("gx")
     ahead = [(i, (i + 1) % count) for i in range(count)]
@@ -586,21 +701,29 @@
         six,
         order_table(8),
     )
-    own_part = pl.pallas_call(
+    vmem = pl.BlockSpec(memory_space=pltpu.VMEM)
+    own_part, own_rows = pl.pallas_call(
         pack_body,
-        out_shape=jax.ShapeDtypeStruct((ROWS, 128), F32),
-        in_specs=[pl.BlockSpec(memory_space=pl.ANY)] * 9,
-        out_specs=pl.BlockSpec(memory_space=pltpu.VMEM),
+        out_shape=[jax.ShapeDtypeStruct((16, ROWS, 128), F32), jax.ShapeDtypeStruct((4, 32, 128), F32)],
+        in_specs=[pl.BlockSpec(memory_space=pltpu.SMEM)] + [pl.BlockSpec(memory_space=pl.ANY)] * 9,
+        out_specs=[vmem, vmem],
         scratch_shapes=[pltpu.VMEM(value.shape, F32) for value in arguments]
-        + [pltpu.VMEM((48, 192), F32), pltpu.SemaphoreType.DMA((9,))],
-        compiler_params=pltpu.CompilerParams(vmem_limit_bytes=60 * 1024 * 1024),
-    )(*arguments)
-    everything = tell_all(own_part, ("gy", "col"), 16)
+        + [
+            pltpu.VMEM((40, 192), F32),
+            pltpu.VMEM((248, 128), F32),
+            pltpu.VMEM((4, 32, 128), F32),
+            pltpu.SemaphoreType.DMA((9,)),
+        ],
+        compiler_params=pltpu.CompilerParams(vmem_limit_bytes=40 * 1024 * 1024),
+    )(me, *arguments)
+    everything = lax.all_to_all(own_part, ("gy", "col"), 0, 0)
 
     dense, rhs, helm, vectors, small, boxes, state, up, down = call(
         unpack_body,
-        [(512, 512), field, velocity, (NB, 192, 128), (NB, 48, 128), velocity, state_shape, wide, wide],
-    )(everything)
+        [(4, 512, 128), field, velocity, (NB, 192, 128), (NB, 40, 128), velocity, state_shape, wide, wide],
+        [pltpu.VMEM((4, 512, 128), F32)],
+        scalars=1,
+    )(me, everything, own_rows)
 
     def precondition(boxes, state, left, right):
         state, message = call(middle_body, [state_shape, state_shape])(dense, state, left, right)
@@ -629,11 +752,11 @@
     )(t, left, right, inverse, small, backward, dense)
     left, right = exchange(up, down)
     q, t, left, right = precondition(boxes, state, left, right)
-    v, sums = call(last_image_body, [field, (8, 128)], spread)(
-        t, left, right, inverse, small, backward, rhs, z, w, q
-    )
+    (products,) = call(products_body, [(8, 128)])(rhs, z, w, q)
+    (sums,) = call(energy_body, [(8, 128)])(t, left, right, inverse, products)
+    sums = sum_slabs(sums)
+    (v,) = call(last_image_body, [field], spread)(t, left, right, inverse, small, backward)
     own = call(own_body, [(6, 6, 192)] * 4, scalars=1)(me, z, w, q, v, six.T.copy())
-    sums = tell_all(sums, "gx", count)
     return tuple(
         pl.pallas_call(
             last_body,

time: 144 us -> 149 us (1.035)
  starting transfers between devices: 45.2 us -> 60.1 us
  waiting for transfers between devices: 21.9 us -> 7.24 us
  local copies, waits for them, and re-layouts: 1.82 us -> 10.9 us
  blocking collectives: 46 us -> 38.6 us
  Pallas kernels: 26.8 us -> 30.1 us
    all_to_all x1, waiting for transfers between devices: 14.5 us -> 0.01 us  [tell_all(): lax.all_to_all(jnp.broadcast_to(block[None], (count,) + block.shape), axe...]
    unnamed x8 -> x30, local copies, waits for them, and re-layouts: 0.01 us -> 10.3 us
    all_to_all x1, starting transfers between devices: 14.6 us -> 24 us  [tell_all(): lax.all_to_all(jnp.broadcast_to(block[None], (count,) + block.shape), axe...]
    all_to_all x1, blocking collectives: 46 us -> 38.6 us  [local(): everything = lax.all_to_all(own_part, ('gy', 'col'), 0, 0)]
    ppermute x0 -> x2, starting transfers between devices: none -> 6.26 us  [sum_slabs(): part = lax.ppermute(sums, ('gx', 'gy', 'col'), pairs)]
    pallas_call x13 -> x15, Pallas kernels: 23.6 us -> 27.3 us  [run(): pl.pallas_call(body, out_shape=[jax.ShapeDtypeStruct(shape, F32) for shap...]
  transfers between devices with their start and end apart: 17 -> 19, of which waited for: 13 -> 13; matrix products, arithmetic and copies ran while one was open for 0% -> 0% of each run, Pallas kernels for 7% -> 8%
where the time goes in v5:
time: 149 us
  starting transfers between devices  60.1 us (40%)
  blocking collectives  38.6 us (26%)
  Pallas kernels  30.1 us (20%)
  local copies, waits for them, and re-layouts  10.9 us (7%)
  waiting for transfers between devices  7.24 us (5%)
  between operations  1.69 us (1%)
    all_to_all x1, blocking collectives, local(): everything = lax.all_to_all(own_part, ('gy', 'col'), 0, 0)  38.6 us
    ppermute x16, starting transfers between devices, exchange(): return (lax.ppermute(up, 'gx', ahead), lax.ppermute(down, 'gx', behind))  29.9 us
    pallas_call x15, Pallas kernels, run(): pl.pallas_call(body, out_shape=[jax.ShapeDtypeStruct(shape, F32) for shap...  27.3 us
    all_to_all x1, starting transfers between devices, tell_all(): lax.all_to_all(jnp.broadcast_to(block[None], (count,) + block.shape), axe...  24 us
    unnamed x30, local copies, waits for them, and re-layouts  10.3 us
    ppermute x16, waiting for transfers between devices, exchange(): return (lax.ppermute(up, 'gx', ahead), lax.ppermute(down, 'gx', behind))  7.1 us
    ppermute x2, starting transfers between devices, sum_slabs(): part = lax.ppermute(sums, ('gx', 'gy', 'col'), pairs)  6.26 us
  transfers between devices with their start and end apart: 19, of which 13 were waited for; matrix products, arithmetic and copies ran while one was open for 0% of the time, Pallas kernels for 8%

profile of v5, /device:TPU:1, one launch (start us, length us, event | category | flops | bytes accessed | tf_op | source)
XLA Modules:
  0.0 148.7 jit_solution(13403426324531610880)
XLA Ops:
  1.3 0.1 pad_add_fusion.refs_0_.me_ref
  1.4 0.9 copy-done.5
  2.3 0.8 copy-done.6
  3.1 0.9 copy-done.8
  4.0 0.9 copy-done.10
  4.9 0.8 copy-done.11
  5.8 0.8 copy-done.12
  6.6 0.7 copy-done.13
  7.3 0.7 copy-done.14
  8.0 1.9 %shard_map.131 = (f32[16,312,128]{2,1,0:T(8,128)S(1)}, f32[4,32,128]{2,1,0:T(8,128)S(1)}) custom-call(s32[2]{0:T(128)S(1)} %pad_add_fusion.refs_0_.me_ref, f32[6,6,192]{2,1,0:T(8,128)S(1)} %copy-done.6, f32[8,8,256]{2,1,0:T(8,128)S(1)} %copy-done.11, f32[192,32]{1,0:T(8,128)S(1)} %bitcast.4, f32[24,32]{1,0:T(8,128)S(1)} %bitcast.5, f32[3,32]{1,0:T(4,128)S(1)} %copy-done.14, ...), custom_call_target="tpu_custom_call" | custom-call | tf_op jit(solution)/shard_map/pallas_call | solution.py:705
  9.9 38.6 %all_to_all.10.all_ref = f32[16,312,128]{2,1,0:T(8,128)S(1)} all-to-all(f32[16,312,128]{2,1,0:T(8,128)S(1)} %get-tuple-element.46), channel_id=1, replica_groups=mesh['gx'=32,'gy'=4,'col'=4] {'gy','col'}, dimensions={0} | all-to-all | bytes 5111808 | tf_op jit(solution)/shard_map/all_to_all | solution.py:719
  48.5 5.3 %shard_map.132 = (f32[4,512,128]{2,1,0:T(8,128)S(1)}, f32[4,288,128]{2,1,0:T(8,128)S(1)}, f32[4,512,128]{2,1,0:T(8,128)S(1)}, f32[4,192,128]{2,1,0:T(8,128)S(1)}...) custom-call(s32[2]{0:T(128)S(1)} %pad_add_fusion.refs_0_.me_ref, ...), custom_call_target="tpu_custom_call" | custom-call | tf_op jit(solution)/shard_map/pallas_call | solution.py:643
  53.8 4.5 %collective-permute-start = (f32[80,128]{1,0:T(8,128)S(1)}, f32[80,128]{1,0:T(8,128)S(1)}, u32[]{:S(2)}, u32[]{:S(2)}) collective-permute-start(f32[80,128]{1,0:T(8,128)S(1)} %get-tuple-element.50), channel_id=1, source_target_pairs={{0,16},{16,32},{32,48},{48,64},{64,80},{80,96},{96,112},{112,128},... | collective-permute-start | bytes 122888 | tf_op jit(solution)/shard_map/ppermute | solution.py:682
  58.3 0.0 collective-permute-start.1
  58.3 1.1 collective-permute-done.left_ref
  59.4 2.3 %collective-permute-done.1.right_ref = f32[80,128]{1,0:T(8,128)S(1)} collective-permute-done((f32[80,128]{1,0:T(8,128)S(1)}, f32[80,128]{1,0:T(8,128)S(1)}, u32[]{:S(2)}, u32[]{:S(2)}) %collective-permute-start.1) | collective-permute-done | bytes 40992 | tf_op jit(solution)/shard_map/ppermute | solution.py:682
  61.7 0.6 shard_map.133
  62.3 3.8 %collective-permute-start.3 = (f32[16,128]{1,0:T(8,128)S(1)}, f32[16,128]{1,0:T(8,128)S(1)}, u32[]{:S(2)}, u32[]{:S(2)}) collective-permute-start(f32[16,128]{1,0:T(8,128)S(1)} %get-tuple-element.53), channel_id=1, source_target_pairs={{16,0},{32,16},{48,32},{64,48},{80,64},{96,80},{112,96},{128,112},... | collective-permute-start | bytes 24584 | tf_op jit(solution)/shard_map/ppermute | solution.py:682
  66.1 3.9 %shard_map.134 = (f32[4,288,128]{2,1,0:T(8,128)S(1)}, f32[64,128]{1,0:T(8,128)S(1)}, f32[64,128]{1,0:T(8,128)S(1)}) custom-call(f32[4,512,128]{2,1,0:T(8,128)S(1)} %get-tuple-element.54.box_ref, f32[4,192,128]{2,1,0:T(8,128)S(1)} %get-tuple-element.55.vec_ref, f32[4,40,128]{2,1,0:T(8,128)S(1)} %get-tuple-element.56.small_ref, ...), custom_call_target="tpu_custom_call" | custom-call | tf_op jit(solution)/shard_map/pallas_call | solution.py:643
  70.0 0.0 collective-permute-done.3.right_ref
  70.0 0.0 collective-permute-done.2.left_ref
  70.0 0.6 shard_map.135
  70.7 0.0 collective-permute-start.4
  70.7 3.4 %collective-permute-start.5 = (f32[80,128]{1,0:T(8,128)S(1)}, f32[80,128]{1,0:T(8,128)S(1)}, u32[]{:S(2)}, u32[]{:S(2)}) collective-permute-start(f32[80,128]{1,0:T(8,128)S(1)} %get-tuple-element.61), channel_id=1, source_target_pairs={{16,0},{32,16},{48,32},{64,48},{80,64},{96,80},{112,96},{128,112},... | collective-permute-start | bytes 122888 | tf_op jit(solution)/shard_map/ppermute | solution.py:682
  74.0 0.7 collective-permute-done.4.left_ref
  74.7 0.2 collective-permute-done.5.right_ref
  74.9 2.6 %shard_map.136 = (f32[4,288,128]{2,1,0:T(8,128)S(1)}, f32[4,1536,128]{2,1,0:T(8,128)S(1)}, f32[64,128]{1,0:T(8,128)S(1)}, f32[64,128]{1,0:T(8,128)S(1)}) custom-call(f32[4,512,128]{2,1,0:T(8,128)S(1)} %get-tuple-element.48.dense_ref, f32[16,128]{1,0:T(8,128)S(1)} %get-tuple-element.59.state_ref, f32[80,128]{1,0:T(8,128)S(1)} %collective-permute-done.4.left_ref, ...), custom_call_target="tpu_custom_call" | custom-call | tf_op jit(solution)/shard_map/pallas_call | solution.py:643
  77.5 0.0 collective-permute-start.6
  77.5 3.8 %collective-permute-start.7 = (f32[64,128]{1,0:T(8,128)S(1)}, f32[64,128]{1,0:T(8,128)S(1)}, u32[]{:S(2)}, u32[]{:S(2)}) collective-permute-start(f32[64,128]{1,0:T(8,128)S(1)} %get-tuple-element.65), channel_id=1, source_target_pairs={{16,0},{32,16},{48,32},{64,48},{80,64},{96,80},{112,96},{128,112},... | collective-permute-start | bytes 98312 | tf_op jit(solution)/shard_map/ppermute | solution.py:682
  81.3 0.4 shard_map.137.inverse_ref
  81.7 0.3 collective-permute-done.6.left_ref
  82.0 0.2 collective-permute-done.7.right_ref
  82.1 2.3 %shard_map.138 = (f32[4,288,128]{2,1,0:T(8,128)S(1)}, f32[4,512,128]{2,1,0:T(8,128)S(1)}, f32[16,128]{1,0:T(8,128)S(1)}, f32[80,128]{1,0:T(8,128)S(1)}, f32[80,128]{1,0:T(8,128)S(1)}) custom-call(f32[4,1536,128]{2,1,0:T(8,128)S(1)} %get-tuple-element.63.t_ref, f32[64,128]{1,0:T(8,128)S(1)} %collective-permute-done.6.left_ref, ...), custom_call_target="tpu_custom_call" | custom-call | tf_op jit(solution)/shard_map/pallas_call | solution.py:643
  84.4 0.0 collective-permute-start.8
  84.5 3.7 %collective-permute-start.9 = (f32[80,128]{1,0:T(8,128)S(1)}, f32[80,128]{1,0:T(8,128)S(1)}, u32[]{:S(2)}, u32[]{:S(2)}) collective-permute-start(f32[80,128]{1,0:T(8,128)S(1)} %get-tuple-element.69), channel_id=1, source_target_pairs={{16,0},{32,16},{48,32},{64,48},{80,64},{96,80},{112,96},{128,112},... | collective-permute-start | bytes 122888 | tf_op jit(solution)/shard_map/ppermute | solution.py:682
  88.2 0.7 collective-permute-done.8.left_ref
  88.8 0.2 collective-permute-done.9.right_ref
  89.0 0.6 shard_map.139
  89.7 3.8 %collective-permute-start.11 = (f32[16,128]{1,0:T(8,128)S(1)}, f32[16,128]{1,0:T(8,128)S(1)}, u32[]{:S(2)}, u32[]{:S(2)}) collective-permute-start(f32[16,128]{1,0:T(8,128)S(1)} %get-tuple-element.71), channel_id=1, source_target_pairs={{16,0},{32,16},{48,32},{64,48},{80,64},{96,80},{112,96},{128,112},... | collective-permute-start | bytes 24584 | tf_op jit(solution)/shard_map/ppermute | solution.py:682
  93.4 4.1 %shard_map.140 = (f32[4,288,128]{2,1,0:T(8,128)S(1)}, f32[64,128]{1,0:T(8,128)S(1)}, f32[64,128]{1,0:T(8,128)S(1)}) custom-call(f32[4,512,128]{2,1,0:T(8,128)S(1)} %get-tuple-element.72.box_ref, f32[4,192,128]{2,1,0:T(8,128)S(1)} %get-tuple-element.55.vec_ref, f32[4,40,128]{2,1,0:T(8,128)S(1)} %get-tuple-element.56.small_ref, ...), custom_call_target="tpu_custom_call" | custom-call | tf_op jit(solution)/shard_map/pallas_call | solution.py:643
  97.5 0.0 collective-permute-done.11.right_ref
  97.5 0.6 shard_map.141
  98.2 0.0 collective-permute-start.12
  98.2 3.2 %collective-permute-start.13 = (f32[80,128]{1,0:T(8,128)S(1)}, f32[80,128]{1,0:T(8,128)S(1)}, u32[]{:S(2)}, u32[]{:S(2)}) collective-permute-start(f32[80,128]{1,0:T(8,128)S(1)} %get-tuple-element.77), channel_id=1, source_target_pairs={{16,0},{32,16},{48,32},{64,48},{80,64},{96,80},{112,96},{128,112},... | collective-permute-start | bytes 122888 | tf_op jit(solution)/shard_map/ppermute | solution.py:682
  101.4 0.7 collective-permute-done.12.left_ref
  102.0 0.2 collective-permute-done.13.right_ref
  102.2 2.6 %shard_map.142 = (f32[4,288,128]{2,1,0:T(8,128)S(1)}, f32[4,1536,128]{2,1,0:T(8,128)S(1)}, f32[64,128]{1,0:T(8,128)S(1)}, f32[64,128]{1,0:T(8,128)S(1)}) custom-call(f32[4,512,128]{2,1,0:T(8,128)S(1)} %get-tuple-element.48.dense_ref, f32[16,128]{1,0:T(8,128)S(1)} %get-tuple-element.75.state_ref, f32[80,128]{1,0:T(8,128)S(1)} %collective-permute-done.12.left_ref, ...), custom_call_target="tpu_custom_call" | custom-call | tf_op jit(solution)/shard_map/pallas_call | solution.py:643
  104.8 0.0 collective-permute-start.14
  104.8 3.8 %collective-permute-start.15 = (f32[64,128]{1,0:T(8,128)S(1)}, f32[64,128]{1,0:T(8,128)S(1)}, u32[]{:S(2)}, u32[]{:S(2)}) collective-permute-start(f32[64,128]{1,0:T(8,128)S(1)} %get-tuple-element.81), channel_id=1, source_target_pairs={{16,0},{32,16},{48,32},{64,48},{80,64},{96,80},{112,96},{128,112},... | collective-permute-start | bytes 98312 | tf_op jit(solution)/shard_map/ppermute | solution.py:682
  108.6 0.3 shard_map.143.products_ref
  108.9 0.4 collective-permute-done.14.left_ref
  109.3 0.2 collective-permute-done.15.right_ref
  109.5 0.4 shard_map.144
  109.9 5.6 %collective-permute-start.17 = (f32[8,128]{1,0:T(8,128)S(1)}, f32[8,128]{1,0:T(8,128)S(1)}, u32[]{:S(2)}, u32[]{:S(2)}) collective-permute-start(f32[8,128]{1,0:T(8,128)S(1)} %shard_map.144), channel_id=1, source_target_pairs={{16,0},{49,1},{82,2},{115,3},{148,4},{181,5},{214,6},{247,7},{280,... | collective-permute-start | bytes 12296 | tf_op jit(solution)/shard_map/ppermute | solution.py:671
  115.5 0.7 collective-permute-start.16
  116.2 0.1 collective-permute-done.17
  116.3 0.0 collective-permute-done.16
  116.3 0.6 broadcast_in_dim.2
  116.9 24.0 %all-to-all-start.1 = ((f32[16,8,128]{2,1,0:T(8,128)}), f32[16,8,128]{2,1,0:T(8,128)S(1)}, u32[]{:S(2)}, u32[]{:S(2)}) async-start(f32[16,8,128]{2,1,0:T(8,128)} %broadcast_in_dim.2), calls=%async_computation.1 | async-start | bytes 131072 | tf_op jit(solution)/shard_map/all_to_all | solution.py:656
  141.0 1.9 %copy-done.1 = f32[4,1536,128]{2,1,0:T(8,128)S(1)} copy-done((f32[4,1536,128]{2,1,0:T(8,128)S(1)}, f32[4,1536,128]{2,1,0:T(8,128)}, u32[]{:S(2)}) %copy-start.1) | copy-done | bytes 3145752
  142.9 1.7 %copy-done.4 = bf16[288,4608]{1,0:T(8,128)(2,1)S(1)} copy-done((bf16[288,4608]{1,0:T(8,128)(2,1)S(1)}, bf16[288,4608]{1,0:T(8,128)(2,1)}, u32[]{:S(2)}) %copy-start.4) | copy-done | bytes 2654232
  144.6 1.8 %shard_map.145.v_ref = f32[4,288,128]{2,1,0:T(8,128)S(1)} custom-call(f32[4,1536,128]{2,1,0:T(8,128)S(1)} %copy-done.1, f32[64,128]{1,0:T(8,128)S(1)} %collective-permute-done.14.left_ref, f32[64,128]{1,0:T(8,128)S(1)} %collective-permute-done.15.right_ref, f32[4,512,128]{2,1,0:T(8,128)S(1)} %shard_map.137.inverse_ref, ...), custom_call_target="tpu_custom_call" | custom-call | tf_op jit(solution)/shard_map/pallas_call | solution.py:643
  146.5 1.2 shard_map.146
  147.7 0.8 shard_map.147
  (25 shorter events, 0.0 us)
Async XLA Ops:
  1.4 1.0 copy-start.5
  2.3 0.8 copy-start.6
  3.1 0.9 copy-start.8
  4.0 0.9 copy-start.10
  4.9 0.8 copy-start.11
  5.8 0.8 copy-start.12
  6.6 0.7 copy-start.13
  7.3 0.7 copy-start.14
  48.5 26.4 %copy-start.2 = (bf16[1536,864]{1,0:T(8,128)(2,1)S(1)}, bf16[1536,864]{1,0:T(8,128)(2,1)}, u32[]{:S(2)}) copy-start(bf16[1536,864]{1,0:T(8,128)(2,1)} %constant.19.clone.table_ref) | copy-start | bytes 7962628
  53.8 5.6 %collective-permute-start = (f32[80,128]{1,0:T(8,128)S(1)}, f32[80,128]{1,0:T(8,128)S(1)}, u32[]{:S(2)}, u32[]{:S(2)}) collective-permute-start(f32[80,128]{1,0:T(8,128)S(1)} %get-tuple-element.50), channel_id=1, source_target_pairs={{0,16},{16,32},{32,48},{48,64},{64,80},{80,96},{96,112},{112,128},... | collective-permute-start | bytes 122888 | tf_op jit(solution)/shard_map/ppermute | solution.py:682
  58.3 3.4 %collective-permute-start.1 = (f32[80,128]{1,0:T(8,128)S(1)}, f32[80,128]{1,0:T(8,128)S(1)}, u32[]{:S(2)}, u32[]{:S(2)}) collective-permute-start(f32[80,128]{1,0:T(8,128)S(1)} %get-tuple-element.51), channel_id=1, source_target_pairs={{16,0},{32,16},{48,32},{64,48},{80,64},{96,80},{112,96},{128,112},... | collective-permute-start | bytes 122888 | tf_op jit(solution)/shard_map/ppermute | solution.py:682
  62.3 7.7 %collective-permute-start.3 = (f32[16,128]{1,0:T(8,128)S(1)}, f32[16,128]{1,0:T(8,128)S(1)}, u32[]{:S(2)}, u32[]{:S(2)}) collective-permute-start(f32[16,128]{1,0:T(8,128)S(1)} %get-tuple-element.53), channel_id=1, source_target_pairs={{16,0},{32,16},{48,32},{64,48},{80,64},{96,80},{112,96},{128,112},... | collective-permute-start | bytes 24584 | tf_op jit(solution)/shard_map/ppermute | solution.py:682
  66.1 3.9 %collective-permute-start.2 = (f32[16,128]{1,0:T(8,128)S(1)}, f32[16,128]{1,0:T(8,128)S(1)}, u32[]{:S(2)}, u32[]{:S(2)}) collective-permute-start(f32[16,128]{1,0:T(8,128)S(1)} %get-tuple-element.53), channel_id=1, source_target_pairs={{0,16},{16,32},{32,48},{48,64},{64,80},{80,96},{96,112},{112,128},... | collective-permute-start | bytes 24584 | tf_op jit(solution)/shard_map/ppermute | solution.py:682
  70.7 4.1 %collective-permute-start.4 = (f32[80,128]{1,0:T(8,128)S(1)}, f32[80,128]{1,0:T(8,128)S(1)}, u32[]{:S(2)}, u32[]{:S(2)}) collective-permute-start(f32[80,128]{1,0:T(8,128)S(1)} %get-tuple-element.60), channel_id=1, source_target_pairs={{0,16},{16,32},{32,48},{48,64},{64,80},{80,96},{96,112},{112,128},... | collective-permute-start | bytes 122888 | tf_op jit(solution)/shard_map/ppermute | solution.py:682
  70.7 4.2 %collective-permute-start.5 = (f32[80,128]{1,0:T(8,128)S(1)}, f32[80,128]{1,0:T(8,128)S(1)}, u32[]{:S(2)}, u32[]{:S(2)}) collective-permute-start(f32[80,128]{1,0:T(8,128)S(1)} %get-tuple-element.61), channel_id=1, source_target_pairs={{16,0},{32,16},{48,32},{64,48},{80,64},{96,80},{112,96},{128,112},... | collective-permute-start | bytes 122888 | tf_op jit(solution)/shard_map/ppermute | solution.py:682
  74.9 7.2 %copy-start.3 = (bf16[288,4608]{1,0:T(8,128)(2,1)S(1)}, bf16[288,4608]{1,0:T(8,128)(2,1)}, u32[]{:S(2)}) copy-start(bf16[288,4608]{1,0:T(8,128)(2,1)} %constant.20.clone.table_ref) | copy-start | bytes 7962628
  77.5 4.5 %collective-permute-start.6 = (f32[64,128]{1,0:T(8,128)S(1)}, f32[64,128]{1,0:T(8,128)S(1)}, u32[]{:S(2)}, u32[]{:S(2)}) collective-permute-start(f32[64,128]{1,0:T(8,128)S(1)} %get-tuple-element.64), channel_id=1, source_target_pairs={{0,16},{16,32},{32,48},{48,64},{64,80},{80,96},{96,112},{112,128},... | collective-permute-start | bytes 98312 | tf_op jit(solution)/shard_map/ppermute | solution.py:682
  77.5 4.6 %collective-permute-start.7 = (f32[64,128]{1,0:T(8,128)S(1)}, f32[64,128]{1,0:T(8,128)S(1)}, u32[]{:S(2)}, u32[]{:S(2)}) collective-permute-start(f32[64,128]{1,0:T(8,128)S(1)} %get-tuple-element.65), channel_id=1, source_target_pairs={{16,0},{32,16},{48,32},{64,48},{80,64},{96,80},{112,96},{128,112},... | collective-permute-start | bytes 98312 | tf_op jit(solution)/shard_map/ppermute | solution.py:682
  84.4 4.4 %collective-permute-start.8 = (f32[80,128]{1,0:T(8,128)S(1)}, f32[80,128]{1,0:T(8,128)S(1)}, u32[]{:S(2)}, u32[]{:S(2)}) collective-permute-start(f32[80,128]{1,0:T(8,128)S(1)} %get-tuple-element.68), channel_id=1, source_target_pairs={{0,16},{16,32},{32,48},{48,64},{64,80},{80,96},{96,112},{112,128},... | collective-permute-start | bytes 122888 | tf_op jit(solution)/shard_map/ppermute | solution.py:682
  84.5 4.6 %collective-permute-start.9 = (f32[80,128]{1,0:T(8,128)S(1)}, f32[80,128]{1,0:T(8,128)S(1)}, u32[]{:S(2)}, u32[]{:S(2)}) collective-permute-start(f32[80,128]{1,0:T(8,128)S(1)} %get-tuple-element.69), channel_id=1, source_target_pairs={{16,0},{32,16},{48,32},{64,48},{80,64},{96,80},{112,96},{128,112},... | collective-permute-start | bytes 122888 | tf_op jit(solution)/shard_map/ppermute | solution.py:682
  89.7 7.8 %collective-permute-start.11 = (f32[16,128]{1,0:T(8,128)S(1)}, f32[16,128]{1,0:T(8,128)S(1)}, u32[]{:S(2)}, u32[]{:S(2)}) collective-permute-start(f32[16,128]{1,0:T(8,128)S(1)} %get-tuple-element.71), channel_id=1, source_target_pairs={{16,0},{32,16},{48,32},{64,48},{80,64},{96,80},{112,96},{128,112},... | collective-permute-start | bytes 24584 | tf_op jit(solution)/shard_map/ppermute | solution.py:682
  93.4 4.1 %collective-permute-start.10 = (f32[16,128]{1,0:T(8,128)S(1)}, f32[16,128]{1,0:T(8,128)S(1)}, u32[]{:S(2)}, u32[]{:S(2)}) collective-permute-start(f32[16,128]{1,0:T(8,128)S(1)} %get-tuple-element.71), channel_id=1, source_target_pairs={{0,16},{16,32},{32,48},{48,64},{64,80},{80,96},{96,112},{112,128},... | collective-permute-start | bytes 24584 | tf_op jit(solution)/shard_map/ppermute | solution.py:682
  98.2 3.9 %collective-permute-start.12 = (f32[80,128]{1,0:T(8,128)S(1)}, f32[80,128]{1,0:T(8,128)S(1)}, u32[]{:S(2)}, u32[]{:S(2)}) collective-permute-start(f32[80,128]{1,0:T(8,128)S(1)} %get-tuple-element.76), channel_id=1, source_target_pairs={{0,16},{16,32},{32,48},{48,64},{64,80},{80,96},{96,112},{112,128},... | collective-permute-start | bytes 122888 | tf_op jit(solution)/shard_map/ppermute | solution.py:682
  98.2 4.0 %collective-permute-start.13 = (f32[80,128]{1,0:T(8,128)S(1)}, f32[80,128]{1,0:T(8,128)S(1)}, u32[]{:S(2)}, u32[]{:S(2)}) collective-permute-start(f32[80,128]{1,0:T(8,128)S(1)} %get-tuple-element.77), channel_id=1, source_target_pairs={{16,0},{32,16},{48,32},{64,48},{80,64},{96,80},{112,96},{128,112},... | collective-permute-start | bytes 122888 | tf_op jit(solution)/shard_map/ppermute | solution.py:682
  104.8 5.1 %copy-start = (f32[4,1536,128]{2,1,0:T(8,128)}, f32[4,1536,128]{2,1,0:T(8,128)S(1)}, u32[]{:S(2)}) copy-start(f32[4,1536,128]{2,1,0:T(8,128)S(1)} %get-tuple-element.79.t_ref) | copy-start | bytes 9437188
  104.8 4.5 %collective-permute-start.14 = (f32[64,128]{1,0:T(8,128)S(1)}, f32[64,128]{1,0:T(8,128)S(1)}, u32[]{:S(2)}, u32[]{:S(2)}) collective-permute-start(f32[64,128]{1,0:T(8,128)S(1)} %get-tuple-element.80), channel_id=1, source_target_pairs={{0,16},{16,32},{32,48},{48,64},{64,80},{80,96},{96,112},{112,128},... | collective-permute-start | bytes 98312 | tf_op jit(solution)/shard_map/ppermute | solution.py:682
  104.8 4.6 %collective-permute-start.15 = (f32[64,128]{1,0:T(8,128)S(1)}, f32[64,128]{1,0:T(8,128)S(1)}, u32[]{:S(2)}, u32[]{:S(2)}) collective-permute-start(f32[64,128]{1,0:T(8,128)S(1)} %get-tuple-element.81), channel_id=1, source_target_pairs={{16,0},{32,16},{48,32},{64,48},{80,64},{96,80},{112,96},{128,112},... | collective-permute-start | bytes 98312 | tf_op jit(solution)/shard_map/ppermute | solution.py:682
  109.9 6.4 %collective-permute-start.17 = (f32[8,128]{1,0:T(8,128)S(1)}, f32[8,128]{1,0:T(8,128)S(1)}, u32[]{:S(2)}, u32[]{:S(2)}) collective-permute-start(f32[8,128]{1,0:T(8,128)S(1)} %shard_map.144), channel_id=1, source_target_pairs={{16,0},{49,1},{82,2},{115,3},{148,4},{181,5},{214,6},{247,7},{280,... | collective-permute-start | bytes 12296 | tf_op jit(solution)/shard_map/ppermute | solution.py:671
  115.5 0.8 collective-permute-start.16
  116.9 30.8 %all-to-all-start.1 = ((f32[16,8,128]{2,1,0:T(8,128)}), f32[16,8,128]{2,1,0:T(8,128)S(1)}, u32[]{:S(2)}, u32[]{:S(2)}) async-start(f32[16,8,128]{2,1,0:T(8,128)} %broadcast_in_dim.2), calls=%async_computation.1 | async-start | bytes 131072 | tf_op jit(solution)/shard_map/all_to_all | solution.py:656
  141.0 1.9 %copy-start.1 = (f32[4,1536,128]{2,1,0:T(8,128)S(1)}, f32[4,1536,128]{2,1,0:T(8,128)}, u32[]{:S(2)}) copy-start(f32[4,1536,128]{2,1,0:T(8,128)} %copy-done) | copy-start | bytes 9437188
  142.9 1.7 %copy-start.4 = (bf16[288,4608]{1,0:T(8,128)(2,1)S(1)}, bf16[288,4608]{1,0:T(8,128)(2,1)}, u32[]{:S(2)}) copy-start(bf16[288,4608]{1,0:T(8,128)(2,1)} %constant.20.clone.table_ref) | copy-start | bytes 7962628
  144.6 1.8 %copy-start.9 = (f32[192,192]{1,0:T(8,128)S(1)}, f32[192,192]{1,0:T(8,128)}, u32[]{:S(2)}) copy-start(f32[192,192]{1,0:T(8,128)} %constant.21.clone.table_ref) | copy-start | bytes 442372
  144.6 3.1 %copy-start.7 = (f32[6,6,192]{2,1,0:T(8,128)S(1)}, f32[6,6,192]{2,1,0:T(8,128)}, u32[]{:S(2)}) copy-start(f32[6,6,192]{2,1,0:T(8,128)} %rhs_ref.1) | copy-start | bytes 82948

commit v6 on v5

--- a/solution.py
+++ b/solution.py
@@ -260,7 +260,7 @@
 
 
 def pack_body(*refs):
-    me_ref, sources, (out_ref, own_ref), held, (tmp, common, tiles, ready) = (
+    me_ref, sources, (out_ref, tiles), held, (tmp, common, own_ref, ready) = (
         refs[0], refs[1:10], refs[10:12], refs[12:21], refs[21:]
     )
     copies = [pltpu.make_async_copy(sources[n], held[n], ready.at[n]) for n in range(9)]
@@ -311,35 +311,38 @@
 
 def unpack_body(
     me_ref, all_ref, own_ref,
-    dense_ref, rhs_ref, helm_ref, vec_ref, small_ref, box_ref, state_ref, ahead_ref, behind_ref, near,
+    dense_ref, rhs_ref, small_ref, box_ref, state_ref, ahead_ref, behind_ref, half_matrix,
 ):
     mine_b = me_ref[0]
     mine_c = me_ref[1]
+    own_at = pl.multiple_of((mine_b * 4 + mine_c) * 32, 32)
     for t in range(4):
-        near[t, 0:32, :] = own_ref[t]
+        half_matrix[t, pl.ds(own_at, 32), :] = own_ref[t]
+    block = lanes((32, 128)) // EA
     for r in range(1, 16):
         other = ((mine_b ^ (r >> 2)) << 2) | (mine_c ^ (r & 3))
         halves = [all_ref[other, half * 32 : half * 32 + 32, :] for half in range(2)]
+        at = pl.multiple_of(other * 32, 32)
         for tile in range(4):
-            pieces = []
+            total = jnp.zeros((32, 128), F32)
             for q in range(4):
                 t = r ^ (tile * 4 + q)
                 if t in BLOCKS[r]:
                     slot = BLOCKS[r].index(t)
-                    pieces.append((halves[slot // 4], slot % 4, q))
-            near[tile, r * 32 : r * 32 + 32, :] = place_blocks(pieces) if pieces else jnp.zeros((32, 128), F32)
+                    target = mine_c ^ q
+                    moved = pltpu.roll(halves[slot // 4], ((target - slot) & 3) * 32, 1)
+                    total = jnp.where(block == target, moved, total)
+            half_matrix[mine_b ^ tile, pl.ds(at, 32), :] = total
     row_block = lax.broadcasted_iota(jnp.int32, (128, 128), 0) // 32
     for tile in range(4):
         for row_tile in range(4):
-            mirrored = near[row_tile, tile * 128 : (tile + 1) * 128, :].T
+            mirrored = half_matrix[row_tile, tile * 128 : (tile + 1) * 128, :].T
             if tile == row_tile:
                 mirrored = jnp.where(row_block == lanes((128, 128)) // EA, 0.0, mirrored)
-            value = near[tile, row_tile * 128 : (row_tile + 1) * 128, :] + mirrored
-            value = flip_blocks(value, mine_c)
-            for q in range(4):
-                start = pl.multiple_of((mine_b ^ row_tile) * 128 + (mine_c ^ q) * 32, 32)
-                dense_ref[mine_b ^ tile, pl.ds(start, 32), :] = value[q * 32 : (q + 1) * 32, :]
+            rows = slice(row_tile * 128, (row_tile + 1) * 128)
+            dense_ref[tile, rows, :] = half_matrix[tile, rows, :] + mirrored
     rhs_ref[...] = jnp.zeros(rhs_ref.shape, F32)
+    helm_first, helm_last = [], []
     for b in range(NB):
         column = [all_ref.at[b * 4 + c] for c in range(4)]
         for k in range(6):
@@ -347,16 +350,22 @@
             for i in range(6):
                 rhs_ref[b, k * 48 + i * 8 + 1 : k * 48 + i * 8 + 7, :] = value[i * 6 : i * 6 + 6, :]
         small_ref[b, :, :] = joined(column, 104, 40, 2)
+        helm_first.append(joined(column, 184, 64, 0))
+        helm_last.append(joined(column, 248, 64, 3))
+    begin_kernel_part(
+        rhs_ref, small_ref, dense_ref, box_ref, state_ref, ahead_ref, behind_ref, (helm_last, helm_first)
+    )
+
+
+def unpack_rest_body(all_ref, helm_ref, vec_ref):
+    for b in range(NB):
+        column = [all_ref.at[b * 4 + c] for c in range(4)]
         vec_ref[b, 0:40, :] = joined(column, 104, 40, 3)
         for t in range(4):
             rows = 40 if t < 3 else 32
             vec_ref[b, 40 + t * 40 : 40 + t * 40 + rows, :] = joined(column, 144, rows, t)
         for k in range(8):
             helm_ref[b, k * 64 : (k + 1) * 64, :] = joined(column, 184 + 64 * (k // 4), 64, k % 4)
-    begin_kernel_part(
-        rhs_ref, small_ref, dense_ref, box_ref, state_ref, ahead_ref, behind_ref,
-        ([helm_ref[b, 448:512, :] for b in range(NB)], [helm_ref[b, 0:64, :] for b in range(NB)]),
-    )
 
 
 def middle_body(dense_ref, state_ref, left_ref, right_ref, state_out, message_out):
@@ -656,23 +665,6 @@
     return lax.all_to_all(jnp.broadcast_to(block[None], (count,) + block.shape), axes, 0, 0)
 
 
-def sum_slabs(sums):
-    slabs, across, around = (lax.axis_size(axis) for axis in ("gx", "gy", "col"))
-    group = across * around
-    chips = slabs // 2
-    assert chips == group
-    total = None
-    for core in range(2):
-        pairs = []
-        for slab in range(slabs):
-            for n in range(group):
-                source = (slab // 2 + n) % chips * 2 + (slab + core) % 2
-                pairs.append((source * group + n, slab * group + n))
-        part = lax.ppermute(sums, ("gx", "gy", "col"), pairs)
-        total = part if total is None else total + part
-    return tell_all(total, ("gy", "col"), group)
-
-
 def local(divergence, elem_size, helm_diag, fdm_vectors, fdm_values, coarse_rows, axial_link):
     count = lax.axis_size("gx")
     ahead = [(i, (i + 1) % count) for i in range(count)]
@@ -714,16 +706,17 @@
             pltpu.VMEM((4, 32, 128), F32),
             pltpu.SemaphoreType.DMA((9,)),
         ],
-        compiler_params=pltpu.CompilerParams(vmem_limit_bytes=40 * 1024 * 1024),
+        compiler_params=pltpu.CompilerParams(vmem_limit_bytes=60 * 1024 * 1024),
     )(me, *arguments)
     everything = lax.all_to_all(own_part, ("gy", "col"), 0, 0)
 
-    dense, rhs, helm, vectors, small, boxes, state, up, down = call(
+    dense, rhs, small, boxes, state, up, down = call(
         unpack_body,
-        [(4, 512, 128), field, velocity, (NB, 192, 128), (NB, 40, 128), velocity, state_shape, wide, wide],
+        [(4, 512, 128), field, (NB, 40, 128), velocity, state_shape, wide, wide],
         [pltpu.VMEM((4, 512, 128), F32)],
         scalars=1,
     )(me, everything, own_rows)
+    helm, vectors = call(unpack_rest_body, [velocity, (NB, 192, 128)])(everything)
 
     def precondition(boxes, state, left, right):
         state, message = call(middle_body, [state_shape, state_shape])(dense, state, left, right)
@@ -745,6 +738,7 @@
 
     spread = [pltpu.VMEM((3072, 512), BF16)]
     left, right = exchange(up, down)
+    left, right, helm, vectors = lax.optimization_barrier((left, right, helm, vectors))
     (inverse,) = call(helm_body, [velocity])(helm, left, right)
     z, t, left, right = precondition(boxes, state, left, right)
     w, boxes, state, up, down = call(
@@ -754,7 +748,7 @@
     q, t, left, right = precondition(boxes, state, left, right)
     (products,) = call(products_body, [(8, 128)])(rhs, z, w, q)
     (sums,) = call(energy_body, [(8, 128)])(t, left, right, inverse, products)
-    sums = sum_slabs(sums)
+    sums = tell_all(sums, "gx", count)
     (v,) = call(last_image_body, [field], spread)(t, left, right, inverse, small, backward)
     own = call(own_body, [(6, 6, 192)] * 4, scalars=1)(me, z, w, q, v, six.T.copy())
     return tuple(

time: 149 us -> 137 us (0.919)
  starting transfers between devices: 60.1 us -> 46.7 us
  waiting for transfers between devices: 7.24 us -> 15 us
  local copies, waits for them, and re-layouts: 10.9 us -> 4.31 us
    all_to_all x1, waiting for transfers between devices: 0.01 us -> 9.12 us  [tell_all(): lax.all_to_all(jnp.broadcast_to(block[None], (count,) + block.shape), axe...]
    all_to_all x1, starting transfers between devices: 24 us -> 15.1 us  [tell_all(): lax.all_to_all(jnp.broadcast_to(block[None], (count,) + block.shape), axe...]
    unnamed x30 -> x18, local copies, waits for them, and re-layouts: 10.3 us -> 3.66 us
    ppermute x2 -> x0, starting transfers between devices: 6.26 us -> none  [sum_slabs(): part = lax.ppermute(sums, ('gx', 'gy', 'col'), pairs)]
    pallas_call x1, Pallas kernels: 1.91 us -> 4.14 us  [local(): pl.pallas_call(pack_body, out_shape=[jax.ShapeDtypeStruct((16, ROWS, 128)...]
    ppermute x16, starting transfers between devices: 29.9 us -> 31.6 us  [exchange(): return (lax.ppermute(up, 'gx', ahead), lax.ppermute(down, 'gx', behind))]
    pallas_call x15 -> x16, Pallas kernels: 27.3 us -> 26 us  [run(): pl.pallas_call(body, out_shape=[jax.ShapeDtypeStruct(shape, F32) for shap...]
  transfers between devices with their start and end apart: 19 -> 17, of which waited for: 13 -> 12; matrix products, arithmetic and copies ran while one was open for 0% -> 0% of each run, Pallas kernels for 8% -> 9%
where the time goes in v6:
time: 137 us; the launch traced here: 136 us
  starting transfers between devices  46.7 us (34%)
  blocking collectives  37.2 us (27%)
  Pallas kernels  30.9 us (23%)
  waiting for transfers between devices  15 us (11%)
  local copies, waits for them, and re-layouts  4.31 us (3%)
  between operations  1.67 us (1%)
    all_to_all x1, blocking collectives, local(): everything = lax.all_to_all(own_part, ('gy', 'col'), 0, 0)  37.2 us
    ppermute x16, starting transfers between devices, exchange(): return (lax.ppermute(up, 'gx', ahead), lax.ppermute(down, 'gx', behind))  31.6 us
    pallas_call x16, Pallas kernels, run(): pl.pallas_call(body, out_shape=[jax.ShapeDtypeStruct(shape, F32) for shap...  26 us
    all_to_all x1, starting transfers between devices, tell_all(): lax.all_to_all(jnp.broadcast_to(block[None], (count,) + block.shape), axe...  15.1 us
    all_to_all x1, waiting for transfers between devices, tell_all(): lax.all_to_all(jnp.broadcast_to(block[None], (count,) + block.shape), axe...  9.12 us
    ppermute x16, waiting for transfers between devices, exchange(): return (lax.ppermute(up, 'gx', ahead), lax.ppermute(down, 'gx', behind))  5.9 us
    pallas_call x1, Pallas kernels, local(): pl.pallas_call(pack_body, out_shape=[jax.ShapeDtypeStruct((16, ROWS, 128)...  4.14 us
    unnamed x18, local copies, waits for them, and re-layouts  3.66 us
  transfers between devices with their start and end apart: 17, of which 12 were waited for; matrix products, arithmetic and copies ran while one was open for 0% of the time, Pallas kernels for 9%

profile of v6, /device:TPU:1, one launch (start us, length us, event | category | flops | bytes accessed | tf_op | source)
XLA Modules:
  0.0 136.4 jit_solution(9860617872113759364)
XLA Ops:
  1.3 0.6 pad_add_fusion.refs_0_.me_ref
  1.9 4.1 %shard_map.131 = (f32[16,312,128]{2,1,0:T(8,128)}, f32[4,32,128]{2,1,0:T(8,128)}) custom-call(s32[2]{0:T(128)} %pad_add_fusion.refs_0_.me_ref, f32[6,6,192]{2,1,0:T(8,128)} %rhs_ref.1, f32[8,8,256]{2,1,0:T(8,128)} %refs_2_.1, f32[192,32]{1,0:T(8,128)} %bitcast.4, f32[24,32]{1,0:T(8,128)} %bitcast.5, f32[3,32]{1,0:T(4,128)} %refs_5_.1, f32[32,512]{1,0:T(8,128)} %refs_6_.1, ...), custom_call_target="tpu_custom_call" | custom-call | tf_op jit(solution)/shard_map/pallas_call | solution.py:697
  6.0 0.0 copy-start.7
  6.0 37.2 %all_to_all.10.all_ref = f32[16,312,128]{2,1,0:T(8,128)S(1)} all-to-all(f32[16,312,128]{2,1,0:T(8,128)} %get-tuple-element.50), channel_id=1, replica_groups=mesh['gx'=32,'gy'=4,'col'=4] {'gy','col'}, dimensions={0} | all-to-all | bytes 5111808 | tf_op jit(solution)/shard_map/all_to_all | solution.py:711
  43.2 0.0 copy-done.8
  43.2 0.0 copy-done.7
  43.2 2.7 %shard_map.132 = (f32[4,512,128]{2,1,0:T(8,128)S(1)}, f32[4,288,128]{2,1,0:T(8,128)S(1)}, f32[4,40,128]{2,1,0:T(8,128)S(1)}, f32[4,512,128]{2,1,0:T(8,128)S(1)},...) custom-call(s32[2]{0:T(128)S(1)} %copy-done.8, f32[16,312,128]{2,1,0:T(8,128)S(1)} %all_to_all.10.all_ref, ...), custom_call_target="tpu_custom_call" | custom-call | tf_op jit(solution)/shard_map/pallas_call | solution.py:652
  46.0 6.2 %collective-permute-start = (f32[80,128]{1,0:T(8,128)S(1)}, f32[80,128]{1,0:T(8,128)S(1)}, u32[]{:S(2)}, u32[]{:S(2)}) collective-permute-start(f32[80,128]{1,0:T(8,128)S(1)} %get-tuple-element.54), channel_id=1, source_target_pairs={{0,16},{16,32},{32,48},{48,64},{64,80},{80,96},{96,112},{112,128},... | collective-permute-start | bytes 122888 | tf_op jit(solution)/shard_map/ppermute | solution.py:674
  52.2 0.0 collective-permute-start.1
  52.2 1.2 shard_map.133
  53.3 0.0 collective-permute-done.left_ref
  53.3 2.2 %collective-permute-done.1.right_ref = f32[80,128]{1,0:T(8,128)S(1)} collective-permute-done((f32[80,128]{1,0:T(8,128)S(1)}, f32[80,128]{1,0:T(8,128)S(1)}, u32[]{:S(2)}, u32[]{:S(2)}) %collective-permute-start.1) | collective-permute-done | bytes 40992 | tf_op jit(solution)/shard_map/ppermute | solution.py:674
  55.6 0.6 shard_map.134
  56.2 3.8 %collective-permute-start.3 = (f32[16,128]{1,0:T(8,128)S(1)}, f32[16,128]{1,0:T(8,128)S(1)}, u32[]{:S(2)}, u32[]{:S(2)}) collective-permute-start(f32[16,128]{1,0:T(8,128)S(1)} %get-tuple-element.61), channel_id=1, source_target_pairs={{16,0},{32,16},{48,32},{64,48},{80,64},{96,80},{112,96},{128,112},... | collective-permute-start | bytes 24584 | tf_op jit(solution)/shard_map/ppermute | solution.py:674
  60.0 0.0 collective-permute-start.2
  60.0 3.9 %shard_map.135 = (f32[4,288,128]{2,1,0:T(8,128)S(1)}, f32[64,128]{1,0:T(8,128)S(1)}, f32[64,128]{1,0:T(8,128)S(1)}) custom-call(f32[4,512,128]{2,1,0:T(8,128)S(1)} %get-tuple-element.62.box_ref, f32[4,192,128]{2,1,0:T(8,128)S(1)} %get-tuple-element.63.vec_ref, f32[4,40,128]{2,1,0:T(8,128)S(1)} %get-tuple-element.64.small_ref, ...), custom_call_target="tpu_custom_call" | custom-call | tf_op jit(solution)/shard_map/pallas_call | solution.py:652
  63.9 0.0 collective-permute-done.3.right_ref
  63.9 0.0 collective-permute-done.2.left_ref
  63.9 0.6 shard_map.136
  64.6 0.0 collective-permute-start.4
  64.6 3.3 %collective-permute-start.5 = (f32[80,128]{1,0:T(8,128)S(1)}, f32[80,128]{1,0:T(8,128)S(1)}, u32[]{:S(2)}, u32[]{:S(2)}) collective-permute-start(f32[80,128]{1,0:T(8,128)S(1)} %get-tuple-element.69), channel_id=1, source_target_pairs={{16,0},{32,16},{48,32},{64,48},{80,64},{96,80},{112,96},{128,112},... | collective-permute-start | bytes 122888 | tf_op jit(solution)/shard_map/ppermute | solution.py:674
  67.9 0.7 collective-permute-done.4.left_ref
  68.6 0.2 collective-permute-done.5.right_ref
  68.8 0.0 copy-done.2
  68.8 2.6 %shard_map.137 = (f32[4,288,128]{2,1,0:T(8,128)S(1)}, f32[4,1536,128]{2,1,0:T(8,128)S(1)}, f32[64,128]{1,0:T(8,128)S(1)}, f32[64,128]{1,0:T(8,128)S(1)}) custom-call(f32[4,512,128]{2,1,0:T(8,128)S(1)} %get-tuple-element.52.dense_ref, f32[16,128]{1,0:T(8,128)S(1)} %get-tuple-element.67.state_ref, f32[80,128]{1,0:T(8,128)S(1)} %collective-permute-done.4.left_ref, ...), custom_call_target="tpu_custom_call" | custom-call | tf_op jit(solution)/shard_map/pallas_call | solution.py:652
  71.4 0.0 collective-permute-start.6
  71.4 3.8 %collective-permute-start.7 = (f32[64,128]{1,0:T(8,128)S(1)}, f32[64,128]{1,0:T(8,128)S(1)}, u32[]{:S(2)}, u32[]{:S(2)}) collective-permute-start(f32[64,128]{1,0:T(8,128)S(1)} %get-tuple-element.73), channel_id=1, source_target_pairs={{16,0},{32,16},{48,32},{64,48},{80,64},{96,80},{112,96},{128,112},... | collective-permute-start | bytes 98312 | tf_op jit(solution)/shard_map/ppermute | solution.py:674
  75.2 0.4 shard_map.138.inverse_ref
  75.6 0.3 collective-permute-done.6.left_ref
  75.9 0.2 collective-permute-done.7.right_ref
  76.0 0.0 copy-done.3
  76.1 2.3 %shard_map.139 = (f32[4,288,128]{2,1,0:T(8,128)S(1)}, f32[4,512,128]{2,1,0:T(8,128)S(1)}, f32[16,128]{1,0:T(8,128)S(1)}, f32[80,128]{1,0:T(8,128)S(1)}, f32[80,128]{1,0:T(8,128)S(1)}) custom-call(f32[4,1536,128]{2,1,0:T(8,128)S(1)} %get-tuple-element.71.t_ref, f32[64,128]{1,0:T(8,128)S(1)} %collective-permute-done.6.left_ref, ...), custom_call_target="tpu_custom_call" | custom-call | tf_op jit(solution)/shard_map/pallas_call | solution.py:652
  78.3 0.0 collective-permute-start.8
  78.4 3.7 %collective-permute-start.9 = (f32[80,128]{1,0:T(8,128)S(1)}, f32[80,128]{1,0:T(8,128)S(1)}, u32[]{:S(2)}, u32[]{:S(2)}) collective-permute-start(f32[80,128]{1,0:T(8,128)S(1)} %get-tuple-element.77), channel_id=1, source_target_pairs={{16,0},{32,16},{48,32},{64,48},{80,64},{96,80},{112,96},{128,112},... | collective-permute-start | bytes 122888 | tf_op jit(solution)/shard_map/ppermute | solution.py:674
  82.1 0.7 collective-permute-done.8.left_ref
  82.8 0.2 collective-permute-done.9.right_ref
  82.9 0.6 shard_map.140
  83.6 3.8 %collective-permute-start.11 = (f32[16,128]{1,0:T(8,128)S(1)}, f32[16,128]{1,0:T(8,128)S(1)}, u32[]{:S(2)}, u32[]{:S(2)}) collective-permute-start(f32[16,128]{1,0:T(8,128)S(1)} %get-tuple-element.79), channel_id=1, source_target_pairs={{16,0},{32,16},{48,32},{64,48},{80,64},{96,80},{112,96},{128,112},... | collective-permute-start | bytes 24584 | tf_op jit(solution)/shard_map/ppermute | solution.py:674
  87.3 0.0 collective-permute-start.10
  87.3 4.1 %shard_map.141 = (f32[4,288,128]{2,1,0:T(8,128)S(1)}, f32[64,128]{1,0:T(8,128)S(1)}, f32[64,128]{1,0:T(8,128)S(1)}) custom-call(f32[4,512,128]{2,1,0:T(8,128)S(1)} %get-tuple-element.80.box_ref, f32[4,192,128]{2,1,0:T(8,128)S(1)} %get-tuple-element.63.vec_ref, f32[4,40,128]{2,1,0:T(8,128)S(1)} %get-tuple-element.64.small_ref, ...), custom_call_target="tpu_custom_call" | custom-call | tf_op jit(solution)/shard_map/pallas_call | solution.py:652
  91.4 0.0 collective-permute-done.11.right_ref
  91.4 0.0 collective-permute-done.10.left_ref
  91.4 0.6 shard_map.142
  92.1 0.0 collective-permute-start.12
  92.1 3.2 %collective-permute-start.13 = (f32[80,128]{1,0:T(8,128)S(1)}, f32[80,128]{1,0:T(8,128)S(1)}, u32[]{:S(2)}, u32[]{:S(2)}) collective-permute-start(f32[80,128]{1,0:T(8,128)S(1)} %get-tuple-element.85), channel_id=1, source_target_pairs={{16,0},{32,16},{48,32},{64,48},{80,64},{96,80},{112,96},{128,112},... | collective-permute-start | bytes 122888 | tf_op jit(solution)/shard_map/ppermute | solution.py:674
  95.3 0.7 collective-permute-done.12.left_ref
  96.0 0.2 collective-permute-done.13.right_ref
  96.1 2.6 %shard_map.143 = (f32[4,288,128]{2,1,0:T(8,128)S(1)}, f32[4,1536,128]{2,1,0:T(8,128)S(1)}, f32[64,128]{1,0:T(8,128)S(1)}, f32[64,128]{1,0:T(8,128)S(1)}) custom-call(f32[4,512,128]{2,1,0:T(8,128)S(1)} %get-tuple-element.52.dense_ref, f32[16,128]{1,0:T(8,128)S(1)} %get-tuple-element.83.state_ref, f32[80,128]{1,0:T(8,128)S(1)} %collective-permute-done.12.left_ref, ...), custom_call_target="tpu_custom_call" | custom-call | tf_op jit(solution)/shard_map/pallas_call | solution.py:652
  98.7 0.0 copy-start
  98.7 0.0 collective-permute-start.14
  98.8 3.8 %collective-permute-start.15 = (f32[64,128]{1,0:T(8,128)S(1)}, f32[64,128]{1,0:T(8,128)S(1)}, u32[]{:S(2)}, u32[]{:S(2)}) collective-permute-start(f32[64,128]{1,0:T(8,128)S(1)} %get-tuple-element.89), channel_id=1, source_target_pairs={{16,0},{32,16},{48,32},{64,48},{80,64},{96,80},{112,96},{128,112},... | collective-permute-start | bytes 98312 | tf_op jit(solution)/shard_map/ppermute | solution.py:674
  102.5 0.3 shard_map.144.products_ref
  102.8 0.4 collective-permute-done.14.left_ref
  103.2 0.2 collective-permute-done.15.right_ref
  103.4 0.4 shard_map.145
  103.8 0.0 copy-done
  103.8 0.7 broadcast_in_dim.2
  104.5 15.1 %all-to-all-start.1 = ((f32[32,8,128]{2,1,0:T(8,128)}), f32[32,8,128]{2,1,0:T(8,128)S(1)}, u32[]{:S(2)}, u32[]{:S(2)}) async-start(f32[32,8,128]{2,1,0:T(8,128)} %broadcast_in_dim.2), calls=%async_computation.1 | async-start | bytes 262144 | tf_op jit(solution)/shard_map/all_to_all | solution.py:665
  119.6 1.9 %copy-done.1 = f32[4,1536,128]{2,1,0:T(8,128)S(1)} copy-done((f32[4,1536,128]{2,1,0:T(8,128)S(1)}, f32[4,1536,128]{2,1,0:T(8,128)}, u32[]{:S(2)}) %copy-start.1) | copy-done | bytes 3145752
  121.5 1.7 %copy-done.4 = bf16[288,4608]{1,0:T(8,128)(2,1)S(1)} copy-done((bf16[288,4608]{1,0:T(8,128)(2,1)S(1)}, bf16[288,4608]{1,0:T(8,128)(2,1)}, u32[]{:S(2)}) %copy-start.4) | copy-done | bytes 2654232
  123.2 1.8 %shard_map.146.v_ref = f32[4,288,128]{2,1,0:T(8,128)S(1)} custom-call(f32[4,1536,128]{2,1,0:T(8,128)S(1)} %copy-done.1, f32[64,128]{1,0:T(8,128)S(1)} %collective-permute-done.14.left_ref, f32[64,128]{1,0:T(8,128)S(1)} %collective-permute-done.15.right_ref, f32[4,512,128]{2,1,0:T(8,128)S(1)} %shard_map.138.inverse_ref, ...), custom_call_target="tpu_custom_call" | custom-call | tf_op jit(solution)/shard_map/pallas_call | solution.py:652
  125.1 1.2 shard_map.147
  126.3 9.1 %all-to-all-done.1.sums_ref = f32[32,8,128]{2,1,0:T(8,128)S(1)} async-done(((f32[32,8,128]{2,1,0:T(8,128)}), f32[32,8,128]{2,1,0:T(8,128)S(1)}, u32[]{:S(2)}, u32[]{:S(2)}) %all-to-all-start.1) | async-done | bytes 131104 | tf_op jit(solution)/shard_map/all_to_all | solution.py:665
  135.4 0.8 shard_map.148
  (9 shorter events, 0.0 us)
Async XLA Ops:
  1.9 41.4 %copy-start.8 = (s32[2]{0:T(128)S(1)}, s32[2]{0:T(128)}, u32[]{:S(2)}) copy-start(s32[2]{0:T(128)} %pad_add_fusion.refs_0_.me_ref) | copy-start | bytes 28
  6.0 37.2 %copy-start.7 = (f32[4,32,128]{2,1,0:T(8,128)S(1)}, f32[4,32,128]{2,1,0:T(8,128)}, u32[]{:S(2)}) copy-start(f32[4,32,128]{2,1,0:T(8,128)} %get-tuple-element.51.own_ref) | copy-start | bytes 196612
  46.0 7.4 %collective-permute-start = (f32[80,128]{1,0:T(8,128)S(1)}, f32[80,128]{1,0:T(8,128)S(1)}, u32[]{:S(2)}, u32[]{:S(2)}) collective-permute-start(f32[80,128]{1,0:T(8,128)S(1)} %get-tuple-element.54), channel_id=1, source_target_pairs={{0,16},{16,32},{32,48},{48,64},{64,80},{80,96},{96,112},{112,128},... | collective-permute-start | bytes 122888 | tf_op jit(solution)/shard_map/ppermute | solution.py:674
  52.1 16.7 %copy-start.2 = (bf16[1536,864]{1,0:T(8,128)(2,1)S(1)}, bf16[1536,864]{1,0:T(8,128)(2,1)}, u32[]{:S(2)}) copy-start(bf16[1536,864]{1,0:T(8,128)(2,1)} %constant.19.clone.table_ref) | copy-start | bytes 7962628
  52.2 3.4 %collective-permute-start.1 = (f32[80,128]{1,0:T(8,128)S(1)}, f32[80,128]{1,0:T(8,128)S(1)}, u32[]{:S(2)}, u32[]{:S(2)}) collective-permute-start(f32[80,128]{1,0:T(8,128)S(1)} %get-tuple-element.55), channel_id=1, source_target_pairs={{16,0},{32,16},{48,32},{64,48},{80,64},{96,80},{112,96},{128,112},... | collective-permute-start | bytes 122888 | tf_op jit(solution)/shard_map/ppermute | solution.py:674
  56.2 7.7 %collective-permute-start.3 = (f32[16,128]{1,0:T(8,128)S(1)}, f32[16,128]{1,0:T(8,128)S(1)}, u32[]{:S(2)}, u32[]{:S(2)}) collective-permute-start(f32[16,128]{1,0:T(8,128)S(1)} %get-tuple-element.61), channel_id=1, source_target_pairs={{16,0},{32,16},{48,32},{64,48},{80,64},{96,80},{112,96},{128,112},... | collective-permute-start | bytes 24584 | tf_op jit(solution)/shard_map/ppermute | solution.py:674
  60.0 3.9 %collective-permute-start.2 = (f32[16,128]{1,0:T(8,128)S(1)}, f32[16,128]{1,0:T(8,128)S(1)}, u32[]{:S(2)}, u32[]{:S(2)}) collective-permute-start(f32[16,128]{1,0:T(8,128)S(1)} %get-tuple-element.61), channel_id=1, source_target_pairs={{0,16},{16,32},{32,48},{48,64},{64,80},{80,96},{96,112},{112,128},... | collective-permute-start | bytes 24584 | tf_op jit(solution)/shard_map/ppermute | solution.py:674
  64.6 4.1 %collective-permute-start.4 = (f32[80,128]{1,0:T(8,128)S(1)}, f32[80,128]{1,0:T(8,128)S(1)}, u32[]{:S(2)}, u32[]{:S(2)}) collective-permute-start(f32[80,128]{1,0:T(8,128)S(1)} %get-tuple-element.68), channel_id=1, source_target_pairs={{0,16},{16,32},{32,48},{48,64},{64,80},{80,96},{96,112},{112,128},... | collective-permute-start | bytes 122888 | tf_op jit(solution)/shard_map/ppermute | solution.py:674
  64.6 4.2 %collective-permute-start.5 = (f32[80,128]{1,0:T(8,128)S(1)}, f32[80,128]{1,0:T(8,128)S(1)}, u32[]{:S(2)}, u32[]{:S(2)}) collective-permute-start(f32[80,128]{1,0:T(8,128)S(1)} %get-tuple-element.69), channel_id=1, source_target_pairs={{16,0},{32,16},{48,32},{64,48},{80,64},{96,80},{112,96},{128,112},... | collective-permute-start | bytes 122888 | tf_op jit(solution)/shard_map/ppermute | solution.py:674
  68.8 7.2 %copy-start.3 = (bf16[288,4608]{1,0:T(8,128)(2,1)S(1)}, bf16[288,4608]{1,0:T(8,128)(2,1)}, u32[]{:S(2)}) copy-start(bf16[288,4608]{1,0:T(8,128)(2,1)} %constant.20.clone.table_ref) | copy-start | bytes 7962628
  71.4 4.5 %collective-permute-start.6 = (f32[64,128]{1,0:T(8,128)S(1)}, f32[64,128]{1,0:T(8,128)S(1)}, u32[]{:S(2)}, u32[]{:S(2)}) collective-permute-start(f32[64,128]{1,0:T(8,128)S(1)} %get-tuple-element.72), channel_id=1, source_target_pairs={{0,16},{16,32},{32,48},{48,64},{64,80},{80,96},{96,112},{112,128},... | collective-permute-start | bytes 98312 | tf_op jit(solution)/shard_map/ppermute | solution.py:674
  71.4 4.6 %collective-permute-start.7 = (f32[64,128]{1,0:T(8,128)S(1)}, f32[64,128]{1,0:T(8,128)S(1)}, u32[]{:S(2)}, u32[]{:S(2)}) collective-permute-start(f32[64,128]{1,0:T(8,128)S(1)} %get-tuple-element.73), channel_id=1, source_target_pairs={{16,0},{32,16},{48,32},{64,48},{80,64},{96,80},{112,96},{128,112},... | collective-permute-start | bytes 98312 | tf_op jit(solution)/shard_map/ppermute | solution.py:674
  78.3 4.4 %collective-permute-start.8 = (f32[80,128]{1,0:T(8,128)S(1)}, f32[80,128]{1,0:T(8,128)S(1)}, u32[]{:S(2)}, u32[]{:S(2)}) collective-permute-start(f32[80,128]{1,0:T(8,128)S(1)} %get-tuple-element.76), channel_id=1, source_target_pairs={{0,16},{16,32},{32,48},{48,64},{64,80},{80,96},{96,112},{112,128},... | collective-permute-start | bytes 122888 | tf_op jit(solution)/shard_map/ppermute | solution.py:674
  78.4 4.6 %collective-permute-start.9 = (f32[80,128]{1,0:T(8,128)S(1)}, f32[80,128]{1,0:T(8,128)S(1)}, u32[]{:S(2)}, u32[]{:S(2)}) collective-permute-start(f32[80,128]{1,0:T(8,128)S(1)} %get-tuple-element.77), channel_id=1, source_target_pairs={{16,0},{32,16},{48,32},{64,48},{80,64},{96,80},{112,96},{128,112},... | collective-permute-start | bytes 122888 | tf_op jit(solution)/shard_map/ppermute | solution.py:674
  83.6 7.8 %collective-permute-start.11 = (f32[16,128]{1,0:T(8,128)S(1)}, f32[16,128]{1,0:T(8,128)S(1)}, u32[]{:S(2)}, u32[]{:S(2)}) collective-permute-start(f32[16,128]{1,0:T(8,128)S(1)} %get-tuple-element.79), channel_id=1, source_target_pairs={{16,0},{32,16},{48,32},{64,48},{80,64},{96,80},{112,96},{128,112},... | collective-permute-start | bytes 24584 | tf_op jit(solution)/shard_map/ppermute | solution.py:674
  87.3 4.1 %collective-permute-start.10 = (f32[16,128]{1,0:T(8,128)S(1)}, f32[16,128]{1,0:T(8,128)S(1)}, u32[]{:S(2)}, u32[]{:S(2)}) collective-permute-start(f32[16,128]{1,0:T(8,128)S(1)} %get-tuple-element.79), channel_id=1, source_target_pairs={{0,16},{16,32},{32,48},{48,64},{64,80},{80,96},{96,112},{112,128},... | collective-permute-start | bytes 24584 | tf_op jit(solution)/shard_map/ppermute | solution.py:674
  92.1 3.9 %collective-permute-start.12 = (f32[80,128]{1,0:T(8,128)S(1)}, f32[80,128]{1,0:T(8,128)S(1)}, u32[]{:S(2)}, u32[]{:S(2)}) collective-permute-start(f32[80,128]{1,0:T(8,128)S(1)} %get-tuple-element.84), channel_id=1, source_target_pairs={{0,16},{16,32},{32,48},{48,64},{64,80},{80,96},{96,112},{112,128},... | collective-permute-start | bytes 122888 | tf_op jit(solution)/shard_map/ppermute | solution.py:674
  92.1 4.0 %collective-permute-start.13 = (f32[80,128]{1,0:T(8,128)S(1)}, f32[80,128]{1,0:T(8,128)S(1)}, u32[]{:S(2)}, u32[]{:S(2)}) collective-permute-start(f32[80,128]{1,0:T(8,128)S(1)} %get-tuple-element.85), channel_id=1, source_target_pairs={{16,0},{32,16},{48,32},{64,48},{80,64},{96,80},{112,96},{128,112},... | collective-permute-start | bytes 122888 | tf_op jit(solution)/shard_map/ppermute | solution.py:674
  98.7 5.1 %copy-start = (f32[4,1536,128]{2,1,0:T(8,128)}, f32[4,1536,128]{2,1,0:T(8,128)S(1)}, u32[]{:S(2)}) copy-start(f32[4,1536,128]{2,1,0:T(8,128)S(1)} %get-tuple-element.87.t_ref) | copy-start | bytes 9437188
  98.7 4.5 %collective-permute-start.14 = (f32[64,128]{1,0:T(8,128)S(1)}, f32[64,128]{1,0:T(8,128)S(1)}, u32[]{:S(2)}, u32[]{:S(2)}) collective-permute-start(f32[64,128]{1,0:T(8,128)S(1)} %get-tuple-element.88), channel_id=1, source_target_pairs={{0,16},{16,32},{32,48},{48,64},{64,80},{80,96},{96,112},{112,128},... | collective-permute-start | bytes 98312 | tf_op jit(solution)/shard_map/ppermute | solution.py:674
  98.8 4.6 %collective-permute-start.15 = (f32[64,128]{1,0:T(8,128)S(1)}, f32[64,128]{1,0:T(8,128)S(1)}, u32[]{:S(2)}, u32[]{:S(2)}) collective-permute-start(f32[64,128]{1,0:T(8,128)S(1)} %get-tuple-element.89), channel_id=1, source_target_pairs={{16,0},{32,16},{48,32},{64,48},{80,64},{96,80},{112,96},{128,112},... | collective-permute-start | bytes 98312 | tf_op jit(solution)/shard_map/ppermute | solution.py:674
  104.5 31.0 %all-to-all-start.1 = ((f32[32,8,128]{2,1,0:T(8,128)}), f32[32,8,128]{2,1,0:T(8,128)S(1)}, u32[]{:S(2)}, u32[]{:S(2)}) async-start(f32[32,8,128]{2,1,0:T(8,128)} %broadcast_in_dim.2), calls=%async_computation.1 | async-start | bytes 262144 | tf_op jit(solution)/shard_map/all_to_all | solution.py:665
  119.6 1.9 %copy-start.1 = (f32[4,1536,128]{2,1,0:T(8,128)S(1)}, f32[4,1536,128]{2,1,0:T(8,128)}, u32[]{:S(2)}) copy-start(f32[4,1536,128]{2,1,0:T(8,128)} %copy-done) | copy-start | bytes 9437188
  121.5 1.7 %copy-start.4 = (bf16[288,4608]{1,0:T(8,128)(2,1)S(1)}, bf16[288,4608]{1,0:T(8,128)(2,1)}, u32[]{:S(2)}) copy-start(bf16[288,4608]{1,0:T(8,128)(2,1)} %constant.20.clone.table_ref) | copy-start | bytes 7962628
  123.2 1.8 %copy-start.6 = (f32[192,192]{1,0:T(8,128)S(1)}, f32[192,192]{1,0:T(8,128)}, u32[]{:S(2)}) copy-start(f32[192,192]{1,0:T(8,128)} %constant.21.clone.table_ref) | copy-start | bytes 442372
  123.2 12.2 %copy-start.5 = (f32[6,6,192]{2,1,0:T(8,128)S(1)}, f32[6,6,192]{2,1,0:T(8,128)}, u32[]{:S(2)}) copy-start(f32[6,6,192]{2,1,0:T(8,128)} %rhs_ref.1) | copy-start | bytes 82948

commit v7 on v6

--- a/solution.py
+++ b/solution.py
@@ -260,7 +260,7 @@
 
 
 def pack_body(*refs):
-    me_ref, sources, (out_ref, tiles), held, (tmp, common, own_ref, ready) = (
+    me_ref, sources, (out_ref, tiles), held, (tmp, common, chosen_blocks, own_ref, ready) = (
         refs[0], refs[1:10], refs[10:12], refs[12:21], refs[21:]
     )
     copies = [pltpu.make_async_copy(sources[n], held[n], ready.at[n]) for n in range(9)]
@@ -295,14 +295,23 @@
     )
     common[120:184, :] = helm[:, 0:128]
     common[184:248, :] = helm[:, 128:256]
+    sends = [pltpu.make_async_copy(common, out_ref.at[n, 64:312], ready.at[9 + n]) for n in range(16)]
+    sends += [
+        pltpu.make_async_copy(chosen_blocks.at[n], out_ref.at[n, 0:64], ready.at[25 + n]) for n in range(16)
+    ]
+    for send in sends[:16]:
+        send.start()
     for r in range(16):
         other = ((mine_b ^ (r >> 2)) << 2) | (mine_c ^ (r & 3))
-        out_ref[other, 64:312, :] = common[...]
         for half in range(2):
             chosen = BLOCKS[r][half * 4 : half * 4 + 4]
-            out_ref[other, half * 32 : half * 32 + 32, :] = place_blocks(
+            chosen_blocks[other, half * 32 : half * 32 + 32, :] = place_blocks(
                 [(own_ref[t >> 2], t & 3, n) for n, t in enumerate(chosen)]
             )
+    for send in sends[16:]:
+        send.start()
+    for send in sends:
+        send.wait()
 
 
 def joined(column, start, rows, quarter):
@@ -414,7 +423,37 @@
         out_ref[b] = 1.0 / out_ref[b]
 
 
-def schwarz_body(box_ref, vec_ref, small_ref, left_ref, right_ref, out_ref, up_ref, down_ref, one, two, full):
+def across_planes(planes, vec_ref, b, mid):
+    for m in range(8):
+        total = None
+        for i in range(8):
+            part = planes[:, i] * vec_ref[b, pl.ds(i * 8 + m, 1), :][None]
+            total = part if total is None else total + part
+        mid[:, m] = total
+    results = []
+    for k in range(planes.shape[0]):
+        total = None
+        for j in range(8):
+            part = mid[k, :, j : j + 1, :] * vec_ref[b, 64 + j * 8 : 72 + j * 8, :][None]
+            total = part if total is None else total + part
+        results.append(total)
+    return results
+
+
+def schwarz_front_body(box_ref, vec_ref, out_ref, mid):
+    def element_row(b, carry):
+        results = across_planes(box_ref[b, 64:448, :].reshape(6, 8, 8, 128), vec_ref, b, mid)
+        for k in range(6):
+            out_ref[b, k * 64 : (k + 1) * 64, :] = results[k].reshape(64, 128)
+        return carry
+
+    lax.fori_loop(0, NB, element_row, 0)
+
+
+def schwarz_body(
+    box_ref, front_ref, vec_ref, small_ref, left_ref, right_ref, out_ref, up_ref, down_ref,
+    one, two, full, ends, mid,
+):
     def element_row(b, carry):
         def row(side, first, second):
             return vec_ref[b, pl.ds(side * 64 + first * 8 + second, 1), :]
@@ -424,47 +463,36 @@
         place = lanes((64, 128)) % EA
         from_left = pltpu.roll(left_ref[16:80, :], 97 + b, 1)
         from_right = pltpu.roll(right_ref[16:80, :], 31 - b, 1)
-        one[0] = jnp.where(place == 0, from_left, last).reshape(8, 8, 128)
-        one[7] = jnp.where(place == EA - 1, from_right, first).reshape(8, 8, 128)
-        one[1:7] = box_ref[b, 64:448, :].reshape(6, 8, 8, 128)
-        for m in range(8):
-            total = None
-            for i in range(8):
-                part = one[:, i] * row(0, i, m)[None]
-                total = part if total is None else total + part
-            two[:, m] = total
+        ends[0] = jnp.where(place == 0, from_left, last).reshape(8, 8, 128)
+        ends[1] = jnp.where(place == EA - 1, from_right, first).reshape(8, 8, 128)
+        two[0], two[7] = across_planes(ends, vec_ref, b, mid)
+        two[1:7] = front_ref[b].reshape(6, 8, 8, 128)
         for m in range(8):
             total = None
             for i in range(8):
                 part = two[i] * row(2, i, m)[None]
                 total = part if total is None else total + part
-            one[m] = total
-        for k in range(8):
-            total = None
-            for j in range(8):
-                part = one[k, :, j : j + 1, :] * vec_ref[b, 64 + j * 8 : 72 + j * 8, :][None]
-                total = part if total is None else total + part
             bottom = small_ref[b, 0:8, :][:, None, :] + small_ref[b, 8:16, :][None, :, :]
-            two[k] = total / (bottom + small_ref[b, 16 + k : 17 + k, :][None])
+            one[m] = total / (bottom + small_ref[b, pl.ds(16 + m, 1), :][None])
         for k in range(8):
             total = None
             for n in range(8):
-                part = two[k, :, n : n + 1, :] * vec_ref[b, pl.ds(64 + n, 8, stride=8), :][None]
+                part = one[k, :, n : n + 1, :] * vec_ref[b, pl.ds(64 + n, 8, stride=8), :][None]
                 total = part if total is None else total + part
-            one[k] = total
+            two[k] = total
         for i in range(8):
             total = None
             for m in range(8):
-                part = one[m] * row(2, i, m)[None]
+                part = two[m] * row(2, i, m)[None]
                 total = part if total is None else total + part
-            two[i] = total
+            one[i] = total
         for i in range(8):
             total = None
             for m in range(8):
-                part = two[:, m] * row(0, i, m)[None]
+                part = one[:, m] * row(0, i, m)[None]
                 total = part if total is None else total + part
-            one[:, i] = total
-        full[b] = one[...].reshape(512, 128)
+            two[:, i] = total
+        full[b] = two[...].reshape(512, 128)
         return carry
 
     lax.fori_loop(0, NB, element_row, 0)
@@ -607,8 +635,10 @@
             if k in (0, 7):
                 part = part * 0.5
             total = part if total is None else total + part
-    sums_ref[...] = products_ref[...]
-    sums_ref[4:5, :] = jnp.sum(total, axis=0, keepdims=True)
+    row = lax.broadcasted_iota(jnp.int32, (8, 128), 0)
+    sums = jnp.where(row == 4, jnp.sum(total, axis=0, keepdims=True), products_ref[...])
+    for n in range(sums_ref.shape[0]):
+        sums_ref[n] = sums
 
 
 def own_body(me_ref, z_ref, w_ref, q_ref, v_ref, table_ref, z_out, w_out, q_out, v_out):
@@ -661,10 +691,6 @@
     return run
 
 
-def tell_all(block, axes, count):
-    return lax.all_to_all(jnp.broadcast_to(block[None], (count,) + block.shape), axes, 0, 0)
-
-
 def local(divergence, elem_size, helm_diag, fdm_vectors, fdm_values, coarse_rows, axial_link):
     count = lax.axis_size("gx")
     ahead = [(i, (i + 1) % count) for i in range(count)]
@@ -698,13 +724,14 @@
         pack_body,
         out_shape=[jax.ShapeDtypeStruct((16, ROWS, 128), F32), jax.ShapeDtypeStruct((4, 32, 128), F32)],
         in_specs=[pl.BlockSpec(memory_space=pltpu.SMEM)] + [pl.BlockSpec(memory_space=pl.ANY)] * 9,
-        out_specs=[vmem, vmem],
+        out_specs=[pl.BlockSpec(memory_space=pl.ANY), vmem],
         scratch_shapes=[pltpu.VMEM(value.shape, F32) for value in arguments]
         + [
             pltpu.VMEM((40, 192), F32),
             pltpu.VMEM((248, 128), F32),
+            pltpu.VMEM((16, 64, 128), F32),
             pltpu.VMEM((4, 32, 128), F32),
-            pltpu.SemaphoreType.DMA((9,)),
+            pltpu.SemaphoreType.DMA((41,)),
         ],
         compiler_params=pltpu.CompilerParams(vmem_limit_bytes=60 * 1024 * 1024),
     )(me, *arguments)
@@ -718,14 +745,23 @@
     )(me, everything, own_rows)
     helm, vectors = call(unpack_rest_body, [velocity, (NB, 192, 128)])(everything)
 
-    def precondition(boxes, state, left, right):
+    def schwarz_front(boxes):
+        return call(schwarz_front_body, [(NB, 384, 128)], [pltpu.VMEM((6, 8, 8, 128), F32)])(boxes, vectors)[0]
+
+    def precondition(boxes, state, left, right, front):
         state, message = call(middle_body, [state_shape, state_shape])(dense, state, left, right)
         left_mid, right_mid = exchange(message, message)
         part, up, down = call(
             schwarz_body,
             [field, plane, plane],
-            [pltpu.VMEM((8, 8, 8, 128), F32), pltpu.VMEM((8, 8, 8, 128), F32), pltpu.VMEM(velocity, F32)],
-        )(boxes, vectors, small, left, right)
+            [
+                pltpu.VMEM((8, 8, 8, 128), F32),
+                pltpu.VMEM((8, 8, 8, 128), F32),
+                pltpu.VMEM(velocity, F32),
+                pltpu.VMEM((2, 8, 8, 128), F32),
+                pltpu.VMEM((2, 8, 8, 128), F32),
+            ],
+        )(boxes, front, vectors, small, left, right)
         state, up, down = call(late_body, [state_shape, wide, wide])(
             dense, state, left_mid, right_mid, up, down
         )
@@ -738,17 +774,20 @@
 
     spread = [pltpu.VMEM((3072, 512), BF16)]
     left, right = exchange(up, down)
-    left, right, helm, vectors = lax.optimization_barrier((left, right, helm, vectors))
+    front = schwarz_front(boxes)
+    left, right, helm, front = lax.optimization_barrier((left, right, helm, front))
     (inverse,) = call(helm_body, [velocity])(helm, left, right)
-    z, t, left, right = precondition(boxes, state, left, right)
+    z, t, left, right = precondition(boxes, state, left, right, front)
     w, boxes, state, up, down = call(
         first_image_body, [field, velocity, state_shape, wide, wide], spread
     )(t, left, right, inverse, small, backward, dense)
     left, right = exchange(up, down)
-    q, t, left, right = precondition(boxes, state, left, right)
+    front = schwarz_front(boxes)
+    left, right, front = lax.optimization_barrier((left, right, front))
+    q, t, left, right = precondition(boxes, state, left, right, front)
     (products,) = call(products_body, [(8, 128)])(rhs, z, w, q)
-    (sums,) = call(energy_body, [(8, 128)])(t, left, right, inverse, products)
-    sums = tell_all(sums, "gx", count)
+    (sums,) = call(energy_body, [(count, 8, 128)])(t, left, right, inverse, products)
+    sums = lax.all_to_all(sums, "gx", 0, 0)
     (v,) = call(last_image_body, [field], spread)(t, left, right, inverse, small, backward)
     own = call(own_body, [(6, 6, 192)] * 4, scalars=1)(me, z, w, q, v, six.T.copy())
     return tuple(

time: 137 us -> 139 us (1.015)
  Pallas kernels: 30.9 us -> 32.8 us
  waiting for transfers between devices: 15 us -> 13.4 us
    unnamed x18, local copies, waits for them, and re-layouts: 3.66 us -> 5.28 us
    ppermute x16, waiting for transfers between devices: 5.9 us -> 4.29 us  [exchange(): return (lax.ppermute(up, 'gx', ahead), lax.ppermute(down, 'gx', behind))]
    pallas_call x16 -> x18, Pallas kernels: 26 us -> 27.2 us  [run(): pl.pallas_call(body, out_shape=[jax.ShapeDtypeStruct(shape, F32) for shap...]
  transfers between devices with their start and end apart: 17 -> 17, of which waited for: 12 -> 11; matrix products, arithmetic and copies ran while one was open for 0% -> 0% of each run, Pallas kernels for 9% -> 10%
where the time goes in v7:
time: 139 us
  starting transfers between devices  47.7 us (34%)
  blocking collectives  37.2 us (27%)
  Pallas kernels  32.8 us (24%)
  waiting for transfers between devices  13.4 us (10%)
  local copies, waits for them, and re-layouts  5.28 us (4%)
  between operations  1.68 us (1%)
    all_to_all x1, blocking collectives, local(): everything = lax.all_to_all(own_part, ('gy', 'col'), 0, 0)  37.2 us
    ppermute x16, starting transfers between devices, exchange(): return (lax.ppermute(up, 'gx', ahead), lax.ppermute(down, 'gx', behind))  32.6 us
    pallas_call x18, Pallas kernels, run(): pl.pallas_call(body, out_shape=[jax.ShapeDtypeStruct(shape, F32) for shap...  27.2 us
    all_to_all x1, starting transfers between devices, local(): sums = lax.all_to_all(sums, 'gx', 0, 0)  15.1 us
    all_to_all x1, waiting for transfers between devices, local(): sums = lax.all_to_all(sums, 'gx', 0, 0)  9.12 us
    unnamed x18, local copies, waits for them, and re-layouts  5.28 us
    pallas_call x1, Pallas kernels, local(): pl.pallas_call(pack_body, out_shape=[jax.ShapeDtypeStruct((16, ROWS, 128)...  4.79 us
    ppermute x16, waiting for transfers between devices, exchange(): return (lax.ppermute(up, 'gx', ahead), lax.ppermute(down, 'gx', behind))  4.29 us
  transfers between devices with their start and end apart: 17, of which 11 were waited for; matrix products, arithmetic and copies ran while one was open for 0% of the time, Pallas kernels for 10%

profile of v7, /device:TPU:1, one launch (start us, length us, event | category | flops | bytes accessed | tf_op | source)
XLA Modules:
  0.0 138.7 jit_solution(6281725174728055857)
XLA Ops:
  1.3 0.6 pad_add_fusion.refs_0_.me_ref
  1.9 4.8 %shard_map.131 = (f32[16,312,128]{2,1,0:T(8,128)}, f32[4,32,128]{2,1,0:T(8,128)}) custom-call(s32[2]{0:T(128)} %pad_add_fusion.refs_0_.me_ref, f32[6,6,192]{2,1,0:T(8,128)} %rhs_ref.1, f32[8,8,256]{2,1,0:T(8,128)} %refs_2_.1, f32[192,32]{1,0:T(8,128)} %bitcast.4, f32[24,32]{1,0:T(8,128)} %bitcast.5, f32[3,32]{1,0:T(4,128)} %refs_5_.1, f32[32,512]{1,0:T(8,128)} %refs_6_.1, ...), custom_call_target="tpu_custom_call" | custom-call | tf_op jit(solution)/shard_map/pallas_call | solution.py:723
  6.7 0.0 copy-start.7
  6.7 37.2 %all_to_all.10.all_ref = f32[16,312,128]{2,1,0:T(8,128)S(1)} all-to-all(f32[16,312,128]{2,1,0:T(8,128)} %get-tuple-element.53), channel_id=1, replica_groups=mesh['gx'=32,'gy'=4,'col'=4] {'gy','col'}, dimensions={0} | all-to-all | bytes 5111808 | tf_op jit(solution)/shard_map/all_to_all | solution.py:738
  43.9 0.0 copy-done.8
  43.9 0.0 copy-done.7
  43.9 2.7 %shard_map.132 = (f32[4,512,128]{2,1,0:T(8,128)S(1)}, f32[4,288,128]{2,1,0:T(8,128)S(1)}, f32[4,40,128]{2,1,0:T(8,128)S(1)}, f32[4,512,128]{2,1,0:T(8,128)S(1)},...) custom-call(s32[2]{0:T(128)S(1)} %copy-done.8, f32[16,312,128]{2,1,0:T(8,128)S(1)} %all_to_all.10.all_ref, ...), custom_call_target="tpu_custom_call" | custom-call | tf_op jit(solution)/shard_map/pallas_call | solution.py:682
  46.6 6.2 %collective-permute-start = (f32[80,128]{1,0:T(8,128)S(1)}, f32[80,128]{1,0:T(8,128)S(1)}, u32[]{:S(2)}, u32[]{:S(2)}) collective-permute-start(f32[80,128]{1,0:T(8,128)S(1)} %get-tuple-element.57), channel_id=1, source_target_pairs={{0,16},{16,32},{32,48},{48,64},{64,80},{80,96},{96,112},{112,128},... | collective-permute-start | bytes 122888 | tf_op jit(solution)/shard_map/ppermute | solution.py:700
  52.8 0.0 collective-permute-start.1
  52.8 1.2 shard_map.133
  54.0 0.8 shard_map.134.front_ref
  54.8 0.0 copy-start.2
  54.8 0.0 collective-permute-done.left_ref
  54.9 1.4 collective-permute-done.1.right_ref
  56.2 0.6 shard_map.135
  56.9 4.2 %collective-permute-start.3 = (f32[16,128]{1,0:T(8,128)S(1)}, f32[16,128]{1,0:T(8,128)S(1)}, u32[]{:S(2)}, u32[]{:S(2)}) collective-permute-start(f32[16,128]{1,0:T(8,128)S(1)} %get-tuple-element.65), channel_id=1, source_target_pairs={{16,0},{32,16},{48,32},{64,48},{80,64},{96,80},{112,96},{128,112},... | collective-permute-start | bytes 24584 | tf_op jit(solution)/shard_map/ppermute | solution.py:700
  61.0 0.0 collective-permute-start.2
  61.0 3.3 %shard_map.136 = (f32[4,288,128]{2,1,0:T(8,128)S(1)}, f32[64,128]{1,0:T(8,128)S(1)}, f32[64,128]{1,0:T(8,128)S(1)}) custom-call(f32[4,512,128]{2,1,0:T(8,128)S(1)} %get-tuple-element.60.box_ref, f32[4,384,128]{2,1,0:T(8,128)S(1)} %shard_map.134.front_ref, f32[4,192,128]{2,1,0:T(8,128)S(1)} %get-tuple-element.61.vec_ref, ...), custom_call_target="tpu_custom_call" | custom-call | tf_op jit(solution)/shard_map/pallas_call | solution.py:682
  64.4 0.0 collective-permute-done.3.right_ref
  64.4 0.0 collective-permute-done.2.left_ref
  64.4 0.6 shard_map.137
  65.0 0.0 collective-permute-start.4
  65.0 3.5 %collective-permute-start.5 = (f32[80,128]{1,0:T(8,128)S(1)}, f32[80,128]{1,0:T(8,128)S(1)}, u32[]{:S(2)}, u32[]{:S(2)}) collective-permute-start(f32[80,128]{1,0:T(8,128)S(1)} %get-tuple-element.72), channel_id=1, source_target_pairs={{16,0},{32,16},{48,32},{64,48},{80,64},{96,80},{112,96},{128,112},... | collective-permute-start | bytes 122888 | tf_op jit(solution)/shard_map/ppermute | solution.py:700
  68.6 0.7 collective-permute-done.4.left_ref
  69.3 0.2 collective-permute-done.5.right_ref
  69.5 2.6 %shard_map.138 = (f32[4,288,128]{2,1,0:T(8,128)S(1)}, f32[4,1536,128]{2,1,0:T(8,128)S(1)}, f32[64,128]{1,0:T(8,128)S(1)}, f32[64,128]{1,0:T(8,128)S(1)}) custom-call(f32[4,512,128]{2,1,0:T(8,128)S(1)} %get-tuple-element.55.dense_ref, f32[16,128]{1,0:T(8,128)S(1)} %get-tuple-element.70.state_ref, f32[80,128]{1,0:T(8,128)S(1)} %collective-permute-done.4.left_ref, ...), custom_call_target="tpu_custom_call" | custom-call | tf_op jit(solution)/shard_map/pallas_call | solution.py:682
  72.0 0.0 collective-permute-start.6
  72.1 3.8 %collective-permute-start.7 = (f32[64,128]{1,0:T(8,128)S(1)}, f32[64,128]{1,0:T(8,128)S(1)}, u32[]{:S(2)}, u32[]{:S(2)}) collective-permute-start(f32[64,128]{1,0:T(8,128)S(1)} %get-tuple-element.76), channel_id=1, source_target_pairs={{16,0},{32,16},{48,32},{64,48},{80,64},{96,80},{112,96},{128,112},... | collective-permute-start | bytes 98312 | tf_op jit(solution)/shard_map/ppermute | solution.py:700
  75.8 0.4 shard_map.139.inverse_ref
  76.2 0.3 collective-permute-done.6.left_ref
  76.5 0.2 collective-permute-done.7.right_ref
  76.7 2.3 %shard_map.140 = (f32[4,288,128]{2,1,0:T(8,128)S(1)}, f32[4,512,128]{2,1,0:T(8,128)S(1)}, f32[16,128]{1,0:T(8,128)S(1)}, f32[80,128]{1,0:T(8,128)S(1)}, f32[80,128]{1,0:T(8,128)S(1)}) custom-call(f32[4,1536,128]{2,1,0:T(8,128)S(1)} %get-tuple-element.74.t_ref, f32[64,128]{1,0:T(8,128)S(1)} %collective-permute-done.6.left_ref, ...), custom_call_target="tpu_custom_call" | custom-call | tf_op jit(solution)/shard_map/pallas_call | solution.py:682
  79.0 0.0 collective-permute-start.8
  79.0 3.7 %collective-permute-start.9 = (f32[80,128]{1,0:T(8,128)S(1)}, f32[80,128]{1,0:T(8,128)S(1)}, u32[]{:S(2)}, u32[]{:S(2)}) collective-permute-start(f32[80,128]{1,0:T(8,128)S(1)} %get-tuple-element.80), channel_id=1, source_target_pairs={{16,0},{32,16},{48,32},{64,48},{80,64},{96,80},{112,96},{128,112},... | collective-permute-start | bytes 122888 | tf_op jit(solution)/shard_map/ppermute | solution.py:700
  82.7 0.8 shard_map.141.front_ref
  83.6 0.0 collective-permute-done.8.left_ref
  83.6 0.0 collective-permute-done.9.right_ref
  83.6 0.6 shard_map.142
  84.2 3.8 %collective-permute-start.11 = (f32[16,128]{1,0:T(8,128)S(1)}, f32[16,128]{1,0:T(8,128)S(1)}, u32[]{:S(2)}, u32[]{:S(2)}) collective-permute-start(f32[16,128]{1,0:T(8,128)S(1)} %get-tuple-element.85), channel_id=1, source_target_pairs={{16,0},{32,16},{48,32},{64,48},{80,64},{96,80},{112,96},{128,112},... | collective-permute-start | bytes 24584 | tf_op jit(solution)/shard_map/ppermute | solution.py:700
  88.0 0.0 collective-permute-start.10
  88.0 3.5 %shard_map.143 = (f32[4,288,128]{2,1,0:T(8,128)S(1)}, f32[64,128]{1,0:T(8,128)S(1)}, f32[64,128]{1,0:T(8,128)S(1)}) custom-call(f32[4,512,128]{2,1,0:T(8,128)S(1)} %get-tuple-element.81.box_ref, f32[4,384,128]{2,1,0:T(8,128)S(1)} %shard_map.141.front_ref, f32[4,192,128]{2,1,0:T(8,128)S(1)} %get-tuple-element.61.vec_ref, ...), custom_call_target="tpu_custom_call" | custom-call | tf_op jit(solution)/shard_map/pallas_call | solution.py:682
  91.5 0.0 collective-permute-done.11.right_ref
  91.5 0.1 collective-permute-done.10.left_ref
  91.6 0.6 shard_map.144
  92.3 0.0 collective-permute-start.12
  92.3 3.6 %collective-permute-start.13 = (f32[80,128]{1,0:T(8,128)S(1)}, f32[80,128]{1,0:T(8,128)S(1)}, u32[]{:S(2)}, u32[]{:S(2)}) collective-permute-start(f32[80,128]{1,0:T(8,128)S(1)} %get-tuple-element.91), channel_id=1, source_target_pairs={{16,0},{32,16},{48,32},{64,48},{80,64},{96,80},{112,96},{128,112},... | collective-permute-start | bytes 122888 | tf_op jit(solution)/shard_map/ppermute | solution.py:700
  95.9 0.7 collective-permute-done.12.left_ref
  96.6 0.2 collective-permute-done.13.right_ref
  96.8 2.6 %shard_map.145 = (f32[4,288,128]{2,1,0:T(8,128)S(1)}, f32[4,1536,128]{2,1,0:T(8,128)S(1)}, f32[64,128]{1,0:T(8,128)S(1)}, f32[64,128]{1,0:T(8,128)S(1)}) custom-call(f32[4,512,128]{2,1,0:T(8,128)S(1)} %get-tuple-element.55.dense_ref, f32[16,128]{1,0:T(8,128)S(1)} %get-tuple-element.89.state_ref, f32[80,128]{1,0:T(8,128)S(1)} %collective-permute-done.12.left_ref, ...), custom_call_target="tpu_custom_call" | custom-call | tf_op jit(solution)/shard_map/pallas_call | solution.py:682
  99.4 0.0 collective-permute-start.14
  99.4 3.8 %collective-permute-start.15 = (f32[64,128]{1,0:T(8,128)S(1)}, f32[64,128]{1,0:T(8,128)S(1)}, u32[]{:S(2)}, u32[]{:S(2)}) collective-permute-start(f32[64,128]{1,0:T(8,128)S(1)} %get-tuple-element.95), channel_id=1, source_target_pairs={{16,0},{32,16},{48,32},{64,48},{80,64},{96,80},{112,96},{128,112},... | collective-permute-start | bytes 98312 | tf_op jit(solution)/shard_map/ppermute | solution.py:700
  103.2 0.3 shard_map.146.products_ref
  103.5 0.4 collective-permute-done.14.left_ref
  103.8 0.2 collective-permute-done.15.right_ref
  104.0 1.1 shard_map.147
  105.1 1.6 %copy-done = f32[4,1536,128]{2,1,0:T(8,128)} copy-done((f32[4,1536,128]{2,1,0:T(8,128)}, f32[4,1536,128]{2,1,0:T(8,128)S(1)}, u32[]{:S(2)}) %copy-start) | copy-done | bytes 3145752
  106.7 15.1 %all-to-all-start.1 = ((f32[32,8,128]{2,1,0:T(8,128)}), f32[32,8,128]{2,1,0:T(8,128)S(1)}, u32[]{:S(2)}, u32[]{:S(2)}) async-start(f32[32,8,128]{2,1,0:T(8,128)} %shard_map.147), calls=%async_computation.1 | async-start | bytes 262144 | tf_op jit(solution)/shard_map/all_to_all | solution.py:790
  121.8 1.9 %copy-done.1 = f32[4,1536,128]{2,1,0:T(8,128)S(1)} copy-done((f32[4,1536,128]{2,1,0:T(8,128)S(1)}, f32[4,1536,128]{2,1,0:T(8,128)}, u32[]{:S(2)}) %copy-start.1) | copy-done | bytes 3145752
  123.7 1.7 %copy-done.4 = bf16[288,4608]{1,0:T(8,128)(2,1)S(1)} copy-done((bf16[288,4608]{1,0:T(8,128)(2,1)S(1)}, bf16[288,4608]{1,0:T(8,128)(2,1)}, u32[]{:S(2)}) %copy-start.4) | copy-done | bytes 2654232
  125.5 1.8 %shard_map.148.v_ref = f32[4,288,128]{2,1,0:T(8,128)S(1)} custom-call(f32[4,1536,128]{2,1,0:T(8,128)S(1)} %copy-done.1, f32[64,128]{1,0:T(8,128)S(1)} %collective-permute-done.14.left_ref, f32[64,128]{1,0:T(8,128)S(1)} %collective-permute-done.15.right_ref, f32[4,512,128]{2,1,0:T(8,128)S(1)} %shard_map.139.inverse_ref, ...), custom_call_target="tpu_custom_call" | custom-call | tf_op jit(solution)/shard_map/pallas_call | solution.py:682
  127.3 1.2 shard_map.149
  128.6 9.1 %all-to-all-done.1.sums_ref = f32[32,8,128]{2,1,0:T(8,128)S(1)} async-done(((f32[32,8,128]{2,1,0:T(8,128)}), f32[32,8,128]{2,1,0:T(8,128)S(1)}, u32[]{:S(2)}, u32[]{:S(2)}) %all-to-all-start.1) | async-done | bytes 131104 | tf_op jit(solution)/shard_map/all_to_all | solution.py:790
  137.7 0.0 copy-done.5
  137.7 0.8 shard_map.150
  (10 shorter events, 0.0 us)
Async XLA Ops:
  1.9 42.0 %copy-start.8 = (s32[2]{0:T(128)S(1)}, s32[2]{0:T(128)}, u32[]{:S(2)}) copy-start(s32[2]{0:T(128)} %pad_add_fusion.refs_0_.me_ref) | copy-start | bytes 28
  6.7 37.2 %copy-start.7 = (f32[4,32,128]{2,1,0:T(8,128)S(1)}, f32[4,32,128]{2,1,0:T(8,128)}, u32[]{:S(2)}) copy-start(f32[4,32,128]{2,1,0:T(8,128)} %get-tuple-element.54.own_ref) | copy-start | bytes 196612
  46.6 8.2 %collective-permute-start = (f32[80,128]{1,0:T(8,128)S(1)}, f32[80,128]{1,0:T(8,128)S(1)}, u32[]{:S(2)}, u32[]{:S(2)}) collective-permute-start(f32[80,128]{1,0:T(8,128)S(1)} %get-tuple-element.57), channel_id=1, source_target_pairs={{0,16},{16,32},{32,48},{48,64},{64,80},{80,96},{96,112},{112,128},... | collective-permute-start | bytes 122888 | tf_op jit(solution)/shard_map/ppermute | solution.py:700
  52.8 3.4 %collective-permute-start.1 = (f32[80,128]{1,0:T(8,128)S(1)}, f32[80,128]{1,0:T(8,128)S(1)}, u32[]{:S(2)}, u32[]{:S(2)}) collective-permute-start(f32[80,128]{1,0:T(8,128)S(1)} %get-tuple-element.58), channel_id=1, source_target_pairs={{16,0},{32,16},{48,32},{64,48},{80,64},{96,80},{112,96},{128,112},... | collective-permute-start | bytes 122888 | tf_op jit(solution)/shard_map/ppermute | solution.py:700
  54.8 14.6 %copy-start.2 = (bf16[1536,864]{1,0:T(8,128)(2,1)S(1)}, bf16[1536,864]{1,0:T(8,128)(2,1)}, u32[]{:S(2)}) copy-start(bf16[1536,864]{1,0:T(8,128)(2,1)} %constant.19.clone.table_ref) | copy-start | bytes 7962628
  56.9 7.5 %collective-permute-start.3 = (f32[16,128]{1,0:T(8,128)S(1)}, f32[16,128]{1,0:T(8,128)S(1)}, u32[]{:S(2)}, u32[]{:S(2)}) collective-permute-start(f32[16,128]{1,0:T(8,128)S(1)} %get-tuple-element.65), channel_id=1, source_target_pairs={{16,0},{32,16},{48,32},{64,48},{80,64},{96,80},{112,96},{128,112},... | collective-permute-start | bytes 24584 | tf_op jit(solution)/shard_map/ppermute | solution.py:700
  61.0 3.3 %collective-permute-start.2 = (f32[16,128]{1,0:T(8,128)S(1)}, f32[16,128]{1,0:T(8,128)S(1)}, u32[]{:S(2)}, u32[]{:S(2)}) collective-permute-start(f32[16,128]{1,0:T(8,128)S(1)} %get-tuple-element.65), channel_id=1, source_target_pairs={{0,16},{16,32},{32,48},{48,64},{64,80},{80,96},{96,112},{112,128},... | collective-permute-start | bytes 24584 | tf_op jit(solution)/shard_map/ppermute | solution.py:700
  65.0 4.3 %collective-permute-start.4 = (f32[80,128]{1,0:T(8,128)S(1)}, f32[80,128]{1,0:T(8,128)S(1)}, u32[]{:S(2)}, u32[]{:S(2)}) collective-permute-start(f32[80,128]{1,0:T(8,128)S(1)} %get-tuple-element.71), channel_id=1, source_target_pairs={{0,16},{16,32},{32,48},{48,64},{64,80},{80,96},{96,112},{112,128},... | collective-permute-start | bytes 122888 | tf_op jit(solution)/shard_map/ppermute | solution.py:700
  65.0 4.4 %collective-permute-start.5 = (f32[80,128]{1,0:T(8,128)S(1)}, f32[80,128]{1,0:T(8,128)S(1)}, u32[]{:S(2)}, u32[]{:S(2)}) collective-permute-start(f32[80,128]{1,0:T(8,128)S(1)} %get-tuple-element.72), channel_id=1, source_target_pairs={{16,0},{32,16},{48,32},{64,48},{80,64},{96,80},{112,96},{128,112},... | collective-permute-start | bytes 122888 | tf_op jit(solution)/shard_map/ppermute | solution.py:700
  69.5 7.2 %copy-start.3 = (bf16[288,4608]{1,0:T(8,128)(2,1)S(1)}, bf16[288,4608]{1,0:T(8,128)(2,1)}, u32[]{:S(2)}) copy-start(bf16[288,4608]{1,0:T(8,128)(2,1)} %constant.20.clone.table_ref) | copy-start | bytes 7962628
  72.0 4.5 %collective-permute-start.6 = (f32[64,128]{1,0:T(8,128)S(1)}, f32[64,128]{1,0:T(8,128)S(1)}, u32[]{:S(2)}, u32[]{:S(2)}) collective-permute-start(f32[64,128]{1,0:T(8,128)S(1)} %get-tuple-element.75), channel_id=1, source_target_pairs={{0,16},{16,32},{32,48},{48,64},{64,80},{80,96},{96,112},{112,128},... | collective-permute-start | bytes 98312 | tf_op jit(solution)/shard_map/ppermute | solution.py:700
  72.1 4.6 %collective-permute-start.7 = (f32[64,128]{1,0:T(8,128)S(1)}, f32[64,128]{1,0:T(8,128)S(1)}, u32[]{:S(2)}, u32[]{:S(2)}) collective-permute-start(f32[64,128]{1,0:T(8,128)S(1)} %get-tuple-element.76), channel_id=1, source_target_pairs={{16,0},{32,16},{48,32},{64,48},{80,64},{96,80},{112,96},{128,112},... | collective-permute-start | bytes 98312 | tf_op jit(solution)/shard_map/ppermute | solution.py:700
  79.0 4.6 %collective-permute-start.8 = (f32[80,128]{1,0:T(8,128)S(1)}, f32[80,128]{1,0:T(8,128)S(1)}, u32[]{:S(2)}, u32[]{:S(2)}) collective-permute-start(f32[80,128]{1,0:T(8,128)S(1)} %get-tuple-element.79), channel_id=1, source_target_pairs={{0,16},{16,32},{32,48},{48,64},{64,80},{80,96},{96,112},{112,128},... | collective-permute-start | bytes 122888 | tf_op jit(solution)/shard_map/ppermute | solution.py:700
  79.0 4.6 %collective-permute-start.9 = (f32[80,128]{1,0:T(8,128)S(1)}, f32[80,128]{1,0:T(8,128)S(1)}, u32[]{:S(2)}, u32[]{:S(2)}) collective-permute-start(f32[80,128]{1,0:T(8,128)S(1)} %get-tuple-element.80), channel_id=1, source_target_pairs={{16,0},{32,16},{48,32},{64,48},{80,64},{96,80},{112,96},{128,112},... | collective-permute-start | bytes 122888 | tf_op jit(solution)/shard_map/ppermute | solution.py:700
  84.2 7.3 %collective-permute-start.11 = (f32[16,128]{1,0:T(8,128)S(1)}, f32[16,128]{1,0:T(8,128)S(1)}, u32[]{:S(2)}, u32[]{:S(2)}) collective-permute-start(f32[16,128]{1,0:T(8,128)S(1)} %get-tuple-element.85), channel_id=1, source_target_pairs={{16,0},{32,16},{48,32},{64,48},{80,64},{96,80},{112,96},{128,112},... | collective-permute-start | bytes 24584 | tf_op jit(solution)/shard_map/ppermute | solution.py:700
  88.0 3.6 %collective-permute-start.10 = (f32[16,128]{1,0:T(8,128)S(1)}, f32[16,128]{1,0:T(8,128)S(1)}, u32[]{:S(2)}, u32[]{:S(2)}) collective-permute-start(f32[16,128]{1,0:T(8,128)S(1)} %get-tuple-element.85), channel_id=1, source_target_pairs={{0,16},{16,32},{32,48},{48,64},{64,80},{80,96},{96,112},{112,128},... | collective-permute-start | bytes 24584 | tf_op jit(solution)/shard_map/ppermute | solution.py:700
  92.3 4.3 %collective-permute-start.12 = (f32[80,128]{1,0:T(8,128)S(1)}, f32[80,128]{1,0:T(8,128)S(1)}, u32[]{:S(2)}, u32[]{:S(2)}) collective-permute-start(f32[80,128]{1,0:T(8,128)S(1)} %get-tuple-element.90), channel_id=1, source_target_pairs={{0,16},{16,32},{32,48},{48,64},{64,80},{80,96},{96,112},{112,128},... | collective-permute-start | bytes 122888 | tf_op jit(solution)/shard_map/ppermute | solution.py:700
  92.3 4.5 %collective-permute-start.13 = (f32[80,128]{1,0:T(8,128)S(1)}, f32[80,128]{1,0:T(8,128)S(1)}, u32[]{:S(2)}, u32[]{:S(2)}) collective-permute-start(f32[80,128]{1,0:T(8,128)S(1)} %get-tuple-element.91), channel_id=1, source_target_pairs={{16,0},{32,16},{48,32},{64,48},{80,64},{96,80},{112,96},{128,112},... | collective-permute-start | bytes 122888 | tf_op jit(solution)/shard_map/ppermute | solution.py:700
  99.4 4.5 %collective-permute-start.14 = (f32[64,128]{1,0:T(8,128)S(1)}, f32[64,128]{1,0:T(8,128)S(1)}, u32[]{:S(2)}, u32[]{:S(2)}) collective-permute-start(f32[64,128]{1,0:T(8,128)S(1)} %get-tuple-element.94), channel_id=1, source_target_pairs={{0,16},{16,32},{32,48},{48,64},{64,80},{80,96},{96,112},{112,128},... | collective-permute-start | bytes 98312 | tf_op jit(solution)/shard_map/ppermute | solution.py:700
  99.4 4.6 %collective-permute-start.15 = (f32[64,128]{1,0:T(8,128)S(1)}, f32[64,128]{1,0:T(8,128)S(1)}, u32[]{:S(2)}, u32[]{:S(2)}) collective-permute-start(f32[64,128]{1,0:T(8,128)S(1)} %get-tuple-element.95), channel_id=1, source_target_pairs={{16,0},{32,16},{48,32},{64,48},{80,64},{96,80},{112,96},{128,112},... | collective-permute-start | bytes 98312 | tf_op jit(solution)/shard_map/ppermute | solution.py:700
  105.1 1.6 %copy-start = (f32[4,1536,128]{2,1,0:T(8,128)}, f32[4,1536,128]{2,1,0:T(8,128)S(1)}, u32[]{:S(2)}) copy-start(f32[4,1536,128]{2,1,0:T(8,128)S(1)} %get-tuple-element.93.t_ref) | copy-start | bytes 9437188
  106.7 31.0 %all-to-all-start.1 = ((f32[32,8,128]{2,1,0:T(8,128)}), f32[32,8,128]{2,1,0:T(8,128)S(1)}, u32[]{:S(2)}, u32[]{:S(2)}) async-start(f32[32,8,128]{2,1,0:T(8,128)} %shard_map.147), calls=%async_computation.1 | async-start | bytes 262144 | tf_op jit(solution)/shard_map/all_to_all | solution.py:790
  121.8 1.9 %copy-start.1 = (f32[4,1536,128]{2,1,0:T(8,128)S(1)}, f32[4,1536,128]{2,1,0:T(8,128)}, u32[]{:S(2)}) copy-start(f32[4,1536,128]{2,1,0:T(8,128)} %copy-done) | copy-start | bytes 9437188
  123.7 1.7 %copy-start.4 = (bf16[288,4608]{1,0:T(8,128)(2,1)S(1)}, bf16[288,4608]{1,0:T(8,128)(2,1)}, u32[]{:S(2)}) copy-start(bf16[288,4608]{1,0:T(8,128)(2,1)} %constant.20.clone.table_ref) | copy-start | bytes 7962628
  125.5 1.8 %copy-start.6 = (f32[192,192]{1,0:T(8,128)S(1)}, f32[192,192]{1,0:T(8,128)}, u32[]{:S(2)}) copy-start(f32[192,192]{1,0:T(8,128)} %constant.21.clone.table_ref) | copy-start | bytes 442372
  125.5 12.2 %copy-start.5 = (f32[6,6,192]{2,1,0:T(8,128)S(1)}, f32[6,6,192]{2,1,0:T(8,128)}, u32[]{:S(2)}) copy-start(f32[6,6,192]{2,1,0:T(8,128)} %rhs_ref.1) | copy-start | bytes 82948

commit v8 on v7

--- a/solution.py
+++ b/solution.py
@@ -260,8 +260,8 @@
 
 
 def pack_body(*refs):
-    me_ref, sources, (out_ref, tiles), held, (tmp, common, chosen_blocks, own_ref, ready) = (
-        refs[0], refs[1:10], refs[10:12], refs[12:21], refs[21:]
+    (b_ref, c_ref), sources, (out_ref, tiles), held, (tmp, common, own_ref, ready) = (
+        refs[:2], refs[2:11], refs[11:13], refs[13:22], refs[22:]
     )
     copies = [pltpu.make_async_copy(sources[n], held[n], ready.at[n]) for n in range(9)]
     for copy in copies:
@@ -269,8 +269,8 @@
     for copy in copies:
         copy.wait()
     rhs_ref, helm_ref, vec_ref, val_ref, size_ref, rows_ref, link_ref, six_ref, eight_ref = held
-    mine_b = me_ref[0]
-    mine_c = me_ref[1]
+    mine_b = b_ref[0]
+    mine_c = c_ref[0]
     for t in range(4):
         tiles[t] = rows_ref[:, t * 128 : (t + 1) * 128]
     for t in range(4):
@@ -295,23 +295,14 @@
     )
     common[120:184, :] = helm[:, 0:128]
     common[184:248, :] = helm[:, 128:256]
-    sends = [pltpu.make_async_copy(common, out_ref.at[n, 64:312], ready.at[9 + n]) for n in range(16)]
-    sends += [
-        pltpu.make_async_copy(chosen_blocks.at[n], out_ref.at[n, 0:64], ready.at[25 + n]) for n in range(16)
-    ]
-    for send in sends[:16]:
-        send.start()
     for r in range(16):
         other = ((mine_b ^ (r >> 2)) << 2) | (mine_c ^ (r & 3))
+        out_ref[other, 64:312, :] = common[...]
         for half in range(2):
             chosen = BLOCKS[r][half * 4 : half * 4 + 4]
-            chosen_blocks[other, half * 32 : half * 32 + 32, :] = place_blocks(
+            out_ref[other, half * 32 : half * 32 + 32, :] = place_blocks(
                 [(own_ref[t >> 2], t & 3, n) for n, t in enumerate(chosen)]
             )
-    for send in sends[16:]:
-        send.start()
-    for send in sends:
-        send.wait()
 
 
 def joined(column, start, rows, quarter):
@@ -319,11 +310,11 @@
 
 
 def unpack_body(
-    me_ref, all_ref, own_ref,
+    b_ref, c_ref, all_ref, own_ref,
     dense_ref, rhs_ref, small_ref, box_ref, state_ref, ahead_ref, behind_ref, half_matrix,
 ):
-    mine_b = me_ref[0]
-    mine_c = me_ref[1]
+    mine_b = b_ref[0]
+    mine_c = c_ref[0]
     own_at = pl.multiple_of((mine_b * 4 + mine_c) * 32, 32)
     for t in range(4):
         half_matrix[t, pl.ds(own_at, 32), :] = own_ref[t]
@@ -635,15 +626,13 @@
             if k in (0, 7):
                 part = part * 0.5
             total = part if total is None else total + part
-    row = lax.broadcasted_iota(jnp.int32, (8, 128), 0)
-    sums = jnp.where(row == 4, jnp.sum(total, axis=0, keepdims=True), products_ref[...])
-    for n in range(sums_ref.shape[0]):
-        sums_ref[n] = sums
-
-
-def own_body(me_ref, z_ref, w_ref, q_ref, v_ref, table_ref, z_out, w_out, q_out, v_out):
-    mine_b = me_ref[0]
-    mine_c = me_ref[1]
+    sums_ref[...] = products_ref[...]
+    sums_ref[4:5, :] = jnp.sum(total, axis=0, keepdims=True)
+
+
+def own_body(b_ref, c_ref, z_ref, w_ref, q_ref, v_ref, table_ref, z_out, w_out, q_out, v_out):
+    mine_b = b_ref[0]
+    mine_c = c_ref[0]
     for field_ref, out_ref in ((z_ref, z_out), (w_ref, w_out), (q_ref, q_out), (v_ref, v_out)):
         moved = pltpu.roll(field_ref[mine_b], ((4 - mine_c) & 3) * 32, 1)
         nodes = jnp.concatenate([moved[k * 48 : (k + 1) * 48, 0:32] for k in range(6)], axis=1)
@@ -701,7 +690,7 @@
 
     forward, backward = gradient_tables()
     six = order_table(6)
-    me = jnp.stack([lax.axis_index("gy"), lax.axis_index("col")]).astype(jnp.int32)
+    me = [lax.axis_index(axis).astype(jnp.int32).reshape(1) for axis in ("gy", "col")]
     field = (NB, ROWS_P, 128)
     velocity = (NB, ROWS_V, 128)
     state_shape = (16, 128)
@@ -723,26 +712,25 @@
     own_part, own_rows = pl.pallas_call(
         pack_body,
         out_shape=[jax.ShapeDtypeStruct((16, ROWS, 128), F32), jax.ShapeDtypeStruct((4, 32, 128), F32)],
-        in_specs=[pl.BlockSpec(memory_space=pltpu.SMEM)] + [pl.BlockSpec(memory_space=pl.ANY)] * 9,
-        out_specs=[pl.BlockSpec(memory_space=pl.ANY), vmem],
+        in_specs=[pl.BlockSpec(memory_space=pltpu.SMEM)] * 2 + [pl.BlockSpec(memory_space=pl.ANY)] * 9,
+        out_specs=[vmem, vmem],
         scratch_shapes=[pltpu.VMEM(value.shape, F32) for value in arguments]
         + [
             pltpu.VMEM((40, 192), F32),
             pltpu.VMEM((248, 128), F32),
-            pltpu.VMEM((16, 64, 128), F32),
             pltpu.VMEM((4, 32, 128), F32),
-            pltpu.SemaphoreType.DMA((41,)),
+            pltpu.SemaphoreType.DMA((9,)),
         ],
         compiler_params=pltpu.CompilerParams(vmem_limit_bytes=60 * 1024 * 1024),
-    )(me, *arguments)
+    )(*me, *arguments)
     everything = lax.all_to_all(own_part, ("gy", "col"), 0, 0)
 
     dense, rhs, small, boxes, state, up, down = call(
         unpack_body,
         [(4, 512, 128), field, (NB, 40, 128), velocity, state_shape, wide, wide],
         [pltpu.VMEM((4, 512, 128), F32)],
-        scalars=1,
-    )(me, everything, own_rows)
+        scalars=2,
+    )(*me, everything, own_rows)
     helm, vectors = call(unpack_rest_body, [velocity, (NB, 192, 128)])(everything)
 
     def schwarz_front(boxes):
@@ -786,10 +774,10 @@
     left, right, front = lax.optimization_barrier((left, right, front))
     q, t, left, right = precondition(boxes, state, left, right, front)
     (products,) = call(products_body, [(8, 128)])(rhs, z, w, q)
-    (sums,) = call(energy_body, [(count, 8, 128)])(t, left, right, inverse, products)
-    sums = lax.all_to_all(sums, "gx", 0, 0)
+    (sums,) = call(energy_body, [(8, 128)])(t, left, right, inverse, products)
+    sums = lax.all_to_all(jnp.broadcast_to(sums[None], (count, 8, 128)), "gx", 0, 0)
     (v,) = call(last_image_body, [field], spread)(t, left, right, inverse, small, backward)
-    own = call(own_body, [(6, 6, 192)] * 4, scalars=1)(me, z, w, q, v, six.T.copy())
+    own = call(own_body, [(6, 6, 192)] * 4, scalars=2)(*me, z, w, q, v, six.T.copy())
     return tuple(
         pl.pallas_call(
             last_body,

time: 139 us -> 135 us (0.971)
  Pallas kernels: 32.8 us -> 29.7 us
    pallas_call x18, Pallas kernels: 27.2 us -> 25.4 us  [run(): pl.pallas_call(body, out_shape=[jax.ShapeDtypeStruct(shape, F32) for shap...]
    unnamed x18 -> x16, local copies, waits for them, and re-layouts: 5.28 us -> 3.66 us
where the time goes in v8:
time: 135 us
  starting transfers between devices  47.7 us (35%)
  blocking collectives  37.2 us (28%)
  Pallas kernels  29.7 us (22%)
  waiting for transfers between devices  14 us (10%)
  local copies, waits for them, and re-layouts  4.32 us (3%)
  between operations  1.7 us (1%)
    all_to_all x1, blocking collectives, local(): everything = lax.all_to_all(own_part, ('gy', 'col'), 0, 0)  37.2 us
    ppermute x16, starting transfers between devices, exchange(): return (lax.ppermute(up, 'gx', ahead), lax.ppermute(down, 'gx', behind))  32.6 us
    pallas_call x18, Pallas kernels, run(): pl.pallas_call(body, out_shape=[jax.ShapeDtypeStruct(shape, F32) for shap...  25.4 us
    all_to_all x1, starting transfers between devices, local(): lax.all_to_all(jnp.broadcast_to(sums[None], (count, 8, 128)), 'gx', 0, 0)  15.1 us
    all_to_all x1, waiting for transfers between devices, local(): lax.all_to_all(jnp.broadcast_to(sums[None], (count, 8, 128)), 'gx', 0, 0)  9.66 us
    ppermute x16, waiting for transfers between devices, exchange(): return (lax.ppermute(up, 'gx', ahead), lax.ppermute(down, 'gx', behind))  4.3 us
    unnamed x16, local copies, waits for them, and re-layouts  3.66 us
    pallas_call x1, Pallas kernels, local(): pl.pallas_call(pack_body, out_shape=[jax.ShapeDtypeStruct((16, ROWS, 128)...  3.4 us
  transfers between devices with their start and end apart: 17, of which 11 were waited for; matrix products, arithmetic and copies ran while one was open for 0% of the time, Pallas kernels for 10%

profile of v8, /device:TPU:1, one launch (start us, length us, event | category | flops | bytes accessed | tf_op | source)
XLA Modules:
  0.0 134.5 jit_solution(7425597162264131270)
XLA Ops:
  1.3 3.4 %shard_map.131 = (f32[16,312,128]{2,1,0:T(8,128)}, f32[4,32,128]{2,1,0:T(8,128)}) custom-call(s32[1]{0:T(128)} %bitcast.refs_0_.b_ref, s32[1]{0:T(128)} %bitcast.1.refs_1_.c_ref, f32[6,6,192]{2,1,0:T(8,128)} %rhs_ref.1, f32[8,8,256]{2,1,0:T(8,128)} %refs_3_.1, f32[192,32]{1,0:T(8,128)} %bitcast.4, f32[24,32]{1,0:T(8,128)} %bitcast.5, f32[3,32]{1,0:T(4,128)} %refs_6_.1, ...), custom_call_target="tpu_custom_call" | custom-call | tf_op jit(solution)/shard_map/pallas_call | solution.py:712
  4.7 0.0 copy-start.7
  4.7 37.2 %all_to_all.10.all_ref = f32[16,312,128]{2,1,0:T(8,128)S(1)} all-to-all(f32[16,312,128]{2,1,0:T(8,128)} %get-tuple-element.53), channel_id=1, replica_groups=mesh['gx'=32,'gy'=4,'col'=4] {'gy','col'}, dimensions={0} | all-to-all | bytes 5111808 | tf_op jit(solution)/shard_map/all_to_all | solution.py:726
  41.9 0.0 copy-done.7
  41.9 2.2 %shard_map.132 = (f32[4,512,128]{2,1,0:T(8,128)S(1)}, f32[4,288,128]{2,1,0:T(8,128)S(1)}, f32[4,40,128]{2,1,0:T(8,128)S(1)}, f32[4,512,128]{2,1,0:T(8,128)S(1)},...) custom-call(s32[1]{0:T(128)} %bitcast.refs_0_.b_ref, s32[1]{0:T(128)} %bitcast.1.refs_1_.c_ref, ...), custom_call_target="tpu_custom_call" | custom-call | tf_op jit(solution)/shard_map/pallas_call | solution.py:671
  44.1 6.2 %collective-permute-start = (f32[80,128]{1,0:T(8,128)S(1)}, f32[80,128]{1,0:T(8,128)S(1)}, u32[]{:S(2)}, u32[]{:S(2)}) collective-permute-start(f32[80,128]{1,0:T(8,128)S(1)} %get-tuple-element.57), channel_id=1, source_target_pairs={{0,16},{16,32},{32,48},{48,64},{64,80},{80,96},{96,112},{112,128},... | collective-permute-start | bytes 122888 | tf_op jit(solution)/shard_map/ppermute | solution.py:689
  50.3 0.0 collective-permute-start.1
  50.3 1.2 shard_map.133
  51.5 0.8 shard_map.134.front_ref
  52.3 0.0 copy-start.2
  52.3 0.0 collective-permute-done.left_ref
  52.3 1.4 %collective-permute-done.1.right_ref = f32[80,128]{1,0:T(8,128)S(1)} collective-permute-done((f32[80,128]{1,0:T(8,128)S(1)}, f32[80,128]{1,0:T(8,128)S(1)}, u32[]{:S(2)}, u32[]{:S(2)}) %collective-permute-start.1) | collective-permute-done | bytes 40992 | tf_op jit(solution)/shard_map/ppermute | solution.py:689
  53.7 0.6 shard_map.135
  54.3 4.2 %collective-permute-start.3 = (f32[16,128]{1,0:T(8,128)S(1)}, f32[16,128]{1,0:T(8,128)S(1)}, u32[]{:S(2)}, u32[]{:S(2)}) collective-permute-start(f32[16,128]{1,0:T(8,128)S(1)} %get-tuple-element.65), channel_id=1, source_target_pairs={{16,0},{32,16},{48,32},{64,48},{80,64},{96,80},{112,96},{128,112},... | collective-permute-start | bytes 24584 | tf_op jit(solution)/shard_map/ppermute | solution.py:689
  58.5 0.0 collective-permute-start.2
  58.5 3.3 %shard_map.136 = (f32[4,288,128]{2,1,0:T(8,128)S(1)}, f32[64,128]{1,0:T(8,128)S(1)}, f32[64,128]{1,0:T(8,128)S(1)}) custom-call(f32[4,512,128]{2,1,0:T(8,128)S(1)} %get-tuple-element.60.box_ref, f32[4,384,128]{2,1,0:T(8,128)S(1)} %shard_map.134.front_ref, f32[4,192,128]{2,1,0:T(8,128)S(1)} %get-tuple-element.61.vec_ref, ...), custom_call_target="tpu_custom_call" | custom-call | tf_op jit(solution)/shard_map/pallas_call | solution.py:671
  61.8 0.0 collective-permute-done.3.right_ref
  61.8 0.0 collective-permute-done.2.left_ref
  61.9 0.6 shard_map.137
  62.5 0.0 collective-permute-start.4
  62.5 3.5 %collective-permute-start.5 = (f32[80,128]{1,0:T(8,128)S(1)}, f32[80,128]{1,0:T(8,128)S(1)}, u32[]{:S(2)}, u32[]{:S(2)}) collective-permute-start(f32[80,128]{1,0:T(8,128)S(1)} %get-tuple-element.72), channel_id=1, source_target_pairs={{16,0},{32,16},{48,32},{64,48},{80,64},{96,80},{112,96},{128,112},... | collective-permute-start | bytes 122888 | tf_op jit(solution)/shard_map/ppermute | solution.py:689
  66.0 0.7 collective-permute-done.4.left_ref
  66.7 0.2 collective-permute-done.5.right_ref
  66.9 0.0 copy-done.2
  66.9 2.6 %shard_map.138 = (f32[4,288,128]{2,1,0:T(8,128)S(1)}, f32[4,1536,128]{2,1,0:T(8,128)S(1)}, f32[64,128]{1,0:T(8,128)S(1)}, f32[64,128]{1,0:T(8,128)S(1)}) custom-call(f32[4,512,128]{2,1,0:T(8,128)S(1)} %get-tuple-element.55.dense_ref, f32[16,128]{1,0:T(8,128)S(1)} %get-tuple-element.70.state_ref, f32[80,128]{1,0:T(8,128)S(1)} %collective-permute-done.4.left_ref, ...), custom_call_target="tpu_custom_call" | custom-call | tf_op jit(solution)/shard_map/pallas_call | solution.py:671
  69.5 0.0 collective-permute-start.6
  69.5 3.8 %collective-permute-start.7 = (f32[64,128]{1,0:T(8,128)S(1)}, f32[64,128]{1,0:T(8,128)S(1)}, u32[]{:S(2)}, u32[]{:S(2)}) collective-permute-start(f32[64,128]{1,0:T(8,128)S(1)} %get-tuple-element.76), channel_id=1, source_target_pairs={{16,0},{32,16},{48,32},{64,48},{80,64},{96,80},{112,96},{128,112},... | collective-permute-start | bytes 98312 | tf_op jit(solution)/shard_map/ppermute | solution.py:689
  73.3 0.4 shard_map.139.inverse_ref
  73.7 0.3 collective-permute-done.6.left_ref
  74.0 0.2 collective-permute-done.7.right_ref
  74.2 2.3 %shard_map.140 = (f32[4,288,128]{2,1,0:T(8,128)S(1)}, f32[4,512,128]{2,1,0:T(8,128)S(1)}, f32[16,128]{1,0:T(8,128)S(1)}, f32[80,128]{1,0:T(8,128)S(1)}, f32[80,128]{1,0:T(8,128)S(1)}) custom-call(f32[4,1536,128]{2,1,0:T(8,128)S(1)} %get-tuple-element.74.t_ref, f32[64,128]{1,0:T(8,128)S(1)} %collective-permute-done.6.left_ref, ...), custom_call_target="tpu_custom_call" | custom-call | tf_op jit(solution)/shard_map/pallas_call | solution.py:671
  76.5 0.0 collective-permute-start.8
  76.5 3.7 %collective-permute-start.9 = (f32[80,128]{1,0:T(8,128)S(1)}, f32[80,128]{1,0:T(8,128)S(1)}, u32[]{:S(2)}, u32[]{:S(2)}) collective-permute-start(f32[80,128]{1,0:T(8,128)S(1)} %get-tuple-element.80), channel_id=1, source_target_pairs={{16,0},{32,16},{48,32},{64,48},{80,64},{96,80},{112,96},{128,112},... | collective-permute-start | bytes 122888 | tf_op jit(solution)/shard_map/ppermute | solution.py:689
  80.2 0.8 shard_map.141.front_ref
  81.0 0.0 collective-permute-done.8.left_ref
  81.0 0.0 collective-permute-done.9.right_ref
  81.1 0.6 shard_map.142
  81.7 3.8 %collective-permute-start.11 = (f32[16,128]{1,0:T(8,128)S(1)}, f32[16,128]{1,0:T(8,128)S(1)}, u32[]{:S(2)}, u32[]{:S(2)}) collective-permute-start(f32[16,128]{1,0:T(8,128)S(1)} %get-tuple-element.85), channel_id=1, source_target_pairs={{16,0},{32,16},{48,32},{64,48},{80,64},{96,80},{112,96},{128,112},... | collective-permute-start | bytes 24584 | tf_op jit(solution)/shard_map/ppermute | solution.py:689
  85.5 0.0 collective-permute-start.10
  85.5 3.5 %shard_map.143 = (f32[4,288,128]{2,1,0:T(8,128)S(1)}, f32[64,128]{1,0:T(8,128)S(1)}, f32[64,128]{1,0:T(8,128)S(1)}) custom-call(f32[4,512,128]{2,1,0:T(8,128)S(1)} %get-tuple-element.81.box_ref, f32[4,384,128]{2,1,0:T(8,128)S(1)} %shard_map.141.front_ref, f32[4,192,128]{2,1,0:T(8,128)S(1)} %get-tuple-element.61.vec_ref, ...), custom_call_target="tpu_custom_call" | custom-call | tf_op jit(solution)/shard_map/pallas_call | solution.py:671
  89.0 0.0 collective-permute-done.11.right_ref
  89.0 0.1 collective-permute-done.10.left_ref
  89.1 0.6 shard_map.144
  89.7 0.0 collective-permute-start.12
  89.7 3.6 %collective-permute-start.13 = (f32[80,128]{1,0:T(8,128)S(1)}, f32[80,128]{1,0:T(8,128)S(1)}, u32[]{:S(2)}, u32[]{:S(2)}) collective-permute-start(f32[80,128]{1,0:T(8,128)S(1)} %get-tuple-element.91), channel_id=1, source_target_pairs={{16,0},{32,16},{48,32},{64,48},{80,64},{96,80},{112,96},{128,112},... | collective-permute-start | bytes 122888 | tf_op jit(solution)/shard_map/ppermute | solution.py:689
  93.4 0.7 collective-permute-done.12.left_ref
  94.1 0.2 collective-permute-done.13.right_ref
  94.2 2.6 %shard_map.145 = (f32[4,288,128]{2,1,0:T(8,128)S(1)}, f32[4,1536,128]{2,1,0:T(8,128)S(1)}, f32[64,128]{1,0:T(8,128)S(1)}, f32[64,128]{1,0:T(8,128)S(1)}) custom-call(f32[4,512,128]{2,1,0:T(8,128)S(1)} %get-tuple-element.55.dense_ref, f32[16,128]{1,0:T(8,128)S(1)} %get-tuple-element.89.state_ref, f32[80,128]{1,0:T(8,128)S(1)} %collective-permute-done.12.left_ref, ...), custom_call_target="tpu_custom_call" | custom-call | tf_op jit(solution)/shard_map/pallas_call | solution.py:671
  96.8 0.0 collective-permute-start.14
  96.9 3.8 %collective-permute-start.15 = (f32[64,128]{1,0:T(8,128)S(1)}, f32[64,128]{1,0:T(8,128)S(1)}, u32[]{:S(2)}, u32[]{:S(2)}) collective-permute-start(f32[64,128]{1,0:T(8,128)S(1)} %get-tuple-element.95), channel_id=1, source_target_pairs={{16,0},{32,16},{48,32},{64,48},{80,64},{96,80},{112,96},{128,112},... | collective-permute-start | bytes 98312 | tf_op jit(solution)/shard_map/ppermute | solution.py:689
  100.6 0.3 shard_map.146.products_ref
  100.9 0.4 collective-permute-done.14.left_ref
  101.3 0.2 collective-permute-done.15.right_ref
  101.5 0.4 shard_map.147
  101.9 0.7 broadcast_in_dim.2
  102.6 15.1 %all-to-all-start.1 = ((f32[32,8,128]{2,1,0:T(8,128)}), f32[32,8,128]{2,1,0:T(8,128)S(1)}, u32[]{:S(2)}, u32[]{:S(2)}) async-start(f32[32,8,128]{2,1,0:T(8,128)} %broadcast_in_dim.2), calls=%async_computation.1 | async-start | bytes 262144 | tf_op jit(solution)/shard_map/all_to_all | solution.py:778
  117.7 1.9 %copy-done.1 = f32[4,1536,128]{2,1,0:T(8,128)S(1)} copy-done((f32[4,1536,128]{2,1,0:T(8,128)S(1)}, f32[4,1536,128]{2,1,0:T(8,128)}, u32[]{:S(2)}) %copy-start.1) | copy-done | bytes 3145752
  119.6 1.7 %copy-done.4 = bf16[288,4608]{1,0:T(8,128)(2,1)S(1)} copy-done((bf16[288,4608]{1,0:T(8,128)(2,1)S(1)}, bf16[288,4608]{1,0:T(8,128)(2,1)}, u32[]{:S(2)}) %copy-start.4) | copy-done | bytes 2654232
  121.3 1.8 %shard_map.148.v_ref = f32[4,288,128]{2,1,0:T(8,128)S(1)} custom-call(f32[4,1536,128]{2,1,0:T(8,128)S(1)} %copy-done.1, f32[64,128]{1,0:T(8,128)S(1)} %collective-permute-done.14.left_ref, f32[64,128]{1,0:T(8,128)S(1)} %collective-permute-done.15.right_ref, f32[4,512,128]{2,1,0:T(8,128)S(1)} %shard_map.139.inverse_ref, ...), custom_call_target="tpu_custom_call" | custom-call | tf_op jit(solution)/shard_map/pallas_call | solution.py:671
  123.2 0.0 copy-done.5
  123.2 0.7 shard_map.149
  123.9 9.7 %all-to-all-done.1.sums_ref = f32[32,8,128]{2,1,0:T(8,128)S(1)} async-done(((f32[32,8,128]{2,1,0:T(8,128)}), f32[32,8,128]{2,1,0:T(8,128)S(1)}, u32[]{:S(2)}, u32[]{:S(2)}) %all-to-all-start.1) | async-done | bytes 131104 | tf_op jit(solution)/shard_map/all_to_all | solution.py:778
  133.6 0.0 copy-done.6
  133.6 0.8 shard_map.150
  (8 shorter events, 0.0 us)
Async XLA Ops:
  4.7 37.2 %copy-start.7 = (f32[4,32,128]{2,1,0:T(8,128)S(1)}, f32[4,32,128]{2,1,0:T(8,128)}, u32[]{:S(2)}) copy-start(f32[4,32,128]{2,1,0:T(8,128)} %get-tuple-element.54.own_ref) | copy-start | bytes 196612
  44.1 8.2 %collective-permute-start = (f32[80,128]{1,0:T(8,128)S(1)}, f32[80,128]{1,0:T(8,128)S(1)}, u32[]{:S(2)}, u32[]{:S(2)}) collective-permute-start(f32[80,128]{1,0:T(8,128)S(1)} %get-tuple-element.57), channel_id=1, source_target_pairs={{0,16},{16,32},{32,48},{48,64},{64,80},{80,96},{96,112},{112,128},... | collective-permute-start | bytes 122888 | tf_op jit(solution)/shard_map/ppermute | solution.py:689
  50.3 3.4 %collective-permute-start.1 = (f32[80,128]{1,0:T(8,128)S(1)}, f32[80,128]{1,0:T(8,128)S(1)}, u32[]{:S(2)}, u32[]{:S(2)}) collective-permute-start(f32[80,128]{1,0:T(8,128)S(1)} %get-tuple-element.58), channel_id=1, source_target_pairs={{16,0},{32,16},{48,32},{64,48},{80,64},{96,80},{112,96},{128,112},... | collective-permute-start | bytes 122888 | tf_op jit(solution)/shard_map/ppermute | solution.py:689
  52.3 14.6 %copy-start.2 = (bf16[1536,864]{1,0:T(8,128)(2,1)S(1)}, bf16[1536,864]{1,0:T(8,128)(2,1)}, u32[]{:S(2)}) copy-start(bf16[1536,864]{1,0:T(8,128)(2,1)} %constant.19.clone.table_ref) | copy-start | bytes 7962628
  54.3 7.5 %collective-permute-start.3 = (f32[16,128]{1,0:T(8,128)S(1)}, f32[16,128]{1,0:T(8,128)S(1)}, u32[]{:S(2)}, u32[]{:S(2)}) collective-permute-start(f32[16,128]{1,0:T(8,128)S(1)} %get-tuple-element.65), channel_id=1, source_target_pairs={{16,0},{32,16},{48,32},{64,48},{80,64},{96,80},{112,96},{128,112},... | collective-permute-start | bytes 24584 | tf_op jit(solution)/shard_map/ppermute | solution.py:689
  58.5 3.3 %collective-permute-start.2 = (f32[16,128]{1,0:T(8,128)S(1)}, f32[16,128]{1,0:T(8,128)S(1)}, u32[]{:S(2)}, u32[]{:S(2)}) collective-permute-start(f32[16,128]{1,0:T(8,128)S(1)} %get-tuple-element.65), channel_id=1, source_target_pairs={{0,16},{16,32},{32,48},{48,64},{64,80},{80,96},{96,112},{112,128},... | collective-permute-start | bytes 24584 | tf_op jit(solution)/shard_map/ppermute | solution.py:689
  62.5 4.2 %collective-permute-start.4 = (f32[80,128]{1,0:T(8,128)S(1)}, f32[80,128]{1,0:T(8,128)S(1)}, u32[]{:S(2)}, u32[]{:S(2)}) collective-permute-start(f32[80,128]{1,0:T(8,128)S(1)} %get-tuple-element.71), channel_id=1, source_target_pairs={{0,16},{16,32},{32,48},{48,64},{64,80},{80,96},{96,112},{112,128},... | collective-permute-start | bytes 122888 | tf_op jit(solution)/shard_map/ppermute | solution.py:689
  62.5 4.4 %collective-permute-start.5 = (f32[80,128]{1,0:T(8,128)S(1)}, f32[80,128]{1,0:T(8,128)S(1)}, u32[]{:S(2)}, u32[]{:S(2)}) collective-permute-start(f32[80,128]{1,0:T(8,128)S(1)} %get-tuple-element.72), channel_id=1, source_target_pairs={{16,0},{32,16},{48,32},{64,48},{80,64},{96,80},{112,96},{128,112},... | collective-permute-start | bytes 122888 | tf_op jit(solution)/shard_map/ppermute | solution.py:689
  66.9 7.2 %copy-start.3 = (bf16[288,4608]{1,0:T(8,128)(2,1)S(1)}, bf16[288,4608]{1,0:T(8,128)(2,1)}, u32[]{:S(2)}) copy-start(bf16[288,4608]{1,0:T(8,128)(2,1)} %constant.20.clone.table_ref) | copy-start | bytes 7962628
  69.5 4.5 %collective-permute-start.6 = (f32[64,128]{1,0:T(8,128)S(1)}, f32[64,128]{1,0:T(8,128)S(1)}, u32[]{:S(2)}, u32[]{:S(2)}) collective-permute-start(f32[64,128]{1,0:T(8,128)S(1)} %get-tuple-element.75), channel_id=1, source_target_pairs={{0,16},{16,32},{32,48},{48,64},{64,80},{80,96},{96,112},{112,128},... | collective-permute-start | bytes 98312 | tf_op jit(solution)/shard_map/ppermute | solution.py:689
  69.5 4.6 %collective-permute-start.7 = (f32[64,128]{1,0:T(8,128)S(1)}, f32[64,128]{1,0:T(8,128)S(1)}, u32[]{:S(2)}, u32[]{:S(2)}) collective-permute-start(f32[64,128]{1,0:T(8,128)S(1)} %get-tuple-element.76), channel_id=1, source_target_pairs={{16,0},{32,16},{48,32},{64,48},{80,64},{96,80},{112,96},{128,112},... | collective-permute-start | bytes 98312 | tf_op jit(solution)/shard_map/ppermute | solution.py:689
  76.5 4.6 %collective-permute-start.8 = (f32[80,128]{1,0:T(8,128)S(1)}, f32[80,128]{1,0:T(8,128)S(1)}, u32[]{:S(2)}, u32[]{:S(2)}) collective-permute-start(f32[80,128]{1,0:T(8,128)S(1)} %get-tuple-element.79), channel_id=1, source_target_pairs={{0,16},{16,32},{32,48},{48,64},{64,80},{80,96},{96,112},{112,128},... | collective-permute-start | bytes 122888 | tf_op jit(solution)/shard_map/ppermute | solution.py:689
  76.5 4.6 %collective-permute-start.9 = (f32[80,128]{1,0:T(8,128)S(1)}, f32[80,128]{1,0:T(8,128)S(1)}, u32[]{:S(2)}, u32[]{:S(2)}) collective-permute-start(f32[80,128]{1,0:T(8,128)S(1)} %get-tuple-element.80), channel_id=1, source_target_pairs={{16,0},{32,16},{48,32},{64,48},{80,64},{96,80},{112,96},{128,112},... | collective-permute-start | bytes 122888 | tf_op jit(solution)/shard_map/ppermute | solution.py:689
  81.7 7.3 %collective-permute-start.11 = (f32[16,128]{1,0:T(8,128)S(1)}, f32[16,128]{1,0:T(8,128)S(1)}, u32[]{:S(2)}, u32[]{:S(2)}) collective-permute-start(f32[16,128]{1,0:T(8,128)S(1)} %get-tuple-element.85), channel_id=1, source_target_pairs={{16,0},{32,16},{48,32},{64,48},{80,64},{96,80},{112,96},{128,112},... | collective-permute-start | bytes 24584 | tf_op jit(solution)/shard_map/ppermute | solution.py:689
  85.5 3.6 %collective-permute-start.10 = (f32[16,128]{1,0:T(8,128)S(1)}, f32[16,128]{1,0:T(8,128)S(1)}, u32[]{:S(2)}, u32[]{:S(2)}) collective-permute-start(f32[16,128]{1,0:T(8,128)S(1)} %get-tuple-element.85), channel_id=1, source_target_pairs={{0,16},{16,32},{32,48},{48,64},{64,80},{80,96},{96,112},{112,128},... | collective-permute-start | bytes 24584 | tf_op jit(solution)/shard_map/ppermute | solution.py:689
  89.7 4.3 %collective-permute-start.12 = (f32[80,128]{1,0:T(8,128)S(1)}, f32[80,128]{1,0:T(8,128)S(1)}, u32[]{:S(2)}, u32[]{:S(2)}) collective-permute-start(f32[80,128]{1,0:T(8,128)S(1)} %get-tuple-element.90), channel_id=1, source_target_pairs={{0,16},{16,32},{32,48},{48,64},{64,80},{80,96},{96,112},{112,128},... | collective-permute-start | bytes 122888 | tf_op jit(solution)/shard_map/ppermute | solution.py:689
  89.7 4.5 %collective-permute-start.13 = (f32[80,128]{1,0:T(8,128)S(1)}, f32[80,128]{1,0:T(8,128)S(1)}, u32[]{:S(2)}, u32[]{:S(2)}) collective-permute-start(f32[80,128]{1,0:T(8,128)S(1)} %get-tuple-element.91), channel_id=1, source_target_pairs={{16,0},{32,16},{48,32},{64,48},{80,64},{96,80},{112,96},{128,112},... | collective-permute-start | bytes 122888 | tf_op jit(solution)/shard_map/ppermute | solution.py:689
  96.8 5.1 %copy-start = (f32[4,1536,128]{2,1,0:T(8,128)}, f32[4,1536,128]{2,1,0:T(8,128)S(1)}, u32[]{:S(2)}) copy-start(f32[4,1536,128]{2,1,0:T(8,128)S(1)} %get-tuple-element.93.t_ref) | copy-start | bytes 9437188
  96.8 4.5 %collective-permute-start.14 = (f32[64,128]{1,0:T(8,128)S(1)}, f32[64,128]{1,0:T(8,128)S(1)}, u32[]{:S(2)}, u32[]{:S(2)}) collective-permute-start(f32[64,128]{1,0:T(8,128)S(1)} %get-tuple-element.94), channel_id=1, source_target_pairs={{0,16},{16,32},{32,48},{48,64},{64,80},{80,96},{96,112},{112,128},... | collective-permute-start | bytes 98312 | tf_op jit(solution)/shard_map/ppermute | solution.py:689
  96.9 4.6 %collective-permute-start.15 = (f32[64,128]{1,0:T(8,128)S(1)}, f32[64,128]{1,0:T(8,128)S(1)}, u32[]{:S(2)}, u32[]{:S(2)}) collective-permute-start(f32[64,128]{1,0:T(8,128)S(1)} %get-tuple-element.95), channel_id=1, source_target_pairs={{16,0},{32,16},{48,32},{64,48},{80,64},{96,80},{112,96},{128,112},... | collective-permute-start | bytes 98312 | tf_op jit(solution)/shard_map/ppermute | solution.py:689
  102.6 31.0 %all-to-all-start.1 = ((f32[32,8,128]{2,1,0:T(8,128)}), f32[32,8,128]{2,1,0:T(8,128)S(1)}, u32[]{:S(2)}, u32[]{:S(2)}) async-start(f32[32,8,128]{2,1,0:T(8,128)} %broadcast_in_dim.2), calls=%async_computation.1 | async-start | bytes 262144 | tf_op jit(solution)/shard_map/all_to_all | solution.py:778
  117.7 1.9 %copy-start.1 = (f32[4,1536,128]{2,1,0:T(8,128)S(1)}, f32[4,1536,128]{2,1,0:T(8,128)}, u32[]{:S(2)}) copy-start(f32[4,1536,128]{2,1,0:T(8,128)} %copy-done) | copy-start | bytes 9437188
  119.6 1.7 %copy-start.4 = (bf16[288,4608]{1,0:T(8,128)(2,1)S(1)}, bf16[288,4608]{1,0:T(8,128)(2,1)}, u32[]{:S(2)}) copy-start(bf16[288,4608]{1,0:T(8,128)(2,1)} %constant.20.clone.table_ref) | copy-start | bytes 7962628
  121.3 1.8 %copy-start.5 = (f32[192,192]{1,0:T(8,128)S(1)}, f32[192,192]{1,0:T(8,128)}, u32[]{:S(2)}) copy-start(f32[192,192]{1,0:T(8,128)} %constant.21.clone.table_ref) | copy-start | bytes 442372
  121.3 12.2 %copy-start.6 = (f32[6,6,192]{2,1,0:T(8,128)S(1)}, f32[6,6,192]{2,1,0:T(8,128)}, u32[]{:S(2)}) copy-start(f32[6,6,192]{2,1,0:T(8,128)} %rhs_ref.1) | copy-start | bytes 82948
